TPU v7x, 32 devices: a whole 2x2x4 slice. The times are simulated.
32 devices in a mesh: curve: 16 (over z, x, core), dp: 2 (over y).
Axes of the slice: x: 2, y: 2, z: 4, core: 2. Of those that a mesh axis runs over, the one named last changes fastest.
Arguments:
- points: bfloat16 [2, 8192, 512], P('dp', 'curve'), may hold values from -24 to 24
- grad_out: bfloat16 [2, 8192, 512], P('dp', 'curve'), may hold values from -6 to 6
- dest_dev: int32 [2, 8192], P('dp', 'curve'), may hold values from 0 to 15, as said below
- dest_row: int32 [2, 8192], P('dp', 'curve'), may hold values from 0 to 511
- w_qkv: bfloat16 [512, 1536], replicated, may hold values from -1 to 1
- w_out: bfloat16 [512, 512], replicated, may hold values from -0.25 to 0.25
Outputs:
- grad_points: bfloat16 [2, 8192, 512], P('dp', 'curve')
- grad_w_qkv: float32 [512, 1536], replicated
- grad_w_out: float32 [512, 512], replicated
Inputs may be any that keep to these rules, and one draw needn't show every extreme that they name: `dest_dev`: together with dest_row it maps each group's scan points one to one onto the 8192 curve positions: every curve device of a group receives exactly 512 points, at most 64 of them from one scan device, and in every draw some scan device sends exactly 64 points to some curve device.
All inputs are finite; a program needn't handle non-finite values.
Results may differ from a plain program's by a relative error of at most 0.011.
The roundings to bfloat16 on the way count: a program that leaves them out, or rounds other values in their place, can miss the bound.
Values may be sent and summed in bfloat16 or wider, within the bound.
No kernel may reach another device: no remote copies, remote signals or barrier semaphores. Data moves between devices by JAX's collectives and lax.ppermute only.
A program may use at most 64 MiB of HBM per device.

v0:
```python
import math

import jax
import jax.numpy as jnp
from jax import lax
from jax.sharding import PartitionSpec as P

HEADS = 8
PATCH = 512


def from_behind(block, axis, distance):
    devices = range(lax.axis_size(axis))
    route = [((i - distance) % len(devices), i) for i in devices]
    return lax.ppermute(block, axis, route)


def contract(left, right, left_dim, right_dim):
    return lax.dot_general(
        left, right, (((left_dim,), (right_dim,)), ((), ())), preferred_element_type=jnp.float32
    )


def attend_backward(queries, keys_vals, grad_rows):
    width = queries.shape[1]
    head_dim = width // HEADS
    scale = 1.0 / math.sqrt(head_dim)
    attn_list, query_list, key_list, value_list = ([], [], [], [])
    for head in range(HEADS):
        lower = head * head_dim
        upper = lower + head_dim
        query_part = queries[:, lower:upper]
        key_part = keys_vals[:, lower:upper]
        value_part = keys_vals[:, width + lower : width + upper]
        grad_part = grad_rows[:, lower:upper]
        scores = contract(query_part, key_part, 1, 1) * scale
        probs = jax.nn.softmax(scores, axis=-1)
        probs_low = probs.astype(jnp.bfloat16)
        attn_part = jnp.dot(probs_low, value_part, preferred_element_type=jnp.float32).astype(
            jnp.bfloat16
        )
        delta = jnp.sum(
            grad_part.astype(jnp.float32) * attn_part.astype(jnp.float32), axis=1, keepdims=True
        )
        value_list.append(contract(probs_low, grad_part, 0, 0))
        grad_probs = contract(grad_part, value_part, 1, 1)
        grad_scores = (probs * (grad_probs - delta)).astype(jnp.bfloat16)
        query_list.append(
            jnp.dot(grad_scores, key_part, preferred_element_type=jnp.float32) * scale
        )
        key_list.append(contract(grad_scores, query_part, 0, 0) * scale)
        attn_list.append(attn_part)
    attn = jnp.concatenate(attn_list, axis=1)
    grad_queries = jnp.concatenate(query_list, axis=1)
    grad_kv = jnp.concatenate(key_list + value_list, axis=1)
    return (attn, grad_queries, grad_kv)


def finish(point_rows, grad_rows, attn, grad_qkv, w_qkv):
    input_grads = contract(grad_qkv, w_qkv, 1, 1).astype(jnp.bfloat16)
    part_qkv = contract(point_rows, grad_qkv, 0, 0)
    part_out = contract(attn, grad_rows, 0, 0)
    return (input_grads, part_qkv, part_out)


def work_patches(point_rows, grad_rows, w_qkv, w_out):
    width = w_out.shape[0]
    qkv = jnp.dot(point_rows, w_qkv, preferred_element_type=jnp.float32).astype(jnp.bfloat16)
    grad_attn = contract(grad_rows, w_out, 1, 1).astype(jnp.bfloat16)
    attn_list, grad_list = ([], [])
    upper = PATCH
    attn, grad_queries, grad_kv = attend_backward(
        qkv[0:upper, :width], qkv[0:upper, width:], grad_attn
    )
    attn_list.append(attn)
    grad_list.append(jnp.concatenate([grad_queries, grad_kv], axis=1))
    attn_all = attn_list[0]
    grad_qkv = grad_list[0].astype(jnp.bfloat16)
    return finish(point_rows, grad_rows, attn_all, grad_qkv, w_qkv)


def slot_table(home_dev, n_dev, capacity):
    rows = home_dev.shape[0]
    onehot = (home_dev[:, None] == jnp.arange(n_dev, dtype=jnp.int32)[None, :]).astype(jnp.bfloat16)
    row_ids = jnp.arange(rows, dtype=jnp.int32)
    lower_tri = (row_ids[:, None] >= row_ids[None, :]).astype(jnp.bfloat16)
    running = jnp.dot(lower_tri, onehot, preferred_element_type=jnp.float32)
    rank = jnp.sum(running * onehot.astype(jnp.float32), axis=1).astype(jnp.int32) - 1
    return home_dev * capacity + rank


def pack_rows(slots, home_row, point_rows, grad_rows, n_dev, capacity):
    rows, width = point_rows.shape
    total = n_dev * capacity
    send_points = (
        jnp.zeros((total, width), jnp.bfloat16)
        .at[slots]
        .set(point_rows)
        .reshape(n_dev, capacity, width)
    )
    send_grads = (
        jnp.zeros((total, width), jnp.bfloat16)
        .at[slots]
        .set(grad_rows)
        .reshape(n_dev, capacity, width)
    )
    send_rows = jnp.full((total,), rows, jnp.int32).at[slots].set(home_row).reshape(n_dev, capacity)
    return (send_points, send_grads, send_rows)


def place_rows(got_values, got_rows, rows):
    width = got_values.shape[-1]
    return (
        jnp.zeros((rows, width), jnp.bfloat16)
        .at[got_rows.reshape(-1)]
        .set(got_values.reshape(-1, width), mode="drop")
    )


def pick_rows(values, got_rows):
    rows, width = values.shape
    taken = jnp.take(values, jnp.minimum(got_rows.reshape(-1), rows - 1), axis=0)
    return taken.reshape(got_rows.shape[0], got_rows.shape[1], width)


def on_device(points, grad_out, dest_dev, dest_row, w_qkv, w_out):
    point_rows = points[0]
    grad_rows = grad_out[0]
    device_of = dest_dev[0]
    row_of = dest_row[0]
    rows, width = point_rows.shape
    n_dev = lax.axis_size("curve")
    capacity = 2 * rows // n_dev
    shift_rows = PATCH // 2
    slots = slot_table(device_of, n_dev, capacity)
    send_points, send_grads, send_rows = pack_rows(
        slots, row_of, point_rows, grad_rows, n_dev, capacity
    )
    got_points, got_grads, got_rows = (
        lax.all_to_all(send_points, "curve", split_axis=0, concat_axis=0, tiled=True),
        lax.all_to_all(send_grads, "curve", split_axis=0, concat_axis=0, tiled=True),
        lax.all_to_all(send_rows, "curve", split_axis=0, concat_axis=0, tiled=True),
    )
    own_points = place_rows(got_points, got_rows, rows)
    own_grads = place_rows(got_grads, got_rows, rows)
    head_pair = jnp.stack([own_points[:shift_rows], own_grads[:shift_rows]])
    following = from_behind(head_pair, "curve", -1)
    work_points = jnp.concatenate([own_points[shift_rows:], following[0]], axis=0)
    work_grads = jnp.concatenate([own_grads[shift_rows:], following[1]], axis=0)
    work_input, part_qkv, part_out = work_patches(work_points, work_grads, w_qkv, w_out)
    earlier = from_behind(work_input[rows - shift_rows :], "curve", 1)
    own_input = jnp.concatenate([earlier, work_input[: rows - shift_rows]], axis=0)
    returned = lax.all_to_all(
        pick_rows(own_input, got_rows), "curve", split_axis=0, concat_axis=0, tiled=True
    )
    result_rows = returned.reshape(n_dev * capacity, width)[slots]
    weight_qkv, weight_out = lax.psum((part_qkv, part_out), ("curve", "dp"))
    return (result_rows[None], weight_qkv, weight_out)


def solution(mesh):
    placed = (
        P("dp", "curve", None),
        P("dp", "curve", None),
        P("dp", "curve"),
        P("dp", "curve"),
        P(),
        P(),
    )
    return jax.shard_map(
        on_device,
        mesh=mesh,
        in_specs=placed,
        out_specs=(P("dp", "curve", None), P(), P()),
        check_vma=False,
    )
```

profile of v0, /device:TPU:0, one launch (start us, length us, event | category | flops | bytes accessed | tf_op | source)
XLA Modules:
  0.0 300.7 jit_solution(17670964612221864438)
XLA Ops:
  7.2 1.1 fusion.56
  8.3 0.7 compare_select_fusion.3
  9.0 2.6 scatter_custom_fusion
  11.6 0.7 all_to_all.15
  12.3 7.4 %all-to-all-start = ((s32[16,1,64]{2,1,0:T(1,128)}), s32[16,1,64]{2,1,0:T(1,128)S(1)}, u32[]{:S(2)}, u32[]{:S(2)}) async-start(s32[16,1,64]{2,1,0:T(1,128)} %all_to_all.15), calls=%async_computation | async-start | bytes 16384 | tf_op jit(solution)/shard_map/all_to_all | solution.py:142
  19.6 4.0 %scatter_custom_fusion.3 = bf16[1024,512]{1,0:T(8,128)(2,1)} fusion(s32[512]{0:T(512)S(1)} %bitcast.81, bf16[1,512,512]{2,1,0:T(8,128)(2,1)} %param.7, bf16[]{:T(256)} %constant.18.clone.1), kind=kCustom, calls=%fused_computation.146 | custom fusion | bytes 1572866 | tf_op jit(solution)/shard_map/scatter | solution.py:104
  23.6 2.3 all-to-all-done
  25.9 3.7 %all-to-all-start.2 = ((bf16[16,64,512]{2,1,0:T(8,128)(2,1)}), bf16[16,64,512]{2,1,0:T(8,128)(2,1)S(1)}, u32[]{:S(2)}, u32[]{:S(2)}) async-start(bf16[16,64,512]{2,1,0:T(8,128)(2,1)} %bitcast.12), calls=%async_computation.2 | async-start | bytes 2097152 | tf_op jit(solution)/shard_map/all_to_all | solution.py:141
  29.6 3.5 %scatter_custom_fusion.1 = bf16[1024,512]{1,0:T(8,128)(2,1)} fusion(s32[512]{0:T(512)S(1)} %bitcast.82, bf16[1,512,512]{2,1,0:T(8,128)(2,1)S(1)} %copy-done.4, bf16[]{:T(256)} %constant.18.clone.1), kind=kCustom, calls=%fused_computation.148 | custom fusion | bytes 1572866 | tf_op jit(solution)/shard_map/scatter | solution.py:98
  33.1 19.5 %all-to-all-done.2 = bf16[16,64,512]{2,1,0:T(8,128)(2,1)S(1)} async-done(((bf16[16,64,512]{2,1,0:T(8,128)(2,1)}), bf16[16,64,512]{2,1,0:T(8,128)(2,1)S(1)}, u32[]{:S(2)}, u32[]{:S(2)}) %all-to-all-start.2) | async-done | bytes 1048608 | tf_op jit(solution)/shard_map/all_to_all | solution.py:141
  52.6 1.0 copy-done.2
  53.5 6.9 %all-to-all-start.1 = ((bf16[16,64,512]{2,1,0:T(8,128)(2,1)}), bf16[16,64,512]{2,1,0:T(8,128)(2,1)S(1)}, u32[]{:S(2)}, u32[]{:S(2)}) async-start(bf16[16,64,512]{2,1,0:T(8,128)(2,1)} %bitcast.8), calls=%async_computation.1 | async-start | bytes 2097152 | tf_op jit(solution)/shard_map/all_to_all | solution.py:140
  61.0 0.7 broadcast_minimum_fusion
  61.8 5.6 %scatter_custom_fusion.4 = bf16[512,512]{1,0:T(8,128)(2,1)S(1)} fusion(s32[1024]{0:T(1024)S(1)} %bitcast.85, bf16[1024,512]{1,0:T(8,128)(2,1)} %bitcast.76, bf16[]{:T(256)} %constant.18.clone.1), kind=kCustom, calls=%fused_computation.166 | custom fusion | bytes 524800 | tf_op jit(solution)/shard_map/scatter | solution.py:116
  67.4 0.7 fusion.166
  68.1 15.2 %all-to-all-done.1 = bf16[16,64,512]{2,1,0:T(8,128)(2,1)S(1)} async-done(((bf16[16,64,512]{2,1,0:T(8,128)(2,1)}), bf16[16,64,512]{2,1,0:T(8,128)(2,1)S(1)}, u32[]{:S(2)}, u32[]{:S(2)}) %all-to-all-start.1) | async-done | bytes 1048608 | tf_op jit(solution)/shard_map/all_to_all | solution.py:140
  83.4 5.1 %scatter_custom_fusion.2 = bf16[512,512]{1,0:T(8,128)(2,1)S(1)} fusion(s32[1024]{0:T(1024)S(1)} %bitcast.86, bf16[1024,512]{1,0:T(8,128)(2,1)S(1)} %bitcast.75, bf16[]{:T(256)} %constant.18.clone.1), kind=kCustom, calls=%fused_computation.168 | custom fusion | bytes 524290 | tf_op jit(solution)/shard_map/scatter | solution.py:116
  88.6 5.6 %collective-permute-start = (bf16[2,256,512]{2,1,0:T(8,128)(2,1)S(1)}, bf16[2,256,512]{2,1,0:T(8,128)(2,1)S(1)}, u32[]{:S(2)}, u32[]{:S(2)}) collective-permute-start(bf16[2,256,512]{2,1,0:T(8,128)(2,1)S(1)} %pad_maximum_fusion), channel_id=1, source_target_pairs={{2,0},{4,2},{6,4},{8,6},{10,8},{12,10},{14,12},{16,14},{18,16},{20... | collective-permute-start | bytes 1572872 | tf_op jit(solution)/shard_map/ppermute | solution.py:15
  94.2 6.7 %collective-permute-done = bf16[2,256,512]{2,1,0:T(8,128)(2,1)S(1)} collective-permute-done((bf16[2,256,512]{2,1,0:T(8,128)(2,1)S(1)}, bf16[2,256,512]{2,1,0:T(8,128)(2,1)S(1)}, u32[]{:S(2)}, u32[]{:S(2)}) %collective-permute-start) | collective-permute-done | bytes 524320 | tf_op jit(solution)/shard_map/ppermute | solution.py:15
  101.0 1.0 convolution_convert_fusion
  120.8 1.0 convolution_convert_fusion.1
  121.8 2.7 fusion.80
  124.7 1.4 fusion.79
  126.1 7.2 %collective-permute-done.1 = bf16[256,512]{1,0:T(8,128)(2,1)S(1)} collective-permute-done((bf16[256,512]{1,0:T(8,128)(2,1)S(1)}, bf16[256,512]{1,0:T(8,128)(2,1)S(1)}, u32[]{:S(2)}, u32[]{:S(2)}) %collective-permute-start.1) | collective-permute-done | bytes 262176 | tf_op jit(solution)/shard_map/ppermute | solution.py:15
  133.3 4.0 %gather_fusion = bf16[1024,512]{1,0:T(8,128)(2,1)S(1)} fusion(bf16[512,512]{1,0:T(8,128)(2,1)S(1)} %pad_maximum_fusion.3, s32[1024]{0:T(1024)S(1)} %broadcast_clamp_fusion), kind=kCustom, calls=%fused_computation | custom fusion | bytes 2101248 | tf_op jit(solution)/shard_map/jit(_take)/gather | solution.py:122
  137.3 1.2 broadcast_select_fusion
  138.5 3.7 %all-to-all-start.3 = ((bf16[16,64,512]{2,1,0:T(8,128)(2,1)}), bf16[16,64,512]{2,1,0:T(8,128)(2,1)S(1)}, u32[]{:S(2)}, u32[]{:S(2)}) async-start(bf16[16,64,512]{2,1,0:T(8,128)(2,1)} %broadcast_select_fusion), calls=%async_computation.3 | async-start | bytes 2097152 | tf_op jit(solution)/shard_map/all_to_all | solution.py:153
  142.2 33.3 %all-to-all-done.3 = bf16[16,64,512]{2,1,0:T(8,128)(2,1)S(1)} async-done(((bf16[16,64,512]{2,1,0:T(8,128)(2,1)}), bf16[16,64,512]{2,1,0:T(8,128)(2,1)S(1)}, u32[]{:S(2)}, u32[]{:S(2)}) %all-to-all-start.3) | async-done | bytes 1048608 | tf_op jit(solution)/shard_map/all_to_all | solution.py:153
  175.5 2.6 gather_fusion.1
  178.1 110.9 %all-reduce.3.cloned.1.call-done = (f32[512,1536]{1,0:T(8,128)}, f32[512,512]{1,0:T(8,128)}) async-done(((f32[512,1536]{1,0:T(8,128)}, f32[512,512]{1,0:T(8,128)}), (f32[512,1536]{1,0:T(8,128)}, f32[512,512]{1,0:T(8,128)})) %all-reduce.3.cloned.1.call-update) | async-done | bytes 4194320 | tf_op jit(solution)/shard_map/psum | solution.py:157
  289.1 3.8 %copy.73 = f32[512,1536]{1,0:T(8,128)} copy(f32[512,1536]{1,0:T(8,128)} %get-tuple-element.57) | data formatting | bytes 6291456
  292.9 1.0 copy.74
  (91 shorter events, 19.5 us)
Async XLA Ops:
  7.2 93.8 %copy-start = (bf16[512,1536]{1,0:T(8,128)(2,1)S(1)}, bf16[512,1536]{1,0:T(8,128)(2,1)}, u32[]{:S(2)}) copy-start(bf16[512,1536]{1,0:T(8,128)(2,1)} %param.10) | copy-start | bytes 4718596
  12.3 13.7 %all-to-all-start = ((s32[16,1,64]{2,1,0:T(1,128)}), s32[16,1,64]{2,1,0:T(1,128)S(1)}, u32[]{:S(2)}, u32[]{:S(2)}) async-start(s32[16,1,64]{2,1,0:T(1,128)} %all_to_all.15), calls=%async_computation | async-start | bytes 16384 | tf_op jit(solution)/shard_map/all_to_all | solution.py:142
  19.6 10.0 %copy-start.4 = (bf16[1,512,512]{2,1,0:T(8,128)(2,1)S(1)}, bf16[1,512,512]{2,1,0:T(8,128)(2,1)}, u32[]{:S(2)}) copy-start(bf16[1,512,512]{2,1,0:T(8,128)(2,1)} %param.6) | copy-start | bytes 1572868
  25.9 26.6 %all-to-all-start.2 = ((bf16[16,64,512]{2,1,0:T(8,128)(2,1)}), bf16[16,64,512]{2,1,0:T(8,128)(2,1)S(1)}, u32[]{:S(2)}, u32[]{:S(2)}) async-start(bf16[16,64,512]{2,1,0:T(8,128)(2,1)} %bitcast.12), calls=%async_computation.2 | async-start | bytes 2097152 | tf_op jit(solution)/shard_map/all_to_all | solution.py:141
  52.6 1.0 copy-start.2
  53.5 29.8 %all-to-all-start.1 = ((bf16[16,64,512]{2,1,0:T(8,128)(2,1)}), bf16[16,64,512]{2,1,0:T(8,128)(2,1)S(1)}, u32[]{:S(2)}, u32[]{:S(2)}) async-start(bf16[16,64,512]{2,1,0:T(8,128)(2,1)} %bitcast.8), calls=%async_computation.1 | async-start | bytes 2097152 | tf_op jit(solution)/shard_map/all_to_all | solution.py:140
  60.4 228.7 %all-reduce.3.cloned.1.call-start = ((), (), s32[]{:S(2)}) async-start(), calls=%async_computation.4 | async-start | bytes 8388608 | tf_op jit(solution)/shard_map/psum | solution.py:157
  88.6 12.3 %collective-permute-start = (bf16[2,256,512]{2,1,0:T(8,128)(2,1)S(1)}, bf16[2,256,512]{2,1,0:T(8,128)(2,1)S(1)}, u32[]{:S(2)}, u32[]{:S(2)}) collective-permute-start(bf16[2,256,512]{2,1,0:T(8,128)(2,1)S(1)} %pad_maximum_fusion), channel_id=1, source_target_pairs={{2,0},{4,2},{6,4},{8,6},{10,8},{12,10},{14,12},{16,14},{18,16},{20... | collective-permute-start | bytes 1572872 | tf_op jit(solution)/shard_map/ppermute | solution.py:15
  108.4 1.2 copy-start.3
  108.5 1.2 copy-start.5
  124.6 8.7 %collective-permute-start.1 = (bf16[256,512]{1,0:T(8,128)(2,1)S(1)}, bf16[256,512]{1,0:T(8,128)(2,1)S(1)}, u32[]{:S(2)}, u32[]{:S(2)}) collective-permute-start(bf16[256,512]{1,0:T(8,128)(2,1)S(1)} %get-tuple-element.13), channel_id=1, source_target_pairs={{30,0},{0,2},{2,4},{4,6},{6,8},{8,10},{10,12},{12,14},{14,16},{16,... | collective-permute-start | bytes 786440 | tf_op jit(solution)/shard_map/ppermute | solution.py:15
  138.5 37.0 %all-to-all-start.3 = ((bf16[16,64,512]{2,1,0:T(8,128)(2,1)}), bf16[16,64,512]{2,1,0:T(8,128)(2,1)S(1)}, u32[]{:S(2)}, u32[]{:S(2)}) async-start(bf16[16,64,512]{2,1,0:T(8,128)(2,1)} %broadcast_select_fusion), calls=%async_computation.3 | async-start | bytes 2097152 | tf_op jit(solution)/shard_map/all_to_all | solution.py:153
  289.1 3.8 %copy-start.1 = (f32[512,512]{1,0:T(8,128)S(1)}, f32[512,512]{1,0:T(8,128)}, u32[]{:S(2)}) copy-start(f32[512,512]{1,0:T(8,128)} %get-tuple-element.58) | copy-start | bytes 3145732
Sparse Core Ops, SparseCore 0:
  126.2 162.8 all-reduce.2
where the time goes:
time: 301 us
  waiting for transfers between devices  195 us (65%)
  local copies, waits for them, and re-layouts  35.3 us (12%)
  starting transfers between devices  27.3 us (9%)
  matrix products  23 us (8%)
  between operations  14.5 us (5%)
  other arithmetic  5.46 us (2%)
    psum x1, waiting for transfers between devices, on_device(): weight_qkv, weight_out = lax.psum((part_qkv, part_out), ('curve', 'dp'))  111 us
    all_to_all x1, waiting for transfers between devices, on_device(): lax.all_to_all(pick_rows(own_input, got_rows), 'curve', split_axis=0, con...  33.3 us
    all_to_all x1, waiting for transfers between devices, on_device(): lax.all_to_all(send_grads, 'curve', split_axis=0, concat_axis=0, tiled=True)  19.5 us
    dot_general x36, matrix products, contract(): lax.dot_general(left, right, (((left_dim,), (right_dim,)), ((), ())), pre...  16.3 us
    all_to_all x1, waiting for transfers between devices, on_device(): lax.all_to_all(send_points, 'curve', split_axis=0, concat_axis=0, tiled=T...  15.2 us
    ppermute x2, waiting for transfers between devices, from_behind(): return lax.ppermute(block, axis, route)  13.9 us
    scatter x2, local copies, waits for them, and re-layouts, place_rows(): return jnp.zeros((rows, width), jnp.bfloat16).at[got_rows.reshape(-1)].se...  10.8 us
    all_to_all x1, starting transfers between devices, on_device(): lax.all_to_all(send_rows, 'curve', split_axis=0, concat_axis=0, tiled=True)  7.36 us
  transfers between devices with their start and end apart: 7, of which 7 were waited for; matrix products, arithmetic and copies ran while one was open for 8% of the time, Pallas kernels for 0%

commit v1 on v0

--- a/solution.py
+++ b/solution.py
@@ -123,6 +123,77 @@
     return taken.reshape(got_rows.shape[0], got_rows.shape[1], width)
 
 
+def swap(block, axis, mask):
+    size = lax.axis_size(axis)
+    return lax.ppermute(block, axis, [(i, i ^ mask) for i in range(size)])
+
+
+def split_rows(rows, side):
+    half = rows.shape[0] // 2
+    keep = lax.dynamic_slice_in_dim(rows, side * half, half, 0)
+    send = lax.dynamic_slice_in_dim(rows, (1 - side) * half, half, 0)
+    return (keep, send.astype(jnp.bfloat16))
+
+
+def join_rows(own, got, side):
+    return jnp.concatenate([jnp.where(side == 0, own, got), jnp.where(side == 0, got, own)], axis=0)
+
+
+def order_blocks(blocks, place):
+    count = blocks.shape[0]
+    tail = blocks.shape[1:]
+    bit = 1
+    while bit < count:
+        pairs = blocks.reshape(count // (2 * bit), 2, bit, *tail)
+        blocks = jnp.where((place & bit) != 0, pairs[:, ::-1], pairs).reshape(count, *tail)
+        bit *= 2
+    return blocks
+
+
+def sum_devices(total):
+    me = lax.axis_index("curve")
+    n_line = lax.axis_size("curve") // 4
+    core, side_x, line, side_y = (me & 1, (me >> 1) & 1, me >> 2, lax.axis_index("dp"))
+    keep, send = split_rows(total, core)
+    part = keep + swap(send, "curve", 1).astype(jnp.float32)
+    half = part.shape[0] // 2
+    keep_a, send_a = split_rows(part[:half], side_x)
+    keep_b, send_b = split_rows(part[half:], side_y)
+    part_a = keep_a + swap(send_a, "curve", 2).astype(jnp.float32)
+    part_b = keep_b + swap(send_b, "dp", 1).astype(jnp.float32)
+    keep_a, send_a = split_rows(part_a, side_y)
+    keep_b, send_b = split_rows(part_b, side_x)
+    part_a = keep_a + swap(send_a, "dp", 1).astype(jnp.float32)
+    part_b = keep_b + swap(send_b, "curve", 2).astype(jnp.float32)
+    width = total.shape[1]
+    rows = part_a.shape[0] // n_line
+    both = jnp.stack([part_a.reshape(n_line, rows, width), part_b.reshape(n_line, rows, width)], axis=1)
+    mine = lax.dynamic_index_in_dim(both, line, 0, keepdims=False)
+    others = [
+        swap(
+            lax.dynamic_index_in_dim(both, line ^ k, 0, keepdims=False).astype(jnp.bfloat16),
+            "curve",
+            4 * k,
+        )
+        for k in range(1, n_line)
+    ]
+    for other in others:
+        mine = mine + other.astype(jnp.float32)
+    mine = mine.astype(jnp.bfloat16)
+    blocks = jnp.stack([mine] + [swap(mine, "curve", 4 * k) for k in range(1, n_line)])
+    blocks = order_blocks(blocks, line)
+    full_a = blocks[:, 0].reshape(n_line * rows, width)
+    full_b = blocks[:, 1].reshape(n_line * rows, width)
+    got_a = swap(full_a, "dp", 1)
+    got_b = swap(full_b, "curve", 2)
+    full_a = join_rows(full_a, got_a, side_y)
+    full_b = join_rows(full_b, got_b, side_x)
+    got_a = swap(full_a, "curve", 2)
+    got_b = swap(full_b, "dp", 1)
+    half_rows = jnp.concatenate([join_rows(full_a, got_a, side_x), join_rows(full_b, got_b, side_y)])
+    return join_rows(half_rows, swap(half_rows, "curve", 1), core).astype(jnp.float32)
+
+
 def on_device(points, grad_out, dest_dev, dest_row, w_qkv, w_out):
     point_rows = points[0]
     grad_rows = grad_out[0]
@@ -154,8 +225,9 @@
         pick_rows(own_input, got_rows), "curve", split_axis=0, concat_axis=0, tiled=True
     )
     result_rows = returned.reshape(n_dev * capacity, width)[slots]
-    weight_qkv, weight_out = lax.psum((part_qkv, part_out), ("curve", "dp"))
-    return (result_rows[None], weight_qkv, weight_out)
+    weights = sum_devices(jnp.concatenate([part_qkv, part_out], axis=1))
+    n_qkv = part_qkv.shape[1]
+    return (result_rows[None], weights[:, :n_qkv], weights[:, n_qkv:])
 
 
 def solution(mesh):

time: 301 us -> 209 us (0.69)
  waiting for transfers between devices: 195 us -> 85.8 us
  starting transfers between devices: 27.3 us -> 45 us
  between operations: 14.5 us -> 1.33 us
  other arithmetic: 5.46 us -> 18.1 us
    psum x1 -> x0, waiting for transfers between devices: 111 us -> none  [on_device(): weight_qkv, weight_out = lax.psum((part_qkv, part_out), ('curve', 'dp'))]
    ppermute x0 -> x16, waiting for transfers between devices: none -> 36.1 us  [swap(): return lax.ppermute(block, axis, [(i, i ^ mask) for i in range(size)])]
    all_to_all x1, waiting for transfers between devices: 33.3 us -> 3.07 us  [on_device(): lax.all_to_all(pick_rows(own_input, got_rows), 'curve', split_axis=0, con...]
    ppermute x0 -> x16, starting transfers between devices: none -> 18 us  [swap(): return lax.ppermute(block, axis, [(i, i ^ mask) for i in range(size)])]
    select_n x0 -> x5, other arithmetic: none -> 4.9 us  [the longest x4 4.85 us: join_rows(): jnp.where(side == 0, own, got)]
    ppermute x2, waiting for transfers between devices: 13.9 us -> 9.57 us  [from_behind(): return lax.ppermute(block, axis, route)]
  transfers between devices with their start and end apart: 7 -> 22, of which waited for: 7 -> 15; matrix products, arithmetic and copies ran while one was open for 8% -> 14% of each run, Pallas kernels for 0% -> 0%
where the time goes in v1:
time: 209 us; the launch traced here: 207 us
  waiting for transfers between devices  85.8 us (41%)
  starting transfers between devices  45 us (22%)
  local copies, waits for them, and re-layouts  36.7 us (18%)
  matrix products  20.3 us (10%)
  other arithmetic  18.1 us (9%)
    ppermute x16, waiting for transfers between devices, swap(): return lax.ppermute(block, axis, [(i, i ^ mask) for i in range(size)])  36.1 us
    all_to_all x1, waiting for transfers between devices, on_device(): lax.all_to_all(send_grads, 'curve', split_axis=0, concat_axis=0, tiled=True)  19.5 us
    ppermute x16, starting transfers between devices, swap(): return lax.ppermute(block, axis, [(i, i ^ mask) for i in range(size)])  18 us
    all_to_all x1, waiting for transfers between devices, on_device(): lax.all_to_all(send_points, 'curve', split_axis=0, concat_axis=0, tiled=T...  15.3 us
    dot_general x36, matrix products, contract(): lax.dot_general(left, right, (((left_dim,), (right_dim,)), ((), ())), pre...  13.6 us
    scatter x2, local copies, waits for them, and re-layouts, place_rows(): return jnp.zeros((rows, width), jnp.bfloat16).at[got_rows.reshape(-1)].se...  10.8 us
    ppermute x2, waiting for transfers between devices, from_behind(): return lax.ppermute(block, axis, route)  9.57 us
    all_to_all x1, starting transfers between devices, on_device(): lax.all_to_all(send_rows, 'curve', split_axis=0, concat_axis=0, tiled=True)  7.36 us
  transfers between devices with their start and end apart: 22, of which 15 were waited for; matrix products, arithmetic and copies ran while one was open for 14% of the time, Pallas kernels for 0%

profile of v1, /device:TPU:0, one launch (start us, length us, event | category | flops | bytes accessed | tf_op | source)
XLA Modules:
  0.0 207.3 jit_solution(14442567476846107130)
XLA Ops:
  2.4 2.6 %scatter_custom_fusion = s32[1024]{0:T(1024)S(1)} fusion(s32[512]{0:T(512)S(1)} %bitcast.139, s32[512]{0:T(512)} %bitcast.147, s32[]{:T(128)} %constant.20.clone.1), kind=kCustom, calls=%fused_computation.325 | custom fusion | bytes 4608 | tf_op jit(solution)/shard_map/scatter | solution.py:107
  5.7 7.4 %all-to-all-start = ((s32[16,1,64]{2,1,0:T(1,128)}), s32[16,1,64]{2,1,0:T(1,128)S(1)}, u32[]{:S(2)}, u32[]{:S(2)}) async-start(s32[16,1,64]{2,1,0:T(1,128)} %all_to_all.15), calls=%async_computation | async-start | bytes 16384 | tf_op jit(solution)/shard_map/all_to_all | solution.py:213
  13.1 4.0 %scatter_custom_fusion.3 = bf16[1024,512]{1,0:T(8,128)(2,1)} fusion(s32[512]{0:T(512)S(1)} %bitcast.140, bf16[1,512,512]{2,1,0:T(8,128)(2,1)} %param.7, bf16[]{:T(256)} %constant.27.clone.1), kind=kCustom, calls=%fused_computation.167 | custom fusion | bytes 1572866 | tf_op jit(solution)/shard_map/scatter | solution.py:104
  17.1 2.3 %all-to-all-done = s32[16,1,64]{2,1,0:T(1,128)S(1)} async-done(((s32[16,1,64]{2,1,0:T(1,128)}), s32[16,1,64]{2,1,0:T(1,128)S(1)}, u32[]{:S(2)}, u32[]{:S(2)}) %all-to-all-start) | async-done | bytes 4128 | tf_op jit(solution)/shard_map/all_to_all | solution.py:213
  19.4 3.7 %all-to-all-start.2 = ((bf16[16,64,512]{2,1,0:T(8,128)(2,1)}), bf16[16,64,512]{2,1,0:T(8,128)(2,1)S(1)}, u32[]{:S(2)}, u32[]{:S(2)}) async-start(bf16[16,64,512]{2,1,0:T(8,128)(2,1)} %bitcast.12), calls=%async_computation.2 | async-start | bytes 2097152 | tf_op jit(solution)/shard_map/all_to_all | solution.py:212
  23.1 3.5 %scatter_custom_fusion.1 = bf16[1024,512]{1,0:T(8,128)(2,1)} fusion(s32[512]{0:T(512)S(1)} %bitcast.141, bf16[1,512,512]{2,1,0:T(8,128)(2,1)S(1)} %copy-done.8, bf16[]{:T(256)} %constant.27.clone.1), kind=kCustom, calls=%fused_computation.169 | custom fusion | bytes 1572866 | tf_op jit(solution)/shard_map/scatter | solution.py:98
  26.6 19.5 %all-to-all-done.2 = bf16[16,64,512]{2,1,0:T(8,128)(2,1)S(1)} async-done(((bf16[16,64,512]{2,1,0:T(8,128)(2,1)}), bf16[16,64,512]{2,1,0:T(8,128)(2,1)S(1)}, u32[]{:S(2)}, u32[]{:S(2)}) %all-to-all-start.2) | async-done | bytes 1048608 | tf_op jit(solution)/shard_map/all_to_all | solution.py:212
  47.0 6.9 %all-to-all-start.1 = ((bf16[16,64,512]{2,1,0:T(8,128)(2,1)}), bf16[16,64,512]{2,1,0:T(8,128)(2,1)S(1)}, u32[]{:S(2)}, u32[]{:S(2)}) async-start(bf16[16,64,512]{2,1,0:T(8,128)(2,1)} %bitcast.8), calls=%async_computation.1 | async-start | bytes 2097152 | tf_op jit(solution)/shard_map/all_to_all | solution.py:211
  55.2 5.6 %scatter_custom_fusion.4 = bf16[512,512]{1,0:T(8,128)(2,1)S(1)} fusion(s32[1024]{0:T(1024)S(1)} %bitcast.144, bf16[1024,512]{1,0:T(8,128)(2,1)} %bitcast.131, bf16[]{:T(256)} %constant.27.clone.1), kind=kCustom, calls=%fused_computation.201 | custom fusion | bytes 524800 | tf_op jit(solution)/shard_map/scatter | solution.py:116
  61.5 15.3 %all-to-all-done.1 = bf16[16,64,512]{2,1,0:T(8,128)(2,1)S(1)} async-done(((bf16[16,64,512]{2,1,0:T(8,128)(2,1)}), bf16[16,64,512]{2,1,0:T(8,128)(2,1)S(1)}, u32[]{:S(2)}, u32[]{:S(2)}) %all-to-all-start.1) | async-done | bytes 1048608 | tf_op jit(solution)/shard_map/all_to_all | solution.py:211
  76.8 5.1 %scatter_custom_fusion.2 = bf16[512,512]{1,0:T(8,128)(2,1)S(1)} fusion(s32[1024]{0:T(1024)S(1)} %bitcast.145, bf16[1024,512]{1,0:T(8,128)(2,1)S(1)} %bitcast.130, bf16[]{:T(256)} %constant.27.clone.1), kind=kCustom, calls=%fused_computation.203 | custom fusion | bytes 524290 | tf_op jit(solution)/shard_map/scatter | solution.py:116
  82.9 5.4 %collective-permute-start = (bf16[2,256,512]{2,1,0:T(8,128)(2,1)}, bf16[2,256,512]{2,1,0:T(8,128)(2,1)S(1)}, u32[]{:S(2)}, u32[]{:S(2)}) collective-permute-start(bf16[2,256,512]{2,1,0:T(8,128)(2,1)} %pad_maximum_fusion.1), channel_id=1, source_target_pairs={{2,0},{4,2},{6,4},{8,6},{10,8},{12,10},{14,12},{16,14},{18,16},{20... | collective-permute-start | bytes 1572872 | tf_op jit(solution)/shard_map/ppermute | solution.py:15
  88.2 7.0 %collective-permute-done = bf16[2,256,512]{2,1,0:T(8,128)(2,1)S(1)} collective-permute-done((bf16[2,256,512]{2,1,0:T(8,128)(2,1)}, bf16[2,256,512]{2,1,0:T(8,128)(2,1)S(1)}, u32[]{:S(2)}, u32[]{:S(2)}) %collective-permute-start) | collective-permute-done | bytes 524320 | tf_op jit(solution)/shard_map/ppermute | solution.py:15
  119.8 3.0 %collective-permute-done.2 = bf16[256,2048]{1,0:T(8,128)(2,1)} collective-permute-done((bf16[256,2048]{1,0:T(8,128)(2,1)}, bf16[256,2048]{1,0:T(8,128)(2,1)}, u32[]{:S(2)}, u32[]{:S(2)}) %collective-permute-start.2) | collective-permute-done | bytes 1048608 | tf_op jit(solution)/shard_map/ppermute | solution.py:128
  122.8 2.0 fusion.3
  126.7 6.7 %collective-permute-done.3 = bf16[64,2048]{1,0:T(8,128)(2,1)S(1)} collective-permute-done((bf16[64,2048]{1,0:T(8,128)(2,1)S(1)}, bf16[64,2048]{1,0:T(8,128)(2,1)S(1)}, u32[]{:S(2)}, u32[]{:S(2)}) %collective-permute-start.3) | collective-permute-done | bytes 262176 | tf_op jit(solution)/shard_map/ppermute | solution.py:128
  135.5 3.0 %collective-permute-done.4 = bf16[32,2048]{1,0:T(8,128)(2,1)S(1)} collective-permute-done((bf16[32,2048]{1,0:T(8,128)(2,1)S(1)}, bf16[32,2048]{1,0:T(8,128)(2,1)S(1)}, u32[]{:S(2)}, u32[]{:S(2)}) %collective-permute-start.4) | collective-permute-done | bytes 131104 | tf_op jit(solution)/shard_map/ppermute | solution.py:128
  138.5 1.7 collective-permute-done.6
  141.2 3.2 %collective-permute-start.8 = (bf16[2,8,2048]{2,1,0:T(8,128)(2,1)S(1)}, bf16[2,8,2048]{2,1,0:T(8,128)(2,1)S(1)}, u32[]{:S(2)}, u32[]{:S(2)}) collective-permute-start(bf16[2,8,2048]{2,1,0:T(8,128)(2,1)S(1)} %get-tuple-element.20), channel_id=1, source_target_pairs={{0,16},{2,18},{4,20},{6,22},{8,24},{10,26},{12,28},{14,30},{16,0},... | collective-permute-start | bytes 196616 | tf_op jit(solution)/shard_map/ppermute | solution.py:128
  145.7 2.4 %collective-permute-done.8 = bf16[2,8,2048]{2,1,0:T(8,128)(2,1)S(1)} collective-permute-done((bf16[2,8,2048]{2,1,0:T(8,128)(2,1)S(1)}, bf16[2,8,2048]{2,1,0:T(8,128)(2,1)S(1)}, u32[]{:S(2)}, u32[]{:S(2)}) %collective-permute-start.8) | collective-permute-done | bytes 65568 | tf_op jit(solution)/shard_map/ppermute | solution.py:128
  148.1 2.4 %collective-permute-done.9 = bf16[2,8,2048]{2,1,0:T(8,128)(2,1)S(1)} collective-permute-done((bf16[2,8,2048]{2,1,0:T(8,128)(2,1)S(1)}, bf16[2,8,2048]{2,1,0:T(8,128)(2,1)S(1)}, u32[]{:S(2)}, u32[]{:S(2)}) %collective-permute-start.9) | collective-permute-done | bytes 65568 | tf_op jit(solution)/shard_map/ppermute | solution.py:128
  151.4 3.6 %collective-permute-start.10 = (bf16[2,8,2048]{2,1,0:T(8,128)(2,1)S(1)}, bf16[2,8,2048]{2,1,0:T(8,128)(2,1)S(1)}, u32[]{:S(2)}, u32[]{:S(2)}) collective-permute-start(bf16[2,8,2048]{2,1,0:T(8,128)(2,1)S(1)} %fusion.105), channel_id=1, source_target_pairs={{0,8},{2,10},{4,12},{6,14},{8,0},{10,2},{12,4},{14,6},{16,24},{18,... | collective-permute-start | bytes 196616 | tf_op jit(solution)/shard_map/ppermute | solution.py:128
  155.1 1.7 collective-permute-done.12
  161.1 2.6 %collective-permute-done.1 = bf16[256,512]{1,0:T(8,128)(2,1)S(1)} collective-permute-done((bf16[256,512]{1,0:T(8,128)(2,1)S(1)}, bf16[256,512]{1,0:T(8,128)(2,1)S(1)}, u32[]{:S(2)}, u32[]{:S(2)}) %collective-permute-start.1) | collective-permute-done | bytes 262176 | tf_op jit(solution)/shard_map/ppermute | solution.py:15
  163.7 4.0 %gather_fusion = bf16[1024,512]{1,0:T(8,128)(2,1)S(1)} fusion(bf16[512,512]{1,0:T(8,128)(2,1)S(1)} %pad_maximum_fusion.4, s32[1024]{0:T(1024)S(1)} %broadcast_clamp_fusion), kind=kCustom, calls=%fused_computation | custom fusion | bytes 2101248 | tf_op jit(solution)/shard_map/jit(_take)/gather | solution.py:122
  172.7 3.7 %all-to-all-start.3 = ((bf16[16,64,512]{2,1,0:T(8,128)(2,1)}), bf16[16,64,512]{2,1,0:T(8,128)(2,1)S(1)}, u32[]{:S(2)}, u32[]{:S(2)}) async-start(bf16[16,64,512]{2,1,0:T(8,128)(2,1)} %broadcast_select_fusion.2), calls=%async_computation.3 | async-start | bytes 2097152 | tf_op jit(solution)/shard_map/all_to_all | solution.py:224
  176.4 1.9 collective-permute-start.14
  179.3 14.1 %collective-permute-done.14 = bf16[64,2048]{1,0:T(8,128)(2,1)S(1)} collective-permute-done((bf16[64,2048]{1,0:T(8,128)(2,1)S(1)}, bf16[64,2048]{1,0:T(8,128)(2,1)S(1)}, u32[]{:S(2)}, u32[]{:S(2)}) %collective-permute-start.14) | collective-permute-done | bytes 262176 | tf_op jit(solution)/shard_map/ppermute | solution.py:128
  196.2 3.1 %all-to-all-done.3 = bf16[16,64,512]{2,1,0:T(8,128)(2,1)S(1)} async-done(((bf16[16,64,512]{2,1,0:T(8,128)(2,1)}), bf16[16,64,512]{2,1,0:T(8,128)(2,1)S(1)}, u32[]{:S(2)}, u32[]{:S(2)}) %all-to-all-start.3) | async-done | bytes 1048608 | tf_op jit(solution)/shard_map/all_to_all | solution.py:224
  199.3 2.6 %gather_fusion.1 = bf16[512,512]{1,0:T(8,128)(2,1)} fusion(bf16[1024,512]{1,0:T(8,128)(2,1)S(1)} %bitcast.125, s32[1024]{0:T(1024)S(1)} %pad_clamp_fusion), kind=kCustom, calls=%fused_computation.1 | custom fusion | bytes 1050624 | tf_op jit(solution)/shard_map/gather | solution.py:227
  201.9 1.8 broadcast_select_fusion.1
  205.3 2.0 slice.258
  (156 shorter events, 52.6 us)
Async XLA Ops:
  0.6 94.7 %copy-start = (bf16[512,1536]{1,0:T(8,128)(2,1)S(1)}, bf16[512,1536]{1,0:T(8,128)(2,1)}, u32[]{:S(2)}) copy-start(bf16[512,1536]{1,0:T(8,128)(2,1)} %param.10) | copy-start | bytes 4718596
  5.7 13.7 %all-to-all-start = ((s32[16,1,64]{2,1,0:T(1,128)}), s32[16,1,64]{2,1,0:T(1,128)S(1)}, u32[]{:S(2)}, u32[]{:S(2)}) async-start(s32[16,1,64]{2,1,0:T(1,128)} %all_to_all.15), calls=%async_computation | async-start | bytes 16384 | tf_op jit(solution)/shard_map/all_to_all | solution.py:213
  13.1 10.0 %copy-start.8 = (bf16[1,512,512]{2,1,0:T(8,128)(2,1)S(1)}, bf16[1,512,512]{2,1,0:T(8,128)(2,1)}, u32[]{:S(2)}) copy-start(bf16[1,512,512]{2,1,0:T(8,128)(2,1)} %param.6) | copy-start | bytes 1572868
  19.4 26.6 %all-to-all-start.2 = ((bf16[16,64,512]{2,1,0:T(8,128)(2,1)}), bf16[16,64,512]{2,1,0:T(8,128)(2,1)S(1)}, u32[]{:S(2)}, u32[]{:S(2)}) async-start(bf16[16,64,512]{2,1,0:T(8,128)(2,1)} %bitcast.12), calls=%async_computation.2 | async-start | bytes 2097152 | tf_op jit(solution)/shard_map/all_to_all | solution.py:212
  46.0 1.0 copy-start.6
  47.0 29.8 %all-to-all-start.1 = ((bf16[16,64,512]{2,1,0:T(8,128)(2,1)}), bf16[16,64,512]{2,1,0:T(8,128)(2,1)S(1)}, u32[]{:S(2)}, u32[]{:S(2)}) async-start(bf16[16,64,512]{2,1,0:T(8,128)(2,1)} %bitcast.8), calls=%async_computation.1 | async-start | bytes 2097152 | tf_op jit(solution)/shard_map/all_to_all | solution.py:211
  82.9 12.4 %collective-permute-start = (bf16[2,256,512]{2,1,0:T(8,128)(2,1)}, bf16[2,256,512]{2,1,0:T(8,128)(2,1)S(1)}, u32[]{:S(2)}, u32[]{:S(2)}) collective-permute-start(bf16[2,256,512]{2,1,0:T(8,128)(2,1)} %pad_maximum_fusion.1), channel_id=1, source_target_pairs={{2,0},{4,2},{6,4},{8,6},{10,8},{12,10},{14,12},{16,14},{18,16},{20... | collective-permute-start | bytes 1572872 | tf_op jit(solution)/shard_map/ppermute | solution.py:15
  102.8 1.2 copy-start.7
  102.8 1.2 copy-start.10
  115.5 1.2 copy-start.3
  117.7 2.0 copy-start.1
  119.8 3.0 %collective-permute-start.2 = (bf16[256,2048]{1,0:T(8,128)(2,1)}, bf16[256,2048]{1,0:T(8,128)(2,1)}, u32[]{:S(2)}, u32[]{:S(2)}) collective-permute-start(bf16[256,2048]{1,0:T(8,128)(2,1)} %fusion.1), channel_id=1, source_target_pairs={{0,2},{2,0},{4,6},{6,4},{8,10},{10,8},{12,14},{14,12},{16,18},{18,... | collective-permute-start | bytes 3145736 | tf_op jit(solution)/shard_map/ppermute | solution.py:128
  124.9 8.4 %collective-permute-start.3 = (bf16[64,2048]{1,0:T(8,128)(2,1)S(1)}, bf16[64,2048]{1,0:T(8,128)(2,1)S(1)}, u32[]{:S(2)}, u32[]{:S(2)}) collective-permute-start(bf16[64,2048]{1,0:T(8,128)(2,1)S(1)} %dynamic-slice_convert_fusion.1), channel_id=1, source_target_pairs={{0,4},{2,6},{4,0},{6,2},{8,12},{10,14},{12,8},{14,10},{16,20},{18,... | collective-permute-start | bytes 786440 | tf_op jit(solution)/shard_map/ppermute | solution.py:128
  125.1 10.0 %collective-permute-start.5 = (bf16[64,2048]{1,0:T(8,128)(2,1)S(1)}, bf16[64,2048]{1,0:T(8,128)(2,1)S(1)}, u32[]{:S(2)}, u32[]{:S(2)}) collective-permute-start(bf16[64,2048]{1,0:T(8,128)(2,1)S(1)} %dynamic-slice_convert_fusion), channel_id=1, source_target_pairs={{0,1},{1,0},{2,3},{3,2},{4,5},{5,4},{6,7},{7,6},{8,9},{9,8},{10,11... | collective-permute-start | bytes 786440 | tf_op jit(solution)/shard_map/ppermute | solution.py:128
  133.4 11.3 %copy-start.4 = (bf16[512,1536]{0,1:T(8,128)(2,1)S(1)}, bf16[512,1536]{0,1:T(8,128)(2,1)}, u32[]{:S(2)}) copy-start(bf16[512,1536]{0,1:T(8,128)(2,1)} %copy-done.3) | copy-start | bytes 4718596
  133.5 5.0 %collective-permute-start.4 = (bf16[32,2048]{1,0:T(8,128)(2,1)S(1)}, bf16[32,2048]{1,0:T(8,128)(2,1)S(1)}, u32[]{:S(2)}, u32[]{:S(2)}) collective-permute-start(bf16[32,2048]{1,0:T(8,128)(2,1)S(1)} %dynamic-slice_convert_fusion.3), channel_id=1, source_target_pairs={{0,1},{1,0},{2,3},{3,2},{4,5},{5,4},{6,7},{7,6},{8,9},{9,8},{10,11... | collective-permute-start | bytes 393224 | tf_op jit(solution)/shard_map/ppermute | solution.py:128
  135.1 5.0 %collective-permute-start.6 = (bf16[32,2048]{1,0:T(8,128)(2,1)S(1)}, bf16[32,2048]{1,0:T(8,128)(2,1)S(1)}, u32[]{:S(2)}, u32[]{:S(2)}) collective-permute-start(bf16[32,2048]{1,0:T(8,128)(2,1)S(1)} %dynamic-slice_convert_fusion.2), channel_id=1, source_target_pairs={{0,4},{2,6},{4,0},{6,2},{8,12},{10,14},{12,8},{14,10},{16,20},{18,... | collective-permute-start | bytes 393224 | tf_op jit(solution)/shard_map/ppermute | solution.py:128
  140.2 5.5 %collective-permute-start.7 = (bf16[2,8,2048]{2,1,0:T(8,128)(2,1)S(1)}, bf16[2,8,2048]{2,1,0:T(8,128)(2,1)S(1)}, u32[]{:S(2)}, u32[]{:S(2)}) collective-permute-start(bf16[2,8,2048]{2,1,0:T(8,128)(2,1)S(1)} %get-tuple-element.19), channel_id=1, source_target_pairs={{0,8},{2,10},{4,12},{6,14},{8,0},{10,2},{12,4},{14,6},{16,24},{18,... | collective-permute-start | bytes 196616 | tf_op jit(solution)/shard_map/ppermute | solution.py:128
  141.2 6.9 %collective-permute-start.8 = (bf16[2,8,2048]{2,1,0:T(8,128)(2,1)S(1)}, bf16[2,8,2048]{2,1,0:T(8,128)(2,1)S(1)}, u32[]{:S(2)}, u32[]{:S(2)}) collective-permute-start(bf16[2,8,2048]{2,1,0:T(8,128)(2,1)S(1)} %get-tuple-element.20), channel_id=1, source_target_pairs={{0,16},{2,18},{4,20},{6,22},{8,24},{10,26},{12,28},{14,30},{16,0},... | collective-permute-start | bytes 196616 | tf_op jit(solution)/shard_map/ppermute | solution.py:128
  144.5 6.1 %collective-permute-start.9 = (bf16[2,8,2048]{2,1,0:T(8,128)(2,1)S(1)}, bf16[2,8,2048]{2,1,0:T(8,128)(2,1)S(1)}, u32[]{:S(2)}, u32[]{:S(2)}) collective-permute-start(bf16[2,8,2048]{2,1,0:T(8,128)(2,1)S(1)} %get-tuple-element.21), channel_id=1, source_target_pairs={{0,24},{2,26},{4,28},{6,30},{8,16},{10,18},{12,20},{14,22},{16,8},... | collective-permute-start | bytes 196616 | tf_op jit(solution)/shard_map/ppermute | solution.py:128
  150.6 6.3 %collective-permute-start.12 = (bf16[2,8,2048]{2,1,0:T(8,128)(2,1)S(1)}, bf16[2,8,2048]{2,1,0:T(8,128)(2,1)S(1)}, u32[]{:S(2)}, u32[]{:S(2)}) collective-permute-start(bf16[2,8,2048]{2,1,0:T(8,128)(2,1)S(1)} %fusion.105), channel_id=1, source_target_pairs={{0,24},{2,26},{4,28},{6,30},{8,16},{10,18},{12,20},{14,22},{16,8},... | collective-permute-start | bytes 196616 | tf_op jit(solution)/shard_map/ppermute | solution.py:128
  151.4 6.6 %collective-permute-start.11 = (bf16[2,8,2048]{2,1,0:T(8,128)(2,1)S(1)}, bf16[2,8,2048]{2,1,0:T(8,128)(2,1)S(1)}, u32[]{:S(2)}, u32[]{:S(2)}) collective-permute-start(bf16[2,8,2048]{2,1,0:T(8,128)(2,1)S(1)} %fusion.105), channel_id=1, source_target_pairs={{0,16},{2,18},{4,20},{6,22},{8,24},{10,26},{12,28},{14,30},{16,0},... | collective-permute-start | bytes 196616 | tf_op jit(solution)/shard_map/ppermute | solution.py:128
  151.4 6.6 %collective-permute-start.10 = (bf16[2,8,2048]{2,1,0:T(8,128)(2,1)S(1)}, bf16[2,8,2048]{2,1,0:T(8,128)(2,1)S(1)}, u32[]{:S(2)}, u32[]{:S(2)}) collective-permute-start(bf16[2,8,2048]{2,1,0:T(8,128)(2,1)S(1)} %fusion.105), channel_id=1, source_target_pairs={{0,8},{2,10},{4,12},{6,14},{8,0},{10,2},{12,4},{14,6},{16,24},{18,... | collective-permute-start | bytes 196616 | tf_op jit(solution)/shard_map/ppermute | solution.py:128
  155.0 8.7 %collective-permute-start.1 = (bf16[256,512]{1,0:T(8,128)(2,1)S(1)}, bf16[256,512]{1,0:T(8,128)(2,1)S(1)}, u32[]{:S(2)}, u32[]{:S(2)}) collective-permute-start(bf16[256,512]{1,0:T(8,128)(2,1)S(1)} %get-tuple-element.22), channel_id=1, source_target_pairs={{30,0},{0,2},{2,4},{4,6},{6,8},{8,10},{10,12},{12,14},{14,16},{16,... | collective-permute-start | bytes 786440 | tf_op jit(solution)/shard_map/ppermute | solution.py:15
  158.9 8.8 %collective-permute-start.13 = (bf16[32,2048]{1,0:T(8,128)(2,1)}, bf16[32,2048]{1,0:T(8,128)(2,1)S(1)}, u32[]{:S(2)}, u32[]{:S(2)}) collective-permute-start(bf16[32,2048]{1,0:T(8,128)(2,1)} %get-tuple-element.36), channel_id=1, source_target_pairs={{0,1},{1,0},{2,3},{3,2},{4,5},{5,4},{6,7},{7,6},{8,9},{9,8},{10,11... | collective-permute-start | bytes 393224 | tf_op jit(solution)/shard_map/ppermute | solution.py:128
  160.3 8.1 %collective-permute-start.15 = (bf16[32,2048]{1,0:T(8,128)(2,1)}, bf16[32,2048]{1,0:T(8,128)(2,1)}, u32[]{:S(2)}, u32[]{:S(2)}) collective-permute-start(bf16[32,2048]{1,0:T(8,128)(2,1)} %get-tuple-element.37), channel_id=1, source_target_pairs={{0,4},{2,6},{4,0},{6,2},{8,12},{10,14},{12,8},{14,10},{16,20},{18,... | collective-permute-start | bytes 393224 | tf_op jit(solution)/shard_map/ppermute | solution.py:128
  169.4 8.9 %copy-start.5 = (bf16[32,2048]{1,0:T(8,128)(2,1)}, bf16[32,2048]{1,0:T(8,128)(2,1)S(1)}, u32[]{:S(2)}) copy-start(bf16[32,2048]{1,0:T(8,128)(2,1)S(1)} %get-tuple-element.31) | copy-start | bytes 393220
  170.1 8.1 %collective-permute-start.16 = (bf16[64,2048]{1,0:T(8,128)(2,1)}, bf16[64,2048]{1,0:T(8,128)(2,1)}, u32[]{:S(2)}, u32[]{:S(2)}) collective-permute-start(bf16[64,2048]{1,0:T(8,128)(2,1)} %pad_maximum_fusion.11), channel_id=1, source_target_pairs={{0,1},{1,0},{2,3},{3,2},{4,5},{5,4},{6,7},{7,6},{8,9},{9,8},{10,11... | collective-permute-start | bytes 786440 | tf_op jit(solution)/shard_map/ppermute | solution.py:128
  172.7 26.6 %all-to-all-start.3 = ((bf16[16,64,512]{2,1,0:T(8,128)(2,1)}), bf16[16,64,512]{2,1,0:T(8,128)(2,1)S(1)}, u32[]{:S(2)}, u32[]{:S(2)}) async-start(bf16[16,64,512]{2,1,0:T(8,128)(2,1)} %broadcast_select_fusion.2), calls=%async_computation.3 | async-start | bytes 2097152 | tf_op jit(solution)/shard_map/all_to_all | solution.py:224
  176.4 17.0 %collective-permute-start.14 = (bf16[64,2048]{1,0:T(8,128)(2,1)S(1)}, bf16[64,2048]{1,0:T(8,128)(2,1)S(1)}, u32[]{:S(2)}, u32[]{:S(2)}) collective-permute-start(bf16[64,2048]{1,0:T(8,128)(2,1)S(1)} %pad_maximum_fusion.10), channel_id=1, source_target_pairs={{0,4},{2,6},{4,0},{6,2},{8,12},{10,14},{12,8},{14,10},{16,20},{18,... | collective-permute-start | bytes 786440 | tf_op jit(solution)/shard_map/ppermute | solution.py:128
  194.4 0.7 copy-start.2
  196.2 5.7 %collective-permute-start.17 = (bf16[256,2048]{1,0:T(8,128)(2,1)}, bf16[256,2048]{1,0:T(8,128)(2,1)}, u32[]{:S(2)}, u32[]{:S(2)}) collective-permute-start(bf16[256,2048]{1,0:T(8,128)(2,1)} %pad_maximum_fusion), channel_id=1, source_target_pairs={{0,2},{2,0},{4,6},{6,4},{8,10},{10,8},{12,14},{14,12},{16,18},{18,... | collective-permute-start | bytes 3145736 | tf_op jit(solution)/shard_map/ppermute | solution.py:128
  (1 other events, 0.7 us)

commit v2 on v1

v2 whole, which is shorter than its diff:
```python
import functools
import math

import jax
import jax.numpy as jnp
from jax import lax
from jax.experimental import pallas as pl
from jax.experimental.pallas import tpu as pltpu
from jax.sharding import PartitionSpec as P

HEADS = 8
PATCH = 512
INFO_ROWS = 8
LANES = 128


def from_behind(block, axis, distance):
    devices = range(lax.axis_size(axis))
    route = [((i - distance) % len(devices), i) for i in devices]
    return lax.ppermute(block, axis, route)


def contract(left, right, left_dim, right_dim):
    return lax.dot_general(
        left, right, (((left_dim,), (right_dim,)), ((), ())), preferred_element_type=jnp.float32
    )


def iota(shape, dim):
    return lax.broadcasted_iota(jnp.int32, shape, dim)


def hot(mask):
    return jnp.where(mask, 1.0, 0.0).astype(jnp.bfloat16)


def call(kernel, outs, args, flops, scalars=0):
    moved = sum(math.prod(x.shape) * x.dtype.itemsize for x in (*outs, *args))
    smem = [pl.BlockSpec(memory_space=pltpu.SMEM)] * scalars
    vmem = [pl.BlockSpec(memory_space=pltpu.VMEM)] * (len(args) - scalars)
    return pl.pallas_call(
        kernel,
        out_shape=outs,
        in_specs=smem + vmem,
        out_specs=[pl.BlockSpec(memory_space=pltpu.VMEM)] * len(outs),
        compiler_params=pltpu.CompilerParams(vmem_limit_bytes=40 * 2**20),
        cost_estimate=pl.CostEstimate(flops=flops, bytes_accessed=moved, transcendentals=0),
    )(*args)


def low(*shape):
    return jax.ShapeDtypeStruct(shape, jnp.bfloat16)


def pack_points_kernel(dev_ref, row_ref, x_ref, out_ref, slots_ref):
    n_dev, block, width = out_ref.shape
    cap = block - INFO_ROWS
    rows = x_ref.shape[0]
    dev = dev_ref[...]
    mine = iota((n_dev, rows), 0) == dev
    mine_f = jnp.where(mine, 1.0, 0.0)
    upto = hot(iota((rows, rows), 0) <= iota((rows, rows), 1))
    running = contract(mine_f.astype(jnp.bfloat16), upto, 1, 0)
    rank = (jnp.sum(running * mine_f, axis=0, keepdims=True) - 1.0).astype(jnp.int32)
    slots = dev * cap + rank
    slots_ref[...] = slots
    at_rank = hot(iota((LANES, rows), 0) % cap == rank)
    centred = (row_ref[...] - rows // 2).astype(jnp.float32)
    told = jnp.concatenate([mine_f * centred, mine_f], axis=0).astype(jnp.bfloat16)
    got = contract(told, at_rank, 1, 1)
    info = jnp.where(got[n_dev:] > 0.5, got[:n_dev], float(rows))
    per = 256 // cap
    for first in range(0, n_dev, per):
        pick = hot(iota((per * cap, rows), 0) + first * cap == slots)
        data = contract(pick, x_ref[...], 1, 0)
        for j in range(per):
            dest = first + j
            extra = jnp.broadcast_to(info[dest : dest + 1], (INFO_ROWS, LANES))
            extra = jnp.concatenate(
                [extra, jnp.zeros((INFO_ROWS, width - LANES), jnp.float32)], axis=1
            )
            out_ref[dest] = jnp.concatenate(
                [data[j * cap : (j + 1) * cap], extra], axis=0
            ).astype(jnp.bfloat16)


def pack_grads_kernel(slots_ref, x_ref, out_ref, back_ref):
    total = out_ref.shape[0]
    rows = x_ref.shape[0]
    pick = jnp.where(iota((total, rows), 0) == slots_ref[...], 1.0, 0.0)
    out_ref[...] = contract(pick.astype(jnp.bfloat16), x_ref[...], 1, 0).astype(jnp.bfloat16)
    back_ref[...] = pick.T.astype(jnp.bfloat16)


def place_points_kernel(got_ref, head_ref, tail_ref, table_ref, back_ref):
    n_dev, block, width = got_ref.shape
    cap = block - INFO_ROWS
    rows = table_ref.shape[0]
    half = rows // 2
    per = LANES // cap
    source = iota((1, LANES), 1) // cap
    centred = (iota((rows, LANES), 0) - half).astype(jnp.float32)
    parts, data = ([], [])
    for first in range(0, n_dev, per):
        at = jnp.zeros((1, LANES), jnp.float32)
        for j in range(per):
            info = got_ref[first + j][:, :LANES].astype(jnp.float32)[cap : cap + 1]
            at = jnp.where(source == j, info, at)
            if cap % 16 == 0:
                data.append(got_ref[first + j][:cap])
            else:
                data.append(got_ref[first + j].astype(jnp.float32)[:cap])
        parts.append(jnp.where(centred == at, 1.0, 0.0))
    table = jnp.concatenate(parts, axis=1)
    table_low = table.astype(jnp.bfloat16)
    placed = contract(
        table_low, jnp.concatenate(data, axis=0).astype(jnp.bfloat16), 1, 0
    ).astype(jnp.bfloat16)
    head_ref[...] = placed[:half]
    tail_ref[...] = placed[half:]
    table_ref[...] = table_low
    back_ref[...] = table.T.astype(jnp.bfloat16)


def place_grads_kernel(table_ref, got_ref, head_ref, tail_ref):
    half = head_ref.shape[0]
    placed = contract(table_ref[...], got_ref[...], 1, 0).astype(jnp.bfloat16)
    head_ref[...] = placed[:half]
    tail_ref[...] = placed[half:]


def pick_kernel(table_ref, head_ref, tail_ref, out_ref):
    own = jnp.concatenate([head_ref[...], tail_ref[...]], axis=0)
    out_ref[...] = contract(table_ref[...], own, 1, 0).astype(jnp.bfloat16)


def restore_kernel(table_ref, got_ref, out_ref):
    out_ref[...] = contract(table_ref[...], got_ref[...], 1, 0).astype(jnp.bfloat16)


def forward_kernel(
    tail_ref, next_ref, w_ref, w_kv_t_ref, qkv_ref, key_t_ref, attn_t_ref, probs_ref, points_t_ref
):
    width = w_ref.shape[0]
    head_dim = width // HEADS
    points = jnp.concatenate([tail_ref[...], next_ref[...]], axis=0)
    points_t_ref[...] = points.astype(jnp.float32).T.astype(jnp.bfloat16)
    qkv_ref[...] = contract(points, w_ref[...], 1, 0).astype(jnp.bfloat16)
    kv_t = contract(w_kv_t_ref[...], points, 1, 1).astype(jnp.bfloat16)
    key_t_ref[...] = kv_t[:width]
    side = iota((1, LANES), 1) // head_dim
    factor = math.log2(math.e) / math.sqrt(head_dim)
    for head in range(HEADS):
        first = head * head_dim // LANES * LANES
        within = head * head_dim % LANES // head_dim
        query = qkv_ref[:, first : first + LANES]
        query = jnp.where(side == within, query, jnp.zeros_like(query))
        key = qkv_ref[:, width + first : width + first + LANES]
        scores = contract(key, query, 1, 1)
        top = jnp.max(scores, axis=0, keepdims=True)
        weight = jnp.exp2((scores - top) * factor)
        probs = weight * (1.0 / jnp.sum(weight, axis=0, keepdims=True))
        probs_low = probs.astype(jnp.bfloat16)
        probs_ref[head] = probs_low
        value_t = kv_t[width + head * head_dim : width + (head + 1) * head_dim]
        attn_t_ref[head * head_dim : (head + 1) * head_dim, :] = contract(
            value_t, probs_low, 1, 0
        ).astype(jnp.bfloat16)


def backward_kernel(
    tail_ref, next_ref, w_out_ref, qkv_ref, key_t_ref, attn_t_ref, probs_ref, out_ref, query_t_ref
):
    width = w_out_ref.shape[0]
    head_dim = width // HEADS
    scale = 1.0 / math.sqrt(head_dim)
    grads = jnp.concatenate([tail_ref[...], next_ref[...]], axis=0)
    grad_attn = contract(grads, w_out_ref[...], 1, 1).astype(jnp.bfloat16)
    grad_attn_t = contract(w_out_ref[...], grads, 1, 1).astype(jnp.bfloat16)
    side = iota((1, LANES), 1) // head_dim
    for first in range(0, width, LANES):
        cols = slice(first, first + LANES)
        grad = grad_attn[:, cols]
        query = qkv_ref[:, cols]
        value = qkv_ref[:, 2 * width + first : 2 * width + first + LANES]
        grad_key = jnp.zeros((grad.shape[0], LANES), jnp.float32)
        grad_value = grad_key
        for within in range(LANES // head_dim):
            chans = slice(first + within * head_dim, first + (within + 1) * head_dim)
            probs = probs_ref[first // head_dim + within]
            delta = jnp.sum(
                grad_attn_t[chans].astype(jnp.float32) * attn_t_ref[chans, :].astype(jnp.float32),
                axis=0,
                keepdims=True,
            )
            grad_probs = contract(
                value, jnp.where(side == within, grad, jnp.zeros_like(grad)), 1, 1
            )
            grad_scores = (probs.astype(jnp.float32) * (grad_probs - delta)).astype(jnp.bfloat16)
            grad_value = jnp.where(side == within, contract(probs, grad, 1, 0), grad_value)
            grad_key = jnp.where(side == within, contract(grad_scores, query, 1, 0), grad_key)
            query_t_ref[chans, :] = contract(key_t_ref[chans, :], grad_scores, 1, 0) * scale
        out_ref[:, width + first : width + first + LANES] = (grad_key * scale).astype(jnp.bfloat16)
        out_ref[:, 2 * width + first : 2 * width + first + LANES] = grad_value.astype(jnp.bfloat16)
    out_ref[:, :width] = query_t_ref[...].T.astype(jnp.bfloat16)


def weights_kernel(side_ref, points_t_ref, attn_t_ref, grad_qkv_ref, tail_ref, next_ref, out_ref):
    rows = out_ref.shape[0]
    n_qkv = grad_qkv_ref.shape[1]
    from_row = pl.multiple_of(side_ref[0] * rows, rows)
    grads = jnp.concatenate([tail_ref[...], next_ref[...]], axis=0)
    out_ref[:, :n_qkv] = contract(
        points_t_ref[pl.ds(from_row, rows), :], grad_qkv_ref[...], 1, 0
    ).astype(out_ref.dtype)
    out_ref[:, n_qkv:] = contract(attn_t_ref[pl.ds(from_row, rows), :], grads, 1, 0).astype(
        out_ref.dtype
    )


def inputs_kernel(grad_qkv_ref, w_ref, next_ref, tail_ref):
    half = tail_ref.shape[0]
    tail_ref[...] = contract(grad_qkv_ref[:half, :], w_ref[...], 1, 1).astype(jnp.bfloat16)
    next_ref[...] = contract(grad_qkv_ref[half:, :], w_ref[...], 1, 1).astype(jnp.bfloat16)


def exchange(blocks):
    return lax.all_to_all(blocks, "curve", split_axis=0, concat_axis=0, tiled=True)


def swap(block, axis, mask):
    size = lax.axis_size(axis)
    return lax.ppermute(block, axis, [(i, i ^ mask) for i in range(size)])


def split_rows(rows, side):
    half = rows.shape[0] // 2
    keep = lax.dynamic_slice_in_dim(rows, side * half, half, 0)
    send = lax.dynamic_slice_in_dim(rows, (1 - side) * half, half, 0)
    return (keep, send.astype(jnp.bfloat16))


def join_rows(own, got, side):
    return jnp.concatenate([jnp.where(side == 0, own, got), jnp.where(side == 0, got, own)], axis=0)


def order_blocks(blocks, place):
    count = blocks.shape[0]
    tail = blocks.shape[1:]
    bit = 1
    while bit < count:
        pairs = blocks.reshape(count // (2 * bit), 2, bit, *tail)
        blocks = jnp.where((place & bit) != 0, pairs[:, ::-1], pairs).reshape(count, *tail)
        bit *= 2
    return blocks


def sum_devices(keep, send):
    me = lax.axis_index("curve")
    n_line = lax.axis_size("curve") // 4
    core, side_x, line, side_y = (me & 1, (me >> 1) & 1, me >> 2, lax.axis_index("dp"))
    part = keep + swap(send, "curve", 1).astype(jnp.float32)
    half = part.shape[0] // 2
    keep_a, send_a = split_rows(part[:half], side_x)
    keep_b, send_b = split_rows(part[half:], side_y)
    part_a = keep_a + swap(send_a, "curve", 2).astype(jnp.float32)
    part_b = keep_b + swap(send_b, "dp", 1).astype(jnp.float32)
    keep_a, send_a = split_rows(part_a, side_y)
    keep_b, send_b = split_rows(part_b, side_x)
    part_a = keep_a + swap(send_a, "dp", 1).astype(jnp.float32)
    part_b = keep_b + swap(send_b, "curve", 2).astype(jnp.float32)
    width = keep.shape[1]
    rows = part_a.shape[0] // n_line
    both = jnp.stack([part_a.reshape(n_line, rows, width), part_b.reshape(n_line, rows, width)], axis=1)
    mine = lax.dynamic_index_in_dim(both, line, 0, keepdims=False)
    others = [
        swap(
            lax.dynamic_index_in_dim(both, line ^ k, 0, keepdims=False).astype(jnp.bfloat16),
            "curve",
            4 * k,
        )
        for k in range(1, n_line)
    ]
    for other in others:
        mine = mine + other.astype(jnp.float32)
    mine = mine.astype(jnp.bfloat16)
    blocks = jnp.stack([mine] + [swap(mine, "curve", 4 * k) for k in range(1, n_line)])
    blocks = order_blocks(blocks, line)
    full_a = blocks[:, 0].reshape(n_line * rows, width)
    full_b = blocks[:, 1].reshape(n_line * rows, width)
    got_a = swap(full_a, "dp", 1)
    got_b = swap(full_b, "curve", 2)
    full_a = join_rows(full_a, got_a, side_y)
    full_b = join_rows(full_b, got_b, side_x)
    got_a = swap(full_a, "curve", 2)
    got_b = swap(full_b, "dp", 1)
    half_rows = jnp.concatenate([join_rows(full_a, got_a, side_x), join_rows(full_b, got_b, side_y)])
    return join_rows(half_rows, swap(half_rows, "curve", 1), core).astype(jnp.float32)


def on_device(points, grad_out, dest_dev, dest_row, w_qkv, w_out):
    rows, width = points.shape[1:]
    half = rows - PATCH // 2
    n_dev = lax.axis_size("curve")
    cap = 2 * rows // n_dev
    total = n_dev * cap
    place_flops = 2 * total * rows * width
    send_points, slots = call(
        pack_points_kernel,
        [low(n_dev, cap + INFO_ROWS, width), jax.ShapeDtypeStruct((1, rows), jnp.int32)],
        [dest_dev, dest_row, points[0]],
        place_flops,
    )
    got_points = exchange(send_points)
    send_grads, restore_table = call(
        pack_grads_kernel, [low(total, width), low(rows, total)], [slots, grad_out[0]], place_flops
    )
    got_grads = exchange(send_grads.reshape(n_dev, cap, width)).reshape(total, width)
    head, tail_points, place_table, pick_table = call(
        place_points_kernel,
        [low(rows - half, width), low(half, width), low(rows, total), low(total, rows)],
        [got_points],
        place_flops,
    )
    next_points = from_behind(head, "curve", -1)
    qkv, key_t, attn_t, probs, points_t = call(
        forward_kernel,
        [
            low(rows, 3 * width),
            low(width, rows),
            low(width, rows),
            low(HEADS, PATCH, PATCH),
            low(width, rows),
        ],
        [tail_points, next_points, w_qkv, w_qkv[:, width:].T],
        2 * rows * width * 5 * width + 16 * rows * rows * width,
    )
    head, tail_grads = call(
        place_grads_kernel,
        [low(rows - half, width), low(half, width)],
        [place_table, got_grads],
        place_flops,
    )
    next_grads = from_behind(head, "curve", -1)
    grad_qkv = pl.pallas_call(
        backward_kernel,
        out_shape=low(rows, 3 * width),
        in_specs=[pl.BlockSpec(memory_space=pltpu.VMEM)] * 7,
        out_specs=pl.BlockSpec(memory_space=pltpu.VMEM),
        scratch_shapes=[pltpu.VMEM((width, rows), jnp.float32)],
        compiler_params=pltpu.CompilerParams(vmem_limit_bytes=40 * 2**20),
        cost_estimate=pl.CostEstimate(
            flops=32 * rows * rows * width, bytes_accessed=8 * 2**20, transcendentals=0
        ),
    )(tail_grads, next_grads, w_out, qkv, key_t, attn_t, probs)
    core = (lax.axis_index("curve") & 1).reshape(1)
    sums = functools.partial(
        call,
        weights_kernel,
        flops=4 * rows * width * width,
        scalars=1,
    )
    operands = [points_t, attn_t, grad_qkv, tail_grads, next_grads]
    (send,) = sums([low(width // 2, 4 * width)], [1 - core, *operands])
    next_input, tail_input = call(
        inputs_kernel,
        [low(rows - half, width), low(half, width)],
        [grad_qkv, w_qkv],
        6 * rows * width * width,
    )
    head_input = from_behind(next_input, "curve", 1)
    (keep,) = sums(
        [jax.ShapeDtypeStruct((width // 2, 4 * width), jnp.float32)], [core, *operands]
    )
    (picked,) = call(
        pick_kernel, [low(total, width)], [pick_table, head_input, tail_input], place_flops
    )
    returned = exchange(picked.reshape(n_dev, cap, width)).reshape(total, width)
    (result,) = call(restore_kernel, [low(rows, width)], [restore_table, returned], place_flops)
    weights = sum_devices(keep, send)
    return (result[None], weights[:, : 3 * width], weights[:, 3 * width :])


def solution(mesh):
    placed = (
        P("dp", "curve", None),
        P("dp", "curve", None),
        P("dp", "curve"),
        P("dp", "curve"),
        P(),
        P(),
    )
    return jax.shard_map(
        on_device,
        mesh=mesh,
        in_specs=placed,
        out_specs=(P("dp", "curve", None), P(), P()),
        check_vma=False,
    )
```

time: 209 us -> 182 us (0.87)
  Pallas kernels: 0 us -> 24.9 us
  local copies, waits for them, and re-layouts: 36.7 us -> 15 us
  matrix products: 20.3 us -> 0 us
  other arithmetic: 18.1 us -> 11.1 us
  waiting for transfers between devices: 85.8 us -> 79.7 us
  starting transfers between devices: 45 us -> 48.1 us
    pallas_call x0 -> x11, Pallas kernels: none -> 24.9 us  [the longest x10 19.9 us: call(): pl.pallas_call(kernel, out_shape=outs, in_specs=smem + vmem, out_specs=[p...]
    scatter x5 -> x0, local copies, waits for them, and re-layouts: 20.8 us -> none  [the longest x2 10.8 us: place_rows(): return jnp.zeros((rows, width), jnp.bfloat16).at[got_rows.reshape(-1)].se...]
    dot_general x54 -> x0, matrix products: 20.3 us -> none  [the longest x36 13.6 us: contract(): lax.dot_general(left, right, (((left_dim,), (right_dim,)), ((), ())), pre...]
    unnamed x22 -> x41, local copies, waits for them, and re-layouts: 4.24 us -> 12 us
    ppermute x2 -> x3, waiting for transfers between devices: 9.57 us -> 2.01 us  [from_behind(): return lax.ppermute(block, axis, route)]
    ppermute x2 -> x3, starting transfers between devices: 5.44 us -> 12.8 us  [from_behind(): return lax.ppermute(block, axis, route)]
    gather x2 -> x0, local copies, waits for them, and re-layouts: 6.58 us -> none  [the longest x1 3.97 us: pick_rows(): jnp.take(values, jnp.minimum(got_rows.reshape(-1), rows - 1), axis=0)]
    all_to_all x4 -> x3, starting transfers between devices: 21.6 us -> 18.5 us  [exchange(): lax.all_to_all(blocks, 'curve', split_axis=0, concat_axis=0, tiled=True)]
  transfers between devices with their start and end apart: 22 -> 22, of which waited for: 15 -> 15; matrix products, arithmetic and copies ran while one was open for 14% -> 3% of each run, Pallas kernels for 0% -> 9%
where the time goes in v2:
time: 182 us; the launch traced here: 180 us
  waiting for transfers between devices  79.7 us (44%)
  starting transfers between devices  48.1 us (26%)
  Pallas kernels  24.9 us (14%)
  local copies, waits for them, and re-layouts  15 us (8%)
  other arithmetic  11.1 us (6%)
    all_to_all x3, waiting for transfers between devices, exchange(): lax.all_to_all(blocks, 'curve', split_axis=0, concat_axis=0, tiled=True)  39.4 us
    ppermute x16, waiting for transfers between devices, swap(): return lax.ppermute(block, axis, [(i, i ^ mask) for i in range(size)])  38.3 us
    pallas_call x10, Pallas kernels, call(): pl.pallas_call(kernel, out_shape=outs, in_specs=smem + vmem, out_specs=[p...  19.9 us
    all_to_all x3, starting transfers between devices, exchange(): lax.all_to_all(blocks, 'curve', split_axis=0, concat_axis=0, tiled=True)  18.5 us
    ppermute x16, starting transfers between devices, swap(): return lax.ppermute(block, axis, [(i, i ^ mask) for i in range(size)])  16.7 us
    ppermute x3, starting transfers between devices, from_behind(): return lax.ppermute(block, axis, route)  12.8 us
    unnamed x41, local copies, waits for them, and re-layouts  12 us
    pallas_call x1, Pallas kernels, on_device(): pl.pallas_call(backward_kernel, out_shape=low(rows, 3 * width), in_specs=...  4.98 us
  transfers between devices with their start and end apart: 22, of which 15 were waited for; matrix products, arithmetic and copies ran while one was open for 3% of the time, Pallas kernels for 9%

profile of v2, /device:TPU:0, one launch (start us, length us, event | category | flops | bytes accessed | tf_op | source)
XLA Modules:
  0.0 179.7 jit_solution(12665992383844078056)
XLA Ops:
  3.0 2.0 %shard_map.85 = (bf16[16,72,512]{2,1,0:T(8,128)(2,1)}, s32[1,512]{1,0:T(1,128)S(1)}) custom-call(s32[1,512]{1,0:T(1,128)S(1)} %copy-done.12, s32[1,512]{1,0:T(1,128)S(1)} %copy-done.13, bf16[512,512]{1,0:T(8,128)(2,1)S(1)} %bitcast.63), custom_call_target="tpu_custom_call" | custom-call | flops 536870912 | bytes 1710080 | tf_op jit(solution)/shard_map/pallas_call | solution.py:41
  5.0 7.4 %all-to-all-start = ((bf16[16,72,512]{2,1,0:T(8,128)(2,1)}), bf16[16,72,512]{2,1,0:T(8,128)(2,1)S(1)}, u32[]{:S(2)}, u32[]{:S(2)}) async-start(bf16[16,72,512]{2,1,0:T(8,128)(2,1)} %get-tuple-element.22), calls=%async_computation | async-start | bytes 2359296 | tf_op jit(solution)/shard_map/all_to_all | solution.py:228
  12.4 1.8 shard_map.86
  15.2 22.3 %all-to-all-done.got_ref = bf16[16,72,512]{2,1,0:T(8,128)(2,1)S(1)} async-done(((bf16[16,72,512]{2,1,0:T(8,128)(2,1)}), bf16[16,72,512]{2,1,0:T(8,128)(2,1)S(1)}, u32[]{:S(2)}, u32[]{:S(2)}) %all-to-all-start) | async-done | bytes 1179680 | tf_op jit(solution)/shard_map/all_to_all | solution.py:228
  37.5 7.5 %all-to-all-start.1 = ((bf16[16,64,512]{2,1,0:T(8,128)(2,1)}), bf16[16,64,512]{2,1,0:T(8,128)(2,1)}, u32[]{:S(2)}, u32[]{:S(2)}) async-start(bf16[16,64,512]{2,1,0:T(8,128)(2,1)} %bitcast.2), calls=%async_computation.1 | async-start | bytes 2097152 | tf_op jit(solution)/shard_map/all_to_all | solution.py:228
  49.1 4.3 %collective-permute-start.1 = (bf16[256,512]{1,0:T(8,128)(2,1)}, bf16[256,512]{1,0:T(8,128)(2,1)S(1)}, u32[]{:S(2)}, u32[]{:S(2)}) collective-permute-start(bf16[256,512]{1,0:T(8,128)(2,1)} %get-tuple-element.29), channel_id=1, source_target_pairs={{2,0},{4,2},{6,4},{8,6},{10,8},{12,10},{14,12},{16,14},{18,16},{20... | collective-permute-start | bytes 786440 | tf_op jit(solution)/shard_map/ppermute | solution.py:20
  54.7 13.3 %all-to-all-done.1 = bf16[16,64,512]{2,1,0:T(8,128)(2,1)} async-done(((bf16[16,64,512]{2,1,0:T(8,128)(2,1)}), bf16[16,64,512]{2,1,0:T(8,128)(2,1)}, u32[]{:S(2)}, u32[]{:S(2)}) %all-to-all-start.1) | async-done | bytes 1048608 | tf_op jit(solution)/shard_map/all_to_all | solution.py:228
  69.4 1.9 %shard_map.88 = (bf16[256,512]{1,0:T(8,128)(2,1)S(1)}, bf16[256,512]{1,0:T(8,128)(2,1)S(1)}) custom-call(bf16[512,1024]{1,0:T(8,128)(2,1)S(1)} %copy-done.8, bf16[1024,512]{1,0:T(8,128)(2,1)} %bitcast.3.got_ref), custom_call_target="tpu_custom_call" | custom-call | flops 536870912 | bytes 2621440 | tf_op jit(solution)/shard_map/pallas_call | solution.py:41
  71.3 8.4 %collective-permute-start = (bf16[256,512]{1,0:T(8,128)(2,1)S(1)}, bf16[256,512]{1,0:T(8,128)(2,1)S(1)}, u32[]{:S(2)}, u32[]{:S(2)}) collective-permute-start(bf16[256,512]{1,0:T(8,128)(2,1)S(1)} %get-tuple-element.27), channel_id=1, source_target_pairs={{2,0},{4,2},{6,4},{8,6},{10,8},{12,10},{14,12},{16,14},{18,16},{20... | collective-permute-start | bytes 786440 | tf_op jit(solution)/shard_map/ppermute | solution.py:20
  80.7 6.3 %shard_map.89 = (bf16[512,1536]{1,0:T(8,128)(2,1)S(1)}, bf16[512,512]{1,0:T(8,128)(2,1)S(1)}, bf16[512,512]{1,0:T(8,128)(2,1)S(1)}, bf16[8,512,512]{2,1,0:T(8,128)(2,1)S(1)}, bf16[512,512]{1,0:T(8,128)(2,1)S(1)}) custom-call(bf16[256,512]{1,0:T(8,128)(2,1)S(1)} %copy-done.15, bf16[256,512]{1,0:T(8,128)(2,1)S(1)} %collective-permute-done.1.next_ref, ...), custom_call_target="tpu_custom_call" | custom-call | flops 3489660928 | bytes 10485760 | tf_op jit(solution)/shard_map/pallas_call | solution.py:41
  87.0 5.0 %shard_map.90.grad_qkv_ref = bf16[512,1536]{1,0:T(8,128)(2,1)S(1)} custom-call(bf16[256,512]{1,0:T(8,128)(2,1)S(1)} %get-tuple-element.26.tail_ref, bf16[256,512]{1,0:T(8,128)(2,1)S(1)} %collective-permute-done.next_ref, bf16[512,512]{1,0:T(8,128)(2,1)S(1)} %copy-done.11, bf16[512,1536]{1,0:T(8,128)(2,1)S(1)} %get-tuple-element.30.qkv_ref, ...), custom_call_target="tpu_custom_call" | custom-call | flops 4294967296 | bytes 8388608 | tf_op jit(solution)/shard_map/pallas_call | solution.py:345
  92.0 1.7 shard_map.95
  94.4 2.3 %collective-permute-done.3 = bf16[256,2048]{1,0:T(8,128)(2,1)} collective-permute-done((bf16[256,2048]{1,0:T(8,128)(2,1)}, bf16[256,2048]{1,0:T(8,128)(2,1)}, u32[]{:S(2)}, u32[]{:S(2)}) %collective-permute-start.3) | collective-permute-done | bytes 1048608 | tf_op jit(solution)/shard_map/ppermute | solution.py:233
  96.7 1.6 convert_add_fusion
  99.6 1.6 collective-permute-start.6
  101.2 6.7 %collective-permute-done.4 = bf16[64,2048]{1,0:T(8,128)(2,1)S(1)} collective-permute-done((bf16[64,2048]{1,0:T(8,128)(2,1)S(1)}, bf16[64,2048]{1,0:T(8,128)(2,1)S(1)}, u32[]{:S(2)}, u32[]{:S(2)}) %collective-permute-start.4) | collective-permute-done | bytes 262176 | tf_op jit(solution)/shard_map/ppermute | solution.py:233
  109.0 1.6 collective-permute-start.5
  111.1 3.0 %collective-permute-done.5 = bf16[32,2048]{1,0:T(8,128)(2,1)S(1)} collective-permute-done((bf16[32,2048]{1,0:T(8,128)(2,1)S(1)}, bf16[32,2048]{1,0:T(8,128)(2,1)S(1)}, u32[]{:S(2)}, u32[]{:S(2)}) %collective-permute-start.5) | collective-permute-done | bytes 131104 | tf_op jit(solution)/shard_map/ppermute | solution.py:233
  114.1 1.7 collective-permute-done.7
  117.4 4.1 %collective-permute-start.8 = (bf16[2,8,2048]{2,1,0:T(8,128)(2,1)S(1)}, bf16[2,8,2048]{2,1,0:T(8,128)(2,1)}, u32[]{:S(2)}, u32[]{:S(2)}) collective-permute-start(bf16[2,8,2048]{2,1,0:T(8,128)(2,1)S(1)} %get-tuple-element.45), channel_id=1, source_target_pairs={{0,8},{2,10},{4,12},{6,14},{8,0},{10,2},{12,4},{14,6},{16,24},{18,... | collective-permute-start | bytes 196616 | tf_op jit(solution)/shard_map/ppermute | solution.py:233
  121.5 2.0 %collective-permute-done.10 = bf16[2,8,2048]{2,1,0:T(8,128)(2,1)} collective-permute-done((bf16[2,8,2048]{2,1,0:T(8,128)(2,1)}, bf16[2,8,2048]{2,1,0:T(8,128)(2,1)}, u32[]{:S(2)}, u32[]{:S(2)}) %collective-permute-start.10) | collective-permute-done | bytes 65568 | tf_op jit(solution)/shard_map/ppermute | solution.py:233
  125.2 2.1 %collective-permute-start.13 = (bf16[2,8,2048]{2,1,0:T(8,128)(2,1)S(1)}, bf16[2,8,2048]{2,1,0:T(8,128)(2,1)S(1)}, u32[]{:S(2)}, u32[]{:S(2)}) collective-permute-start(bf16[2,8,2048]{2,1,0:T(8,128)(2,1)S(1)} %fusion.8), channel_id=1, source_target_pairs={{0,24},{2,26},{4,28},{6,30},{8,16},{10,18},{12,20},{14,22},{16,8},... | collective-permute-start | bytes 196616 | tf_op jit(solution)/shard_map/ppermute | solution.py:233
  129.6 1.7 collective-permute-done.13
  136.2 3.2 %collective-permute-done.14 = bf16[32,2048]{1,0:T(8,128)(2,1)S(1)} collective-permute-done((bf16[32,2048]{1,0:T(8,128)(2,1)}, bf16[32,2048]{1,0:T(8,128)(2,1)S(1)}, u32[]{:S(2)}, u32[]{:S(2)}) %collective-permute-start.14) | collective-permute-done | bytes 131104 | tf_op jit(solution)/shard_map/ppermute | solution.py:233
  142.7 2.0 %collective-permute-done.2.head_ref = bf16[256,512]{1,0:T(8,128)(2,1)S(1)} collective-permute-done((bf16[256,512]{1,0:T(8,128)(2,1)S(1)}, bf16[256,512]{1,0:T(8,128)(2,1)S(1)}, u32[]{:S(2)}, u32[]{:S(2)}) %collective-permute-start.2) | collective-permute-done | bytes 262176 | tf_op jit(solution)/shard_map/ppermute | solution.py:20
  144.7 1.7 shard_map.92
  146.4 3.7 %all-to-all-start.2 = ((bf16[16,64,512]{2,1,0:T(8,128)(2,1)}), bf16[16,64,512]{2,1,0:T(8,128)(2,1)S(1)}, u32[]{:S(2)}, u32[]{:S(2)}) async-start(bf16[16,64,512]{2,1,0:T(8,128)(2,1)} %bitcast.5), calls=%async_computation.2 | async-start | bytes 2097152 | tf_op jit(solution)/shard_map/all_to_all | solution.py:228
  150.1 1.9 %collective-permute-start.15 = (bf16[64,2048]{1,0:T(8,128)(2,1)S(1)}, bf16[64,2048]{1,0:T(8,128)(2,1)S(1)}, u32[]{:S(2)}, u32[]{:S(2)}) collective-permute-start(bf16[64,2048]{1,0:T(8,128)(2,1)S(1)} %pad_maximum_fusion.2), channel_id=1, source_target_pairs={{0,4},{2,6},{4,0},{6,2},{8,12},{10,14},{12,8},{14,10},{16,20},{18,... | collective-permute-start | bytes 786440 | tf_op jit(solution)/shard_map/ppermute | solution.py:233
  152.0 15.0 %collective-permute-done.15 = bf16[64,2048]{1,0:T(8,128)(2,1)S(1)} collective-permute-done((bf16[64,2048]{1,0:T(8,128)(2,1)S(1)}, bf16[64,2048]{1,0:T(8,128)(2,1)S(1)}, u32[]{:S(2)}, u32[]{:S(2)}) %collective-permute-start.15) | collective-permute-done | bytes 262176 | tf_op jit(solution)/shard_map/ppermute | solution.py:233
  169.1 3.8 %all-to-all-done.2 = bf16[16,64,512]{2,1,0:T(8,128)(2,1)S(1)} async-done(((bf16[16,64,512]{2,1,0:T(8,128)(2,1)}), bf16[16,64,512]{2,1,0:T(8,128)(2,1)S(1)}, u32[]{:S(2)}, u32[]{:S(2)}) %all-to-all-start.2) | async-done | bytes 1048608 | tf_op jit(solution)/shard_map/all_to_all | solution.py:228
  174.4 1.8 broadcast_select_fusion.1
  177.8 2.0 %slice.32 = f32[512,1536]{1,0:T(8,128)} slice(f32[512,2048]{1,0:T(8,128)S(1)} %maximum_convert_fusion), slice={[0:512], [0:1536]} | slice | bytes 6291456 | tf_op jit(solution)/shard_map/slice | solution.py:381
  (93 shorter events, 33.6 us)
Async XLA Ops:
  3.0 9.4 %copy-start.10 = (bf16[1,512,512]{2,1,0:T(8,128)(2,1)S(1)}, bf16[1,512,512]{2,1,0:T(8,128)(2,1)}, u32[]{:S(2)}) copy-start(bf16[1,512,512]{2,1,0:T(8,128)(2,1)} %param.7) | copy-start | bytes 1572868
  5.0 32.5 %all-to-all-start = ((bf16[16,72,512]{2,1,0:T(8,128)(2,1)}), bf16[16,72,512]{2,1,0:T(8,128)(2,1)S(1)}, u32[]{:S(2)}, u32[]{:S(2)}) async-start(bf16[16,72,512]{2,1,0:T(8,128)(2,1)} %get-tuple-element.22), calls=%async_computation | async-start | bytes 2359296 | tf_op jit(solution)/shard_map/all_to_all | solution.py:228
  37.5 30.5 %all-to-all-start.1 = ((bf16[16,64,512]{2,1,0:T(8,128)(2,1)}), bf16[16,64,512]{2,1,0:T(8,128)(2,1)}, u32[]{:S(2)}, u32[]{:S(2)}) async-start(bf16[16,64,512]{2,1,0:T(8,128)(2,1)} %bitcast.2), calls=%async_computation.1 | async-start | bytes 2097152 | tf_op jit(solution)/shard_map/all_to_all | solution.py:228
  45.1 8.4 %slice-start = ((bf16[512,1536]{1,0:T(8,128)(2,1)}), bf16[512,1024]{1,0:T(8,128)(2,1)S(1)}, s32[]{:S(2)}) async-start(bf16[512,1536]{1,0:T(8,128)(2,1)} %w_ref.3), calls=%async_computation.3 | async-start | bytes 2097152 | tf_op jit(solution)/shard_map/slice | solution.py:335
  49.1 30.7 %collective-permute-start.1 = (bf16[256,512]{1,0:T(8,128)(2,1)}, bf16[256,512]{1,0:T(8,128)(2,1)S(1)}, u32[]{:S(2)}, u32[]{:S(2)}) collective-permute-start(bf16[256,512]{1,0:T(8,128)(2,1)} %get-tuple-element.29), channel_id=1, source_target_pairs={{2,0},{4,2},{6,4},{8,6},{10,8},{12,10},{14,12},{16,14},{18,16},{20... | collective-permute-start | bytes 786440 | tf_op jit(solution)/shard_map/ppermute | solution.py:20
  53.4 26.3 %copy-start = (bf16[512,1536]{1,0:T(8,128)(2,1)S(1)}, bf16[512,1536]{1,0:T(8,128)(2,1)}, u32[]{:S(2)}) copy-start(bf16[512,1536]{1,0:T(8,128)(2,1)} %w_ref.3) | copy-start | bytes 4718596
  68.1 11.7 %copy-start.6 = (bf16[512,1024]{0,1:T(8,128)(2,1)S(1)}, bf16[512,1024]{0,1:T(8,128)(2,1)}, u32[]{:S(2)}) copy-start(bf16[512,1024]{0,1:T(8,128)(2,1)} %copy.13) | copy-start | bytes 3145732
  68.1 1.3 copy-start.8
  71.3 15.7 %collective-permute-start = (bf16[256,512]{1,0:T(8,128)(2,1)S(1)}, bf16[256,512]{1,0:T(8,128)(2,1)S(1)}, u32[]{:S(2)}, u32[]{:S(2)}) collective-permute-start(bf16[256,512]{1,0:T(8,128)(2,1)S(1)} %get-tuple-element.27), channel_id=1, source_target_pairs={{2,0},{4,2},{6,4},{8,6},{10,8},{12,10},{14,12},{16,14},{18,16},{20... | collective-permute-start | bytes 786440 | tf_op jit(solution)/shard_map/ppermute | solution.py:20
  80.7 6.3 %copy-start.11 = (bf16[512,512]{1,0:T(8,128)(2,1)S(1)}, bf16[512,512]{1,0:T(8,128)(2,1)}, u32[]{:S(2)}) copy-start(bf16[512,512]{1,0:T(8,128)(2,1)} %w_out_ref.1) | copy-start | bytes 1572868
  93.7 3.0 %collective-permute-start.3 = (bf16[256,2048]{1,0:T(8,128)(2,1)}, bf16[256,2048]{1,0:T(8,128)(2,1)}, u32[]{:S(2)}, u32[]{:S(2)}) collective-permute-start(bf16[256,2048]{1,0:T(8,128)(2,1)} %shard_map.95), channel_id=1, source_target_pairs={{0,2},{2,0},{4,6},{6,4},{8,10},{10,8},{12,14},{14,12},{16,18},{18,... | collective-permute-start | bytes 3145736 | tf_op jit(solution)/shard_map/ppermute | solution.py:233
  99.5 8.4 %collective-permute-start.4 = (bf16[64,2048]{1,0:T(8,128)(2,1)S(1)}, bf16[64,2048]{1,0:T(8,128)(2,1)S(1)}, u32[]{:S(2)}, u32[]{:S(2)}) collective-permute-start(bf16[64,2048]{1,0:T(8,128)(2,1)S(1)} %dynamic-slice_convert_fusion.1), channel_id=1, source_target_pairs={{0,4},{2,6},{4,0},{6,2},{8,12},{10,14},{12,8},{14,10},{16,20},{18,... | collective-permute-start | bytes 786440 | tf_op jit(solution)/shard_map/ppermute | solution.py:233
  99.6 11.0 %collective-permute-start.6 = (bf16[64,2048]{1,0:T(8,128)(2,1)S(1)}, bf16[64,2048]{1,0:T(8,128)(2,1)S(1)}, u32[]{:S(2)}, u32[]{:S(2)}) collective-permute-start(bf16[64,2048]{1,0:T(8,128)(2,1)S(1)} %dynamic-slice_convert_fusion), channel_id=1, source_target_pairs={{0,1},{1,0},{2,3},{3,2},{4,5},{5,4},{6,7},{7,6},{8,9},{9,8},{10,11... | collective-permute-start | bytes 786440 | tf_op jit(solution)/shard_map/ppermute | solution.py:233
  109.0 5.0 %collective-permute-start.5 = (bf16[32,2048]{1,0:T(8,128)(2,1)S(1)}, bf16[32,2048]{1,0:T(8,128)(2,1)S(1)}, u32[]{:S(2)}, u32[]{:S(2)}) collective-permute-start(bf16[32,2048]{1,0:T(8,128)(2,1)S(1)} %dynamic-slice_convert_fusion.3), channel_id=1, source_target_pairs={{0,1},{1,0},{2,3},{3,2},{4,5},{5,4},{6,7},{7,6},{8,9},{9,8},{10,11... | collective-permute-start | bytes 393224 | tf_op jit(solution)/shard_map/ppermute | solution.py:233
  110.7 5.0 %collective-permute-start.7 = (bf16[32,2048]{1,0:T(8,128)(2,1)S(1)}, bf16[32,2048]{1,0:T(8,128)(2,1)S(1)}, u32[]{:S(2)}, u32[]{:S(2)}) collective-permute-start(bf16[32,2048]{1,0:T(8,128)(2,1)S(1)} %dynamic-slice_convert_fusion.2), channel_id=1, source_target_pairs={{0,4},{2,6},{4,0},{6,2},{8,12},{10,14},{12,8},{14,10},{16,20},{18,... | collective-permute-start | bytes 393224 | tf_op jit(solution)/shard_map/ppermute | solution.py:233
  116.5 18.6 %copy-start.1 = (bf16[512,1536]{1,0:T(8,128)(2,1)S(1)}, bf16[512,1536]{1,0:T(8,128)(2,1)}, u32[]{:S(2)}) copy-start(bf16[512,1536]{1,0:T(8,128)(2,1)} %w_ref.3) | copy-start | bytes 4718596
  117.1 6.4 %collective-permute-start.10 = (bf16[2,8,2048]{2,1,0:T(8,128)(2,1)}, bf16[2,8,2048]{2,1,0:T(8,128)(2,1)}, u32[]{:S(2)}, u32[]{:S(2)}) collective-permute-start(bf16[2,8,2048]{2,1,0:T(8,128)(2,1)} %get-tuple-element.47), channel_id=1, source_target_pairs={{0,24},{2,26},{4,28},{6,30},{8,16},{10,18},{12,20},{14,22},{16,8},... | collective-permute-start | bytes 196616 | tf_op jit(solution)/shard_map/ppermute | solution.py:233
  117.4 6.1 %collective-permute-start.9 = (bf16[2,8,2048]{2,1,0:T(8,128)(2,1)S(1)}, bf16[2,8,2048]{2,1,0:T(8,128)(2,1)}, u32[]{:S(2)}, u32[]{:S(2)}) collective-permute-start(bf16[2,8,2048]{2,1,0:T(8,128)(2,1)S(1)} %get-tuple-element.46), channel_id=1, source_target_pairs={{0,16},{2,18},{4,20},{6,22},{8,24},{10,26},{12,28},{14,30},{16,0},... | collective-permute-start | bytes 196616 | tf_op jit(solution)/shard_map/ppermute | solution.py:233
  117.4 6.8 %collective-permute-start.8 = (bf16[2,8,2048]{2,1,0:T(8,128)(2,1)S(1)}, bf16[2,8,2048]{2,1,0:T(8,128)(2,1)}, u32[]{:S(2)}, u32[]{:S(2)}) collective-permute-start(bf16[2,8,2048]{2,1,0:T(8,128)(2,1)S(1)} %get-tuple-element.45), channel_id=1, source_target_pairs={{0,8},{2,10},{4,12},{6,14},{8,0},{10,2},{12,4},{14,6},{16,24},{18,... | collective-permute-start | bytes 196616 | tf_op jit(solution)/shard_map/ppermute | solution.py:233
  125.2 6.1 %collective-permute-start.13 = (bf16[2,8,2048]{2,1,0:T(8,128)(2,1)S(1)}, bf16[2,8,2048]{2,1,0:T(8,128)(2,1)S(1)}, u32[]{:S(2)}, u32[]{:S(2)}) collective-permute-start(bf16[2,8,2048]{2,1,0:T(8,128)(2,1)S(1)} %fusion.8), channel_id=1, source_target_pairs={{0,24},{2,26},{4,28},{6,30},{8,16},{10,18},{12,20},{14,22},{16,8},... | collective-permute-start | bytes 196616 | tf_op jit(solution)/shard_map/ppermute | solution.py:233
  127.3 5.6 %collective-permute-start.12 = (bf16[2,8,2048]{2,1,0:T(8,128)(2,1)S(1)}, bf16[2,8,2048]{2,1,0:T(8,128)(2,1)S(1)}, u32[]{:S(2)}, u32[]{:S(2)}) collective-permute-start(bf16[2,8,2048]{2,1,0:T(8,128)(2,1)S(1)} %fusion.8), channel_id=1, source_target_pairs={{0,16},{2,18},{4,20},{6,22},{8,24},{10,26},{12,28},{14,30},{16,0},... | collective-permute-start | bytes 196616 | tf_op jit(solution)/shard_map/ppermute | solution.py:233
  128.4 4.9 %collective-permute-start.11 = (bf16[2,8,2048]{2,1,0:T(8,128)(2,1)S(1)}, bf16[2,8,2048]{2,1,0:T(8,128)(2,1)S(1)}, u32[]{:S(2)}, u32[]{:S(2)}) collective-permute-start(bf16[2,8,2048]{2,1,0:T(8,128)(2,1)S(1)} %fusion.8), channel_id=1, source_target_pairs={{0,8},{2,10},{4,12},{6,14},{8,0},{10,2},{12,4},{14,6},{16,24},{18,... | collective-permute-start | bytes 196616 | tf_op jit(solution)/shard_map/ppermute | solution.py:233
  134.2 5.2 %collective-permute-start.14 = (bf16[32,2048]{1,0:T(8,128)(2,1)}, bf16[32,2048]{1,0:T(8,128)(2,1)S(1)}, u32[]{:S(2)}, u32[]{:S(2)}) collective-permute-start(bf16[32,2048]{1,0:T(8,128)(2,1)} %get-tuple-element.54), channel_id=1, source_target_pairs={{0,1},{1,0},{2,3},{3,2},{4,5},{5,4},{6,7},{7,6},{8,9},{9,8},{10,11... | collective-permute-start | bytes 393224 | tf_op jit(solution)/shard_map/ppermute | solution.py:233
  134.7 5.3 %collective-permute-start.16 = (bf16[32,2048]{1,0:T(8,128)(2,1)}, bf16[32,2048]{1,0:T(8,128)(2,1)}, u32[]{:S(2)}, u32[]{:S(2)}) collective-permute-start(bf16[32,2048]{1,0:T(8,128)(2,1)} %get-tuple-element.55), channel_id=1, source_target_pairs={{0,4},{2,6},{4,0},{6,2},{8,12},{10,14},{12,8},{14,10},{16,20},{18,... | collective-permute-start | bytes 393224 | tf_op jit(solution)/shard_map/ppermute | solution.py:233
  135.1 9.6 %copy-start.5 = (bf16[1024,512]{1,0:T(8,128)(2,1)S(1)}, bf16[1024,512]{1,0:T(8,128)(2,1)}, u32[]{:S(2)}) copy-start(bf16[1024,512]{1,0:T(8,128)(2,1)} %copy-done.4) | copy-start | bytes 3145732
  136.1 8.5 %collective-permute-start.2 = (bf16[256,512]{1,0:T(8,128)(2,1)S(1)}, bf16[256,512]{1,0:T(8,128)(2,1)S(1)}, u32[]{:S(2)}, u32[]{:S(2)}) collective-permute-start(bf16[256,512]{1,0:T(8,128)(2,1)S(1)} %get-tuple-element.34), channel_id=1, source_target_pairs={{30,0},{0,2},{2,4},{4,6},{6,8},{8,10},{10,12},{12,14},{14,16},{16,... | collective-permute-start | bytes 786440 | tf_op jit(solution)/shard_map/ppermute | solution.py:20
  141.1 8.9 %copy-start.18 = (bf16[32,2048]{1,0:T(8,128)(2,1)}, bf16[32,2048]{1,0:T(8,128)(2,1)S(1)}, u32[]{:S(2)}) copy-start(bf16[32,2048]{1,0:T(8,128)(2,1)S(1)} %get-tuple-element.49) | copy-start | bytes 393220
  141.1 10.8 %collective-permute-start.17 = (bf16[64,2048]{1,0:T(8,128)(2,1)S(1)}, bf16[64,2048]{1,0:T(8,128)(2,1)S(1)}, u32[]{:S(2)}, u32[]{:S(2)}) collective-permute-start(bf16[64,2048]{1,0:T(8,128)(2,1)S(1)} %pad_maximum_fusion.3), channel_id=1, source_target_pairs={{0,1},{1,0},{2,3},{3,2},{4,5},{5,4},{6,7},{7,6},{8,9},{9,8},{10,11... | collective-permute-start | bytes 786440 | tf_op jit(solution)/shard_map/ppermute | solution.py:233
  146.4 26.6 %all-to-all-start.2 = ((bf16[16,64,512]{2,1,0:T(8,128)(2,1)}), bf16[16,64,512]{2,1,0:T(8,128)(2,1)S(1)}, u32[]{:S(2)}, u32[]{:S(2)}) async-start(bf16[16,64,512]{2,1,0:T(8,128)(2,1)} %bitcast.5), calls=%async_computation.2 | async-start | bytes 2097152 | tf_op jit(solution)/shard_map/all_to_all | solution.py:228
  150.1 22.9 %copy-start.3 = (bf16[512,1024]{1,0:T(8,128)(2,1)S(1)}, bf16[512,1024]{1,0:T(8,128)(2,1)}, u32[]{:S(2)}) copy-start(bf16[512,1024]{1,0:T(8,128)(2,1)} %copy-done.2) | copy-start | bytes 3145732
  150.1 17.0 %collective-permute-start.15 = (bf16[64,2048]{1,0:T(8,128)(2,1)S(1)}, bf16[64,2048]{1,0:T(8,128)(2,1)S(1)}, u32[]{:S(2)}, u32[]{:S(2)}) collective-permute-start(bf16[64,2048]{1,0:T(8,128)(2,1)S(1)} %pad_maximum_fusion.2), channel_id=1, source_target_pairs={{0,4},{2,6},{4,0},{6,2},{8,12},{10,14},{12,8},{14,10},{16,20},{18,... | collective-permute-start | bytes 786440 | tf_op jit(solution)/shard_map/ppermute | solution.py:233
  169.1 5.3 %collective-permute-start.18 = (bf16[256,2048]{1,0:T(8,128)(2,1)}, bf16[256,2048]{1,0:T(8,128)(2,1)}, u32[]{:S(2)}, u32[]{:S(2)}) collective-permute-start(bf16[256,2048]{1,0:T(8,128)(2,1)} %pad_maximum_fusion), channel_id=1, source_target_pairs={{0,2},{2,0},{4,6},{6,4},{8,10},{10,8},{12,14},{14,12},{16,18},{18,... | collective-permute-start | bytes 3145736 | tf_op jit(solution)/shard_map/ppermute | solution.py:233
  (11 other events, 9.4 us)

commit v3 on v2

v3 whole, which is shorter than its diff:
```python
import functools
import math

import jax
import jax.numpy as jnp
from jax import lax
from jax.experimental import pallas as pl
from jax.experimental.pallas import tpu as pltpu
from jax.sharding import PartitionSpec as P

HEADS = 8
PATCH = 512
INFO_ROWS = 8
LANES = 128


def from_behind(block, axis, distance):
    devices = range(lax.axis_size(axis))
    route = [((i - distance) % len(devices), i) for i in devices]
    return lax.ppermute(block, axis, route)


def contract(left, right, left_dim, right_dim):
    return lax.dot_general(
        left, right, (((left_dim,), (right_dim,)), ((), ())), preferred_element_type=jnp.float32
    )


def iota(shape, dim):
    return lax.broadcasted_iota(jnp.int32, shape, dim)


def hot(mask):
    return jnp.where(mask, 1.0, 0.0).astype(jnp.bfloat16)


def call(kernel, outs, args, flops, scalars=0, scratch=(), mib=16):
    moved = sum(math.prod(x.shape) * x.dtype.itemsize for x in (*outs, *args))
    smem = [pl.BlockSpec(memory_space=pltpu.SMEM)] * scalars
    vmem = [pl.BlockSpec(memory_space=pltpu.VMEM)] * (len(args) - scalars)
    return pl.pallas_call(
        kernel,
        out_shape=outs,
        in_specs=smem + vmem,
        out_specs=[pl.BlockSpec(memory_space=pltpu.VMEM)] * len(outs),
        scratch_shapes=list(scratch),
        compiler_params=pltpu.CompilerParams(vmem_limit_bytes=mib * 2**20),
        cost_estimate=pl.CostEstimate(flops=flops, bytes_accessed=moved, transcendentals=0),
    )(*args)


def low(*shape):
    return jax.ShapeDtypeStruct(shape, jnp.bfloat16)


def wide(*shape):
    return jax.ShapeDtypeStruct(shape, jnp.float32)


def pack_points_kernel(dev_ref, row_ref, x_ref, out_ref, slots_ref):
    n_dev, block, width = out_ref.shape
    cap = block - INFO_ROWS
    rows = x_ref.shape[0]
    dev = dev_ref[...]
    mine = iota((n_dev, rows), 0) == dev
    mine_f = jnp.where(mine, 1.0, 0.0)
    upto = hot(iota((rows, rows), 0) <= iota((rows, rows), 1))
    running = contract(mine_f.astype(jnp.bfloat16), upto, 1, 0)
    rank = (jnp.sum(running * mine_f, axis=0, keepdims=True) - 1.0).astype(jnp.int32)
    slots = dev * cap + rank
    slots_ref[...] = slots
    at_rank = hot(iota((LANES, rows), 0) % cap == rank)
    centred = (row_ref[...] - rows // 2).astype(jnp.float32)
    told = jnp.concatenate([mine_f * centred, mine_f], axis=0).astype(jnp.bfloat16)
    got = contract(told, at_rank, 1, 1)
    info = jnp.where(got[n_dev:] > 0.5, got[:n_dev], float(rows))
    per = 256 // cap
    for first in range(0, n_dev, per):
        pick = hot(iota((per * cap, rows), 0) + first * cap == slots)
        data = contract(pick, x_ref[...], 1, 0)
        for j in range(per):
            dest = first + j
            extra = jnp.broadcast_to(info[dest : dest + 1], (INFO_ROWS, LANES))
            extra = jnp.concatenate(
                [extra, jnp.zeros((INFO_ROWS, width - LANES), jnp.float32)], axis=1
            )
            out_ref[dest] = jnp.concatenate(
                [data[j * cap : (j + 1) * cap], extra], axis=0
            ).astype(jnp.bfloat16)


def pack_grads_kernel(slots_ref, x_ref, out_ref, back_ref):
    total = out_ref.shape[0]
    rows = x_ref.shape[0]
    pick = jnp.where(iota((total, rows), 0) == slots_ref[...], 1.0, 0.0)
    out_ref[...] = contract(pick.astype(jnp.bfloat16), x_ref[...], 1, 0).astype(jnp.bfloat16)
    back_ref[...] = pick.T.astype(jnp.bfloat16)


def place_points_kernel(got_ref, head_ref, tail_ref, table_ref, back_ref):
    n_dev, block, width = got_ref.shape
    cap = block - INFO_ROWS
    rows = table_ref.shape[0]
    half = rows // 2
    per = LANES // cap
    source = iota((1, LANES), 1) // cap
    centred = (iota((rows, LANES), 0) - half).astype(jnp.float32)
    parts, data = ([], [])
    for first in range(0, n_dev, per):
        at = jnp.zeros((1, LANES), jnp.float32)
        for j in range(per):
            info = got_ref[first + j][:, :LANES].astype(jnp.float32)[cap : cap + 1]
            at = jnp.where(source == j, info, at)
            if cap % 16 == 0:
                data.append(got_ref[first + j][:cap])
            else:
                data.append(got_ref[first + j].astype(jnp.float32)[:cap])
        parts.append(jnp.where(centred == at, 1.0, 0.0))
    table = jnp.concatenate(parts, axis=1)
    table_low = table.astype(jnp.bfloat16)
    placed = contract(
        table_low, jnp.concatenate(data, axis=0).astype(jnp.bfloat16), 1, 0
    ).astype(jnp.bfloat16)
    head_ref[...] = placed[:half]
    tail_ref[...] = placed[half:]
    table_ref[...] = table_low
    back_ref[...] = table.T.astype(jnp.bfloat16)


def pick_kernel(table_ref, own_ref, from_before_ref, from_after_ref, out_ref):
    half = from_before_ref.shape[0]
    own = jnp.concatenate(
        [
            own_ref[:half, :] + from_before_ref[...].astype(jnp.float32),
            own_ref[half:, :] + from_after_ref[...].astype(jnp.float32),
        ],
        axis=0,
    ).astype(jnp.bfloat16)
    out_ref[...] = contract(table_ref[...], own, 1, 0).astype(jnp.bfloat16)


def restore_kernel(table_ref, got_ref, out_ref):
    out_ref[...] = contract(table_ref[...], got_ref[...], 1, 0).astype(jnp.bfloat16)


def forward_kernel(
    before_ref,
    head_ref,
    tail_ref,
    after_ref,
    w_ref,
    w_kv_t_ref,
    query_ref,
    kv_ref,
    key_t_ref,
    attn_t_ref,
    probs_ref,
    points_t_ref,
):
    width = w_ref.shape[0]
    head_dim = width // HEADS
    half = head_ref.shape[0]
    points = jnp.concatenate([before_ref[...], head_ref[...], tail_ref[...], after_ref[...]], axis=0)
    points_t_ref[...] = points.astype(jnp.float32).T.astype(jnp.bfloat16)
    query_ref[...] = contract(points[half : 3 * half], w_ref[:, :width], 1, 0).astype(jnp.bfloat16)
    kv_ref[...] = contract(points, w_ref[:, width:], 1, 0).astype(jnp.bfloat16)
    kv_t = contract(w_kv_t_ref[...], points, 1, 1).astype(jnp.bfloat16)
    key_t_ref[...] = kv_t[:width]
    side = iota((1, LANES), 1) // head_dim
    factor = math.log2(math.e) / math.sqrt(head_dim)
    for head in range(HEADS):
        first = head * head_dim // LANES * LANES
        within = head * head_dim % LANES // head_dim
        query = query_ref[:, first : first + LANES]
        query = jnp.where(side == within, query, jnp.zeros_like(query))
        key = kv_ref[:, first : first + LANES]
        scores = jnp.concatenate(
            [
                contract(key[: 2 * half], query[:half], 1, 1),
                contract(key[2 * half :], query[half:], 1, 1),
            ],
            axis=1,
        )
        top = jnp.max(scores, axis=0, keepdims=True)
        weight = jnp.exp2((scores - top) * factor)
        probs = weight * (1.0 / jnp.sum(weight, axis=0, keepdims=True))
        probs_low = probs.astype(jnp.bfloat16)
        probs_ref[head] = probs_low
        value_t = kv_t[width + head * head_dim : width + (head + 1) * head_dim]
        attn_t_ref[head * head_dim : (head + 1) * head_dim, :] = jnp.concatenate(
            [
                contract(value_t[:, : 2 * half], probs_low[:, :half], 1, 0),
                contract(value_t[:, 2 * half :], probs_low[:, half:], 1, 0),
            ],
            axis=1,
        ).astype(jnp.bfloat16)


def backward_kernel(
    table_ref,
    got_ref,
    w_out_ref,
    query_ref,
    kv_ref,
    key_t_ref,
    attn_t_ref,
    probs_ref,
    grads_ref,
    grad_query_ref,
    grad_kv_ref,
    query_t_ref,
):
    width = w_out_ref.shape[0]
    head_dim = width // HEADS
    half = query_ref.shape[0] // 2
    scale = 1.0 / math.sqrt(head_dim)
    grads = contract(table_ref[...], got_ref[...], 1, 0).astype(jnp.bfloat16)
    grads_ref[...] = grads
    grad_attn = contract(grads, w_out_ref[...], 1, 1).astype(jnp.bfloat16)
    grad_attn_t = contract(w_out_ref[...], grads, 1, 1).astype(jnp.bfloat16)
    side = iota((1, LANES), 1) // head_dim
    sides = ((slice(0, half), slice(0, 2 * half)), (slice(half, 2 * half), slice(2 * half, 4 * half)))
    for first in range(0, width, LANES):
        cols = slice(first, first + LANES)
        value_cols = slice(width + first, width + first + LANES)
        grad = grad_attn[:, cols]
        query = query_ref[:, cols]
        for mine, patch in sides:
            value = kv_ref[patch, value_cols]
            grad_key = jnp.zeros((2 * half, LANES), jnp.float32)
            grad_value = grad_key
            for within in range(LANES // head_dim):
                chans = slice(first + within * head_dim, first + (within + 1) * head_dim)
                probs = probs_ref[first // head_dim + within][:, mine]
                delta = jnp.sum(
                    grad_attn_t[chans, mine].astype(jnp.float32)
                    * attn_t_ref[chans, mine].astype(jnp.float32),
                    axis=0,
                    keepdims=True,
                )
                masked = jnp.where(side == within, grad[mine], jnp.zeros_like(grad[mine]))
                grad_probs = contract(value, masked, 1, 1)
                grad_scores = (probs.astype(jnp.float32) * (grad_probs - delta)).astype(jnp.bfloat16)
                grad_value = jnp.where(
                    side == within, contract(probs, grad[mine], 1, 0), grad_value
                )
                grad_key = jnp.where(
                    side == within, contract(grad_scores, query[mine], 1, 0), grad_key
                )
                query_t_ref[chans, mine] = (
                    contract(key_t_ref[chans, patch], grad_scores, 1, 0) * scale
                )
            grad_kv_ref[patch, cols] = (grad_key * scale).astype(jnp.bfloat16)
            grad_kv_ref[patch, value_cols] = grad_value.astype(jnp.bfloat16)
    grad_query_ref[...] = query_t_ref[...].T.astype(jnp.bfloat16)


def weights_kernel(
    side_ref, points_t_ref, attn_t_ref, grad_query_ref, grad_kv_ref, grads_ref, out_ref
):
    rows = out_ref.shape[0]
    own, width = grad_query_ref.shape
    half = own // 2
    from_row = pl.multiple_of(side_ref[0] * rows, rows)
    points_t = points_t_ref[pl.ds(from_row, rows), :]
    kind = out_ref.dtype
    out_ref[:, :width] = contract(
        points_t[:, half : 3 * half], grad_query_ref[...], 1, 0
    ).astype(kind)
    out_ref[:, width : 3 * width] = contract(points_t, grad_kv_ref[...], 1, 0).astype(kind)
    out_ref[:, 3 * width :] = contract(
        attn_t_ref[pl.ds(from_row, rows), :], grads_ref[...], 1, 0
    ).astype(kind)


def inputs_kernel(grad_query_ref, grad_kv_ref, w_ref, own_ref, before_ref, after_ref):
    half = before_ref.shape[0]
    width = w_ref.shape[0]
    w_kv = w_ref[:, width:]
    before_ref[...] = contract(grad_kv_ref[:half, :], w_kv, 1, 1).astype(jnp.bfloat16)
    after_ref[...] = contract(grad_kv_ref[3 * half :, :], w_kv, 1, 1).astype(jnp.bfloat16)
    own_ref[...] = contract(grad_query_ref[...], w_ref[:, :width], 1, 1) + contract(
        grad_kv_ref[half : 3 * half, :], w_kv, 1, 1
    )


def exchange(blocks):
    return lax.all_to_all(blocks, "curve", split_axis=0, concat_axis=0, tiled=True)


def swap(block, axis, mask):
    size = lax.axis_size(axis)
    return lax.ppermute(block, axis, [(i, i ^ mask) for i in range(size)])


def order_blocks(blocks, place):
    count = blocks.shape[0]
    tail = blocks.shape[1:]
    bit = 1
    while bit < count:
        pairs = blocks.reshape(count // (2 * bit), 2, bit, *tail)
        blocks = jnp.where((place & bit) != 0, pairs[:, ::-1], pairs).reshape(count, *tail)
        bit *= 2
    return blocks


def part_rows(total, side, keep_ref, send_ref):
    half = keep_ref.shape[0]
    keep_ref[...] = jnp.where(side == 0, total[:half], total[half:])
    send_ref[...] = jnp.where(side == 0, total[half:], total[:half]).astype(jnp.bfloat16)


def first_sum_kernel(sides_ref, kept_ref, got_ref, keep_a, send_a, keep_b, send_b):
    half = kept_ref.shape[0] // 2
    part_rows(
        kept_ref[:half, :] + got_ref[:half, :].astype(jnp.float32), sides_ref[0], keep_a, send_a
    )
    part_rows(
        kept_ref[half:, :] + got_ref[half:, :].astype(jnp.float32), sides_ref[1], keep_b, send_b
    )


def second_sum_kernel(
    sides_ref, kept_a_ref, got_a_ref, kept_b_ref, got_b_ref, keep_a, send_a, keep_b, send_b
):
    part_rows(
        kept_a_ref[...] + got_a_ref[...].astype(jnp.float32), sides_ref[1], keep_a, send_a
    )
    part_rows(
        kept_b_ref[...] + got_b_ref[...].astype(jnp.float32), sides_ref[0], keep_b, send_b
    )


def spread_kernel(place_ref, *refs):
    pieces, qkv_ref, out_ref = (refs[:-2], refs[-2], refs[-1])
    n_qkv = qkv_ref.shape[1]
    core, side_x, side_y, line, unit = (place_ref[i] for i in range(5))
    side = ((side_x, side_y), (side_y, side_x))
    piece_rows = pieces[0].shape[0]
    step = 8 if piece_rows % 16 == 0 else piece_rows
    for index, piece in enumerate(pieces):
        far_core, rest = divmod(index, 4)
        part, far_first = divmod(rest, 2)
        first, second = side[part]
        base = ((core ^ far_core) * 2 + part) * 2 + (first ^ far_first)
        values = piece[...].astype(jnp.float32)
        per = piece_rows // 2 // step
        for block in range(2 * per):
            far_second, at = divmod(block, per)
            row = ((base * 2 + (second ^ far_second)) * per + (line ^ at)) * step
            row = pl.multiple_of(row, step)
            data = values[block * step : (block + 1) * step]
            qkv_ref[pl.ds(row, step), :] = data[:, :n_qkv]
            out_ref[pl.ds(row, step), :] = data[:, n_qkv:]


def sum_devices(keep, send, sides, width_qkv):
    me = lax.axis_index("curve")
    n_line = lax.axis_size("curve") // 4
    line = me >> 2
    rows, width = keep.shape
    kept_a, send_a, kept_b, send_b = call(
        first_sum_kernel,
        [wide(rows // 4, width), low(rows // 4, width)] * 2,
        [sides, keep, swap(send, "curve", 1)],
        rows * width,
        scalars=1,
    )
    got_a = swap(send_a, "curve", 2)
    got_b = swap(send_b, "dp", 1)
    kept_a, send_a, kept_b, send_b = call(
        second_sum_kernel,
        [wide(rows // 8, width), low(rows // 8, width)] * 2,
        [sides, kept_a, got_a, kept_b, got_b],
        rows * width // 2,
        scalars=1,
    )
    part_a = kept_a + swap(send_a, "dp", 1).astype(jnp.float32)
    part_b = kept_b + swap(send_b, "curve", 2).astype(jnp.float32)
    rows = part_a.shape[0] // n_line
    both = jnp.stack([part_a.reshape(n_line, rows, width), part_b.reshape(n_line, rows, width)], axis=1)
    mine = lax.dynamic_index_in_dim(both, line, 0, keepdims=False)
    others = [
        swap(
            lax.dynamic_index_in_dim(both, line ^ k, 0, keepdims=False).astype(jnp.bfloat16),
            "curve",
            4 * k,
        )
        for k in range(1, n_line)
    ]
    for other in others:
        mine = mine + other.astype(jnp.float32)
    mine = mine.astype(jnp.bfloat16)
    blocks = jnp.stack([mine] + [swap(mine, "curve", 4 * k) for k in range(1, n_line)])
    place = line
    if rows != 8:
        blocks, place = (order_blocks(blocks, line), jnp.zeros_like(line))
    part_a = blocks[:, 0].reshape(n_line * rows, width)
    part_b = blocks[:, 1].reshape(n_line * rows, width)
    part_a = jnp.concatenate([part_a, swap(part_a, "dp", 1)])
    part_b = jnp.concatenate([part_b, swap(part_b, "curve", 2)])
    pieces = [part_a, swap(part_a, "curve", 2), part_b, swap(part_b, "dp", 1)]
    pieces += [swap(piece, "curve", 1) for piece in pieces]
    where = jnp.stack([me & 1, sides[0], sides[1], place, place])
    return call(
        spread_kernel,
        [wide(8 * part_a.shape[0], width_qkv), wide(8 * part_a.shape[0], width - width_qkv)],
        [where, *pieces],
        0,
        scalars=1,
    )


def on_device(points, grad_out, dest_dev, dest_row, w_qkv, w_out):
    rows, width = points.shape[1:]
    half = rows - PATCH // 2
    n_dev = lax.axis_size("curve")
    cap = 2 * rows // n_dev
    total = n_dev * cap
    place_flops = 2 * total * rows * width
    me = lax.axis_index("curve")
    core = (me & 1).reshape(1)
    sides = jnp.stack([(me >> 1) & 1, lax.axis_index("dp")])
    send_points, slots = call(
        pack_points_kernel,
        [low(n_dev, cap + INFO_ROWS, width), jax.ShapeDtypeStruct((1, rows), jnp.int32)],
        [dest_dev, dest_row, points[0]],
        place_flops,
    )
    got_points = exchange(send_points)
    send_grads, restore_table = call(
        pack_grads_kernel, [low(total, width), low(rows, total)], [slots, grad_out[0]], place_flops
    )
    got_grads = exchange(send_grads.reshape(n_dev, cap, width)).reshape(total, width)
    head, tail, place_table, pick_table = call(
        place_points_kernel,
        [low(half, width), low(half, width), low(rows, total), low(total, rows)],
        [got_points],
        place_flops,
    )
    after = from_behind(head, "curve", -1)
    before = from_behind(tail, "curve", 1)
    query, kv, key_t, attn_t, probs, points_t = call(
        forward_kernel,
        [
            low(rows, width),
            low(2 * rows, 2 * width),
            low(width, 2 * rows),
            low(width, rows),
            low(HEADS, PATCH, PATCH),
            low(width, 2 * rows),
        ],
        [before, head, tail, after, w_qkv, w_qkv[:, width:].T],
        2 * rows * width * 9 * width + 16 * rows * rows * width,
        mib=32,
    )
    grads, grad_query, grad_kv = call(
        backward_kernel,
        [low(rows, width), low(rows, width), low(2 * rows, 2 * width)],
        [place_table, got_grads, w_out, query, kv, key_t, attn_t, probs],
        32 * rows * rows * width,
        scratch=[pltpu.VMEM((width, rows), jnp.float32)],
        mib=32,
    )
    sums = functools.partial(call, weights_kernel, flops=6 * rows * width * width, scalars=1)
    operands = [points_t, attn_t, grad_query, grad_kv, grads]
    (send,) = sums([low(width // 2, 4 * width)], [1 - core, *operands])
    own_input, to_before, to_after = call(
        inputs_kernel,
        [wide(rows, width), low(half, width), low(half, width)],
        [grad_query, grad_kv, w_qkv],
        10 * rows * width * width,
    )
    (keep,) = sums([wide(width // 2, 4 * width)], [core, *operands])
    from_before = from_behind(to_after, "curve", 1)
    from_after = from_behind(to_before, "curve", -1)
    (picked,) = call(
        pick_kernel,
        [low(total, width)],
        [pick_table, own_input, from_before, from_after],
        place_flops,
    )
    returned = exchange(picked.reshape(n_dev, cap, width)).reshape(total, width)
    (result,) = call(restore_kernel, [low(rows, width)], [restore_table, returned], place_flops)
    weight_qkv, weight_out = sum_devices(keep, send, sides, 3 * width)
    return (result[None], weight_qkv, weight_out)


def solution(mesh):
    placed = (
        P("dp", "curve", None),
        P("dp", "curve", None),
        P("dp", "curve"),
        P("dp", "curve"),
        P(),
        P(),
    )
    return jax.shard_map(
        on_device,
        mesh=mesh,
        in_specs=placed,
        out_specs=(P("dp", "curve", None), P(), P()),
        check_vma=False,
    )
```

time: 182 us -> 208 us (1.14)
  local copies, waits for them, and re-layouts: 15 us -> 33.9 us
  waiting for transfers between devices: 79.7 us -> 91.6 us
  other arithmetic: 11.1 us -> 1.17 us
  Pallas kernels: 24.9 us -> 33.6 us
  starting transfers between devices: 48.1 us -> 45.4 us
    unnamed x41 -> x79, local copies, waits for them, and re-layouts: 12 us -> 33.8 us
    all_to_all x3, waiting for transfers between devices: 39.4 us -> 22.3 us  [exchange(): lax.all_to_all(blocks, 'curve', split_axis=0, concat_axis=0, tiled=True)]
    ppermute x3 -> x4, waiting for transfers between devices: 2.01 us -> 17.7 us  [from_behind(): return lax.ppermute(block, axis, route)]
    pallas_call x10 -> x13, Pallas kernels: 19.9 us -> 33.6 us  [call(): pl.pallas_call(kernel, out_shape=outs, in_specs=smem + vmem, out_specs=[p...]
    ppermute x16 -> x19, waiting for transfers between devices: 38.3 us -> 51.6 us  [swap(): return lax.ppermute(block, axis, [(i, i ^ mask) for i in range(size)])]
    pallas_call x1 -> x0, Pallas kernels: 4.98 us -> none  [on_device(): pl.pallas_call(backward_kernel, out_shape=low(rows, 3 * width), in_specs=...]
    ppermute x3 -> x4, starting transfers between devices: 12.8 us -> 8.89 us  [from_behind(): return lax.ppermute(block, axis, route)]
    select_n x5 -> x0, other arithmetic: 3.9 us -> none  [the longest x4 3.85 us: join_rows(): jnp.where(side == 0, own, got)]
  transfers between devices with their start and end apart: 22 -> 26, of which waited for: 15 -> 11; matrix products, arithmetic and copies ran while one was open for 3% -> 1% of each run, Pallas kernels for 9% -> 8%
where the time goes in v3:
time: 208 us; the launch traced here: 207 us
  waiting for transfers between devices  91.6 us (44%)
  starting transfers between devices  45.4 us (22%)
  local copies, waits for them, and re-layouts  33.9 us (16%)
  Pallas kernels  33.6 us (16%)
    ppermute x19, waiting for transfers between devices, swap(): return lax.ppermute(block, axis, [(i, i ^ mask) for i in range(size)])  51.6 us
    unnamed x79, local copies, waits for them, and re-layouts  33.8 us
    pallas_call x13, Pallas kernels, call(): pl.pallas_call(kernel, out_shape=outs, in_specs=smem + vmem, out_specs=[p...  33.6 us
    all_to_all x3, waiting for transfers between devices, exchange(): lax.all_to_all(blocks, 'curve', split_axis=0, concat_axis=0, tiled=True)  22.3 us
    all_to_all x3, starting transfers between devices, exchange(): lax.all_to_all(blocks, 'curve', split_axis=0, concat_axis=0, tiled=True)  19.3 us
    ppermute x4, waiting for transfers between devices, from_behind(): return lax.ppermute(block, axis, route)  17.7 us
    ppermute x19, starting transfers between devices, swap(): return lax.ppermute(block, axis, [(i, i ^ mask) for i in range(size)])  17.2 us
    ppermute x4, starting transfers between devices, from_behind(): return lax.ppermute(block, axis, route)  8.89 us
  transfers between devices with their start and end apart: 26, of which 11 were waited for; matrix products, arithmetic and copies ran while one was open for 1% of the time, Pallas kernels for 8%

profile of v3, /device:TPU:0, one launch (start us, length us, event | category | flops | bytes accessed | tf_op | source)
XLA Modules:
  0.0 206.8 jit_solution(16936313448178141728)
XLA Ops:
  3.0 2.0 shard_map.85
  5.0 7.4 %all-to-all-start = ((bf16[16,72,512]{2,1,0:T(8,128)(2,1)}), bf16[16,72,512]{2,1,0:T(8,128)(2,1)S(1)}, u32[]{:S(2)}, u32[]{:S(2)}) async-start(bf16[16,72,512]{2,1,0:T(8,128)(2,1)} %get-tuple-element.35), calls=%async_computation | async-start | bytes 2359296 | tf_op jit(solution)/shard_map/all_to_all | solution.py:288
  12.4 1.8 shard_map.86
  15.2 22.3 %all-to-all-done.got_ref = bf16[16,72,512]{2,1,0:T(8,128)(2,1)S(1)} async-done(((bf16[16,72,512]{2,1,0:T(8,128)(2,1)}), bf16[16,72,512]{2,1,0:T(8,128)(2,1)S(1)}, u32[]{:S(2)}, u32[]{:S(2)}) %all-to-all-start) | async-done | bytes 1179680 | tf_op jit(solution)/shard_map/all_to_all | solution.py:288
  37.5 7.5 %all-to-all-start.1 = ((bf16[16,64,512]{2,1,0:T(8,128)(2,1)}), bf16[16,64,512]{2,1,0:T(8,128)(2,1)}, u32[]{:S(2)}, u32[]{:S(2)}) async-start(bf16[16,64,512]{2,1,0:T(8,128)(2,1)} %bitcast.2), calls=%async_computation.1 | async-start | bytes 2097152 | tf_op jit(solution)/shard_map/all_to_all | solution.py:288
  48.2 4.1 %collective-permute-start.1 = (bf16[256,512]{1,0:T(8,128)(2,1)S(1)}, bf16[256,512]{1,0:T(8,128)(2,1)S(1)}, u32[]{:S(2)}, u32[]{:S(2)}) collective-permute-start(bf16[256,512]{1,0:T(8,128)(2,1)S(1)} %get-tuple-element.40.head_ref), channel_id=1, source_target_pairs={{2,0},{4,2},{6,4},{8,6},{10,8},{12,10},{14,12},{16,14},{18,16},{20... | collective-permute-start | bytes 786440 | tf_op jit(solution)/shard_map/ppermute | solution.py:20
  53.1 17.7 %collective-permute-done.before_ref = bf16[256,512]{1,0:T(8,128)(2,1)S(1)} collective-permute-done((bf16[256,512]{1,0:T(8,128)(2,1)S(1)}, bf16[256,512]{1,0:T(8,128)(2,1)S(1)}, u32[]{:S(2)}, u32[]{:S(2)}) %collective-permute-start) | collective-permute-done | bytes 262176 | tf_op jit(solution)/shard_map/ppermute | solution.py:20
  76.5 7.5 %shard_map.88 = (bf16[512,512]{1,0:T(8,128)(2,1)S(1)}, bf16[1024,1024]{1,0:T(8,128)(2,1)S(1)}, bf16[512,1024]{1,0:T(8,128)(2,1)S(1)}, bf16[512,512]{1,0:T(8,128)...) custom-call(bf16[256,512]{1,0:T(8,128)(2,1)S(1)} %copy-done.22, ...), custom_call_target="tpu_custom_call" | custom-call | flops 4563402752 | bytes 13107200 | tf_op jit(solution)/shard_map/pallas_call | solution.py:41
  84.8 2.0 copy-done.29
  93.2 2.2 %copy-done.30 = bf16[8,512,512]{2,1,0:T(8,128)(2,1)S(1)} copy-done((bf16[8,512,512]{2,1,0:T(8,128)(2,1)S(1)}, bf16[8,512,512]{2,1,0:T(8,128)(2,1)}, u32[]{:S(2)}) %copy-start.30) | copy-done | bytes 4194328
  95.3 1.6 copy-done.32
  99.2 7.5 %shard_map.89 = (bf16[512,512]{1,0:T(8,128)(2,1)S(1)}, bf16[512,512]{1,0:T(8,128)(2,1)S(1)}, bf16[1024,1024]{1,0:T(8,128)(2,1)S(1)}) custom-call(bf16[512,1024]{1,0:T(8,128)(2,1)S(1)} %copy-done.28, bf16[1024,512]{1,0:T(8,128)(2,1)} %bitcast.3.got_ref, bf16[512,512]{1,0:T(8,128)(2,1)S(1)} %copy-done.18, bf16[512,512]{1,0:T(8,128)(2,1)S(1)} %copy-done.36, ...), custom_call_target="tpu_custom_call" | custom-call | flops 4294967296 | bytes 14155776 | tf_op jit(solution)/shard_map/pallas_call | solution.py:41
  106.7 2.2 %shard_map.94 = bf16[256,2048]{1,0:T(8,128)(2,1)} custom-call(s32[1]{0:T(128)S(6)} %sub.3.side_ref, bf16[512,1024]{1,0:T(8,128)(2,1)S(1)} %get-tuple-element.51.points_t_ref, bf16[512,512]{1,0:T(8,128)(2,1)S(1)} %copy-done.4, bf16[512,512]{1,0:T(8,128)(2,1)S(1)} %get-tuple-element.46.grad_query_ref, bf16[1024,1024]{1,0:T(8,128)(2,1)S(1)} %get-tuple-element.47.grad_kv_ref, ...), custom_call_target="tpu_custom_call" | custom-call | flops 805306368 | bytes 5767172 | tf_op jit(solution)/shard_map/pallas_call | solution.py:41
  113.1 1.6 shard_map.95
  114.8 1.6 collective-permute-start.6
  116.4 7.1 %collective-permute-done.5.got_a_ref = bf16[64,2048]{1,0:T(8,128)(2,1)S(1)} collective-permute-done((bf16[64,2048]{1,0:T(8,128)(2,1)S(1)}, bf16[64,2048]{1,0:T(8,128)(2,1)S(1)}, u32[]{:S(2)}, u32[]{:S(2)}) %collective-permute-start.5) | collective-permute-done | bytes 262176 | tf_op jit(solution)/shard_map/ppermute | solution.py:293
  124.8 1.5 collective-permute-start.7
  127.8 1.5 shard_map.90
  130.3 4.4 %collective-permute-start.3 = (bf16[256,512]{1,0:T(8,128)(2,1)S(1)}, bf16[256,512]{1,0:T(8,128)(2,1)S(1)}, u32[]{:S(2)}, u32[]{:S(2)}) collective-permute-start(bf16[256,512]{1,0:T(8,128)(2,1)S(1)} %get-tuple-element.50), channel_id=1, source_target_pairs={{2,0},{4,2},{6,4},{8,6},{10,8},{12,10},{14,12},{16,14},{18,16},{20... | collective-permute-start | bytes 786440 | tf_op jit(solution)/shard_map/ppermute | solution.py:20
  135.7 8.0 %collective-permute-done.8 = bf16[32,2048]{1,0:T(8,128)(2,1)S(1)} collective-permute-done((bf16[32,2048]{1,0:T(8,128)(2,1)S(1)}, bf16[32,2048]{1,0:T(8,128)(2,1)S(1)}, u32[]{:S(2)}, u32[]{:S(2)}) %collective-permute-start.8) | collective-permute-done | bytes 131104 | tf_op jit(solution)/shard_map/ppermute | solution.py:293
  143.8 4.3 %collective-permute-start.10 = (bf16[2,8,2048]{2,1,0:T(8,128)(2,1)S(1)}, bf16[2,8,2048]{2,1,0:T(8,128)(2,1)S(1)}, u32[]{:S(2)}, u32[]{:S(2)}) collective-permute-start(bf16[2,8,2048]{2,1,0:T(8,128)(2,1)S(1)} %get-tuple-element.64), channel_id=1, source_target_pairs={{0,16},{2,18},{4,20},{6,22},{8,24},{10,26},{12,28},{14,30},{16,0},... | collective-permute-start | bytes 196616 | tf_op jit(solution)/shard_map/ppermute | solution.py:293
  149.9 1.7 shard_map.91
  151.6 4.4 %all-to-all-start.2 = ((bf16[16,64,512]{2,1,0:T(8,128)(2,1)}), bf16[16,64,512]{2,1,0:T(8,128)(2,1)S(1)}, u32[]{:S(2)}, u32[]{:S(2)}) async-start(bf16[16,64,512]{2,1,0:T(8,128)(2,1)} %bitcast.5), calls=%async_computation.2 | async-start | bytes 2097152 | tf_op jit(solution)/shard_map/all_to_all | solution.py:288
  156.1 3.8 %collective-permute-start.14 = (bf16[2,8,2048]{2,1,0:T(8,128)(2,1)S(1)}, bf16[2,8,2048]{2,1,0:T(8,128)(2,1)S(1)}, u32[]{:S(2)}, u32[]{:S(2)}) collective-permute-start(bf16[2,8,2048]{2,1,0:T(8,128)(2,1)S(1)} %fusion.7), channel_id=1, source_target_pairs={{0,24},{2,26},{4,28},{6,30},{8,16},{10,18},{12,20},{14,22},{16,8},... | collective-permute-start | bytes 196616 | tf_op jit(solution)/shard_map/ppermute | solution.py:293
  160.5 19.4 %collective-permute-done.14 = bf16[2,8,2048]{2,1,0:T(8,128)(2,1)S(1)} collective-permute-done((bf16[2,8,2048]{2,1,0:T(8,128)(2,1)S(1)}, bf16[2,8,2048]{2,1,0:T(8,128)(2,1)S(1)}, u32[]{:S(2)}, u32[]{:S(2)}) %collective-permute-start.14) | collective-permute-done | bytes 65568 | tf_op jit(solution)/shard_map/ppermute | solution.py:293
  179.9 8.3 %collective-permute-done.13 = bf16[2,8,2048]{2,1,0:T(8,128)(2,1)S(1)} collective-permute-done((bf16[2,8,2048]{2,1,0:T(8,128)(2,1)S(1)}, bf16[2,8,2048]{2,1,0:T(8,128)(2,1)S(1)}, u32[]{:S(2)}, u32[]{:S(2)}) %collective-permute-start.13) | collective-permute-done | bytes 65568 | tf_op jit(solution)/shard_map/ppermute | solution.py:293
  188.8 1.5 collective-permute-start.17
  190.3 3.0 %collective-permute-done.15 = bf16[32,2048]{1,0:T(8,128)(2,1)S(1)} collective-permute-done((bf16[32,2048]{1,0:T(8,128)(2,1)S(1)}, bf16[32,2048]{1,0:T(8,128)(2,1)S(1)}, u32[]{:S(2)}, u32[]{:S(2)}) %collective-permute-start.15) | collective-permute-done | bytes 131104 | tf_op jit(solution)/shard_map/ppermute | solution.py:293
  193.4 1.5 collective-permute-start.16
  196.0 4.4 %collective-permute-done.16.refs_1_ = bf16[64,2048]{1,0:T(8,128)(2,1)S(1)} collective-permute-done((bf16[64,2048]{1,0:T(8,128)(2,1)S(1)}, bf16[64,2048]{1,0:T(8,128)(2,1)S(1)}, u32[]{:S(2)}, u32[]{:S(2)}) %collective-permute-start.16) | collective-permute-done | bytes 262176 | tf_op jit(solution)/shard_map/ppermute | solution.py:293
  201.8 1.5 shard_map.92
  203.4 3.4 %shard_map.97 = (f32[512,1536]{1,0:T(8,128)}, f32[512,512]{1,0:T(8,128)}) custom-call(s32[5]{0:T(128)S(1)} %stack.41.place_ref, bf16[64,2048]{1,0:T(8,128)(2,1)S(1)} %pad_maximum_fusion.1.refs_0_, bf16[64,2048]{1,0:T(8,128)(2,1)S(1)} %collective-permute-done.16.refs_1_, bf16[64,2048]{1,0:T(8,128)(2,1)S(1)} %pad_maximum_fusion.2.refs_2_, ...), custom_call_target="tpu_custom_call" | custom-call | bytes 6291476 | tf_op jit(solution)/shard_map/pallas_call | solution.py:41
  (124 shorter events, 37.1 us)
Async XLA Ops:
  3.0 9.4 %copy-start.17 = (bf16[1,512,512]{2,1,0:T(8,128)(2,1)S(1)}, bf16[1,512,512]{2,1,0:T(8,128)(2,1)}, u32[]{:S(2)}) copy-start(bf16[1,512,512]{2,1,0:T(8,128)(2,1)} %param.7) | copy-start | bytes 1572868
  5.0 32.5 %all-to-all-start = ((bf16[16,72,512]{2,1,0:T(8,128)(2,1)}), bf16[16,72,512]{2,1,0:T(8,128)(2,1)S(1)}, u32[]{:S(2)}, u32[]{:S(2)}) async-start(bf16[16,72,512]{2,1,0:T(8,128)(2,1)} %get-tuple-element.35), calls=%async_computation | async-start | bytes 2359296 | tf_op jit(solution)/shard_map/all_to_all | solution.py:288
  37.5 52.3 %all-to-all-start.1 = ((bf16[16,64,512]{2,1,0:T(8,128)(2,1)}), bf16[16,64,512]{2,1,0:T(8,128)(2,1)}, u32[]{:S(2)}, u32[]{:S(2)}) async-start(bf16[16,64,512]{2,1,0:T(8,128)(2,1)} %bitcast.2), calls=%async_computation.1 | async-start | bytes 2097152 | tf_op jit(solution)/shard_map/all_to_all | solution.py:288
  45.1 7.3 %slice-start = ((bf16[512,1536]{1,0:T(8,128)(2,1)}), bf16[512,1024]{1,0:T(8,128)(2,1)S(1)}, s32[]{:S(2)}) async-start(bf16[512,1536]{1,0:T(8,128)(2,1)} %w_ref.3), calls=%async_computation.3 | async-start | bytes 2097152 | tf_op jit(solution)/shard_map/slice | solution.py:453
  47.9 22.9 %collective-permute-start = (bf16[256,512]{1,0:T(8,128)(2,1)S(1)}, bf16[256,512]{1,0:T(8,128)(2,1)S(1)}, u32[]{:S(2)}, u32[]{:S(2)}) collective-permute-start(bf16[256,512]{1,0:T(8,128)(2,1)S(1)} %get-tuple-element.39.tail_ref), channel_id=1, source_target_pairs={{30,0},{0,2},{2,4},{4,6},{6,8},{8,10},{10,12},{12,14},{14,16},{16,... | collective-permute-start | bytes 786440 | tf_op jit(solution)/shard_map/ppermute | solution.py:20
  48.2 23.2 %collective-permute-start.1 = (bf16[256,512]{1,0:T(8,128)(2,1)S(1)}, bf16[256,512]{1,0:T(8,128)(2,1)S(1)}, u32[]{:S(2)}, u32[]{:S(2)}) collective-permute-start(bf16[256,512]{1,0:T(8,128)(2,1)S(1)} %get-tuple-element.40.head_ref), channel_id=1, source_target_pairs={{2,0},{4,2},{6,4},{8,6},{10,8},{12,10},{14,12},{16,14},{18,16},{20... | collective-permute-start | bytes 786440 | tf_op jit(solution)/shard_map/ppermute | solution.py:20
  108.9 4.2 %collective-permute-start.4 = (bf16[256,2048]{1,0:T(8,128)(2,1)}, bf16[256,2048]{1,0:T(8,128)(2,1)}, u32[]{:S(2)}, u32[]{:S(2)}) collective-permute-start(bf16[256,2048]{1,0:T(8,128)(2,1)} %shard_map.94), channel_id=1, source_target_pairs={{0,2},{2,0},{4,6},{6,4},{8,10},{10,8},{12,14},{14,12},{16,18},{18,... | collective-permute-start | bytes 3145736 | tf_op jit(solution)/shard_map/ppermute | solution.py:293
  113.1 13.3 %copy-start.2 = (bf16[512,512]{1,0:T(8,128)(2,1)S(1)}, bf16[512,512]{1,0:T(8,128)(2,1)}, u32[]{:S(2)}) copy-start(bf16[512,512]{1,0:T(8,128)(2,1)} %copy-done) | copy-start | bytes 1572868
  114.7 8.8 %collective-permute-start.5 = (bf16[64,2048]{1,0:T(8,128)(2,1)S(1)}, bf16[64,2048]{1,0:T(8,128)(2,1)S(1)}, u32[]{:S(2)}, u32[]{:S(2)}) collective-permute-start(bf16[64,2048]{1,0:T(8,128)(2,1)S(1)} %get-tuple-element.54), channel_id=1, source_target_pairs={{0,4},{2,6},{4,0},{6,2},{8,12},{10,14},{12,8},{14,10},{16,20},{18,... | collective-permute-start | bytes 786440 | tf_op jit(solution)/shard_map/ppermute | solution.py:293
  114.8 8.8 %collective-permute-start.6 = (bf16[64,2048]{1,0:T(8,128)(2,1)S(1)}, bf16[64,2048]{1,0:T(8,128)(2,1)S(1)}, u32[]{:S(2)}, u32[]{:S(2)}) collective-permute-start(bf16[64,2048]{1,0:T(8,128)(2,1)S(1)} %get-tuple-element.56), channel_id=1, source_target_pairs={{0,1},{1,0},{2,3},{3,2},{4,5},{5,4},{6,7},{7,6},{8,9},{9,8},{10,11... | collective-permute-start | bytes 786440 | tf_op jit(solution)/shard_map/ppermute | solution.py:293
  124.8 9.9 %collective-permute-start.7 = (bf16[32,2048]{1,0:T(8,128)(2,1)}, bf16[32,2048]{1,0:T(8,128)(2,1)}, u32[]{:S(2)}, u32[]{:S(2)}) collective-permute-start(bf16[32,2048]{1,0:T(8,128)(2,1)} %get-tuple-element.58), channel_id=1, source_target_pairs={{0,1},{1,0},{2,3},{3,2},{4,5},{5,4},{6,7},{7,6},{8,9},{9,8},{10,11... | collective-permute-start | bytes 393224 | tf_op jit(solution)/shard_map/ppermute | solution.py:293
  130.3 18.3 %copy-start.9 = (bf16[1024,512]{1,0:T(8,128)(2,1)S(1)}, bf16[1024,512]{1,0:T(8,128)(2,1)}, u32[]{:S(2)}) copy-start(bf16[1024,512]{1,0:T(8,128)(2,1)} %copy-done.8) | copy-start | bytes 3145732
  130.3 18.3 %collective-permute-start.2 = (bf16[256,512]{1,0:T(8,128)(2,1)}, bf16[256,512]{1,0:T(8,128)(2,1)S(1)}, u32[]{:S(2)}, u32[]{:S(2)}) collective-permute-start(bf16[256,512]{1,0:T(8,128)(2,1)} %get-tuple-element.49), channel_id=1, source_target_pairs={{30,0},{0,2},{2,4},{4,6},{6,8},{8,10},{10,12},{12,14},{14,16},{16,... | collective-permute-start | bytes 786440 | tf_op jit(solution)/shard_map/ppermute | solution.py:20
  130.3 18.3 %collective-permute-start.3 = (bf16[256,512]{1,0:T(8,128)(2,1)S(1)}, bf16[256,512]{1,0:T(8,128)(2,1)S(1)}, u32[]{:S(2)}, u32[]{:S(2)}) collective-permute-start(bf16[256,512]{1,0:T(8,128)(2,1)S(1)} %get-tuple-element.50), channel_id=1, source_target_pairs={{2,0},{4,2},{6,4},{8,6},{10,8},{12,10},{14,12},{16,14},{18,16},{20... | collective-permute-start | bytes 786440 | tf_op jit(solution)/shard_map/ppermute | solution.py:20
  134.7 8.9 %collective-permute-start.8 = (bf16[32,2048]{1,0:T(8,128)(2,1)S(1)}, bf16[32,2048]{1,0:T(8,128)(2,1)S(1)}, u32[]{:S(2)}, u32[]{:S(2)}) collective-permute-start(bf16[32,2048]{1,0:T(8,128)(2,1)S(1)} %get-tuple-element.60), channel_id=1, source_target_pairs={{0,4},{2,6},{4,0},{6,2},{8,12},{10,14},{12,8},{14,10},{16,20},{18,... | collective-permute-start | bytes 393224 | tf_op jit(solution)/shard_map/ppermute | solution.py:293
  135.7 15.9 %copy-start.37 = (f32[4,1,8,2048]{3,2,1,0:T(8,128)}, f32[4,1,8,2048]{3,2,1,0:T(8,128)S(1)}, u32[]{:S(2)}) copy-start(f32[4,1,8,2048]{3,2,1,0:T(8,128)S(1)} %add_bitcast_fusion.1) | copy-start | bytes 786436
  143.7 12.3 %collective-permute-start.11 = (bf16[2,8,2048]{2,1,0:T(8,128)(2,1)S(1)}, bf16[2,8,2048]{2,1,0:T(8,128)(2,1)S(1)}, u32[]{:S(2)}, u32[]{:S(2)}) collective-permute-start(bf16[2,8,2048]{2,1,0:T(8,128)(2,1)S(1)} %get-tuple-element.65), channel_id=1, source_target_pairs={{0,24},{2,26},{4,28},{6,30},{8,16},{10,18},{12,20},{14,22},{16,8},... | collective-permute-start | bytes 196616 | tf_op jit(solution)/shard_map/ppermute | solution.py:293
  143.8 12.2 %collective-permute-start.10 = (bf16[2,8,2048]{2,1,0:T(8,128)(2,1)S(1)}, bf16[2,8,2048]{2,1,0:T(8,128)(2,1)S(1)}, u32[]{:S(2)}, u32[]{:S(2)}) collective-permute-start(bf16[2,8,2048]{2,1,0:T(8,128)(2,1)S(1)} %get-tuple-element.64), channel_id=1, source_target_pairs={{0,16},{2,18},{4,20},{6,22},{8,24},{10,26},{12,28},{14,30},{16,0},... | collective-permute-start | bytes 196616 | tf_op jit(solution)/shard_map/ppermute | solution.py:293
  148.1 7.9 %collective-permute-start.9 = (bf16[2,8,2048]{2,1,0:T(8,128)(2,1)S(1)}, bf16[2,8,2048]{2,1,0:T(8,128)(2,1)S(1)}, u32[]{:S(2)}, u32[]{:S(2)}) collective-permute-start(bf16[2,8,2048]{2,1,0:T(8,128)(2,1)S(1)} %get-tuple-element.63), channel_id=1, source_target_pairs={{0,8},{2,10},{4,12},{6,14},{8,0},{10,2},{12,4},{14,6},{16,24},{18,... | collective-permute-start | bytes 196616 | tf_op jit(solution)/shard_map/ppermute | solution.py:293
  151.6 50.2 %copy-start.13 = (bf16[512,1024]{1,0:T(8,128)(2,1)S(1)}, bf16[512,1024]{1,0:T(8,128)(2,1)}, u32[]{:S(2)}) copy-start(bf16[512,1024]{1,0:T(8,128)(2,1)} %copy-done.12) | copy-start | bytes 3145732
  151.6 50.2 %all-to-all-start.2 = ((bf16[16,64,512]{2,1,0:T(8,128)(2,1)}), bf16[16,64,512]{2,1,0:T(8,128)(2,1)S(1)}, u32[]{:S(2)}, u32[]{:S(2)}) async-start(bf16[16,64,512]{2,1,0:T(8,128)(2,1)} %bitcast.5), calls=%async_computation.2 | async-start | bytes 2097152 | tf_op jit(solution)/shard_map/all_to_all | solution.py:288
  156.1 23.8 %collective-permute-start.14 = (bf16[2,8,2048]{2,1,0:T(8,128)(2,1)S(1)}, bf16[2,8,2048]{2,1,0:T(8,128)(2,1)S(1)}, u32[]{:S(2)}, u32[]{:S(2)}) collective-permute-start(bf16[2,8,2048]{2,1,0:T(8,128)(2,1)S(1)} %fusion.7), channel_id=1, source_target_pairs={{0,24},{2,26},{4,28},{6,30},{8,16},{10,18},{12,20},{14,22},{16,8},... | collective-permute-start | bytes 196616 | tf_op jit(solution)/shard_map/ppermute | solution.py:293
  159.9 28.3 %collective-permute-start.13 = (bf16[2,8,2048]{2,1,0:T(8,128)(2,1)S(1)}, bf16[2,8,2048]{2,1,0:T(8,128)(2,1)S(1)}, u32[]{:S(2)}, u32[]{:S(2)}) collective-permute-start(bf16[2,8,2048]{2,1,0:T(8,128)(2,1)S(1)} %fusion.7), channel_id=1, source_target_pairs={{0,16},{2,18},{4,20},{6,22},{8,24},{10,26},{12,28},{14,30},{16,0},... | collective-permute-start | bytes 196616 | tf_op jit(solution)/shard_map/ppermute | solution.py:293
  159.9 28.3 %collective-permute-start.12 = (bf16[2,8,2048]{2,1,0:T(8,128)(2,1)S(1)}, bf16[2,8,2048]{2,1,0:T(8,128)(2,1)S(1)}, u32[]{:S(2)}, u32[]{:S(2)}) collective-permute-start(bf16[2,8,2048]{2,1,0:T(8,128)(2,1)S(1)} %fusion.7), channel_id=1, source_target_pairs={{0,8},{2,10},{4,12},{6,14},{8,0},{10,2},{12,4},{14,6},{16,24},{18,... | collective-permute-start | bytes 196616 | tf_op jit(solution)/shard_map/ppermute | solution.py:293
  188.2 5.1 %collective-permute-start.15 = (bf16[32,2048]{1,0:T(8,128)(2,1)S(1)}, bf16[32,2048]{1,0:T(8,128)(2,1)S(1)}, u32[]{:S(2)}, u32[]{:S(2)}) collective-permute-start(bf16[32,2048]{1,0:T(8,128)(2,1)S(1)} %get-tuple-element.67), channel_id=1, source_target_pairs={{0,1},{1,0},{2,3},{3,2},{4,5},{5,4},{6,7},{7,6},{8,9},{9,8},{10,11... | collective-permute-start | bytes 393224 | tf_op jit(solution)/shard_map/ppermute | solution.py:293
  188.8 6.1 %collective-permute-start.17 = (bf16[32,2048]{1,0:T(8,128)(2,1)S(1)}, bf16[32,2048]{1,0:T(8,128)(2,1)S(1)}, u32[]{:S(2)}, u32[]{:S(2)}) collective-permute-start(bf16[32,2048]{1,0:T(8,128)(2,1)S(1)} %get-tuple-element.66), channel_id=1, source_target_pairs={{0,4},{2,6},{4,0},{6,2},{8,12},{10,14},{12,8},{14,10},{16,20},{18,... | collective-permute-start | bytes 393224 | tf_op jit(solution)/shard_map/ppermute | solution.py:293
  193.4 7.0 %collective-permute-start.16 = (bf16[64,2048]{1,0:T(8,128)(2,1)S(1)}, bf16[64,2048]{1,0:T(8,128)(2,1)S(1)}, u32[]{:S(2)}, u32[]{:S(2)}) collective-permute-start(bf16[64,2048]{1,0:T(8,128)(2,1)S(1)} %pad_maximum_fusion.1.refs_0_), channel_id=1, source_target_pairs={{0,4},{2,6},{4,0},{6,2},{8,12},{10,14},{12,8},{14,10},{16,20},{18,... | collective-permute-start | bytes 786440 | tf_op jit(solution)/shard_map/ppermute | solution.py:293
  194.9 6.7 %collective-permute-start.18 = (bf16[64,2048]{1,0:T(8,128)(2,1)S(1)}, bf16[64,2048]{1,0:T(8,128)(2,1)S(1)}, u32[]{:S(2)}, u32[]{:S(2)}) collective-permute-start(bf16[64,2048]{1,0:T(8,128)(2,1)S(1)} %pad_maximum_fusion.2.refs_2_), channel_id=1, source_target_pairs={{0,1},{1,0},{2,3},{3,2},{4,5},{5,4},{6,7},{7,6},{8,9},{9,8},{10,11... | collective-permute-start | bytes 786440 | tf_op jit(solution)/shard_map/ppermute | solution.py:293
  195.5 7.8 %collective-permute-start.19 = (bf16[64,2048]{1,0:T(8,128)(2,1)S(1)}, bf16[64,2048]{1,0:T(8,128)(2,1)S(1)}, u32[]{:S(2)}, u32[]{:S(2)}) collective-permute-start(bf16[64,2048]{1,0:T(8,128)(2,1)S(1)} %pad_maximum_fusion.1.refs_0_), channel_id=1, source_target_pairs={{0,2},{2,0},{4,6},{6,4},{8,10},{10,8},{12,14},{14,12},{16,18},{18,... | collective-permute-start | bytes 786440 | tf_op jit(solution)/shard_map/ppermute | solution.py:293
  195.5 7.8 %collective-permute-start.21 = (bf16[64,2048]{1,0:T(8,128)(2,1)S(1)}, bf16[64,2048]{1,0:T(8,128)(2,1)}, u32[]{:S(2)}, u32[]{:S(2)}) collective-permute-start(bf16[64,2048]{1,0:T(8,128)(2,1)S(1)} %pad_maximum_fusion.2.refs_2_), channel_id=1, source_target_pairs={{0,2},{2,0},{4,6},{6,4},{8,10},{10,8},{12,14},{14,12},{16,18},{18,... | collective-permute-start | bytes 786440 | tf_op jit(solution)/shard_map/ppermute | solution.py:293
  200.4 2.9 %collective-permute-start.20 = (bf16[64,2048]{1,0:T(8,128)(2,1)S(1)}, bf16[64,2048]{1,0:T(8,128)(2,1)}, u32[]{:S(2)}, u32[]{:S(2)}) collective-permute-start(bf16[64,2048]{1,0:T(8,128)(2,1)S(1)} %collective-permute-done.16.refs_1_), channel_id=1, source_target_pairs={{0,2},{2,0},{4,6},{6,4},{8,10},{10,8},{12,14},{14,12},{16,18},{18,... | collective-permute-start | bytes 786440 | tf_op jit(solution)/shard_map/ppermute | solution.py:293
  201.7 1.7 collective-permute-start.22
  (34 other events, 47.2 us)

commit v4 on v3

v4 whole, which is shorter than its diff:
```python
import functools
import math

import jax
import jax.numpy as jnp
from jax import lax
from jax.experimental import pallas as pl
from jax.experimental.pallas import tpu as pltpu
from jax.sharding import PartitionSpec as P

HEADS = 8
PATCH = 512
INFO_ROWS = 8
GATE_FLOPS = 10**10
FORWARD_FLOPS = 10**11
SPREAD_FLOPS = 13 * 10**9
LANES = 128


def from_behind(block, axis, distance):
    devices = range(lax.axis_size(axis))
    route = [((i - distance) % len(devices), i) for i in devices]
    return lax.ppermute(block, axis, route)


def contract(left, right, left_dim, right_dim):
    return lax.dot_general(
        left, right, (((left_dim,), (right_dim,)), ((), ())), preferred_element_type=jnp.float32
    )


def iota(shape, dim):
    return lax.broadcasted_iota(jnp.int32, shape, dim)


def hot(mask):
    return jnp.where(mask, 1.0, 0.0).astype(jnp.bfloat16)


VMEM = pl.BlockSpec(memory_space=pltpu.VMEM)
SMEM = pl.BlockSpec(memory_space=pltpu.SMEM)
HBM = pl.BlockSpec(memory_space=pltpu.HBM)
ANY = pl.BlockSpec(memory_space=pl.ANY)


def low(*shape):
    return jax.ShapeDtypeStruct(shape, jnp.bfloat16)


def wide(*shape):
    return jax.ShapeDtypeStruct(shape, jnp.float32)


def space(shape):
    return pltpu.VMEM(shape.shape, shape.dtype)


def call(kernel, outs, args, flops, ins=None, out_specs=None, scratch=(), mib=16):
    moved = sum(math.prod(x.shape) * x.dtype.itemsize for x in (*outs, *args))
    return pl.pallas_call(
        kernel,
        out_shape=outs,
        in_specs=ins or [VMEM] * len(args),
        out_specs=out_specs or [VMEM] * len(outs),
        scratch_shapes=list(scratch),
        compiler_params=pltpu.CompilerParams(vmem_limit_bytes=mib * 2**20),
        cost_estimate=pl.CostEstimate(flops=flops, bytes_accessed=moved, transcendentals=0),
    )(*args)


def fetch(sources, places, sems, first=0):
    copies = [
        pltpu.make_async_copy(source, place, sems.at[first + i])
        for i, (source, place) in enumerate(zip(sources, places, strict=True))
    ]
    for copy in copies:
        copy.start()
    return copies


def gate(block, *others, flops=0):
    return pl.pallas_call(
        lambda *refs: None,
        out_shape=jax.ShapeDtypeStruct(block.shape, block.dtype),
        in_specs=[HBM] + [ANY] * len(others),
        out_specs=HBM,
        input_output_aliases={0: 0},
        cost_estimate=pl.CostEstimate(flops=flops, bytes_accessed=0, transcendentals=0),
    )(block, *others)


def pack_points_kernel(dev_hbm, row_hbm, x_hbm, out_ref, slots_ref, dev_ref, row_ref, x_ref, sems):
    copies = fetch([dev_hbm, row_hbm, x_hbm], [dev_ref, row_ref, x_ref], sems)
    n_dev, block, width = out_ref.shape
    cap = block - INFO_ROWS
    rows = x_ref.shape[0]
    copies[0].wait()
    dev = dev_ref[...]
    mine = iota((n_dev, rows), 0) == dev
    mine_f = jnp.where(mine, 1.0, 0.0)
    upto = hot(iota((rows, rows), 0) <= iota((rows, rows), 1))
    running = contract(mine_f.astype(jnp.bfloat16), upto, 1, 0)
    rank = (jnp.sum(running * mine_f, axis=0, keepdims=True) - 1.0).astype(jnp.int32)
    slots = dev * cap + rank
    slots_ref[...] = slots
    at_rank = hot(iota((LANES, rows), 0) % cap == rank)
    copies[1].wait()
    centred = (row_ref[...] - rows // 2).astype(jnp.float32)
    told = jnp.concatenate([mine_f * centred, mine_f], axis=0).astype(jnp.bfloat16)
    got = contract(told, at_rank, 1, 1)
    info = jnp.where(got[n_dev:] > 0.5, got[:n_dev], float(rows))
    per = 256 // cap
    copies[2].wait()
    for first in range(0, n_dev, per):
        pick = hot(iota((per * cap, rows), 0) + first * cap == slots)
        data = contract(pick, x_ref[...], 1, 0)
        for j in range(per):
            dest = first + j
            extra = jnp.broadcast_to(info[dest : dest + 1], (INFO_ROWS, LANES))
            extra = jnp.concatenate(
                [extra, jnp.zeros((INFO_ROWS, width - LANES), jnp.float32)], axis=1
            )
            out_ref[dest] = jnp.concatenate(
                [data[j * cap : (j + 1) * cap], extra], axis=0
            ).astype(jnp.bfloat16)


def pack_grads_kernel(slots_ref, x_ref, out_ref, back_ref):
    total = out_ref.shape[0]
    rows = x_ref.shape[0]
    pick = jnp.where(iota((total, rows), 0) == slots_ref[...], 1.0, 0.0)
    out_ref[...] = contract(pick.astype(jnp.bfloat16), x_ref[...], 1, 0).astype(jnp.bfloat16)
    back_ref[...] = pick.T.astype(jnp.bfloat16)


def place_points_kernel(got_ref, head_ref, tail_ref, at_ref):
    n_dev, block, width = got_ref.shape
    cap = block - INFO_ROWS
    half = head_ref.shape[0]
    rows = 2 * half
    per = LANES // cap
    source = iota((1, LANES), 1) // cap
    centred = (iota((rows, LANES), 0) - half).astype(jnp.float32)
    parts, data = ([], [])
    for first in range(0, n_dev, per):
        at = jnp.zeros((1, LANES), jnp.float32)
        for j in range(per):
            info = got_ref[first + j][:, :LANES].astype(jnp.float32)[cap : cap + 1]
            at = jnp.where(source == j, info, at)
            if cap % 16 == 0:
                data.append(got_ref[first + j][:cap])
            else:
                data.append(got_ref[first + j].astype(jnp.float32)[:cap])
        at_ref[first // per : first // per + 1, :] = at
        parts.append(hot(centred == at))
    placed = contract(
        jnp.concatenate(parts, axis=1), jnp.concatenate(data, axis=0).astype(jnp.bfloat16), 1, 0
    ).astype(jnp.bfloat16)
    head_ref[...] = placed[:half]
    tail_ref[...] = placed[half:]


def place_table(at_ref, rows):
    centred = (iota((rows, LANES), 0) - rows // 2).astype(jnp.float32)
    parts = [
        jnp.where(centred == at_ref[g : g + 1, :], 1.0, 0.0) for g in range(at_ref.shape[0])
    ]
    return jnp.concatenate(parts, axis=1)


def pick_kernel(table_ref, own_hbm, from_before_ref, from_after_ref, out_ref, own_ref, sems):
    (copy,) = fetch([own_hbm], [own_ref], sems)
    copy.wait()
    half = from_before_ref.shape[0]
    own = jnp.concatenate(
        [
            own_ref[:half, :] + from_before_ref[...].astype(jnp.float32),
            own_ref[half:, :] + from_after_ref[...].astype(jnp.float32),
        ],
        axis=0,
    ).astype(jnp.bfloat16)
    out_ref[...] = contract(table_ref[...], own, 1, 0).astype(jnp.bfloat16)


def restore_kernel(table_ref, got_ref, out_ref):
    out_ref[...] = contract(table_ref[...], got_ref[...], 1, 0).astype(jnp.bfloat16)


def forward_kernel(
    at_ref,
    before_hbm,
    head_hbm,
    tail_hbm,
    after_hbm,
    w_hbm,
    w_kv_t_hbm,
    query_hbm,
    kv_hbm,
    key_t_hbm,
    attn_t_hbm,
    probs_hbm,
    points_t_hbm,
    table_hbm,
    points_ref,
    w_ref,
    w_kv_t_ref,
    query_ref,
    kv_ref,
    key_t_ref,
    attn_t_ref,
    probs_ref,
    points_t_ref,
    table_ref,
    sems,
):
    width = w_ref.shape[0]
    head_dim = width // HEADS
    half = points_ref.shape[0] // 4
    quarters = [points_ref.at[pl.ds(i * half, half), :] for i in range(4)]
    copies = fetch(
        [before_hbm, head_hbm, tail_hbm, after_hbm, w_hbm, w_kv_t_hbm],
        [*quarters, w_ref, w_kv_t_ref],
        sems,
    )
    table_ref[...] = place_table(at_ref, 2 * half).T.astype(jnp.bfloat16)
    stores = fetch([table_ref], [table_hbm], sems, 6)
    for copy in copies:
        copy.wait()
    points = points_ref[...]
    query_ref[...] = contract(points[half : 3 * half], w_ref[:, :width], 1, 0).astype(jnp.bfloat16)
    kv_ref[...] = contract(points, w_ref[:, width:], 1, 0).astype(jnp.bfloat16)
    kv_t = contract(w_kv_t_ref[...], points, 1, 1).astype(jnp.bfloat16)
    key_t_ref[...] = kv_t[:width]
    points_t_ref[...] = points.astype(jnp.float32).T.astype(jnp.bfloat16)
    stores += fetch(
        [query_ref, kv_ref, key_t_ref, points_t_ref],
        [query_hbm, kv_hbm, key_t_hbm, points_t_hbm],
        sems,
        7,
    )
    side = iota((1, LANES), 1) // head_dim
    factor = math.log2(math.e) / math.sqrt(head_dim)
    for head in range(HEADS):
        first = head * head_dim // LANES * LANES
        within = head * head_dim % LANES // head_dim
        query = query_ref[:, first : first + LANES]
        query = jnp.where(side == within, query, jnp.zeros_like(query))
        key = kv_ref[:, first : first + LANES]
        scores = jnp.concatenate(
            [
                contract(key[: 2 * half], query[:half], 1, 1),
                contract(key[2 * half :], query[half:], 1, 1),
            ],
            axis=1,
        )
        top = jnp.max(scores, axis=0, keepdims=True)
        weight = jnp.exp2((scores - top) * factor)
        probs = weight * (1.0 / jnp.sum(weight, axis=0, keepdims=True))
        probs_low = probs.astype(jnp.bfloat16)
        probs_ref[head] = probs_low
        stores += fetch([probs_ref.at[head]], [probs_hbm.at[head]], sems, 12 + head)
        value_t = kv_t[width + head * head_dim : width + (head + 1) * head_dim]
        attn_t_ref[head * head_dim : (head + 1) * head_dim, :] = jnp.concatenate(
            [
                contract(value_t[:, : 2 * half], probs_low[:, :half], 1, 0),
                contract(value_t[:, 2 * half :], probs_low[:, half:], 1, 0),
            ],
            axis=1,
        ).astype(jnp.bfloat16)
    stores += fetch([attn_t_ref], [attn_t_hbm], sems, 11)
    for store in stores:
        store.wait()


def weights(points_t, attn_t, grad_query, grad_kv, grads):
    half = grads.shape[0] // 2
    return (
        contract(points_t[:, half : 3 * half], grad_query, 1, 0),
        contract(points_t, grad_kv, 1, 0),
        contract(attn_t, grads, 1, 0),
    )


def backward_kernel(
    core_ref,
    at_ref,
    got_hbm,
    w_out_hbm,
    query_hbm,
    kv_hbm,
    key_t_hbm,
    attn_t_hbm,
    points_t_hbm,
    w_hbm,
    probs_hbm,
    send_ref,
    keep_ref,
    own_hbm,
    before_ref,
    after_ref,
    got_ref,
    w_out_ref,
    query_ref,
    kv_ref,
    key_t_ref,
    attn_t_ref,
    points_t_ref,
    w_ref,
    probs_ref,
    grad_query_ref,
    grad_kv_ref,
    query_t_ref,
    own_ref,
    sems,
):
    width = w_out_ref.shape[0]
    head_dim = width // HEADS
    half = query_ref.shape[0] // 2
    scale = 1.0 / math.sqrt(head_dim)
    copies = fetch(
        [got_hbm, w_out_hbm, attn_t_hbm, kv_hbm, query_hbm, key_t_hbm],
        [got_ref, w_out_ref, attn_t_ref, kv_ref, query_ref, key_t_ref],
        sems,
    )
    probs_copies = []
    for head in range(HEADS):
        probs_copies += fetch([probs_hbm.at[head]], [probs_ref.at[head]], sems, 8 + head)
    late = fetch([points_t_hbm, w_hbm], [points_t_ref, w_ref], sems, 6)
    table = place_table(at_ref, 2 * half).astype(jnp.bfloat16)
    copies[0].wait()
    grads = contract(table, got_ref[...], 1, 0).astype(jnp.bfloat16)
    copies[1].wait()
    grad_attn = contract(grads, w_out_ref[...], 1, 1).astype(jnp.bfloat16)
    grad_attn_t = contract(w_out_ref[...], grads, 1, 1).astype(jnp.bfloat16)
    for copy in copies[2:]:
        copy.wait()
    side = iota((1, LANES), 1) // head_dim
    sides = ((slice(0, half), slice(0, 2 * half)), (slice(half, 2 * half), slice(2 * half, 4 * half)))
    for first in range(0, width, LANES):
        cols = slice(first, first + LANES)
        value_cols = slice(width + first, width + first + LANES)
        grad = grad_attn[:, cols]
        query = query_ref[:, cols]
        for head in range(first // head_dim, (first + LANES) // head_dim):
            probs_copies[head].wait()
        for mine, patch in sides:
            value = kv_ref[patch, value_cols]
            grad_key = jnp.zeros((2 * half, LANES), jnp.float32)
            grad_value = grad_key
            for within in range(LANES // head_dim):
                chans = slice(first + within * head_dim, first + (within + 1) * head_dim)
                probs = probs_ref[first // head_dim + within][:, mine]
                delta = jnp.sum(
                    grad_attn_t[chans, mine].astype(jnp.float32)
                    * attn_t_ref[chans, mine].astype(jnp.float32),
                    axis=0,
                    keepdims=True,
                )
                masked = jnp.where(side == within, grad[mine], jnp.zeros_like(grad[mine]))
                grad_probs = contract(value, masked, 1, 1)
                grad_scores = (probs.astype(jnp.float32) * (grad_probs - delta)).astype(jnp.bfloat16)
                grad_value = jnp.where(
                    side == within, contract(probs, grad[mine], 1, 0), grad_value
                )
                grad_key = jnp.where(
                    side == within, contract(grad_scores, query[mine], 1, 0), grad_key
                )
                query_t_ref[chans, mine] = (
                    contract(key_t_ref[chans, patch], grad_scores, 1, 0) * scale
                )
            grad_kv_ref[patch, cols] = (grad_key * scale).astype(jnp.bfloat16)
            grad_kv_ref[patch, value_cols] = grad_value.astype(jnp.bfloat16)
    grad_query_ref[...] = query_t_ref[...].T.astype(jnp.bfloat16)
    for copy in late:
        copy.wait()
    w_kv = w_ref[:, width:]
    own_ref[...] = contract(grad_query_ref[...], w_ref[:, :width], 1, 1) + contract(
        grad_kv_ref[half : 3 * half, :], w_kv, 1, 1
    )
    (store,) = fetch([own_ref], [own_hbm], sems, 8 + HEADS)
    before_ref[...] = contract(grad_kv_ref[:half, :], w_kv, 1, 1).astype(jnp.bfloat16)
    after_ref[...] = contract(grad_kv_ref[3 * half :, :], w_kv, 1, 1).astype(jnp.bfloat16)
    rows = width // 2
    for side, out_ref in ((core_ref[0], keep_ref), (1 - core_ref[0], send_ref)):
        from_row = pl.multiple_of(side * rows, rows)
        of_query, of_kv, of_out = weights(
            points_t_ref[pl.ds(from_row, rows), :],
            attn_t_ref[pl.ds(from_row, rows), :],
            grad_query_ref[...],
            grad_kv_ref[...],
            grads,
        )
        out_ref[:, :width] = of_query.astype(out_ref.dtype)
        out_ref[:, width : 3 * width] = of_kv.astype(out_ref.dtype)
        out_ref[:, 3 * width :] = of_out.astype(out_ref.dtype)
    store.wait()


def exchange(blocks):
    return lax.all_to_all(blocks, "curve", split_axis=0, concat_axis=0, tiled=True)


def swap(block, axis, mask):
    size = lax.axis_size(axis)
    return lax.ppermute(block, axis, [(i, i ^ mask) for i in range(size)])


def order_blocks(blocks, place):
    count = blocks.shape[0]
    tail = blocks.shape[1:]
    bit = 1
    while bit < count:
        pairs = blocks.reshape(count // (2 * bit), 2, bit, *tail)
        blocks = jnp.where((place & bit) != 0, pairs[:, ::-1], pairs).reshape(count, *tail)
        bit *= 2
    return blocks


def part_rows(total, side, keep_ref, send_ref):
    half = keep_ref.shape[0]
    keep_ref[...] = jnp.where(side == 0, total[:half], total[half:])
    send_ref[...] = jnp.where(side == 0, total[half:], total[:half]).astype(jnp.bfloat16)


def first_sum_kernel(sides_ref, kept_ref, got_ref, keep_a, send_a, keep_b, send_b):
    half = kept_ref.shape[0] // 2
    part_rows(
        kept_ref[:half, :] + got_ref[:half, :].astype(jnp.float32), sides_ref[0], keep_a, send_a
    )
    part_rows(
        kept_ref[half:, :] + got_ref[half:, :].astype(jnp.float32), sides_ref[1], keep_b, send_b
    )


def second_sum_kernel(
    sides_ref, kept_a_ref, got_a_ref, kept_b_ref, got_b_ref, keep_a, send_a, keep_b, send_b
):
    part_rows(
        kept_a_ref[...] + got_a_ref[...].astype(jnp.float32), sides_ref[1], keep_a, send_a
    )
    part_rows(
        kept_b_ref[...] + got_b_ref[...].astype(jnp.float32), sides_ref[0], keep_b, send_b
    )


def third_sum_kernel(
    line_ref, kept_a_ref, got_a_ref, kept_b_ref, got_b_ref, _, mine_ref, *refs
):
    sends, total_ref = (refs[:-1], refs[-1])
    rows = mine_ref.shape[0] // 2
    half = kept_a_ref.shape[0]
    total_ref[:half, :] = kept_a_ref[...] + got_a_ref[...].astype(jnp.float32)
    total_ref[half:, :] = kept_b_ref[...] + got_b_ref[...].astype(jnp.float32)
    for distance, out_ref in enumerate((mine_ref, *sends)):
        at = pl.multiple_of((line_ref[0] ^ distance) * rows, rows)
        out_ref[...] = jnp.concatenate(
            [total_ref[pl.ds(at, rows), :], total_ref[pl.ds(half + at, rows), :]], axis=0
        ).astype(out_ref.dtype)


def spread_kernel(n_line, place_ref, *refs):
    pieces, qkv_ref, out_ref = (refs[:-2], refs[-2], refs[-1])
    n_qkv = qkv_ref.shape[1]
    core, side_x, side_y, line = (place_ref[i] for i in range(4))
    rows = qkv_ref.shape[0] // (16 * n_line)
    for index, piece in enumerate(pieces):
        near_x, near_y = (side_x ^ (index & 1), side_y ^ (index >> 1 & 1))
        near_core = core ^ (index >> 2)
        values = piece[...].astype(jnp.float32)
        for block in range(2 * n_line):
            distance, part = divmod(block, 2)
            first, second = ((near_x, near_y), (near_y, near_x))[part]
            unit = (((near_core * 2 + part) * 2 + first) * 2 + second) * n_line + (line ^ distance)
            row = pl.multiple_of(unit * rows, rows)
            data = values[block * rows : (block + 1) * rows]
            qkv_ref[pl.ds(row, rows), :] = data[:, :n_qkv]
            out_ref[pl.ds(row, rows), :] = data[:, n_qkv:]


def sum_start(keep, send, sides, ready):
    n_line = lax.axis_size("curve") // 4
    line = lax.axis_index("curve") >> 2
    rows, width = keep.shape
    scalar = [SMEM] + [VMEM] * 4
    kept_a, send_a, kept_b, send_b = call(
        first_sum_kernel,
        [wide(rows // 4, width), low(rows // 4, width)] * 2,
        [sides, keep, swap(send, "curve", 1)],
        rows * width,
        scalar[:3],
    )
    got_a = swap(send_a, "curve", 2)
    got_b = swap(send_b, "dp", 1)
    kept_a, send_a, kept_b, send_b = call(
        second_sum_kernel,
        [wide(rows // 8, width), low(rows // 8, width)] * 2,
        [sides, kept_a, got_a, kept_b, got_b],
        rows * width // 2,
        scalar,
    )
    got_a = swap(send_a, "dp", 1)
    got_b = swap(send_b, "curve", 2)
    rows = kept_a.shape[0] // n_line
    if rows % 8 == 0:
        mine, *sends = call(
            third_sum_kernel,
            [wide(2 * rows, width)] + [low(2 * rows, width)] * (n_line - 1),
            [line.reshape(1), kept_a, got_a, kept_b, got_b, ready],
            kept_a.size,
            [*scalar, ANY],
            scratch=[pltpu.VMEM((2 * n_line * rows, width), jnp.float32)],
        )
    else:
        part_a = (kept_a + got_a.astype(jnp.float32)).reshape(n_line, rows, width)
        part_b = (kept_b + got_b.astype(jnp.float32)).reshape(n_line, rows, width)
        both = jnp.concatenate([part_a, part_b], axis=1)
        mine, *sends = [
            lax.dynamic_index_in_dim(both, line ^ k, 0, keepdims=False) for k in range(n_line)
        ]
        sends = [block.astype(jnp.bfloat16) for block in sends]
    for k, block in enumerate(sends):
        mine = mine + swap(block, "curve", 4 * (k + 1)).astype(jnp.float32)
    mine = mine.astype(jnp.bfloat16)
    blocks = [mine] + [swap(mine, "curve", 4 * k) for k in range(1, n_line)]
    if rows % 8 == 0:
        return (jnp.concatenate(blocks, axis=0), line)
    blocks = order_blocks(jnp.stack(blocks), line).reshape(2 * n_line * rows, width)
    return (blocks, jnp.zeros_like(line))


def sum_finish(own, line, sides, width_qkv):
    rows, width = own.shape
    over_x = swap(own, "curve", 2)
    over_y = swap(own, "dp", 1)
    pieces = [own, over_x, over_y, swap(over_x, "dp", 1)]
    pieces += [swap(piece, "curve", 1) for piece in pieces]
    where = jnp.stack([lax.axis_index("curve") & 1, sides[0], sides[1], line])
    return call(
        functools.partial(spread_kernel, lax.axis_size("curve") // 4),
        [wide(8 * rows, width_qkv), wide(8 * rows, width - width_qkv)],
        [where, *pieces],
        SPREAD_FLOPS,
        [SMEM] + [VMEM] * 8,
    )


def on_device(points, grad_out, dest_dev, dest_row, w_qkv, w_out):
    rows, width = points.shape[1:]
    half = rows - PATCH // 2
    n_dev = lax.axis_size("curve")
    cap = 2 * rows // n_dev
    total = n_dev * cap
    place_flops = 2 * total * rows * width
    me = lax.axis_index("curve")
    core = (me & 1).reshape(1)
    sides = jnp.stack([(me >> 1) & 1, lax.axis_index("dp")])
    ids = jax.ShapeDtypeStruct((1, rows), jnp.int32)
    send_points, slots = call(
        pack_points_kernel,
        [low(n_dev, cap + INFO_ROWS, width), ids],
        [dest_dev, dest_row, points[0]],
        place_flops,
        [HBM] * 3,
        scratch=[space(ids), space(ids), space(low(rows, width)), pltpu.SemaphoreType.DMA((3,))],
        mib=60,
    )
    got_points = exchange(send_points)
    send_grads, restore_table = call(
        pack_grads_kernel, [low(total, width), low(rows, total)], [slots, grad_out[0]], place_flops
    )
    head, tail, at = call(
        place_points_kernel,
        [low(half, width), low(half, width), wide(total // LANES, LANES)],
        [got_points],
        place_flops,
    )
    after = from_behind(head, "curve", -1)
    before = from_behind(tail, "curve", 1)
    send_grads = gate(send_grads, at, flops=GATE_FLOPS)
    got_grads = exchange(send_grads.reshape(n_dev, cap, width)).reshape(total, width)
    saved = [
        low(rows, width),
        low(2 * rows, 2 * width),
        low(width, 2 * rows),
        low(width, rows),
        low(HEADS, PATCH, PATCH),
        low(width, 2 * rows),
        low(total, rows),
    ]
    query, kv, key_t, attn_t, probs, points_t, pick_table = call(
        forward_kernel,
        saved,
        [at, before, head, tail, after, w_qkv, w_qkv[:, width:].T],
        FORWARD_FLOPS,
        [VMEM] + [HBM] * 6,
        [HBM] * len(saved),
        [space(low(2 * rows, width)), space(low(width, 3 * width)), space(low(2 * width, width))]
        + [space(x) for x in saved]
        + [pltpu.SemaphoreType.DMA((12 + HEADS,))],
        60,
    )
    held = [got_grads, w_out, query, kv, key_t, attn_t, points_t, w_qkv, probs]
    send, keep, own_input, to_before, to_after = call(
        backward_kernel,
        [
            low(width // 2, 4 * width),
            wide(width // 2, 4 * width),
            wide(rows, width),
            low(half, width),
            low(half, width),
        ],
        [core, at, *held],
        32 * rows * rows * width + 22 * rows * width * width,
        [SMEM, VMEM] + [HBM] * len(held),
        [VMEM, VMEM, HBM, VMEM, VMEM],
        [space(x) for x in held]
        + [
            space(low(rows, width)),
            space(low(2 * rows, 2 * width)),
            space(wide(width, rows)),
            space(wide(rows, width)),
            pltpu.SemaphoreType.DMA((9 + HEADS,)),
        ],
        60,
    )
    from_before = from_behind(to_after, "curve", 1)
    from_after = from_behind(to_before, "curve", -1)
    (picked,) = call(
        pick_kernel,
        [low(total, width)],
        [pick_table, own_input, from_before, from_after],
        place_flops,
        [VMEM, HBM, VMEM, VMEM],
        scratch=[space(wide(rows, width)), pltpu.SemaphoreType.DMA((1,))],
    )
    gathered, line = sum_start(keep, send, sides, picked)
    picked = gate(picked, gathered, flops=GATE_FLOPS)
    returned = exchange(picked.reshape(n_dev, cap, width)).reshape(total, width)
    weight_qkv, weight_out = sum_finish(gathered, line, sides, 3 * width)
    (result,) = call(restore_kernel, [low(rows, width)], [restore_table, returned], place_flops)
    return (result[None], weight_qkv, weight_out)


def solution(mesh):
    placed = (
        P("dp", "curve", None),
        P("dp", "curve", None),
        P("dp", "curve"),
        P("dp", "curve"),
        P(),
        P(),
    )
    return jax.shard_map(
        on_device,
        mesh=mesh,
        in_specs=placed,
        out_specs=(P("dp", "curve", None), P(), P()),
        check_vma=False,
    )
```

time: 208 us -> 164 us (0.79)
  waiting for transfers between devices: 91.6 us -> 65.3 us
  local copies, waits for them, and re-layouts: 33.9 us -> 10.3 us
  Pallas kernels: 33.6 us -> 39.3 us
    unnamed x79 -> x43, local copies, waits for them, and re-layouts: 33.8 us -> 10.3 us
    ppermute x19 -> x18, waiting for transfers between devices: 51.6 us -> 30.2 us  [swap(): return lax.ppermute(block, axis, [(i, i ^ mask) for i in range(size)])]
    ppermute x4, waiting for transfers between devices: 17.7 us -> 0.27 us  [from_behind(): return lax.ppermute(block, axis, route)]
    all_to_all x3, waiting for transfers between devices: 22.3 us -> 34.8 us  [exchange(): lax.all_to_all(blocks, 'curve', split_axis=0, concat_axis=0, tiled=True)]
    pallas_call x13, Pallas kernels: 33.6 us -> 39.3 us  [the longest x11 39.3 us: call(): pl.pallas_call(kernel, out_shape=outs, in_specs=ins or [VMEM] * len(args)...]
    all_to_all x3, starting transfers between devices: 19.3 us -> 15.1 us  [exchange(): lax.all_to_all(blocks, 'curve', split_axis=0, concat_axis=0, tiled=True)]
    ppermute x19 -> x18, starting transfers between devices: 17.2 us -> 19.9 us  [swap(): return lax.ppermute(block, axis, [(i, i ^ mask) for i in range(size)])]
  transfers between devices with their start and end apart: 26 -> 25, of which waited for: 11 -> 17; matrix products, arithmetic and copies ran while one was open for 1% -> 1% of each run, Pallas kernels for 8% -> 11%
where the time goes in v4:
time: 164 us; the launch traced here: 162 us
  waiting for transfers between devices  65.3 us (40%)
  starting transfers between devices  45.5 us (28%)
  Pallas kernels  39.3 us (24%)
  local copies, waits for them, and re-layouts  10.3 us (6%)
    pallas_call x11, Pallas kernels, call(): pl.pallas_call(kernel, out_shape=outs, in_specs=ins or [VMEM] * len(args)...  39.3 us
    all_to_all x3, waiting for transfers between devices, exchange(): lax.all_to_all(blocks, 'curve', split_axis=0, concat_axis=0, tiled=True)  34.8 us
    ppermute x18, waiting for transfers between devices, swap(): return lax.ppermute(block, axis, [(i, i ^ mask) for i in range(size)])  30.2 us
    ppermute x18, starting transfers between devices, swap(): return lax.ppermute(block, axis, [(i, i ^ mask) for i in range(size)])  19.9 us
    all_to_all x3, starting transfers between devices, exchange(): lax.all_to_all(blocks, 'curve', split_axis=0, concat_axis=0, tiled=True)  15.1 us
    ppermute x4, starting transfers between devices, from_behind(): return lax.ppermute(block, axis, route)  10.5 us
    unnamed x43, local copies, waits for them, and re-layouts  10.3 us
  transfers between devices with their start and end apart: 25, of which 17 were waited for; matrix products, arithmetic and copies ran while one was open for 1% of the time, Pallas kernels for 11%

profile of v4, /device:TPU:0, one launch (start us, length us, event | category | flops | bytes accessed | tf_op | source)
XLA Modules:
  0.0 162.1 jit_solution(3559853573430185162)
XLA Ops:
  0.6 2.8 %shard_map.85 = (bf16[16,72,512]{2,1,0:T(8,128)(2,1)}, s32[1,512]{1,0:T(1,128)}) custom-call(s32[1,512]{1,0:T(1,128)} %dev_hbm.1, s32[1,512]{1,0:T(1,128)} %row_hbm.1, bf16[512,512]{1,0:T(8,128)(2,1)} %bitcast.19), custom_call_target="tpu_custom_call" | custom-call | flops 536870912 | bytes 1710080 | tf_op jit(solution)/shard_map/pallas_call | solution.py:60
  3.5 7.5 %all-to-all-start = ((bf16[16,72,512]{2,1,0:T(8,128)(2,1)}), bf16[16,72,512]{2,1,0:T(8,128)(2,1)S(1)}, u32[]{:S(2)}, u32[]{:S(2)}) async-start(bf16[16,72,512]{2,1,0:T(8,128)(2,1)} %get-tuple-element.38), calls=%async_computation | async-start | bytes 2359296 | tf_op jit(solution)/shard_map/all_to_all | solution.py:400
  15.1 21.0 %all-to-all-done.got_ref = bf16[16,72,512]{2,1,0:T(8,128)(2,1)S(1)} async-done(((bf16[16,72,512]{2,1,0:T(8,128)(2,1)}), bf16[16,72,512]{2,1,0:T(8,128)(2,1)S(1)}, u32[]{:S(2)}, u32[]{:S(2)}) %all-to-all-start) | async-done | bytes 1179680 | tf_op jit(solution)/shard_map/all_to_all | solution.py:400
  38.2 5.2 %collective-permute-start.1 = (bf16[256,512]{1,0:T(8,128)(2,1)S(1)}, bf16[256,512]{1,0:T(8,128)(2,1)S(1)}, u32[]{:S(2)}, u32[]{:S(2)}) collective-permute-start(bf16[256,512]{1,0:T(8,128)(2,1)S(1)} %get-tuple-element.41.head_hbm), channel_id=1, source_target_pairs={{2,0},{4,2},{6,4},{8,6},{10,8},{12,10},{14,12},{16,14},{18,16},{20... | collective-permute-start | bytes 786440 | tf_op jit(solution)/shard_map/ppermute | solution.py:23
  43.5 3.9 %all-to-all-start.1 = ((bf16[16,64,512]{2,1,0:T(8,128)(2,1)}), bf16[16,64,512]{2,1,0:T(8,128)(2,1)S(1)}, u32[]{:S(2)}, u32[]{:S(2)}) async-start(bf16[16,64,512]{2,1,0:T(8,128)(2,1)} %bitcast.14), calls=%async_computation.1 | async-start | bytes 2097152 | tf_op jit(solution)/shard_map/all_to_all | solution.py:400
  48.5 11.5 %shard_map.88 = (bf16[512,512]{1,0:T(8,128)(2,1)}, bf16[1024,1024]{1,0:T(8,128)(2,1)}, bf16[512,1024]{1,0:T(8,128)(2,1)}, bf16[512,512]{1,0:T(8,128)(2,1)}, bf16...) custom-call(f32[8,128]{1,0:T(8,128)} %copy-done.16, bf16[256,512]{1,0:T(8,128)(2,1)} %copy-done.19, ...), custom_call_target="tpu_custom_call" | custom-call | flops 99999997952 | bytes 14159872 | tf_op jit(solution)/shard_map/pallas_call | solution.py:60
  60.0 10.1 %all-to-all-done.1 = bf16[16,64,512]{2,1,0:T(8,128)(2,1)S(1)} async-done(((bf16[16,64,512]{2,1,0:T(8,128)(2,1)}), bf16[16,64,512]{2,1,0:T(8,128)(2,1)S(1)}, u32[]{:S(2)}, u32[]{:S(2)}) %all-to-all-start.1) | async-done | bytes 1048608 | tf_op jit(solution)/shard_map/all_to_all | solution.py:400
  71.1 14.6 %shard_map.90 = (bf16[256,2048]{1,0:T(8,128)(2,1)}, f32[256,2048]{1,0:T(8,128)}, f32[512,512]{1,0:T(8,128)}, bf16[256,512]{1,0:T(8,128)(2,1)}, bf16[256,512]{1,0:T(8,128)(2,1)}) custom-call(s32[1]{0:T(128)} %bitcast.3.core_ref, f32[8,128]{1,0:T(8,128)} %copy-done.16, bf16[1024,512]{1,0:T(8,128)(2,1)} %bitcast.17, bf16[512,512]{1,0:T(8,128)(2,1)} %w_out_hbm.1, ...), custom_call_target="tpu_custom_call" | custom-call | flops 7247757312 | bytes 17305604 | tf_op jit(solution)/shard_map/pallas_call | solution.py:60
  86.5 2.4 %collective-permute-done.4.got_ref = bf16[256,2048]{1,0:T(8,128)(2,1)S(1)} collective-permute-done((bf16[256,2048]{1,0:T(8,128)(2,1)}, bf16[256,2048]{1,0:T(8,128)(2,1)S(1)}, u32[]{:S(2)}, u32[]{:S(2)}) %collective-permute-start.4) | collective-permute-done | bytes 1048608 | tf_op jit(solution)/shard_map/ppermute | solution.py:405
  88.9 1.6 copy-done.1
  91.3 2.1 %collective-permute-start.5 = (bf16[64,2048]{1,0:T(8,128)(2,1)S(1)}, bf16[64,2048]{1,0:T(8,128)(2,1)S(1)}, u32[]{:S(2)}, u32[]{:S(2)}) collective-permute-start(bf16[64,2048]{1,0:T(8,128)(2,1)S(1)} %get-tuple-element.56), channel_id=1, source_target_pairs={{0,4},{2,6},{4,0},{6,2},{8,12},{10,14},{12,8},{14,10},{16,20},{18,... | collective-permute-start | bytes 786440 | tf_op jit(solution)/shard_map/ppermute | solution.py:405
  93.4 1.5 collective-permute-start.6
  94.9 4.4 %collective-permute-start.3 = (bf16[256,512]{1,0:T(8,128)(2,1)}, bf16[256,512]{1,0:T(8,128)(2,1)S(1)}, u32[]{:S(2)}, u32[]{:S(2)}) collective-permute-start(bf16[256,512]{1,0:T(8,128)(2,1)} %get-tuple-element.52), channel_id=1, source_target_pairs={{2,0},{4,2},{6,4},{8,6},{10,8},{12,10},{14,12},{16,14},{18,16},{20... | collective-permute-start | bytes 786440 | tf_op jit(solution)/shard_map/ppermute | solution.py:23
  100.2 1.5 collective-permute-done.6.got_b_ref
  101.7 1.3 shard_map.93
  104.4 2.9 %collective-permute-start.7 = (bf16[32,2048]{1,0:T(8,128)(2,1)}, bf16[32,2048]{1,0:T(8,128)(2,1)S(1)}, u32[]{:S(2)}, u32[]{:S(2)}) collective-permute-start(bf16[32,2048]{1,0:T(8,128)(2,1)} %get-tuple-element.60), channel_id=1, source_target_pairs={{0,1},{1,0},{2,3},{3,2},{4,5},{5,4},{6,7},{7,6},{8,9},{9,8},{10,11... | collective-permute-start | bytes 393224 | tf_op jit(solution)/shard_map/ppermute | solution.py:405
  110.9 1.6 collective-permute-done.8.got_b_ref
  113.5 4.2 %collective-permute-start.11 = (bf16[16,2048]{1,0:T(8,128)(2,1)S(1)}, bf16[16,2048]{1,0:T(8,128)(2,1)S(1)}, u32[]{:S(2)}, u32[]{:S(2)}) collective-permute-start(bf16[16,2048]{1,0:T(8,128)(2,1)S(1)} %get-tuple-element.66), channel_id=1, source_target_pairs={{0,24},{2,26},{4,28},{6,30},{8,16},{10,18},{12,20},{14,22},{16,8},... | collective-permute-start | bytes 196616 | tf_op jit(solution)/shard_map/ppermute | solution.py:405
  118.5 2.2 %collective-permute-done.11 = bf16[16,2048]{1,0:T(8,128)(2,1)S(1)} collective-permute-done((bf16[16,2048]{1,0:T(8,128)(2,1)S(1)}, bf16[16,2048]{1,0:T(8,128)(2,1)S(1)}, u32[]{:S(2)}, u32[]{:S(2)}) %collective-permute-start.11) | collective-permute-done | bytes 65568 | tf_op jit(solution)/shard_map/ppermute | solution.py:405
  120.8 3.1 %collective-permute-done.10 = bf16[16,2048]{1,0:T(8,128)(2,1)S(1)} collective-permute-done((bf16[16,2048]{1,0:T(8,128)(2,1)S(1)}, bf16[16,2048]{1,0:T(8,128)(2,1)S(1)}, u32[]{:S(2)}, u32[]{:S(2)}) %collective-permute-start.10) | collective-permute-done | bytes 65568 | tf_op jit(solution)/shard_map/ppermute | solution.py:405
  123.9 2.0 %collective-permute-start.14 = (bf16[16,2048]{1,0:T(8,128)(2,1)S(1)}, bf16[16,2048]{1,0:T(8,128)(2,1)S(1)}, u32[]{:S(2)}, u32[]{:S(2)}) collective-permute-start(bf16[16,2048]{1,0:T(8,128)(2,1)S(1)} %add_convert_fusion), channel_id=1, source_target_pairs={{0,24},{2,26},{4,28},{6,30},{8,16},{10,18},{12,20},{14,22},{16,8},... | collective-permute-start | bytes 196616 | tf_op jit(solution)/shard_map/ppermute | solution.py:405
  125.9 2.4 %collective-permute-start.12 = (bf16[16,2048]{1,0:T(8,128)(2,1)S(1)}, bf16[16,2048]{1,0:T(8,128)(2,1)S(1)}, u32[]{:S(2)}, u32[]{:S(2)}) collective-permute-start(bf16[16,2048]{1,0:T(8,128)(2,1)S(1)} %add_convert_fusion), channel_id=1, source_target_pairs={{0,8},{2,10},{4,12},{6,14},{8,0},{10,2},{12,4},{14,6},{16,24},{18,... | collective-permute-start | bytes 196616 | tf_op jit(solution)/shard_map/ppermute | solution.py:405
  128.4 1.7 %collective-permute-done.14 = bf16[16,2048]{1,0:T(8,128)(2,1)S(1)} collective-permute-done((bf16[16,2048]{1,0:T(8,128)(2,1)S(1)}, bf16[16,2048]{1,0:T(8,128)(2,1)S(1)}, u32[]{:S(2)}, u32[]{:S(2)}) %collective-permute-start.14) | collective-permute-done | bytes 65568 | tf_op jit(solution)/shard_map/ppermute | solution.py:405
  130.0 1.4 collective-permute-done.13
  132.2 1.8 %collective-permute-start.15 = (bf16[64,2048]{1,0:T(8,128)(2,1)}, bf16[64,2048]{1,0:T(8,128)(2,1)S(1)}, u32[]{:S(2)}, u32[]{:S(2)}) collective-permute-start(bf16[64,2048]{1,0:T(8,128)(2,1)} %pad_maximum_fusion.refs_1_.refs_0_), channel_id=1, source_target_pairs={{0,4},{2,6},{4,0},{6,2},{8,12},{10,14},{12,8},{14,10},{16,20},{18,... | collective-permute-start | bytes 786440 | tf_op jit(solution)/shard_map/ppermute | solution.py:405
  133.9 3.7 %all-to-all-start.2 = ((bf16[16,64,512]{2,1,0:T(8,128)(2,1)}), bf16[16,64,512]{2,1,0:T(8,128)(2,1)S(1)}, u32[]{:S(2)}, u32[]{:S(2)}) async-start(bf16[16,64,512]{2,1,0:T(8,128)(2,1)} %bitcast.12), calls=%async_computation.2 | async-start | bytes 2097152 | tf_op jit(solution)/shard_map/all_to_all | solution.py:400
  140.3 6.8 %collective-permute-done.16.refs_2_ = bf16[64,2048]{1,0:T(8,128)(2,1)S(1)} collective-permute-done((bf16[64,2048]{1,0:T(8,128)(2,1)}, bf16[64,2048]{1,0:T(8,128)(2,1)S(1)}, u32[]{:S(2)}, u32[]{:S(2)}) %collective-permute-start.16) | collective-permute-done | bytes 262176 | tf_op jit(solution)/shard_map/ppermute | solution.py:405
  147.1 5.0 %collective-permute-done.17.refs_3_ = bf16[64,2048]{1,0:T(8,128)(2,1)S(1)} collective-permute-done((bf16[64,2048]{1,0:T(8,128)(2,1)S(1)}, bf16[64,2048]{1,0:T(8,128)(2,1)S(1)}, u32[]{:S(2)}, u32[]{:S(2)}) %collective-permute-start.17) | collective-permute-done | bytes 262176 | tf_op jit(solution)/shard_map/ppermute | solution.py:405
  152.2 1.4 collective-permute-done.21.refs_7_
  153.6 3.3 %shard_map.97 = (f32[512,1536]{1,0:T(8,128)}, f32[512,512]{1,0:T(8,128)}) custom-call(s32[4]{0:T(128)S(1)} %pad_add_fusion.1.place_ref, bf16[64,2048]{1,0:T(8,128)(2,1)} %pad_maximum_fusion.refs_1_.refs_0_, bf16[64,2048]{1,0:T(8,128)(2,1)S(1)} %collective-permute-done.15.refs_1_, bf16[64,2048]{1,0:T(8,128)(2,1)S(1)} %collective-permute-done.16.refs_2_, ...), custom_call_target="tpu_custom_call" | custom-call | flops 12999999488 | bytes 6291472 | tf_op jit(solution)/shard_map/pallas_call | solution.py:60
  157.0 3.6 %all-to-all-done.2 = bf16[16,64,512]{2,1,0:T(8,128)(2,1)S(1)} async-done(((bf16[16,64,512]{2,1,0:T(8,128)(2,1)}), bf16[16,64,512]{2,1,0:T(8,128)(2,1)S(1)}, u32[]{:S(2)}, u32[]{:S(2)}) %all-to-all-start.2) | async-done | bytes 1048608 | tf_op jit(solution)/shard_map/all_to_all | solution.py:400
  160.6 1.5 shard_map.96
  (80 shorter events, 21.0 us)
Async XLA Ops:
  3.5 7.6 %slice-start = ((bf16[512,1536]{1,0:T(8,128)(2,1)}), bf16[512,1024]{1,0:T(8,128)(2,1)S(1)}, s32[]{:S(2)}) async-start(bf16[512,1536]{1,0:T(8,128)(2,1)} %w_hbm.3), calls=%async_computation.3 | async-start | bytes 2097152 | tf_op jit(solution)/shard_map/slice | solution.py:593
  3.5 32.6 %all-to-all-start = ((bf16[16,72,512]{2,1,0:T(8,128)(2,1)}), bf16[16,72,512]{2,1,0:T(8,128)(2,1)S(1)}, u32[]{:S(2)}, u32[]{:S(2)}) async-start(bf16[16,72,512]{2,1,0:T(8,128)(2,1)} %get-tuple-element.38), calls=%async_computation | async-start | bytes 2359296 | tf_op jit(solution)/shard_map/all_to_all | solution.py:400
  37.4 6.0 %copy-start.14 = (bf16[256,512]{1,0:T(8,128)(2,1)}, bf16[256,512]{1,0:T(8,128)(2,1)S(1)}, u32[]{:S(2)}) copy-start(bf16[256,512]{1,0:T(8,128)(2,1)S(1)} %get-tuple-element.41.head_hbm) | copy-start | bytes 786436
  37.4 6.0 %copy-start.15 = (bf16[256,512]{1,0:T(8,128)(2,1)}, bf16[256,512]{1,0:T(8,128)(2,1)S(1)}, u32[]{:S(2)}) copy-start(bf16[256,512]{1,0:T(8,128)(2,1)S(1)} %get-tuple-element.40.tail_hbm) | copy-start | bytes 786436
  37.4 10.2 %collective-permute-start = (bf16[256,512]{1,0:T(8,128)(2,1)S(1)}, bf16[256,512]{1,0:T(8,128)(2,1)S(1)}, u32[]{:S(2)}, u32[]{:S(2)}) collective-permute-start(bf16[256,512]{1,0:T(8,128)(2,1)S(1)} %get-tuple-element.40.tail_hbm), channel_id=1, source_target_pairs={{30,0},{0,2},{2,4},{4,6},{6,8},{8,10},{10,12},{12,14},{14,16},{16,... | collective-permute-start | bytes 786440 | tf_op jit(solution)/shard_map/ppermute | solution.py:23
  38.2 9.4 %collective-permute-start.1 = (bf16[256,512]{1,0:T(8,128)(2,1)S(1)}, bf16[256,512]{1,0:T(8,128)(2,1)S(1)}, u32[]{:S(2)}, u32[]{:S(2)}) collective-permute-start(bf16[256,512]{1,0:T(8,128)(2,1)S(1)} %get-tuple-element.41.head_hbm), channel_id=1, source_target_pairs={{2,0},{4,2},{6,4},{8,6},{10,8},{12,10},{14,12},{16,14},{18,16},{20... | collective-permute-start | bytes 786440 | tf_op jit(solution)/shard_map/ppermute | solution.py:23
  43.5 26.6 %all-to-all-start.1 = ((bf16[16,64,512]{2,1,0:T(8,128)(2,1)}), bf16[16,64,512]{2,1,0:T(8,128)(2,1)S(1)}, u32[]{:S(2)}, u32[]{:S(2)}) async-start(bf16[16,64,512]{2,1,0:T(8,128)(2,1)} %bitcast.14), calls=%async_computation.1 | async-start | bytes 2097152 | tf_op jit(solution)/shard_map/all_to_all | solution.py:400
  85.7 3.2 %collective-permute-start.4 = (bf16[256,2048]{1,0:T(8,128)(2,1)}, bf16[256,2048]{1,0:T(8,128)(2,1)S(1)}, u32[]{:S(2)}, u32[]{:S(2)}) collective-permute-start(bf16[256,2048]{1,0:T(8,128)(2,1)} %get-tuple-element.54), channel_id=1, source_target_pairs={{0,2},{2,0},{4,6},{6,4},{8,10},{10,8},{12,14},{14,12},{16,18},{18,... | collective-permute-start | bytes 3145736 | tf_op jit(solution)/shard_map/ppermute | solution.py:405
  90.5 17.5 %copy-start.2 = (bf16[1024,512]{1,0:T(8,128)(2,1)S(1)}, bf16[1024,512]{1,0:T(8,128)(2,1)}, u32[]{:S(2)}) copy-start(bf16[1024,512]{1,0:T(8,128)(2,1)} %get-tuple-element.42.table_ref) | copy-start | bytes 3145732
  90.5 17.5 %copy-start.3 = (f32[512,512]{1,0:T(8,128)S(1)}, f32[512,512]{1,0:T(8,128)}, u32[]{:S(2)}) copy-start(f32[512,512]{1,0:T(8,128)} %get-tuple-element.50.own_hbm) | copy-start | bytes 3145732
  91.3 8.9 %collective-permute-start.5 = (bf16[64,2048]{1,0:T(8,128)(2,1)S(1)}, bf16[64,2048]{1,0:T(8,128)(2,1)S(1)}, u32[]{:S(2)}, u32[]{:S(2)}) collective-permute-start(bf16[64,2048]{1,0:T(8,128)(2,1)S(1)} %get-tuple-element.56), channel_id=1, source_target_pairs={{0,4},{2,6},{4,0},{6,2},{8,12},{10,14},{12,8},{14,10},{16,20},{18,... | collective-permute-start | bytes 786440 | tf_op jit(solution)/shard_map/ppermute | solution.py:405
  93.4 8.3 %collective-permute-start.6 = (bf16[64,2048]{1,0:T(8,128)(2,1)S(1)}, bf16[64,2048]{1,0:T(8,128)(2,1)S(1)}, u32[]{:S(2)}, u32[]{:S(2)}) collective-permute-start(bf16[64,2048]{1,0:T(8,128)(2,1)S(1)} %get-tuple-element.58), channel_id=1, source_target_pairs={{0,1},{1,0},{2,3},{3,2},{4,5},{5,4},{6,7},{7,6},{8,9},{9,8},{10,11... | collective-permute-start | bytes 786440 | tf_op jit(solution)/shard_map/ppermute | solution.py:405
  94.9 12.4 %collective-permute-start.2 = (bf16[256,512]{1,0:T(8,128)(2,1)}, bf16[256,512]{1,0:T(8,128)(2,1)S(1)}, u32[]{:S(2)}, u32[]{:S(2)}) collective-permute-start(bf16[256,512]{1,0:T(8,128)(2,1)} %get-tuple-element.51), channel_id=1, source_target_pairs={{30,0},{0,2},{2,4},{4,6},{6,8},{8,10},{10,12},{12,14},{14,16},{16,... | collective-permute-start | bytes 786440 | tf_op jit(solution)/shard_map/ppermute | solution.py:23
  94.9 12.4 %collective-permute-start.3 = (bf16[256,512]{1,0:T(8,128)(2,1)}, bf16[256,512]{1,0:T(8,128)(2,1)S(1)}, u32[]{:S(2)}, u32[]{:S(2)}) collective-permute-start(bf16[256,512]{1,0:T(8,128)(2,1)} %get-tuple-element.52), channel_id=1, source_target_pairs={{2,0},{4,2},{6,4},{8,6},{10,8},{12,10},{14,12},{16,14},{18,16},{20... | collective-permute-start | bytes 786440 | tf_op jit(solution)/shard_map/ppermute | solution.py:23
  104.4 6.6 %collective-permute-start.7 = (bf16[32,2048]{1,0:T(8,128)(2,1)}, bf16[32,2048]{1,0:T(8,128)(2,1)S(1)}, u32[]{:S(2)}, u32[]{:S(2)}) collective-permute-start(bf16[32,2048]{1,0:T(8,128)(2,1)} %get-tuple-element.60), channel_id=1, source_target_pairs={{0,1},{1,0},{2,3},{3,2},{4,5},{5,4},{6,7},{7,6},{8,9},{9,8},{10,11... | collective-permute-start | bytes 393224 | tf_op jit(solution)/shard_map/ppermute | solution.py:405
  107.3 5.3 %collective-permute-start.8 = (bf16[32,2048]{1,0:T(8,128)(2,1)}, bf16[32,2048]{1,0:T(8,128)(2,1)}, u32[]{:S(2)}, u32[]{:S(2)}) collective-permute-start(bf16[32,2048]{1,0:T(8,128)(2,1)} %get-tuple-element.62), channel_id=1, source_target_pairs={{0,4},{2,6},{4,0},{6,2},{8,12},{10,14},{12,8},{14,10},{16,20},{18,... | collective-permute-start | bytes 393224 | tf_op jit(solution)/shard_map/ppermute | solution.py:405
  109.7 24.2 %copy-start = (bf16[1024,512]{1,0:T(8,128)(2,1)}, bf16[1024,512]{1,0:T(8,128)(2,1)S(1)}, u32[]{:S(2)}) copy-start(bf16[1024,512]{1,0:T(8,128)(2,1)S(1)} %shard_map.91._.refs_0_) | copy-start | bytes 3145732
  113.5 7.2 %collective-permute-start.11 = (bf16[16,2048]{1,0:T(8,128)(2,1)S(1)}, bf16[16,2048]{1,0:T(8,128)(2,1)S(1)}, u32[]{:S(2)}, u32[]{:S(2)}) collective-permute-start(bf16[16,2048]{1,0:T(8,128)(2,1)S(1)} %get-tuple-element.66), channel_id=1, source_target_pairs={{0,24},{2,26},{4,28},{6,30},{8,16},{10,18},{12,20},{14,22},{16,8},... | collective-permute-start | bytes 196616 | tf_op jit(solution)/shard_map/ppermute | solution.py:405
  117.7 6.1 %collective-permute-start.10 = (bf16[16,2048]{1,0:T(8,128)(2,1)S(1)}, bf16[16,2048]{1,0:T(8,128)(2,1)S(1)}, u32[]{:S(2)}, u32[]{:S(2)}) collective-permute-start(bf16[16,2048]{1,0:T(8,128)(2,1)S(1)} %get-tuple-element.65), channel_id=1, source_target_pairs={{0,16},{2,18},{4,20},{6,22},{8,24},{10,26},{12,28},{14,30},{16,0},... | collective-permute-start | bytes 196616 | tf_op jit(solution)/shard_map/ppermute | solution.py:405
  118.3 5.6 %collective-permute-start.9 = (bf16[16,2048]{1,0:T(8,128)(2,1)S(1)}, bf16[16,2048]{1,0:T(8,128)(2,1)S(1)}, u32[]{:S(2)}, u32[]{:S(2)}) collective-permute-start(bf16[16,2048]{1,0:T(8,128)(2,1)S(1)} %get-tuple-element.64), channel_id=1, source_target_pairs={{0,8},{2,10},{4,12},{6,14},{8,0},{10,2},{12,4},{14,6},{16,24},{18,... | collective-permute-start | bytes 196616 | tf_op jit(solution)/shard_map/ppermute | solution.py:405
  123.9 6.1 %collective-permute-start.14 = (bf16[16,2048]{1,0:T(8,128)(2,1)S(1)}, bf16[16,2048]{1,0:T(8,128)(2,1)S(1)}, u32[]{:S(2)}, u32[]{:S(2)}) collective-permute-start(bf16[16,2048]{1,0:T(8,128)(2,1)S(1)} %add_convert_fusion), channel_id=1, source_target_pairs={{0,24},{2,26},{4,28},{6,30},{8,16},{10,18},{12,20},{14,22},{16,8},... | collective-permute-start | bytes 196616 | tf_op jit(solution)/shard_map/ppermute | solution.py:405
  125.9 5.5 %collective-permute-start.13 = (bf16[16,2048]{1,0:T(8,128)(2,1)S(1)}, bf16[16,2048]{1,0:T(8,128)(2,1)S(1)}, u32[]{:S(2)}, u32[]{:S(2)}) collective-permute-start(bf16[16,2048]{1,0:T(8,128)(2,1)S(1)} %add_convert_fusion), channel_id=1, source_target_pairs={{0,16},{2,18},{4,20},{6,22},{8,24},{10,26},{12,28},{14,30},{16,0},... | collective-permute-start | bytes 196616 | tf_op jit(solution)/shard_map/ppermute | solution.py:405
  125.9 5.5 %collective-permute-start.12 = (bf16[16,2048]{1,0:T(8,128)(2,1)S(1)}, bf16[16,2048]{1,0:T(8,128)(2,1)S(1)}, u32[]{:S(2)}, u32[]{:S(2)}) collective-permute-start(bf16[16,2048]{1,0:T(8,128)(2,1)S(1)} %add_convert_fusion), channel_id=1, source_target_pairs={{0,8},{2,10},{4,12},{6,14},{8,0},{10,2},{12,4},{14,6},{16,24},{18,... | collective-permute-start | bytes 196616 | tf_op jit(solution)/shard_map/ppermute | solution.py:405
  132.2 6.6 %collective-permute-start.15 = (bf16[64,2048]{1,0:T(8,128)(2,1)}, bf16[64,2048]{1,0:T(8,128)(2,1)S(1)}, u32[]{:S(2)}, u32[]{:S(2)}) collective-permute-start(bf16[64,2048]{1,0:T(8,128)(2,1)} %pad_maximum_fusion.refs_1_.refs_0_), channel_id=1, source_target_pairs={{0,4},{2,6},{4,0},{6,2},{8,12},{10,14},{12,8},{14,10},{16,20},{18,... | collective-permute-start | bytes 786440 | tf_op jit(solution)/shard_map/ppermute | solution.py:405
  133.9 26.7 %all-to-all-start.2 = ((bf16[16,64,512]{2,1,0:T(8,128)(2,1)}), bf16[16,64,512]{2,1,0:T(8,128)(2,1)S(1)}, u32[]{:S(2)}, u32[]{:S(2)}) async-start(bf16[16,64,512]{2,1,0:T(8,128)(2,1)} %bitcast.12), calls=%async_computation.2 | async-start | bytes 2097152 | tf_op jit(solution)/shard_map/all_to_all | solution.py:400
  137.7 9.4 %collective-permute-start.16 = (bf16[64,2048]{1,0:T(8,128)(2,1)}, bf16[64,2048]{1,0:T(8,128)(2,1)S(1)}, u32[]{:S(2)}, u32[]{:S(2)}) collective-permute-start(bf16[64,2048]{1,0:T(8,128)(2,1)} %pad_maximum_fusion.refs_1_.refs_0_), channel_id=1, source_target_pairs={{0,1},{1,0},{2,3},{3,2},{4,5},{5,4},{6,7},{7,6},{8,9},{9,8},{10,11... | collective-permute-start | bytes 786440 | tf_op jit(solution)/shard_map/ppermute | solution.py:405
  138.7 13.4 %collective-permute-start.17 = (bf16[64,2048]{1,0:T(8,128)(2,1)S(1)}, bf16[64,2048]{1,0:T(8,128)(2,1)S(1)}, u32[]{:S(2)}, u32[]{:S(2)}) collective-permute-start(bf16[64,2048]{1,0:T(8,128)(2,1)S(1)} %collective-permute-done.15.refs_1_), channel_id=1, source_target_pairs={{0,1},{1,0},{2,3},{3,2},{4,5},{5,4},{6,7},{7,6},{8,9},{9,8},{10,11... | collective-permute-start | bytes 786440 | tf_op jit(solution)/shard_map/ppermute | solution.py:405
  139.8 12.4 %collective-permute-start.18 = (bf16[64,2048]{1,0:T(8,128)(2,1)}, bf16[64,2048]{1,0:T(8,128)(2,1)S(1)}, u32[]{:S(2)}, u32[]{:S(2)}) collective-permute-start(bf16[64,2048]{1,0:T(8,128)(2,1)} %pad_maximum_fusion.refs_1_.refs_0_), channel_id=1, source_target_pairs={{0,2},{2,0},{4,6},{6,4},{8,10},{10,8},{12,14},{14,12},{16,18},{18,... | collective-permute-start | bytes 786440 | tf_op jit(solution)/shard_map/ppermute | solution.py:405
  139.8 12.4 %collective-permute-start.19 = (bf16[64,2048]{1,0:T(8,128)(2,1)S(1)}, bf16[64,2048]{1,0:T(8,128)(2,1)S(1)}, u32[]{:S(2)}, u32[]{:S(2)}) collective-permute-start(bf16[64,2048]{1,0:T(8,128)(2,1)S(1)} %collective-permute-done.15.refs_1_), channel_id=1, source_target_pairs={{0,2},{2,0},{4,6},{6,4},{8,10},{10,8},{12,14},{14,12},{16,18},{18,... | collective-permute-start | bytes 786440 | tf_op jit(solution)/shard_map/ppermute | solution.py:405
  147.1 5.1 %collective-permute-start.20 = (bf16[64,2048]{1,0:T(8,128)(2,1)S(1)}, bf16[64,2048]{1,0:T(8,128)(2,1)S(1)}, u32[]{:S(2)}, u32[]{:S(2)}) collective-permute-start(bf16[64,2048]{1,0:T(8,128)(2,1)S(1)} %collective-permute-done.16.refs_2_), channel_id=1, source_target_pairs={{0,2},{2,0},{4,6},{6,4},{8,10},{10,8},{12,14},{14,12},{16,18},{18,... | collective-permute-start | bytes 786440 | tf_op jit(solution)/shard_map/ppermute | solution.py:405
  152.1 1.5 collective-permute-start.21
  152.2 8.4 %copy-start.5 = (bf16[512,1024]{1,0:T(8,128)(2,1)S(1)}, bf16[512,1024]{1,0:T(8,128)(2,1)}, u32[]{:S(2)}) copy-start(bf16[512,1024]{1,0:T(8,128)(2,1)} %copy-done.4) | copy-start | bytes 3145732
  (15 other events, 19.6 us)

commit v5 on v4

--- a/solution.py
+++ b/solution.py
@@ -13,14 +13,8 @@
 INFO_ROWS = 8
 GATE_FLOPS = 10**10
 FORWARD_FLOPS = 10**11
-SPREAD_FLOPS = 13 * 10**9
+SPREAD_FLOPS = 16 * 10**9
 LANES = 128
-
-
-def from_behind(block, axis, distance):
-    devices = range(lax.axis_size(axis))
-    route = [((i - distance) % len(devices), i) for i in devices]
-    return lax.ppermute(block, axis, route)
 
 
 def contract(left, right, left_dim, right_dim):
@@ -91,9 +85,9 @@
 
 def pack_points_kernel(dev_hbm, row_hbm, x_hbm, out_ref, slots_ref, dev_ref, row_ref, x_ref, sems):
     copies = fetch([dev_hbm, row_hbm, x_hbm], [dev_ref, row_ref, x_ref], sems)
-    n_dev, block, width = out_ref.shape
-    cap = block - INFO_ROWS
-    rows = x_ref.shape[0]
+    n_dev, block, _ = out_ref.shape
+    rows, width = x_ref.shape
+    cap = (block - INFO_ROWS) * LANES // width
     copies[0].wait()
     dev = dev_ref[...]
     mine = iota((n_dev, rows), 0) == dev
@@ -116,13 +110,11 @@
         data = contract(pick, x_ref[...], 1, 0)
         for j in range(per):
             dest = first + j
-            extra = jnp.broadcast_to(info[dest : dest + 1], (INFO_ROWS, LANES))
-            extra = jnp.concatenate(
-                [extra, jnp.zeros((INFO_ROWS, width - LANES), jnp.float32)], axis=1
-            )
-            out_ref[dest] = jnp.concatenate(
-                [data[j * cap : (j + 1) * cap], extra], axis=0
-            ).astype(jnp.bfloat16)
+            stack = [
+                data[j * cap : (j + 1) * cap, col : col + LANES] for col in range(0, width, LANES)
+            ]
+            stack.append(jnp.broadcast_to(info[dest : dest + 1], (INFO_ROWS, LANES)))
+            out_ref[dest] = jnp.concatenate(stack, axis=0).astype(jnp.bfloat16)
 
 
 def pack_grads_kernel(slots_ref, x_ref, out_ref, back_ref):
@@ -133,11 +125,11 @@
     back_ref[...] = pick.T.astype(jnp.bfloat16)
 
 
-def place_points_kernel(got_ref, head_ref, tail_ref, at_ref):
-    n_dev, block, width = got_ref.shape
-    cap = block - INFO_ROWS
-    half = head_ref.shape[0]
-    rows = 2 * half
+def place_points_kernel(core_ref, got_ref, own_ref, near_ref, far_ref, at_ref):
+    n_dev, block, _ = got_ref.shape
+    rows, width = own_ref.shape
+    cap = (block - INFO_ROWS) * LANES // width
+    half = rows // 2
     per = LANES // cap
     source = iota((1, LANES), 1) // cap
     centred = (iota((rows, LANES), 0) - half).astype(jnp.float32)
@@ -145,19 +137,21 @@
     for first in range(0, n_dev, per):
         at = jnp.zeros((1, LANES), jnp.float32)
         for j in range(per):
-            info = got_ref[first + j][:, :LANES].astype(jnp.float32)[cap : cap + 1]
+            got = got_ref[first + j]
+            info = got.astype(jnp.float32)[block - INFO_ROWS : block - INFO_ROWS + 1]
             at = jnp.where(source == j, info, at)
-            if cap % 16 == 0:
-                data.append(got_ref[first + j][:cap])
-            else:
-                data.append(got_ref[first + j].astype(jnp.float32)[:cap])
+            if cap % 16:
+                got = got.astype(jnp.float32)
+            cols = [got[i * cap : (i + 1) * cap] for i in range(width // LANES)]
+            data.append(jnp.concatenate(cols, axis=1))
         at_ref[first // per : first // per + 1, :] = at
         parts.append(hot(centred == at))
     placed = contract(
         jnp.concatenate(parts, axis=1), jnp.concatenate(data, axis=0).astype(jnp.bfloat16), 1, 0
     ).astype(jnp.bfloat16)
-    head_ref[...] = placed[:half]
-    tail_ref[...] = placed[half:]
+    own_ref[...] = placed
+    near_ref[...] = jnp.where(core_ref[0] == 0, placed[half:], placed[:half])
+    far_ref[...] = jnp.where(core_ref[0] == 0, placed[:half], placed[half:])
 
 
 def place_table(at_ref, rows):
@@ -168,18 +162,46 @@
     return jnp.concatenate(parts, axis=1)
 
 
-def pick_kernel(table_ref, own_hbm, from_before_ref, from_after_ref, out_ref, own_ref, sems):
-    (copy,) = fetch([own_hbm], [own_ref], sems)
-    copy.wait()
-    half = from_before_ref.shape[0]
+def pick_kernel(
+    core_ref,
+    near_hbm,
+    far_hbm,
+    own_hbm,
+    table_hbm,
+    out_hbm,
+    done_ref,
+    near_ref,
+    far_ref,
+    own_ref,
+    table_ref,
+    out_ref,
+    sems,
+):
+    done_ref[...] = jnp.zeros_like(done_ref)
+    copies = fetch(
+        [near_hbm, far_hbm, own_hbm, table_hbm], [near_ref, far_ref, own_ref, table_ref], sems
+    )
+    for copy in copies:
+        copy.wait()
+    half = near_ref.shape[0]
+    near = near_ref[...].astype(jnp.float32)
+    far = far_ref[...].astype(jnp.float32)
     own = jnp.concatenate(
         [
-            own_ref[:half, :] + from_before_ref[...].astype(jnp.float32),
-            own_ref[half:, :] + from_after_ref[...].astype(jnp.float32),
+            own_ref[:half, :] + jnp.where(core_ref[0] == 0, far, near),
+            own_ref[half:, :] + jnp.where(core_ref[0] == 0, near, far),
         ],
         axis=0,
     ).astype(jnp.bfloat16)
-    out_ref[...] = contract(table_ref[...], own, 1, 0).astype(jnp.bfloat16)
+    stores = []
+    parts = 4
+    part = out_ref.shape[0] // parts
+    for i in range(parts):
+        rows = pl.ds(i * part, part)
+        out_ref[rows, :] = contract(table_ref[rows, :], own, 1, 0).astype(jnp.bfloat16)
+        stores += fetch([out_ref.at[rows, :]], [out_hbm.at[rows, :]], sems, 4 + i)
+    for store in stores:
+        store.wait()
 
 
 def restore_kernel(table_ref, got_ref, out_ref):
@@ -187,11 +209,11 @@
 
 
 def forward_kernel(
+    core_ref,
     at_ref,
-    before_hbm,
-    head_hbm,
-    tail_hbm,
-    after_hbm,
+    own_ref,
+    near_ref,
+    far_ref,
     w_hbm,
     w_kv_t_hbm,
     query_hbm,
@@ -216,12 +238,11 @@
     width = w_ref.shape[0]
     head_dim = width // HEADS
     half = points_ref.shape[0] // 4
-    quarters = [points_ref.at[pl.ds(i * half, half), :] for i in range(4)]
-    copies = fetch(
-        [before_hbm, head_hbm, tail_hbm, after_hbm, w_hbm, w_kv_t_hbm],
-        [*quarters, w_ref, w_kv_t_ref],
-        sems,
-    )
+    copies = fetch([w_hbm, w_kv_t_hbm], [w_ref, w_kv_t_ref], sems)
+    near, far = (near_ref[...], far_ref[...])
+    points_ref[:half, :] = jnp.where(core_ref[0] == 0, far, near)
+    points_ref[half : 3 * half, :] = own_ref[...]
+    points_ref[3 * half :, :] = jnp.where(core_ref[0] == 0, near, far)
     table_ref[...] = place_table(at_ref, 2 * half).T.astype(jnp.bfloat16)
     stores = fetch([table_ref], [table_hbm], sems, 6)
     for copy in copies:
@@ -293,11 +314,11 @@
     points_t_hbm,
     w_hbm,
     probs_hbm,
-    send_ref,
-    keep_ref,
+    send_hbm,
+    keep_hbm,
     own_hbm,
-    before_ref,
-    after_ref,
+    near_hbm,
+    far_hbm,
     got_ref,
     w_out_ref,
     query_ref,
@@ -310,29 +331,40 @@
     grad_query_ref,
     grad_kv_ref,
     query_t_ref,
+    send_ref,
+    keep_ref,
     own_ref,
+    near_ref,
+    far_ref,
     sems,
 ):
     width = w_out_ref.shape[0]
     head_dim = width // HEADS
     half = query_ref.shape[0] // 2
     scale = 1.0 / math.sqrt(head_dim)
+    first_copies = fetch([got_hbm, w_out_hbm], [got_ref, w_out_ref], sems)
     copies = fetch(
-        [got_hbm, w_out_hbm, attn_t_hbm, kv_hbm, query_hbm, key_t_hbm],
-        [got_ref, w_out_ref, attn_t_ref, kv_ref, query_ref, key_t_ref],
+        [attn_t_hbm, query_hbm, kv_hbm, key_t_hbm],
+        [attn_t_ref, query_ref, kv_ref, key_t_ref],
         sems,
-    )
-    probs_copies = []
-    for head in range(HEADS):
-        probs_copies += fetch([probs_hbm.at[head]], [probs_ref.at[head]], sems, 8 + head)
-    late = fetch([points_t_hbm, w_hbm], [points_t_ref, w_ref], sems, 6)
+        2,
+    )
+
+    def fetch_probs(first, last):
+        heads = range(first, min(last, HEADS))
+        return fetch(
+            [probs_hbm.at[h] for h in heads], [probs_ref.at[h] for h in heads], sems, 8 + first
+        )
+
+    per = LANES // head_dim
+    probs_copies = fetch_probs(0, per)
     table = place_table(at_ref, 2 * half).astype(jnp.bfloat16)
-    copies[0].wait()
+    first_copies[0].wait()
     grads = contract(table, got_ref[...], 1, 0).astype(jnp.bfloat16)
-    copies[1].wait()
+    first_copies[1].wait()
     grad_attn = contract(grads, w_out_ref[...], 1, 1).astype(jnp.bfloat16)
     grad_attn_t = contract(w_out_ref[...], grads, 1, 1).astype(jnp.bfloat16)
-    for copy in copies[2:]:
+    for copy in copies:
         copy.wait()
     side = iota((1, LANES), 1) // head_dim
     sides = ((slice(0, half), slice(0, 2 * half)), (slice(half, 2 * half), slice(2 * half, 4 * half)))
@@ -341,8 +373,11 @@
         value_cols = slice(width + first, width + first + LANES)
         grad = grad_attn[:, cols]
         query = query_ref[:, cols]
-        for head in range(first // head_dim, (first + LANES) // head_dim):
-            probs_copies[head].wait()
+        for copy in probs_copies:
+            copy.wait()
+        probs_copies = fetch_probs(first // head_dim + per, first // head_dim + 2 * per)
+        if first == 0:
+            late = fetch([points_t_hbm, w_hbm], [points_t_ref, w_ref], sems, 6)
         for mine, patch in sides:
             value = kv_ref[patch, value_cols]
             grad_key = jnp.zeros((2 * half, LANES), jnp.float32)
@@ -377,11 +412,16 @@
     own_ref[...] = contract(grad_query_ref[...], w_ref[:, :width], 1, 1) + contract(
         grad_kv_ref[half : 3 * half, :], w_kv, 1, 1
     )
-    (store,) = fetch([own_ref], [own_hbm], sems, 8 + HEADS)
-    before_ref[...] = contract(grad_kv_ref[:half, :], w_kv, 1, 1).astype(jnp.bfloat16)
-    after_ref[...] = contract(grad_kv_ref[3 * half :, :], w_kv, 1, 1).astype(jnp.bfloat16)
+    stores = fetch([own_ref], [own_hbm], sems, 8 + HEADS)
+    before = contract(grad_kv_ref[:half, :], w_kv, 1, 1).astype(jnp.bfloat16)
+    after = contract(grad_kv_ref[3 * half :, :], w_kv, 1, 1).astype(jnp.bfloat16)
+    near_ref[...] = jnp.where(core_ref[0] == 0, after, before)
+    far_ref[...] = jnp.where(core_ref[0] == 0, before, after)
+    stores += fetch([near_ref, far_ref], [near_hbm, far_hbm], sems, 9 + HEADS)
     rows = width // 2
-    for side, out_ref in ((core_ref[0], keep_ref), (1 - core_ref[0], send_ref)):
+    for index, (side, out_ref, out_hbm) in enumerate(
+        ((core_ref[0], keep_ref, keep_hbm), (1 - core_ref[0], send_ref, send_hbm))
+    ):
         from_row = pl.multiple_of(side * rows, rows)
         of_query, of_kv, of_out = weights(
             points_t_ref[pl.ds(from_row, rows), :],
@@ -393,7 +433,9 @@
         out_ref[:, :width] = of_query.astype(out_ref.dtype)
         out_ref[:, width : 3 * width] = of_kv.astype(out_ref.dtype)
         out_ref[:, 3 * width :] = of_out.astype(out_ref.dtype)
-    store.wait()
+        stores += fetch([out_ref], [out_hbm], sems, 11 + HEADS + index)
+    for store in stores:
+        store.wait()
 
 
 def exchange(blocks):
@@ -422,14 +464,18 @@
     send_ref[...] = jnp.where(side == 0, total[half:], total[:half]).astype(jnp.bfloat16)
 
 
-def first_sum_kernel(sides_ref, kept_ref, got_ref, keep_a, send_a, keep_b, send_b):
+def first_sum_kernel(
+    sides_ref, kept_hbm, got_ref, keep_a, send_a, keep_b, send_b, kept_ref, sems
+):
     half = kept_ref.shape[0] // 2
-    part_rows(
-        kept_ref[:half, :] + got_ref[:half, :].astype(jnp.float32), sides_ref[0], keep_a, send_a
-    )
-    part_rows(
-        kept_ref[half:, :] + got_ref[half:, :].astype(jnp.float32), sides_ref[1], keep_b, send_b
-    )
+    parts = [pl.ds(0, half), pl.ds(half, half)]
+    copies = fetch([kept_hbm.at[p, :] for p in parts], [kept_ref.at[p, :] for p in parts], sems)
+    for index, (part, keep, send) in enumerate(
+        zip(parts, (keep_a, keep_b), (send_a, send_b), strict=True)
+    ):
+        copies[index].wait()
+        total = kept_ref[part, :].astype(jnp.float32) + got_ref[part, :].astype(jnp.float32)
+        part_rows(total, sides_ref[index], keep, send)
 
 
 def second_sum_kernel(
@@ -444,7 +490,7 @@
 
 
 def third_sum_kernel(
-    line_ref, kept_a_ref, got_a_ref, kept_b_ref, got_b_ref, _, mine_ref, *refs
+    line_ref, kept_a_ref, got_a_ref, kept_b_ref, got_b_ref, mine_ref, *refs
 ):
     sends, total_ref = (refs[:-1], refs[-1])
     rows = mine_ref.shape[0] // 2
@@ -458,20 +504,39 @@
         ).astype(out_ref.dtype)
 
 
+def fourth_sum_kernel(mine_ref, *refs):
+    others, out_ref = (refs[:-2], refs[-1])
+    total = mine_ref[...]
+    for other in others:
+        total = total + other[...].astype(jnp.float32)
+    out_ref[...] = total.astype(jnp.bfloat16)
+
+
+def join_kernel(*refs):
+    blocks, out_ref = (refs[:-1], refs[-1])
+    rows = blocks[0].shape[0] // 2
+    values = [block[...].astype(jnp.float32) for block in blocks]
+    halves = [x[:rows] for x in values] + [x[rows:] for x in values]
+    out_ref[...] = jnp.concatenate(halves, axis=0).astype(jnp.bfloat16)
+
+
 def spread_kernel(n_line, place_ref, *refs):
     pieces, qkv_ref, out_ref = (refs[:-2], refs[-2], refs[-1])
     n_qkv = qkv_ref.shape[1]
     core, side_x, side_y, line = (place_ref[i] for i in range(4))
     rows = qkv_ref.shape[0] // (16 * n_line)
     for index, piece in enumerate(pieces):
-        near_x, near_y = (side_x ^ (index & 1), side_y ^ (index >> 1 & 1))
-        near_core = core ^ (index >> 2)
+        far_core, which = divmod(index, 5)
+        far_x, far_y = ((0, 0), (1, 0), (0, 1), (1, 1), (1, 1))[which]
+        near_x, near_y = (side_x ^ far_x, side_y ^ far_y)
         values = piece[...].astype(jnp.float32)
-        for block in range(2 * n_line):
-            distance, part = divmod(block, 2)
+        for block in range(piece.shape[0] // rows):
+            part, distance = divmod(block, n_line)
+            if which == 4:
+                part = 1
             first, second = ((near_x, near_y), (near_y, near_x))[part]
-            unit = (((near_core * 2 + part) * 2 + first) * 2 + second) * n_line + (line ^ distance)
-            row = pl.multiple_of(unit * rows, rows)
+            unit = ((((core ^ far_core) * 2 + part) * 2 + first) * 2 + second) * n_line
+            row = pl.multiple_of((unit + (line ^ distance)) * rows, rows)
             data = values[block * rows : (block + 1) * rows]
             qkv_ref[pl.ds(row, rows), :] = data[:, :n_qkv]
             out_ref[pl.ds(row, rows), :] = data[:, n_qkv:]
@@ -487,7 +552,8 @@
         [wide(rows // 4, width), low(rows // 4, width)] * 2,
         [sides, keep, swap(send, "curve", 1)],
         rows * width,
-        scalar[:3],
+        [SMEM, HBM, VMEM],
+        scratch=[space(keep), pltpu.SemaphoreType.DMA((2,))],
     )
     got_a = swap(send_a, "curve", 2)
     got_b = swap(send_b, "dp", 1)
@@ -505,9 +571,9 @@
         mine, *sends = call(
             third_sum_kernel,
             [wide(2 * rows, width)] + [low(2 * rows, width)] * (n_line - 1),
-            [line.reshape(1), kept_a, got_a, kept_b, got_b, ready],
+            [line.reshape(1), kept_a, got_a, kept_b, got_b],
             kept_a.size,
-            [*scalar, ANY],
+            scalar,
             scratch=[pltpu.VMEM((2 * n_line * rows, width), jnp.float32)],
         )
     else:
@@ -518,30 +584,46 @@
             lax.dynamic_index_in_dim(both, line ^ k, 0, keepdims=False) for k in range(n_line)
         ]
         sends = [block.astype(jnp.bfloat16) for block in sends]
-    for k, block in enumerate(sends):
-        mine = mine + swap(block, "curve", 4 * (k + 1)).astype(jnp.float32)
-    mine = mine.astype(jnp.bfloat16)
+    others = [swap(block, "curve", 4 * (k + 1)) for k, block in enumerate(sends)]
+    (mine,) = call(
+        fourth_sum_kernel,
+        [low(2 * rows, width)],
+        [mine, *others, ready],
+        mine.size,
+        [VMEM] * n_line + [ANY],
+    )
     blocks = [mine] + [swap(mine, "curve", 4 * k) for k in range(1, n_line)]
     if rows % 8 == 0:
-        return (jnp.concatenate(blocks, axis=0), line)
-    blocks = order_blocks(jnp.stack(blocks), line).reshape(2 * n_line * rows, width)
-    return (blocks, jnp.zeros_like(line))
+        (own,) = call(join_kernel, [low(2 * n_line * rows, width)], blocks, mine.size)
+    else:
+        blocks = order_blocks(jnp.stack(blocks), line)
+        own = jnp.swapaxes(blocks.reshape(n_line, 2, rows, width), 0, 1)
+        own = own.reshape(2 * n_line * rows, width)
+        line = jnp.zeros_like(line)
+    return (own, line)
 
 
 def sum_finish(own, line, sides, width_qkv):
-    rows, width = own.shape
+    n_line = lax.axis_size("curve") // 4
+    core = lax.axis_index("curve") & 1
+    half, width = (own.shape[0] // 2, own.shape[1])
     over_x = swap(own, "curve", 2)
     over_y = swap(own, "dp", 1)
-    pieces = [own, over_x, over_y, swap(over_x, "dp", 1)]
+    pieces = [own, over_x, over_y, swap(over_y[:half], "curve", 2), swap(over_x[half:], "dp", 1)]
     pieces += [swap(piece, "curve", 1) for piece in pieces]
-    where = jnp.stack([lax.axis_index("curve") & 1, sides[0], sides[1], line])
     return call(
-        functools.partial(spread_kernel, lax.axis_size("curve") // 4),
-        [wide(8 * rows, width_qkv), wide(8 * rows, width - width_qkv)],
-        [where, *pieces],
+        functools.partial(spread_kernel, n_line),
+        [wide(16 * half, width_qkv), wide(16 * half, width - width_qkv)],
+        [jnp.stack([core, sides[0], sides[1], line]), *pieces],
         SPREAD_FLOPS,
-        [SMEM] + [VMEM] * 8,
-    )
+        [SMEM] + [VMEM] * len(pieces),
+    )
+
+
+def halo(near, far):
+    size = lax.axis_size("curve")
+    route = [(i, (i + 2 * (i % 2) - 1) % size) for i in range(size)]
+    return (swap(near, "curve", 1), lax.ppermute(far, "curve", route))
 
 
 def on_device(points, grad_out, dest_dev, dest_row, w_qkv, w_out):
@@ -557,7 +639,7 @@
     ids = jax.ShapeDtypeStruct((1, rows), jnp.int32)
     send_points, slots = call(
         pack_points_kernel,
-        [low(n_dev, cap + INFO_ROWS, width), ids],
+        [low(n_dev, cap * width // LANES + INFO_ROWS, LANES), ids],
         [dest_dev, dest_row, points[0]],
         place_flops,
         [HBM] * 3,
@@ -568,14 +650,19 @@
     send_grads, restore_table = call(
         pack_grads_kernel, [low(total, width), low(rows, total)], [slots, grad_out[0]], place_flops
     )
-    head, tail, at = call(
+    own, near, far, at = call(
         place_points_kernel,
-        [low(half, width), low(half, width), wide(total // LANES, LANES)],
-        [got_points],
+        [
+            low(rows, width),
+            low(half, width),
+            low(half, width),
+            wide(total // LANES, LANES),
+        ],
+        [core, got_points],
         place_flops,
-    )
-    after = from_behind(head, "curve", -1)
-    before = from_behind(tail, "curve", 1)
+        [SMEM, VMEM],
+    )
+    near, far = halo(near, far)
     send_grads = gate(send_grads, at, flops=GATE_FLOPS)
     got_grads = exchange(send_grads.reshape(n_dev, cap, width)).reshape(total, width)
     saved = [
@@ -590,9 +677,9 @@
     query, kv, key_t, attn_t, probs, points_t, pick_table = call(
         forward_kernel,
         saved,
-        [at, before, head, tail, after, w_qkv, w_qkv[:, width:].T],
+        [core, at, own, near, far, w_qkv, w_qkv[:, width:].T],
         FORWARD_FLOPS,
-        [VMEM] + [HBM] * 6,
+        [SMEM] + [VMEM] * 4 + [HBM] * 2,
         [HBM] * len(saved),
         [space(low(2 * rows, width)), space(low(width, 3 * width)), space(low(2 * width, width))]
         + [space(x) for x in saved]
@@ -600,40 +687,39 @@
         60,
     )
     held = [got_grads, w_out, query, kv, key_t, attn_t, points_t, w_qkv, probs]
-    send, keep, own_input, to_before, to_after = call(
+    made = [
+        low(width // 2, 4 * width),
+        low(width // 2, 4 * width),
+        wide(rows, width),
+        low(half, width),
+        low(half, width),
+    ]
+    send, keep, own_input, near, far = call(
         backward_kernel,
-        [
-            low(width // 2, 4 * width),
-            wide(width // 2, 4 * width),
-            wide(rows, width),
-            low(half, width),
-            low(half, width),
-        ],
+        made,
         [core, at, *held],
         32 * rows * rows * width + 22 * rows * width * width,
         [SMEM, VMEM] + [HBM] * len(held),
-        [VMEM, VMEM, HBM, VMEM, VMEM],
+        [HBM] * len(made),
         [space(x) for x in held]
-        + [
-            space(low(rows, width)),
-            space(low(2 * rows, 2 * width)),
-            space(wide(width, rows)),
-            space(wide(rows, width)),
-            pltpu.SemaphoreType.DMA((9 + HEADS,)),
-        ],
-        60,
-    )
-    from_before = from_behind(to_after, "curve", 1)
-    from_after = from_behind(to_before, "curve", -1)
-    (picked,) = call(
+        + [space(low(rows, width)), space(low(2 * rows, 2 * width)), space(wide(width, rows))]
+        + [space(x) for x in made]
+        + [pltpu.SemaphoreType.DMA((13 + HEADS,))],
+        63,
+    )
+    near, far = halo(near, far)
+    picked = low(total, width)
+    picked, done = call(
         pick_kernel,
-        [low(total, width)],
-        [pick_table, own_input, from_before, from_after],
+        [picked, wide(8, LANES)],
+        [core, near, far, own_input, pick_table],
         place_flops,
-        [VMEM, HBM, VMEM, VMEM],
-        scratch=[space(wide(rows, width)), pltpu.SemaphoreType.DMA((1,))],
-    )
-    gathered, line = sum_start(keep, send, sides, picked)
+        [SMEM] + [HBM] * 4,
+        [HBM, VMEM],
+        [space(x) for x in (near, far, own_input, pick_table, picked)] + [pltpu.SemaphoreType.DMA((8,))],
+        63,
+    )
+    gathered, line = sum_start(keep, send, sides, done)
     picked = gate(picked, gathered, flops=GATE_FLOPS)
     returned = exchange(picked.reshape(n_dev, cap, width)).reshape(total, width)
     weight_qkv, weight_out = sum_finish(gathered, line, sides, 3 * width)

time: 164 us -> 161 us (0.982)
  waiting for transfers between devices: 65.3 us -> 61.2 us
  starting transfers between devices: 45.5 us -> 48.2 us
  local copies, waits for them, and re-layouts: 10.3 us -> 8.13 us
    ppermute x18 -> x22, starting transfers between devices: 19.9 us -> 24.1 us  [swap(): return lax.ppermute(block, axis, [(i, i ^ mask) for i in range(size)])]
    ppermute x18 -> x22, waiting for transfers between devices: 30.2 us -> 26.9 us  [swap(): return lax.ppermute(block, axis, [(i, i ^ mask) for i in range(size)])]
    unnamed x43 -> x29, local copies, waits for them, and re-layouts: 10.3 us -> 8.1 us
    ppermute x4 -> x2, starting transfers between devices: 10.5 us -> 8.48 us  [halo(): return (swap(near, 'curve', 1), lax.ppermute(far, 'curve', route))]
    pallas_call x11 -> x13, Pallas kernels: 39.3 us -> 40.9 us  [call(): pl.pallas_call(kernel, out_shape=outs, in_specs=ins or [VMEM] * len(args)...]
  transfers between devices with their start and end apart: 25 -> 27, of which waited for: 17 -> 14; matrix products, arithmetic and copies ran while one was open for 1% -> 1% of each run, Pallas kernels for 11% -> 13%
where the time goes in v5:
time: 161 us; the launch traced here: 160 us
  waiting for transfers between devices  61.2 us (38%)
  starting transfers between devices  48.2 us (30%)
  Pallas kernels  40.9 us (25%)
  local copies, waits for them, and re-layouts  8.13 us (5%)
    pallas_call x13, Pallas kernels, call(): pl.pallas_call(kernel, out_shape=outs, in_specs=ins or [VMEM] * len(args)...  40.9 us
    all_to_all x3, waiting for transfers between devices, exchange(): lax.all_to_all(blocks, 'curve', split_axis=0, concat_axis=0, tiled=True)  34.4 us
    ppermute x22, waiting for transfers between devices, swap(): return lax.ppermute(block, axis, [(i, i ^ mask) for i in range(size)])  26.9 us
    ppermute x22, starting transfers between devices, swap(): return lax.ppermute(block, axis, [(i, i ^ mask) for i in range(size)])  24.1 us
    all_to_all x3, starting transfers between devices, exchange(): lax.all_to_all(blocks, 'curve', split_axis=0, concat_axis=0, tiled=True)  15.7 us
    ppermute x2, starting transfers between devices, halo(): return (swap(near, 'curve', 1), lax.ppermute(far, 'curve', route))  8.48 us
    unnamed x29, local copies, waits for them, and re-layouts  8.1 us
  transfers between devices with their start and end apart: 27, of which 14 were waited for; matrix products, arithmetic and copies ran while one was open for 1% of the time, Pallas kernels for 13%

profile of v5, /device:TPU:0, one launch (start us, length us, event | category | flops | bytes accessed | tf_op | source)
XLA Modules:
  0.0 159.6 jit_solution(11063782434289788633)
XLA Ops:
  0.6 2.8 %shard_map.85 = (bf16[16,264,128]{2,1,0:T(8,128)(2,1)}, s32[1,512]{1,0:T(1,128)}) custom-call(s32[1,512]{1,0:T(1,128)} %dev_hbm.1, s32[1,512]{1,0:T(1,128)} %row_hbm.1, bf16[512,512]{1,0:T(8,128)(2,1)} %bitcast.18), custom_call_target="tpu_custom_call" | custom-call | flops 536870912 | bytes 1611776 | tf_op jit(solution)/shard_map/pallas_call | solution.py:54
  3.5 7.5 %all-to-all-start = ((bf16[16,264,128]{2,1,0:T(8,128)(2,1)}), bf16[16,264,128]{2,1,0:T(8,128)(2,1)S(1)}, u32[]{:S(2)}, u32[]{:S(2)}) async-start(bf16[16,264,128]{2,1,0:T(8,128)(2,1)} %get-tuple-element.41), calls=%async_computation | async-start | bytes 2162688 | tf_op jit(solution)/shard_map/all_to_all | solution.py:442
  11.0 1.4 copy.12
  15.2 19.3 %all-to-all-done.got_ref = bf16[16,264,128]{2,1,0:T(8,128)(2,1)S(1)} async-done(((bf16[16,264,128]{2,1,0:T(8,128)(2,1)}), bf16[16,264,128]{2,1,0:T(8,128)(2,1)S(1)}, u32[]{:S(2)}, u32[]{:S(2)}) %all-to-all-start) | async-done | bytes 1081376 | tf_op jit(solution)/shard_map/all_to_all | solution.py:442
  37.3 5.1 %collective-permute-start.1 = (bf16[256,512]{1,0:T(8,128)(2,1)S(1)}, bf16[256,512]{1,0:T(8,128)(2,1)S(1)}, u32[]{:S(2)}, u32[]{:S(2)}) collective-permute-start(bf16[256,512]{1,0:T(8,128)(2,1)S(1)} %get-tuple-element.46), channel_id=1, source_target_pairs={{0,30},{2,4},{4,2},{6,8},{8,6},{10,12},{12,10},{14,16},{16,14},{18... | collective-permute-start | bytes 786440 | tf_op jit(solution)/shard_map/ppermute | solution.py:626
  42.3 4.5 %all-to-all-start.1 = ((bf16[16,64,512]{2,1,0:T(8,128)(2,1)}), bf16[16,64,512]{2,1,0:T(8,128)(2,1)}, u32[]{:S(2)}, u32[]{:S(2)}) async-start(bf16[16,64,512]{2,1,0:T(8,128)(2,1)} %bitcast.13), calls=%async_computation.1 | async-start | bytes 2097152 | tf_op jit(solution)/shard_map/all_to_all | solution.py:442
  47.7 11.8 %shard_map.89 = (bf16[512,512]{1,0:T(8,128)(2,1)}, bf16[1024,1024]{1,0:T(8,128)(2,1)}, bf16[512,1024]{1,0:T(8,128)(2,1)}, bf16[512,512]{1,0:T(8,128)(2,1)}, bf16...) custom-call(s32[1]{0:T(128)} %bitcast.2.core_ref, f32[8,128]{1,0:T(8,128)} %copy-done.7, ...), custom_call_target="tpu_custom_call" | custom-call | flops 99999997952 | bytes 14159876 | tf_op jit(solution)/shard_map/pallas_call | solution.py:54
  59.4 10.2 %all-to-all-done.1 = bf16[16,64,512]{2,1,0:T(8,128)(2,1)} async-done(((bf16[16,64,512]{2,1,0:T(8,128)(2,1)}), bf16[16,64,512]{2,1,0:T(8,128)(2,1)}, u32[]{:S(2)}, u32[]{:S(2)}) %all-to-all-start.1) | async-done | bytes 1048608 | tf_op jit(solution)/shard_map/all_to_all | solution.py:442
  69.6 13.8 %shard_map.90 = (bf16[256,2048]{1,0:T(8,128)(2,1)}, bf16[256,2048]{1,0:T(8,128)(2,1)}, f32[512,512]{1,0:T(8,128)}, bf16[256,512]{1,0:T(8,128)(2,1)}, bf16[256,512]{1,0:T(8,128)(2,1)}) custom-call(s32[1]{0:T(128)} %bitcast.2.core_ref, f32[8,128]{1,0:T(8,128)} %copy-done.7, bf16[1024,512]{1,0:T(8,128)(2,1)} %bitcast.4.got_hbm, bf16[512,512]{1,0:T(8,128)(2,1)} %w_out_hbm.1, ...), custom_call_target="tpu_custom_call" | custom-call | flops 7247757312 | bytes 16257028 | tf_op jit(solution)/shard_map/pallas_call | solution.py:54
  84.1 2.4 %collective-permute-done.4.got_ref = bf16[256,2048]{1,0:T(8,128)(2,1)S(1)} collective-permute-done((bf16[256,2048]{1,0:T(8,128)(2,1)}, bf16[256,2048]{1,0:T(8,128)(2,1)S(1)}, u32[]{:S(2)}, u32[]{:S(2)}) %collective-permute-start.4) | collective-permute-done | bytes 1048608 | tf_op jit(solution)/shard_map/ppermute | solution.py:447
  86.5 1.2 copy-done
  88.7 2.0 %collective-permute-start.5 = (bf16[64,2048]{1,0:T(8,128)(2,1)S(1)}, bf16[64,2048]{1,0:T(8,128)(2,1)S(1)}, u32[]{:S(2)}, u32[]{:S(2)}) collective-permute-start(bf16[64,2048]{1,0:T(8,128)(2,1)S(1)} %get-tuple-element.61), channel_id=1, source_target_pairs={{0,4},{2,6},{4,0},{6,2},{8,12},{10,14},{12,8},{14,10},{16,20},{18,... | collective-permute-start | bytes 786440 | tf_op jit(solution)/shard_map/ppermute | solution.py:447
  90.8 1.5 collective-permute-start.6
  92.3 3.4 %collective-permute-start.3 = (bf16[256,512]{1,0:T(8,128)(2,1)S(1)}, bf16[256,512]{1,0:T(8,128)(2,1)}, u32[]{:S(2)}, u32[]{:S(2)}) collective-permute-start(bf16[256,512]{1,0:T(8,128)(2,1)S(1)} %copy-done.10), channel_id=1, source_target_pairs={{0,30},{2,4},{4,2},{6,8},{8,6},{10,12},{12,10},{14,16},{16,14},{18... | collective-permute-start | bytes 786440 | tf_op jit(solution)/shard_map/ppermute | solution.py:626
  95.7 4.5 %collective-permute-done.5.got_a_ref = bf16[64,2048]{1,0:T(8,128)(2,1)S(1)} collective-permute-done((bf16[64,2048]{1,0:T(8,128)(2,1)S(1)}, bf16[64,2048]{1,0:T(8,128)(2,1)S(1)}, u32[]{:S(2)}, u32[]{:S(2)}) %collective-permute-start.5) | collective-permute-done | bytes 262176 | tf_op jit(solution)/shard_map/ppermute | solution.py:447
  100.9 1.8 %collective-permute-start.7 = (bf16[32,2048]{1,0:T(8,128)(2,1)S(1)}, bf16[32,2048]{1,0:T(8,128)(2,1)S(1)}, u32[]{:S(2)}, u32[]{:S(2)}) collective-permute-start(bf16[32,2048]{1,0:T(8,128)(2,1)S(1)} %get-tuple-element.65), channel_id=1, source_target_pairs={{0,1},{1,0},{2,3},{3,2},{4,5},{5,4},{6,7},{7,6},{8,9},{9,8},{10,11... | collective-permute-start | bytes 393224 | tf_op jit(solution)/shard_map/ppermute | solution.py:447
  102.7 2.3 %collective-permute-start.8 = (bf16[32,2048]{1,0:T(8,128)(2,1)S(1)}, bf16[32,2048]{1,0:T(8,128)(2,1)S(1)}, u32[]{:S(2)}, u32[]{:S(2)}) collective-permute-start(bf16[32,2048]{1,0:T(8,128)(2,1)S(1)} %get-tuple-element.67), channel_id=1, source_target_pairs={{0,4},{2,6},{4,0},{6,2},{8,12},{10,14},{12,8},{14,10},{16,20},{18,... | collective-permute-start | bytes 393224 | tf_op jit(solution)/shard_map/ppermute | solution.py:447
  106.2 1.8 %collective-permute-done.8.got_b_ref = bf16[32,2048]{1,0:T(8,128)(2,1)S(1)} collective-permute-done((bf16[32,2048]{1,0:T(8,128)(2,1)S(1)}, bf16[32,2048]{1,0:T(8,128)(2,1)S(1)}, u32[]{:S(2)}, u32[]{:S(2)}) %collective-permute-start.8) | collective-permute-done | bytes 131104 | tf_op jit(solution)/shard_map/ppermute | solution.py:447
  108.0 3.0 %collective-permute-start.9 = (bf16[16,2048]{1,0:T(8,128)(2,1)S(1)}, bf16[16,2048]{1,0:T(8,128)(2,1)S(1)}, u32[]{:S(2)}, u32[]{:S(2)}) collective-permute-start(bf16[16,2048]{1,0:T(8,128)(2,1)S(1)} %get-tuple-element.69), channel_id=1, source_target_pairs={{0,8},{2,10},{4,12},{6,14},{8,0},{10,2},{12,4},{14,6},{16,24},{18,... | collective-permute-start | bytes 196616 | tf_op jit(solution)/shard_map/ppermute | solution.py:447
  111.0 1.4 collective-permute-start.10
  114.3 3.8 %shard_map.91 = (bf16[1024,512]{1,0:T(8,128)(2,1)}, f32[8,128]{1,0:T(8,128)}) custom-call(s32[1]{0:T(128)} %bitcast.2.core_ref, bf16[256,512]{1,0:T(8,128)(2,1)} %copy-done.9, bf16[256,512]{1,0:T(8,128)(2,1)} %collective-permute-done.3.far_hbm, f32[512,512]{1,0:T(8,128)} %get-tuple-element.55.own_hbm, bf16[1024,512]{1,0:T(8,128)(2,1)} %get-tuple-element.56.table_hbm), custom_call_target="tpu_custom_call" | custom-call | flops 536870912 | bytes 3674116 | tf_op jit(solution)/shard_map/pallas_call | solution.py:54
  119.9 2.3 %collective-permute-start.13 = (bf16[16,2048]{1,0:T(8,128)(2,1)S(1)}, bf16[16,2048]{1,0:T(8,128)(2,1)S(1)}, u32[]{:S(2)}, u32[]{:S(2)}) collective-permute-start(bf16[16,2048]{1,0:T(8,128)(2,1)S(1)} %shard_map.95.refs_0_), channel_id=1, source_target_pairs={{0,16},{2,18},{4,20},{6,22},{8,24},{10,26},{12,28},{14,30},{16,0},... | collective-permute-start | bytes 196616 | tf_op jit(solution)/shard_map/ppermute | solution.py:447
  122.2 1.5 collective-permute-start.14
  123.8 1.4 collective-permute-done.13.refs_2_
  125.2 3.1 %collective-permute-done.14.refs_3_ = bf16[16,2048]{1,0:T(8,128)(2,1)S(1)} collective-permute-done((bf16[16,2048]{1,0:T(8,128)(2,1)S(1)}, bf16[16,2048]{1,0:T(8,128)(2,1)S(1)}, u32[]{:S(2)}, u32[]{:S(2)}) %collective-permute-start.14) | collective-permute-done | bytes 65568 | tf_op jit(solution)/shard_map/ppermute | solution.py:447
  129.0 2.0 %collective-permute-start.15 = (bf16[64,2048]{1,0:T(8,128)(2,1)}, bf16[64,2048]{1,0:T(8,128)(2,1)S(1)}, u32[]{:S(2)}, u32[]{:S(2)}) collective-permute-start(bf16[64,2048]{1,0:T(8,128)(2,1)} %shard_map.96.refs_1_.refs_0_), channel_id=1, source_target_pairs={{0,4},{2,6},{4,0},{6,2},{8,12},{10,14},{12,8},{14,10},{16,20},{18,... | collective-permute-start | bytes 786440 | tf_op jit(solution)/shard_map/ppermute | solution.py:447
  131.5 3.7 %all-to-all-start.2 = ((bf16[16,64,512]{2,1,0:T(8,128)(2,1)}), bf16[16,64,512]{2,1,0:T(8,128)(2,1)S(1)}, u32[]{:S(2)}, u32[]{:S(2)}) async-start(bf16[16,64,512]{2,1,0:T(8,128)(2,1)} %bitcast.15), calls=%async_computation.2 | async-start | bytes 2097152 | tf_op jit(solution)/shard_map/all_to_all | solution.py:442
  135.5 2.1 %collective-permute-done.16.refs_2_ = bf16[64,2048]{1,0:T(8,128)(2,1)S(1)} collective-permute-done((bf16[64,2048]{1,0:T(8,128)(2,1)}, bf16[64,2048]{1,0:T(8,128)(2,1)S(1)}, u32[]{:S(2)}, u32[]{:S(2)}) %collective-permute-start.16) | collective-permute-done | bytes 262176 | tf_op jit(solution)/shard_map/ppermute | solution.py:447
  139.4 9.0 %collective-permute-done.17.refs_3_ = bf16[32,2048]{1,0:T(8,128)(2,1)S(1)} collective-permute-done((bf16[32,2048]{1,0:T(8,128)(2,1)S(1)}, bf16[32,2048]{1,0:T(8,128)(2,1)S(1)}, u32[]{:S(2)}, u32[]{:S(2)}) %collective-permute-start.17) | collective-permute-done | bytes 131104 | tf_op jit(solution)/shard_map/ppermute | solution.py:447
  149.9 3.3 %shard_map.99 = (f32[512,1536]{1,0:T(8,128)}, f32[512,512]{1,0:T(8,128)}) custom-call(s32[4]{0:T(128)S(1)} %pad_add_fusion.1.place_ref, bf16[64,2048]{1,0:T(8,128)(2,1)} %shard_map.96.refs_1_.refs_0_, bf16[64,2048]{1,0:T(8,128)(2,1)S(1)} %collective-permute-done.15.refs_1_, bf16[64,2048]{1,0:T(8,128)(2,1)S(1)} %collective-permute-done.16.refs_2_, ...), custom_call_target="tpu_custom_call" | custom-call | flops 16000000000 | bytes 6291472 | tf_op jit(solution)/shard_map/pallas_call | solution.py:54
  153.2 4.9 %all-to-all-done.2 = bf16[16,64,512]{2,1,0:T(8,128)(2,1)S(1)} async-done(((bf16[16,64,512]{2,1,0:T(8,128)(2,1)}), bf16[16,64,512]{2,1,0:T(8,128)(2,1)S(1)}, u32[]{:S(2)}, u32[]{:S(2)}) %all-to-all-start.2) | async-done | bytes 1048608 | tf_op jit(solution)/shard_map/all_to_all | solution.py:442
  158.1 1.5 shard_map.98
  (72 shorter events, 18.3 us)
Async XLA Ops:
  3.4 7.6 %slice-start = ((bf16[512,1536]{1,0:T(8,128)(2,1)}), bf16[512,1024]{1,0:T(8,128)(2,1)S(1)}, s32[]{:S(2)}) async-start(bf16[512,1536]{1,0:T(8,128)(2,1)} %w_hbm.3), calls=%async_computation.3 | async-start | bytes 2097152 | tf_op jit(solution)/shard_map/slice | solution.py:680
  3.5 31.0 %all-to-all-start = ((bf16[16,264,128]{2,1,0:T(8,128)(2,1)}), bf16[16,264,128]{2,1,0:T(8,128)(2,1)S(1)}, u32[]{:S(2)}, u32[]{:S(2)}) async-start(bf16[16,264,128]{2,1,0:T(8,128)(2,1)} %get-tuple-element.41), calls=%async_computation | async-start | bytes 2162688 | tf_op jit(solution)/shard_map/all_to_all | solution.py:442
  11.0 1.4 copy-start.5
  36.6 10.3 %collective-permute-start = (bf16[256,512]{1,0:T(8,128)(2,1)S(1)}, bf16[256,512]{1,0:T(8,128)(2,1)S(1)}, u32[]{:S(2)}, u32[]{:S(2)}) collective-permute-start(bf16[256,512]{1,0:T(8,128)(2,1)S(1)} %get-tuple-element.45), channel_id=1, source_target_pairs={{0,2},{2,0},{4,6},{6,4},{8,10},{10,8},{12,14},{14,12},{16,18},{18,... | collective-permute-start | bytes 786440 | tf_op jit(solution)/shard_map/ppermute | solution.py:447
  37.3 9.6 %collective-permute-start.1 = (bf16[256,512]{1,0:T(8,128)(2,1)S(1)}, bf16[256,512]{1,0:T(8,128)(2,1)S(1)}, u32[]{:S(2)}, u32[]{:S(2)}) collective-permute-start(bf16[256,512]{1,0:T(8,128)(2,1)S(1)} %get-tuple-element.46), channel_id=1, source_target_pairs={{0,30},{2,4},{4,2},{6,8},{8,6},{10,12},{12,10},{14,16},{16,14},{18... | collective-permute-start | bytes 786440 | tf_op jit(solution)/shard_map/ppermute | solution.py:626
  42.3 27.3 %all-to-all-start.1 = ((bf16[16,64,512]{2,1,0:T(8,128)(2,1)}), bf16[16,64,512]{2,1,0:T(8,128)(2,1)}, u32[]{:S(2)}, u32[]{:S(2)}) async-start(bf16[16,64,512]{2,1,0:T(8,128)(2,1)} %bitcast.13), calls=%async_computation.1 | async-start | bytes 2097152 | tf_op jit(solution)/shard_map/all_to_all | solution.py:442
  83.4 3.1 %collective-permute-start.4 = (bf16[256,2048]{1,0:T(8,128)(2,1)}, bf16[256,2048]{1,0:T(8,128)(2,1)S(1)}, u32[]{:S(2)}, u32[]{:S(2)}) collective-permute-start(bf16[256,2048]{1,0:T(8,128)(2,1)} %get-tuple-element.59), channel_id=1, source_target_pairs={{0,2},{2,0},{4,6},{6,4},{8,10},{10,8},{12,14},{14,12},{16,18},{18,... | collective-permute-start | bytes 3145736 | tf_op jit(solution)/shard_map/ppermute | solution.py:447
  87.8 4.5 %copy-start.11 = (bf16[256,512]{1,0:T(8,128)(2,1)S(1)}, bf16[256,512]{1,0:T(8,128)(2,1)}, u32[]{:S(2)}) copy-start(bf16[256,512]{1,0:T(8,128)(2,1)} %get-tuple-element.53) | copy-start | bytes 786436
  87.8 4.5 %copy-start.10 = (bf16[256,512]{1,0:T(8,128)(2,1)S(1)}, bf16[256,512]{1,0:T(8,128)(2,1)}, u32[]{:S(2)}) copy-start(bf16[256,512]{1,0:T(8,128)(2,1)} %get-tuple-element.54) | copy-start | bytes 786436
  88.7 11.5 %collective-permute-start.5 = (bf16[64,2048]{1,0:T(8,128)(2,1)S(1)}, bf16[64,2048]{1,0:T(8,128)(2,1)S(1)}, u32[]{:S(2)}, u32[]{:S(2)}) collective-permute-start(bf16[64,2048]{1,0:T(8,128)(2,1)S(1)} %get-tuple-element.61), channel_id=1, source_target_pairs={{0,4},{2,6},{4,0},{6,2},{8,12},{10,14},{12,8},{14,10},{16,20},{18,... | collective-permute-start | bytes 786440 | tf_op jit(solution)/shard_map/ppermute | solution.py:447
  90.8 9.5 %collective-permute-start.6 = (bf16[64,2048]{1,0:T(8,128)(2,1)S(1)}, bf16[64,2048]{1,0:T(8,128)(2,1)S(1)}, u32[]{:S(2)}, u32[]{:S(2)}) collective-permute-start(bf16[64,2048]{1,0:T(8,128)(2,1)S(1)} %get-tuple-element.63), channel_id=1, source_target_pairs={{0,1},{1,0},{2,3},{3,2},{4,5},{5,4},{6,7},{7,6},{8,9},{9,8},{10,11... | collective-permute-start | bytes 786440 | tf_op jit(solution)/shard_map/ppermute | solution.py:447
  92.3 21.3 %collective-permute-start.2 = (bf16[256,512]{1,0:T(8,128)(2,1)S(1)}, bf16[256,512]{1,0:T(8,128)(2,1)S(1)}, u32[]{:S(2)}, u32[]{:S(2)}) collective-permute-start(bf16[256,512]{1,0:T(8,128)(2,1)S(1)} %copy-done.11), channel_id=1, source_target_pairs={{0,2},{2,0},{4,6},{6,4},{8,10},{10,8},{12,14},{14,12},{16,18},{18,... | collective-permute-start | bytes 786440 | tf_op jit(solution)/shard_map/ppermute | solution.py:447
  92.3 21.3 %collective-permute-start.3 = (bf16[256,512]{1,0:T(8,128)(2,1)S(1)}, bf16[256,512]{1,0:T(8,128)(2,1)}, u32[]{:S(2)}, u32[]{:S(2)}) collective-permute-start(bf16[256,512]{1,0:T(8,128)(2,1)S(1)} %copy-done.10), channel_id=1, source_target_pairs={{0,30},{2,4},{4,2},{6,8},{8,6},{10,12},{12,10},{14,16},{16,14},{18... | collective-permute-start | bytes 786440 | tf_op jit(solution)/shard_map/ppermute | solution.py:626
  100.9 5.3 %collective-permute-start.7 = (bf16[32,2048]{1,0:T(8,128)(2,1)S(1)}, bf16[32,2048]{1,0:T(8,128)(2,1)S(1)}, u32[]{:S(2)}, u32[]{:S(2)}) collective-permute-start(bf16[32,2048]{1,0:T(8,128)(2,1)S(1)} %get-tuple-element.65), channel_id=1, source_target_pairs={{0,1},{1,0},{2,3},{3,2},{4,5},{5,4},{6,7},{7,6},{8,9},{9,8},{10,11... | collective-permute-start | bytes 393224 | tf_op jit(solution)/shard_map/ppermute | solution.py:447
  102.7 5.2 %collective-permute-start.8 = (bf16[32,2048]{1,0:T(8,128)(2,1)S(1)}, bf16[32,2048]{1,0:T(8,128)(2,1)S(1)}, u32[]{:S(2)}, u32[]{:S(2)}) collective-permute-start(bf16[32,2048]{1,0:T(8,128)(2,1)S(1)} %get-tuple-element.67), channel_id=1, source_target_pairs={{0,4},{2,6},{4,0},{6,2},{8,12},{10,14},{12,8},{14,10},{16,20},{18,... | collective-permute-start | bytes 393224 | tf_op jit(solution)/shard_map/ppermute | solution.py:447
  108.0 10.2 %collective-permute-start.9 = (bf16[16,2048]{1,0:T(8,128)(2,1)S(1)}, bf16[16,2048]{1,0:T(8,128)(2,1)S(1)}, u32[]{:S(2)}, u32[]{:S(2)}) collective-permute-start(bf16[16,2048]{1,0:T(8,128)(2,1)S(1)} %get-tuple-element.69), channel_id=1, source_target_pairs={{0,8},{2,10},{4,12},{6,14},{8,0},{10,2},{12,4},{14,6},{16,24},{18,... | collective-permute-start | bytes 196616 | tf_op jit(solution)/shard_map/ppermute | solution.py:447
  111.0 7.1 %collective-permute-start.10 = (bf16[16,2048]{1,0:T(8,128)(2,1)S(1)}, bf16[16,2048]{1,0:T(8,128)(2,1)S(1)}, u32[]{:S(2)}, u32[]{:S(2)}) collective-permute-start(bf16[16,2048]{1,0:T(8,128)(2,1)S(1)} %get-tuple-element.70), channel_id=1, source_target_pairs={{0,16},{2,18},{4,20},{6,22},{8,24},{10,26},{12,28},{14,30},{16,0},... | collective-permute-start | bytes 196616 | tf_op jit(solution)/shard_map/ppermute | solution.py:447
  112.4 6.1 %collective-permute-start.11 = (bf16[16,2048]{1,0:T(8,128)(2,1)S(1)}, bf16[16,2048]{1,0:T(8,128)(2,1)S(1)}, u32[]{:S(2)}, u32[]{:S(2)}) collective-permute-start(bf16[16,2048]{1,0:T(8,128)(2,1)S(1)} %get-tuple-element.71), channel_id=1, source_target_pairs={{0,24},{2,26},{4,28},{6,30},{8,16},{10,18},{12,20},{14,22},{16,8},... | collective-permute-start | bytes 196616 | tf_op jit(solution)/shard_map/ppermute | solution.py:447
  119.3 4.5 %collective-permute-start.12 = (bf16[16,2048]{1,0:T(8,128)(2,1)S(1)}, bf16[16,2048]{1,0:T(8,128)(2,1)S(1)}, u32[]{:S(2)}, u32[]{:S(2)}) collective-permute-start(bf16[16,2048]{1,0:T(8,128)(2,1)S(1)} %shard_map.95.refs_0_), channel_id=1, source_target_pairs={{0,8},{2,10},{4,12},{6,14},{8,0},{10,2},{12,4},{14,6},{16,24},{18,... | collective-permute-start | bytes 196616 | tf_op jit(solution)/shard_map/ppermute | solution.py:447
  119.9 5.2 %collective-permute-start.13 = (bf16[16,2048]{1,0:T(8,128)(2,1)S(1)}, bf16[16,2048]{1,0:T(8,128)(2,1)S(1)}, u32[]{:S(2)}, u32[]{:S(2)}) collective-permute-start(bf16[16,2048]{1,0:T(8,128)(2,1)S(1)} %shard_map.95.refs_0_), channel_id=1, source_target_pairs={{0,16},{2,18},{4,20},{6,22},{8,24},{10,26},{12,28},{14,30},{16,0},... | collective-permute-start | bytes 196616 | tf_op jit(solution)/shard_map/ppermute | solution.py:447
  122.2 6.1 %collective-permute-start.14 = (bf16[16,2048]{1,0:T(8,128)(2,1)S(1)}, bf16[16,2048]{1,0:T(8,128)(2,1)S(1)}, u32[]{:S(2)}, u32[]{:S(2)}) collective-permute-start(bf16[16,2048]{1,0:T(8,128)(2,1)S(1)} %shard_map.95.refs_0_), channel_id=1, source_target_pairs={{0,24},{2,26},{4,28},{6,30},{8,16},{10,18},{12,20},{14,22},{16,8},... | collective-permute-start | bytes 196616 | tf_op jit(solution)/shard_map/ppermute | solution.py:447
  129.0 8.7 %collective-permute-start.15 = (bf16[64,2048]{1,0:T(8,128)(2,1)}, bf16[64,2048]{1,0:T(8,128)(2,1)S(1)}, u32[]{:S(2)}, u32[]{:S(2)}) collective-permute-start(bf16[64,2048]{1,0:T(8,128)(2,1)} %shard_map.96.refs_1_.refs_0_), channel_id=1, source_target_pairs={{0,4},{2,6},{4,0},{6,2},{8,12},{10,14},{12,8},{14,10},{16,20},{18,... | collective-permute-start | bytes 786440 | tf_op jit(solution)/shard_map/ppermute | solution.py:447
  131.0 6.6 %collective-permute-start.16 = (bf16[64,2048]{1,0:T(8,128)(2,1)}, bf16[64,2048]{1,0:T(8,128)(2,1)S(1)}, u32[]{:S(2)}, u32[]{:S(2)}) collective-permute-start(bf16[64,2048]{1,0:T(8,128)(2,1)} %shard_map.96.refs_1_.refs_0_), channel_id=1, source_target_pairs={{0,1},{1,0},{2,3},{3,2},{4,5},{5,4},{6,7},{7,6},{8,9},{9,8},{10,11... | collective-permute-start | bytes 786440 | tf_op jit(solution)/shard_map/ppermute | solution.py:447
  131.5 26.6 %all-to-all-start.2 = ((bf16[16,64,512]{2,1,0:T(8,128)(2,1)}), bf16[16,64,512]{2,1,0:T(8,128)(2,1)S(1)}, u32[]{:S(2)}, u32[]{:S(2)}) async-start(bf16[16,64,512]{2,1,0:T(8,128)(2,1)} %bitcast.15), calls=%async_computation.2 | async-start | bytes 2097152 | tf_op jit(solution)/shard_map/all_to_all | solution.py:442
  135.2 13.8 %collective-permute-start.19 = (bf16[64,2048]{1,0:T(8,128)(2,1)}, bf16[64,2048]{1,0:T(8,128)(2,1)S(1)}, u32[]{:S(2)}, u32[]{:S(2)}) collective-permute-start(bf16[64,2048]{1,0:T(8,128)(2,1)} %shard_map.96.refs_1_.refs_0_), channel_id=1, source_target_pairs={{0,2},{2,0},{4,6},{6,4},{8,10},{10,8},{12,14},{14,12},{16,18},{18,... | collective-permute-start | bytes 786440 | tf_op jit(solution)/shard_map/ppermute | solution.py:447
  137.6 10.8 %collective-permute-start.17 = (bf16[32,2048]{1,0:T(8,128)(2,1)S(1)}, bf16[32,2048]{1,0:T(8,128)(2,1)S(1)}, u32[]{:S(2)}, u32[]{:S(2)}) collective-permute-start(bf16[32,2048]{1,0:T(8,128)(2,1)S(1)} %slice.12), channel_id=1, source_target_pairs={{0,4},{2,6},{4,0},{6,2},{8,12},{10,14},{12,8},{14,10},{16,20},{18,... | collective-permute-start | bytes 393224 | tf_op jit(solution)/shard_map/ppermute | solution.py:447
  137.7 11.3 %collective-permute-start.20 = (bf16[64,2048]{1,0:T(8,128)(2,1)S(1)}, bf16[64,2048]{1,0:T(8,128)(2,1)S(1)}, u32[]{:S(2)}, u32[]{:S(2)}) collective-permute-start(bf16[64,2048]{1,0:T(8,128)(2,1)S(1)} %collective-permute-done.15.refs_1_), channel_id=1, source_target_pairs={{0,2},{2,0},{4,6},{6,4},{8,10},{10,8},{12,14},{14,12},{16,18},{18,... | collective-permute-start | bytes 786440 | tf_op jit(solution)/shard_map/ppermute | solution.py:447
  137.8 11.2 %collective-permute-start.21 = (bf16[64,2048]{1,0:T(8,128)(2,1)S(1)}, bf16[64,2048]{1,0:T(8,128)(2,1)S(1)}, u32[]{:S(2)}, u32[]{:S(2)}) collective-permute-start(bf16[64,2048]{1,0:T(8,128)(2,1)S(1)} %collective-permute-done.16.refs_2_), channel_id=1, source_target_pairs={{0,2},{2,0},{4,6},{6,4},{8,10},{10,8},{12,14},{14,12},{16,18},{18,... | collective-permute-start | bytes 786440 | tf_op jit(solution)/shard_map/ppermute | solution.py:447
  138.3 10.1 %collective-permute-start.18 = (bf16[32,2048]{1,0:T(8,128)(2,1)S(1)}, bf16[32,2048]{1,0:T(8,128)(2,1)S(1)}, u32[]{:S(2)}, u32[]{:S(2)}) collective-permute-start(bf16[32,2048]{1,0:T(8,128)(2,1)S(1)} %slice.13), channel_id=1, source_target_pairs={{0,1},{1,0},{2,3},{3,2},{4,5},{5,4},{6,7},{7,6},{8,9},{9,8},{10,11... | collective-permute-start | bytes 393224 | tf_op jit(solution)/shard_map/ppermute | solution.py:447
  148.4 1.3 collective-permute-start.22
  148.4 1.5 collective-permute-start.23
  149.0 9.1 %copy-start.2 = (bf16[512,1024]{1,0:T(8,128)(2,1)S(1)}, bf16[512,1024]{1,0:T(8,128)(2,1)}, u32[]{:S(2)}) copy-start(bf16[512,1024]{1,0:T(8,128)(2,1)} %copy-done.1) | copy-start | bytes 3145732
  (10 other events, 8.8 us)

commit v6 on v5

--- a/solution.py
+++ b/solution.py
@@ -13,7 +13,7 @@
 INFO_ROWS = 8
 GATE_FLOPS = 10**10
 FORWARD_FLOPS = 10**11
-SPREAD_FLOPS = 16 * 10**9
+SPREAD_FLOPS = 13 * 10**9
 LANES = 128
 
 
@@ -125,9 +125,9 @@
     back_ref[...] = pick.T.astype(jnp.bfloat16)
 
 
-def place_points_kernel(core_ref, got_ref, own_ref, near_ref, far_ref, at_ref):
+def place_points_kernel(core_ref, got_ref, near_ref, far_ref, at_ref):
     n_dev, block, _ = got_ref.shape
-    rows, width = own_ref.shape
+    rows, width = (2 * near_ref.shape[0], near_ref.shape[1])
     cap = (block - INFO_ROWS) * LANES // width
     half = rows // 2
     per = LANES // cap
@@ -149,7 +149,6 @@
     placed = contract(
         jnp.concatenate(parts, axis=1), jnp.concatenate(data, axis=0).astype(jnp.bfloat16), 1, 0
     ).astype(jnp.bfloat16)
-    own_ref[...] = placed
     near_ref[...] = jnp.where(core_ref[0] == 0, placed[half:], placed[:half])
     far_ref[...] = jnp.where(core_ref[0] == 0, placed[:half], placed[half:])
 
@@ -211,13 +210,14 @@
 def forward_kernel(
     core_ref,
     at_ref,
-    own_ref,
+    near_sent_ref,
+    far_sent_ref,
     near_ref,
     far_ref,
     w_hbm,
     w_kv_t_hbm,
     query_hbm,
-    kv_hbm,
+    value_hbm,
     key_t_hbm,
     attn_t_hbm,
     probs_hbm,
@@ -227,7 +227,7 @@
     w_ref,
     w_kv_t_ref,
     query_ref,
-    kv_ref,
+    value_ref,
     key_t_ref,
     attn_t_ref,
     probs_ref,
@@ -239,23 +239,24 @@
     head_dim = width // HEADS
     half = points_ref.shape[0] // 4
     copies = fetch([w_hbm, w_kv_t_hbm], [w_ref, w_kv_t_ref], sems)
-    near, far = (near_ref[...], far_ref[...])
-    points_ref[:half, :] = jnp.where(core_ref[0] == 0, far, near)
-    points_ref[half : 3 * half, :] = own_ref[...]
-    points_ref[3 * half :, :] = jnp.where(core_ref[0] == 0, near, far)
+    even = core_ref[0] == 0
+    quarters = ((far_ref, near_ref), (far_sent_ref, near_sent_ref))
+    for i, (on_even, on_odd) in enumerate((*quarters, *(pair[::-1] for pair in quarters[::-1]))):
+        points_ref[i * half : (i + 1) * half, :] = jnp.where(even, on_even[...], on_odd[...])
     table_ref[...] = place_table(at_ref, 2 * half).T.astype(jnp.bfloat16)
     stores = fetch([table_ref], [table_hbm], sems, 6)
     for copy in copies:
         copy.wait()
     points = points_ref[...]
     query_ref[...] = contract(points[half : 3 * half], w_ref[:, :width], 1, 0).astype(jnp.bfloat16)
-    kv_ref[...] = contract(points, w_ref[:, width:], 1, 0).astype(jnp.bfloat16)
+    keys = contract(points, w_ref[:, width : 2 * width], 1, 0).astype(jnp.bfloat16)
+    value_ref[...] = contract(points, w_ref[:, 2 * width :], 1, 0).astype(jnp.bfloat16)
     kv_t = contract(w_kv_t_ref[...], points, 1, 1).astype(jnp.bfloat16)
     key_t_ref[...] = kv_t[:width]
     points_t_ref[...] = points.astype(jnp.float32).T.astype(jnp.bfloat16)
     stores += fetch(
-        [query_ref, kv_ref, key_t_ref, points_t_ref],
-        [query_hbm, kv_hbm, key_t_hbm, points_t_hbm],
+        [query_ref, value_ref, key_t_ref, points_t_ref],
+        [query_hbm, value_hbm, key_t_hbm, points_t_hbm],
         sems,
         7,
     )
@@ -266,7 +267,7 @@
         within = head * head_dim % LANES // head_dim
         query = query_ref[:, first : first + LANES]
         query = jnp.where(side == within, query, jnp.zeros_like(query))
-        key = kv_ref[:, first : first + LANES]
+        key = keys[:, first : first + LANES]
         scores = jnp.concatenate(
             [
                 contract(key[: 2 * half], query[:half], 1, 1),
@@ -308,7 +309,7 @@
     got_hbm,
     w_out_hbm,
     query_hbm,
-    kv_hbm,
+    value_hbm,
     key_t_hbm,
     attn_t_hbm,
     points_t_hbm,
@@ -322,7 +323,7 @@
     got_ref,
     w_out_ref,
     query_ref,
-    kv_ref,
+    value_ref,
     key_t_ref,
     attn_t_ref,
     points_t_ref,
@@ -344,8 +345,8 @@
     scale = 1.0 / math.sqrt(head_dim)
     first_copies = fetch([got_hbm, w_out_hbm], [got_ref, w_out_ref], sems)
     copies = fetch(
-        [attn_t_hbm, query_hbm, kv_hbm, key_t_hbm],
-        [attn_t_ref, query_ref, kv_ref, key_t_ref],
+        [attn_t_hbm, query_hbm, value_hbm, key_t_hbm],
+        [attn_t_ref, query_ref, value_ref, key_t_ref],
         sems,
         2,
     )
@@ -379,7 +380,7 @@
         if first == 0:
             late = fetch([points_t_hbm, w_hbm], [points_t_ref, w_ref], sems, 6)
         for mine, patch in sides:
-            value = kv_ref[patch, value_cols]
+            value = value_ref[patch, cols]
             grad_key = jnp.zeros((2 * half, LANES), jnp.float32)
             grad_value = grad_key
             for within in range(LANES // head_dim):
@@ -458,53 +459,31 @@
     return blocks
 
 
-def part_rows(total, side, keep_ref, send_ref):
-    half = keep_ref.shape[0]
-    keep_ref[...] = jnp.where(side == 0, total[:half], total[half:])
-    send_ref[...] = jnp.where(side == 0, total[half:], total[:half]).astype(jnp.bfloat16)
-
-
-def first_sum_kernel(
-    sides_ref, kept_hbm, got_ref, keep_a, send_a, keep_b, send_b, kept_ref, sems
-):
-    half = kept_ref.shape[0] // 2
-    parts = [pl.ds(0, half), pl.ds(half, half)]
-    copies = fetch([kept_hbm.at[p, :] for p in parts], [kept_ref.at[p, :] for p in parts], sems)
-    for index, (part, keep, send) in enumerate(
-        zip(parts, (keep_a, keep_b), (send_a, send_b), strict=True)
-    ):
-        copies[index].wait()
-        total = kept_ref[part, :].astype(jnp.float32) + got_ref[part, :].astype(jnp.float32)
-        part_rows(total, sides_ref[index], keep, send)
-
-
-def second_sum_kernel(
-    sides_ref, kept_a_ref, got_a_ref, kept_b_ref, got_b_ref, keep_a, send_a, keep_b, send_b
-):
-    part_rows(
-        kept_a_ref[...] + got_a_ref[...].astype(jnp.float32), sides_ref[1], keep_a, send_a
-    )
-    part_rows(
-        kept_b_ref[...] + got_b_ref[...].astype(jnp.float32), sides_ref[0], keep_b, send_b
-    )
-
-
-def third_sum_kernel(
-    line_ref, kept_a_ref, got_a_ref, kept_b_ref, got_b_ref, mine_ref, *refs
-):
-    sends, total_ref = (refs[:-1], refs[-1])
-    rows = mine_ref.shape[0] // 2
-    half = kept_a_ref.shape[0]
-    total_ref[:half, :] = kept_a_ref[...] + got_a_ref[...].astype(jnp.float32)
-    total_ref[half:, :] = kept_b_ref[...] + got_b_ref[...].astype(jnp.float32)
+def first_sum_kernel(sides_ref, kept_ref, got_ref, keep, send_x, send_y, send_xy):
+    rows = keep.shape[0]
+    side_x, side_y = (sides_ref[0], sides_ref[1])
+    quarters = []
+    for far_x, far_y in ((1, 0), (1, 1), (0, 1), (0, 0)):
+        at = ((side_x ^ far_x) * 2 + (side_y ^ far_y)) * rows
+        quarters.append(pl.ds(pl.multiple_of(at, rows), rows))
+    for quarter, out_ref in zip(quarters, (send_x, send_xy, send_y, keep), strict=True):
+        total = kept_ref[quarter, :].astype(jnp.float32) + got_ref[quarter, :].astype(jnp.float32)
+        out_ref[...] = total.astype(out_ref.dtype)
+
+
+def second_sum_kernel(line_ref, kept_ref, *refs):
+    got, mine_ref, sends, total_ref = (refs[:3], refs[3], refs[4:-1], refs[-1])
+    rows = mine_ref.shape[0]
+    total = kept_ref[...]
+    for ref in got:
+        total = total + ref[...].astype(jnp.float32)
+    total_ref[...] = total
     for distance, out_ref in enumerate((mine_ref, *sends)):
         at = pl.multiple_of((line_ref[0] ^ distance) * rows, rows)
-        out_ref[...] = jnp.concatenate(
-            [total_ref[pl.ds(at, rows), :], total_ref[pl.ds(half + at, rows), :]], axis=0
-        ).astype(out_ref.dtype)
-
-
-def fourth_sum_kernel(mine_ref, *refs):
+        out_ref[...] = total_ref[pl.ds(at, rows), :].astype(out_ref.dtype)
+
+
+def third_sum_kernel(mine_ref, *refs):
     others, out_ref = (refs[:-2], refs[-1])
     total = mine_ref[...]
     for other in others:
@@ -513,107 +492,85 @@
 
 
 def join_kernel(*refs):
-    blocks, out_ref = (refs[:-1], refs[-1])
-    rows = blocks[0].shape[0] // 2
-    values = [block[...].astype(jnp.float32) for block in blocks]
-    halves = [x[:rows] for x in values] + [x[rows:] for x in values]
-    out_ref[...] = jnp.concatenate(halves, axis=0).astype(jnp.bfloat16)
+    refs[-1][...] = jnp.concatenate([ref[...] for ref in refs[:-1]], axis=0)
 
 
 def spread_kernel(n_line, place_ref, *refs):
     pieces, qkv_ref, out_ref = (refs[:-2], refs[-2], refs[-1])
     n_qkv = qkv_ref.shape[1]
     core, side_x, side_y, line = (place_ref[i] for i in range(4))
-    rows = qkv_ref.shape[0] // (16 * n_line)
+    rows = pieces[0].shape[0] // n_line
     for index, piece in enumerate(pieces):
-        far_core, which = divmod(index, 5)
-        far_x, far_y = ((0, 0), (1, 0), (0, 1), (1, 1), (1, 1))[which]
-        near_x, near_y = (side_x ^ far_x, side_y ^ far_y)
-        values = piece[...].astype(jnp.float32)
-        for block in range(piece.shape[0] // rows):
-            part, distance = divmod(block, n_line)
-            if which == 4:
-                part = 1
-            first, second = ((near_x, near_y), (near_y, near_x))[part]
-            unit = ((((core ^ far_core) * 2 + part) * 2 + first) * 2 + second) * n_line
-            row = pl.multiple_of((unit + (line ^ distance)) * rows, rows)
-            data = values[block * rows : (block + 1) * rows]
+        near_x, near_y = (side_x ^ (index & 1), side_y ^ (index >> 1 & 1))
+        quarter = ((core ^ (index >> 2)) * 2 + near_x) * 2 + near_y
+        for distance in range(n_line):
+            row = pl.multiple_of((quarter * n_line + (line ^ distance)) * rows, rows)
+            data = piece[distance * rows : (distance + 1) * rows, :].astype(jnp.float32)
             qkv_ref[pl.ds(row, rows), :] = data[:, :n_qkv]
             out_ref[pl.ds(row, rows), :] = data[:, n_qkv:]
 
 
-def sum_start(keep, send, sides, ready):
+def swap_across(block):
+    size = lax.axis_size("curve")
+    route = [(2 * i + j, 2 * (i ^ 2) + (j ^ 1)) for i in range(size) for j in range(2)]
+    return lax.ppermute(block, ("curve", "dp"), route)
+
+
+def sum_start(keep, send, sides):
     n_line = lax.axis_size("curve") // 4
     line = lax.axis_index("curve") >> 2
     rows, width = keep.shape
-    scalar = [SMEM] + [VMEM] * 4
-    kept_a, send_a, kept_b, send_b = call(
+    rows = rows // 4
+    kept, send_x, send_y, send_xy = call(
         first_sum_kernel,
-        [wide(rows // 4, width), low(rows // 4, width)] * 2,
+        [wide(rows, width)] + [low(rows, width)] * 3,
         [sides, keep, swap(send, "curve", 1)],
-        rows * width,
-        [SMEM, HBM, VMEM],
-        scratch=[space(keep), pltpu.SemaphoreType.DMA((2,))],
-    )
-    got_a = swap(send_a, "curve", 2)
-    got_b = swap(send_b, "dp", 1)
-    kept_a, send_a, kept_b, send_b = call(
-        second_sum_kernel,
-        [wide(rows // 8, width), low(rows // 8, width)] * 2,
-        [sides, kept_a, got_a, kept_b, got_b],
-        rows * width // 2,
-        scalar,
-    )
-    got_a = swap(send_a, "dp", 1)
-    got_b = swap(send_b, "curve", 2)
-    rows = kept_a.shape[0] // n_line
-    if rows % 8 == 0:
+        4 * rows * width,
+        [SMEM, VMEM, VMEM],
+    )
+    got = [swap(send_x, "curve", 2), swap(send_y, "dp", 1), swap_across(send_xy)]
+    rows = rows // n_line
+    if rows % 16 == 0:
         mine, *sends = call(
-            third_sum_kernel,
-            [wide(2 * rows, width)] + [low(2 * rows, width)] * (n_line - 1),
-            [line.reshape(1), kept_a, got_a, kept_b, got_b],
-            kept_a.size,
-            scalar,
-            scratch=[pltpu.VMEM((2 * n_line * rows, width), jnp.float32)],
+            second_sum_kernel,
+            [wide(rows, width)] + [low(rows, width)] * (n_line - 1),
+            [line.reshape(1), kept, *got],
+            kept.size,
+            [SMEM] + [VMEM] * 4,
+            scratch=[space(kept)],
         )
-    else:
-        part_a = (kept_a + got_a.astype(jnp.float32)).reshape(n_line, rows, width)
-        part_b = (kept_b + got_b.astype(jnp.float32)).reshape(n_line, rows, width)
-        both = jnp.concatenate([part_a, part_b], axis=1)
-        mine, *sends = [
-            lax.dynamic_index_in_dim(both, line ^ k, 0, keepdims=False) for k in range(n_line)
-        ]
-        sends = [block.astype(jnp.bfloat16) for block in sends]
+        return (mine, sends)
+    total = kept + sum(x.astype(jnp.float32) for x in got)
+    total = total.reshape(n_line, rows, width)
+    mine, *sends = [
+        lax.dynamic_index_in_dim(total, line ^ k, 0, keepdims=False) for k in range(n_line)
+    ]
+    return (mine, [block.astype(jnp.bfloat16) for block in sends])
+
+
+def sum_line(mine, sends, ready):
+    n_line = len(sends) + 1
+    line = lax.axis_index("curve") >> 2
+    rows, width = mine.shape
     others = [swap(block, "curve", 4 * (k + 1)) for k, block in enumerate(sends)]
-    (mine,) = call(
-        fourth_sum_kernel,
-        [low(2 * rows, width)],
-        [mine, *others, ready],
-        mine.size,
-        [VMEM] * n_line + [ANY],
-    )
+    (mine,) = call(third_sum_kernel, [low(rows, width)], [mine, *others, ready], mine.size)
     blocks = [mine] + [swap(mine, "curve", 4 * k) for k in range(1, n_line)]
-    if rows % 8 == 0:
-        (own,) = call(join_kernel, [low(2 * n_line * rows, width)], blocks, mine.size)
-    else:
-        blocks = order_blocks(jnp.stack(blocks), line)
-        own = jnp.swapaxes(blocks.reshape(n_line, 2, rows, width), 0, 1)
-        own = own.reshape(2 * n_line * rows, width)
-        line = jnp.zeros_like(line)
-    return (own, line)
-
-
-def sum_finish(own, line, sides, width_qkv):
-    n_line = lax.axis_size("curve") // 4
+    if rows % 16 == 0:
+        (own,) = call(join_kernel, [low(n_line * rows, width)], blocks, mine.size)
+        return (own, line, n_line)
+    own = order_blocks(jnp.stack(blocks), line).reshape(n_line * rows, width)
+    return (own, jnp.zeros_like(line), 1)
+
+
+def sum_finish(own, line, n_line, sides, width_qkv):
     core = lax.axis_index("curve") & 1
-    half, width = (own.shape[0] // 2, own.shape[1])
+    rows, width = own.shape
     over_x = swap(own, "curve", 2)
-    over_y = swap(own, "dp", 1)
-    pieces = [own, over_x, over_y, swap(over_y[:half], "curve", 2), swap(over_x[half:], "dp", 1)]
+    pieces = [own, over_x, swap(own, "dp", 1), swap(over_x, "dp", 1)]
     pieces += [swap(piece, "curve", 1) for piece in pieces]
     return call(
         functools.partial(spread_kernel, n_line),
-        [wide(16 * half, width_qkv), wide(16 * half, width - width_qkv)],
+        [wide(8 * rows, width_qkv), wide(8 * rows, width - width_qkv)],
         [jnp.stack([core, sides[0], sides[1], line]), *pieces],
         SPREAD_FLOPS,
         [SMEM] + [VMEM] * len(pieces),
@@ -650,10 +607,9 @@
     send_grads, restore_table = call(
         pack_grads_kernel, [low(total, width), low(rows, total)], [slots, grad_out[0]], place_flops
     )
-    own, near, far, at = call(
+    near_sent, far_sent, at = call(
         place_points_kernel,
         [
-            low(rows, width),
             low(half, width),
             low(half, width),
             wide(total // LANES, LANES),
@@ -662,31 +618,31 @@
         place_flops,
         [SMEM, VMEM],
     )
-    near, far = halo(near, far)
+    near, far = halo(near_sent, far_sent)
     send_grads = gate(send_grads, at, flops=GATE_FLOPS)
     got_grads = exchange(send_grads.reshape(n_dev, cap, width)).reshape(total, width)
     saved = [
         low(rows, width),
-        low(2 * rows, 2 * width),
+        low(2 * rows, width),
         low(width, 2 * rows),
         low(width, rows),
         low(HEADS, PATCH, PATCH),
         low(width, 2 * rows),
         low(total, rows),
     ]
-    query, kv, key_t, attn_t, probs, points_t, pick_table = call(
+    query, value, key_t, attn_t, probs, points_t, pick_table = call(
         forward_kernel,
         saved,
-        [core, at, own, near, far, w_qkv, w_qkv[:, width:].T],
+        [core, at, near_sent, far_sent, near, far, w_qkv, w_qkv[:, width:].T],
         FORWARD_FLOPS,
-        [SMEM] + [VMEM] * 4 + [HBM] * 2,
+        [SMEM] + [VMEM] * 5 + [HBM] * 2,
         [HBM] * len(saved),
         [space(low(2 * rows, width)), space(low(width, 3 * width)), space(low(2 * width, width))]
         + [space(x) for x in saved]
         + [pltpu.SemaphoreType.DMA((12 + HEADS,))],
         60,
     )
-    held = [got_grads, w_out, query, kv, key_t, attn_t, points_t, w_qkv, probs]
+    held = [got_grads, w_out, query, value, key_t, attn_t, points_t, w_qkv, probs]
     made = [
         low(width // 2, 4 * width),
         low(width // 2, 4 * width),
@@ -707,6 +663,7 @@
         + [pltpu.SemaphoreType.DMA((13 + HEADS,))],
         63,
     )
+    mine, sends = sum_start(keep, send, sides)
     near, far = halo(near, far)
     picked = low(total, width)
     picked, done = call(
@@ -719,10 +676,10 @@
         [space(x) for x in (near, far, own_input, pick_table, picked)] + [pltpu.SemaphoreType.DMA((8,))],
         63,
     )
-    gathered, line = sum_start(keep, send, sides, done)
+    gathered, line, n_line = sum_line(mine, sends, done)
     picked = gate(picked, gathered, flops=GATE_FLOPS)
     returned = exchange(picked.reshape(n_dev, cap, width)).reshape(total, width)
-    weight_qkv, weight_out = sum_finish(gathered, line, sides, 3 * width)
+    weight_qkv, weight_out = sum_finish(gathered, line, n_line, sides, 3 * width)
     (result,) = call(restore_kernel, [low(rows, width)], [restore_table, returned], place_flops)
     return (result[None], weight_qkv, weight_out)
 

time: 161 us -> 159 us (0.988)
  starting transfers between devices: 48.2 us -> 45.1 us
    ppermute x0 -> x1, waiting for transfers between devices: none -> 6.44 us  [swap_across(): return lax.ppermute(block, ('curve', 'dp'), route)]
    ppermute x22 -> x18, starting transfers between devices: 24.1 us -> 19.2 us  [swap(): return lax.ppermute(block, axis, [(i, i ^ mask) for i in range(size)])]
    ppermute x22 -> x18, waiting for transfers between devices: 26.9 us -> 24.1 us  [swap(): return lax.ppermute(block, axis, [(i, i ^ mask) for i in range(size)])]
    all_to_all x3, waiting for transfers between devices: 34.4 us -> 32.2 us  [exchange(): lax.all_to_all(blocks, 'curve', split_axis=0, concat_axis=0, tiled=True)]
    ppermute x2, starting transfers between devices: 8.48 us -> 10.4 us  [halo(): return (swap(near, 'curve', 1), lax.ppermute(far, 'curve', route))]
    pallas_call x13 -> x12, Pallas kernels: 40.9 us -> 39.9 us  [call(): pl.pallas_call(kernel, out_shape=outs, in_specs=ins or [VMEM] * len(args)...]
    unnamed x29 -> x27, local copies, waits for them, and re-layouts: 8.1 us -> 7.26 us
  transfers between devices with their start and end apart: 27 -> 24, of which waited for: 14 -> 14; matrix products, arithmetic and copies ran while one was open for 1% -> 1% of each run, Pallas kernels for 13% -> 13%
where the time goes in v6:
time: 159 us; the launch traced here: 157 us
  waiting for transfers between devices  62.7 us (39%)
  starting transfers between devices  45.1 us (28%)
  Pallas kernels  39.9 us (25%)
  local copies, waits for them, and re-layouts  8.47 us (5%)
    pallas_call x12, Pallas kernels, call(): pl.pallas_call(kernel, out_shape=outs, in_specs=ins or [VMEM] * len(args)...  39.9 us
    all_to_all x3, waiting for transfers between devices, exchange(): lax.all_to_all(blocks, 'curve', split_axis=0, concat_axis=0, tiled=True)  32.2 us
    ppermute x18, waiting for transfers between devices, swap(): return lax.ppermute(block, axis, [(i, i ^ mask) for i in range(size)])  24.1 us
    ppermute x18, starting transfers between devices, swap(): return lax.ppermute(block, axis, [(i, i ^ mask) for i in range(size)])  19.2 us
    all_to_all x3, starting transfers between devices, exchange(): lax.all_to_all(blocks, 'curve', split_axis=0, concat_axis=0, tiled=True)  15.6 us
    ppermute x2, starting transfers between devices, halo(): return (swap(near, 'curve', 1), lax.ppermute(far, 'curve', route))  10.4 us
    unnamed x27, local copies, waits for them, and re-layouts  7.26 us
    ppermute x1, waiting for transfers between devices, swap_across(): return lax.ppermute(block, ('curve', 'dp'), route)  6.44 us
  transfers between devices with their start and end apart: 24, of which 14 were waited for; matrix products, arithmetic and copies ran while one was open for 1% of the time, Pallas kernels for 13%

profile of v6, /device:TPU:0, one launch (start us, length us, event | category | flops | bytes accessed | tf_op | source)
XLA Modules:
  0.0 157.2 jit_solution(7084872878996696006)
XLA Ops:
  0.6 2.8 %shard_map.85 = (bf16[16,264,128]{2,1,0:T(8,128)(2,1)}, s32[1,512]{1,0:T(1,128)}) custom-call(s32[1,512]{1,0:T(1,128)} %dev_hbm.1, s32[1,512]{1,0:T(1,128)} %row_hbm.1, bf16[512,512]{1,0:T(8,128)(2,1)} %bitcast.18), custom_call_target="tpu_custom_call" | custom-call | flops 536870912 | bytes 1611776 | tf_op jit(solution)/shard_map/pallas_call | solution.py:54
  3.4 7.4 %all-to-all-start = ((bf16[16,264,128]{2,1,0:T(8,128)(2,1)}), bf16[16,264,128]{2,1,0:T(8,128)(2,1)S(1)}, u32[]{:S(2)}, u32[]{:S(2)}) async-start(bf16[16,264,128]{2,1,0:T(8,128)(2,1)} %get-tuple-element.36), calls=%async_computation | async-start | bytes 2162688 | tf_op jit(solution)/shard_map/all_to_all | solution.py:443
  12.1 1.3 copy.12
  16.2 18.1 %all-to-all-done.got_ref = bf16[16,264,128]{2,1,0:T(8,128)(2,1)S(1)} async-done(((bf16[16,264,128]{2,1,0:T(8,128)(2,1)}), bf16[16,264,128]{2,1,0:T(8,128)(2,1)S(1)}, u32[]{:S(2)}, u32[]{:S(2)}) %all-to-all-start) | async-done | bytes 1081376 | tf_op jit(solution)/shard_map/all_to_all | solution.py:443
  36.3 5.1 %collective-permute-start.1 = (bf16[256,512]{1,0:T(8,128)(2,1)S(1)}, bf16[256,512]{1,0:T(8,128)(2,1)S(1)}, u32[]{:S(2)}, u32[]{:S(2)}) collective-permute-start(bf16[256,512]{1,0:T(8,128)(2,1)S(1)} %get-tuple-element.40.far_sent_ref), channel_id=1, source_target_pairs={{0,30},{2,4},{4,2},{6,8},{8,6},{10,12},{12,10},{14,16},{16,14},{18... | collective-permute-start | bytes 786440 | tf_op jit(solution)/shard_map/ppermute | solution.py:583
  41.4 4.5 %all-to-all-start.1 = ((bf16[16,64,512]{2,1,0:T(8,128)(2,1)}), bf16[16,64,512]{2,1,0:T(8,128)(2,1)}, u32[]{:S(2)}, u32[]{:S(2)}) async-start(bf16[16,64,512]{2,1,0:T(8,128)(2,1)} %bitcast.13), calls=%async_computation.1 | async-start | bytes 2097152 | tf_op jit(solution)/shard_map/all_to_all | solution.py:443
  46.7 11.7 %shard_map.89 = (bf16[512,512]{1,0:T(8,128)(2,1)}, bf16[1024,512]{1,0:T(8,128)(2,1)}, bf16[512,1024]{1,0:T(8,128)(2,1)}, bf16[512,512]{1,0:T(8,128)(2,1)}, bf16[...) custom-call(s32[1]{0:T(128)} %bitcast.2.core_ref, f32[8,128]{1,0:T(8,128)} %copy-done.8, ...), custom_call_target="tpu_custom_call" | custom-call | flops 99999997952 | bytes 13111300 | tf_op jit(solution)/shard_map/pallas_call | solution.py:54
  58.4 10.2 %all-to-all-done.1 = bf16[16,64,512]{2,1,0:T(8,128)(2,1)} async-done(((bf16[16,64,512]{2,1,0:T(8,128)(2,1)}), bf16[16,64,512]{2,1,0:T(8,128)(2,1)}, u32[]{:S(2)}, u32[]{:S(2)}) %all-to-all-start.1) | async-done | bytes 1048608 | tf_op jit(solution)/shard_map/all_to_all | solution.py:443
  68.7 13.5 %shard_map.90 = (bf16[256,2048]{1,0:T(8,128)(2,1)}, bf16[256,2048]{1,0:T(8,128)(2,1)}, f32[512,512]{1,0:T(8,128)}, bf16[256,512]{1,0:T(8,128)(2,1)}, bf16[256,512]{1,0:T(8,128)(2,1)}) custom-call(s32[1]{0:T(128)} %bitcast.2.core_ref, f32[8,128]{1,0:T(8,128)} %copy-done.8, bf16[1024,512]{1,0:T(8,128)(2,1)} %bitcast.4.got_hbm, bf16[512,512]{1,0:T(8,128)(2,1)} %w_out_hbm.1, ...), custom_call_target="tpu_custom_call" | custom-call | flops 7247757312 | bytes 15208452 | tf_op jit(solution)/shard_map/pallas_call | solution.py:54
  82.9 2.4 %collective-permute-done.4.got_ref = bf16[256,2048]{1,0:T(8,128)(2,1)S(1)} collective-permute-done((bf16[256,2048]{1,0:T(8,128)(2,1)}, bf16[256,2048]{1,0:T(8,128)(2,1)S(1)}, u32[]{:S(2)}, u32[]{:S(2)}) %collective-permute-start.4) | collective-permute-done | bytes 1048608 | tf_op jit(solution)/shard_map/ppermute | solution.py:448
  87.4 2.0 %collective-permute-start.5 = (bf16[64,2048]{1,0:T(8,128)(2,1)S(1)}, bf16[64,2048]{1,0:T(8,128)(2,1)S(1)}, u32[]{:S(2)}, u32[]{:S(2)}) collective-permute-start(bf16[64,2048]{1,0:T(8,128)(2,1)S(1)} %get-tuple-element.55), channel_id=1, source_target_pairs={{0,4},{2,6},{4,0},{6,2},{8,12},{10,14},{12,8},{14,10},{16,20},{18,... | collective-permute-start | bytes 786440 | tf_op jit(solution)/shard_map/ppermute | solution.py:448
  89.4 1.5 collective-permute-start.6
  91.0 5.3 %collective-permute-start.3 = (bf16[256,512]{1,0:T(8,128)(2,1)}, bf16[256,512]{1,0:T(8,128)(2,1)}, u32[]{:S(2)}, u32[]{:S(2)}) collective-permute-start(bf16[256,512]{1,0:T(8,128)(2,1)} %get-tuple-element.48), channel_id=1, source_target_pairs={{0,30},{2,4},{4,2},{6,8},{8,6},{10,12},{12,10},{14,16},{16,14},{18... | collective-permute-start | bytes 786440 | tf_op jit(solution)/shard_map/ppermute | solution.py:583
  96.3 2.5 %collective-permute-done.5.refs_0_ = bf16[64,2048]{1,0:T(8,128)(2,1)S(1)} collective-permute-done((bf16[64,2048]{1,0:T(8,128)(2,1)S(1)}, bf16[64,2048]{1,0:T(8,128)(2,1)S(1)}, u32[]{:S(2)}, u32[]{:S(2)}) %collective-permute-start.5) | collective-permute-done | bytes 262176 | tf_op jit(solution)/shard_map/ppermute | solution.py:448
  99.2 6.4 %collective-permute-done.7.refs_2_ = bf16[64,2048]{1,0:T(8,128)(2,1)S(1)} collective-permute-done((bf16[64,2048]{1,0:T(8,128)(2,1)S(1)}, bf16[64,2048]{1,0:T(8,128)(2,1)S(1)}, u32[]{:S(2)}, u32[]{:S(2)}) %collective-permute-start.7) | collective-permute-done | bytes 262176 | tf_op jit(solution)/shard_map/ppermute | solution.py:516
  105.9 3.2 %collective-permute-start.8 = (bf16[16,2048]{1,0:T(8,128)(2,1)S(1)}, bf16[16,2048]{1,0:T(8,128)(2,1)S(1)}, u32[]{:S(2)}, u32[]{:S(2)}) collective-permute-start(bf16[16,2048]{1,0:T(8,128)(2,1)S(1)} %get-tuple-element.59), channel_id=1, source_target_pairs={{0,8},{2,10},{4,12},{6,14},{8,0},{10,2},{12,4},{14,6},{16,24},{18,... | collective-permute-start | bytes 196616 | tf_op jit(solution)/shard_map/ppermute | solution.py:448
  109.0 1.3 collective-permute-start.9
  110.3 1.4 collective-permute-start.10
  112.4 3.9 %shard_map.91 = (bf16[1024,512]{1,0:T(8,128)(2,1)}, f32[8,128]{1,0:T(8,128)}) custom-call(s32[1]{0:T(128)} %bitcast.2.core_ref, bf16[256,512]{1,0:T(8,128)(2,1)} %copy-done.10, bf16[256,512]{1,0:T(8,128)(2,1)} %collective-permute-done.3.far_hbm, f32[512,512]{1,0:T(8,128)} %get-tuple-element.49.own_hbm, bf16[1024,512]{1,0:T(8,128)(2,1)} %get-tuple-element.50.table_hbm), custom_call_target="tpu_custom_call" | custom-call | flops 536870912 | bytes 3674116 | tf_op jit(solution)/shard_map/pallas_call | solution.py:54
  117.4 1.3 collective-permute-start.11
  118.8 1.6 %collective-permute-start.12 = (bf16[16,2048]{1,0:T(8,128)(2,1)S(1)}, bf16[16,2048]{1,0:T(8,128)(2,1)S(1)}, u32[]{:S(2)}, u32[]{:S(2)}) collective-permute-start(bf16[16,2048]{1,0:T(8,128)(2,1)S(1)} %shard_map.94.refs_0_), channel_id=1, source_target_pairs={{0,16},{2,18},{4,20},{6,22},{8,24},{10,26},{12,28},{14,30},{16,0},... | collective-permute-start | bytes 196616 | tf_op jit(solution)/shard_map/ppermute | solution.py:448
  120.4 1.5 collective-permute-start.13
  121.9 3.2 %collective-permute-done.12.refs_2_ = bf16[16,2048]{1,0:T(8,128)(2,1)S(1)} collective-permute-done((bf16[16,2048]{1,0:T(8,128)(2,1)S(1)}, bf16[16,2048]{1,0:T(8,128)(2,1)S(1)}, u32[]{:S(2)}, u32[]{:S(2)}) %collective-permute-start.12) | collective-permute-done | bytes 65568 | tf_op jit(solution)/shard_map/ppermute | solution.py:448
  125.1 1.4 collective-permute-done.13.refs_3_
  127.3 1.9 %collective-permute-start.14 = (bf16[64,2048]{1,0:T(8,128)(2,1)}, bf16[64,2048]{1,0:T(8,128)(2,1)S(1)}, u32[]{:S(2)}, u32[]{:S(2)}) collective-permute-start(bf16[64,2048]{1,0:T(8,128)(2,1)} %shard_map.95.refs_1_.refs_0_), channel_id=1, source_target_pairs={{0,4},{2,6},{4,0},{6,2},{8,12},{10,14},{12,8},{14,10},{16,20},{18,... | collective-permute-start | bytes 786440 | tf_op jit(solution)/shard_map/ppermute | solution.py:448
  129.1 3.7 %all-to-all-start.2 = ((bf16[16,64,512]{2,1,0:T(8,128)(2,1)}), bf16[16,64,512]{2,1,0:T(8,128)(2,1)S(1)}, u32[]{:S(2)}, u32[]{:S(2)}) async-start(bf16[16,64,512]{2,1,0:T(8,128)(2,1)} %bitcast.15), calls=%async_computation.2 | async-start | bytes 2097152 | tf_op jit(solution)/shard_map/all_to_all | solution.py:443
  135.4 6.8 %collective-permute-done.15.refs_2_ = bf16[64,2048]{1,0:T(8,128)(2,1)S(1)} collective-permute-done((bf16[64,2048]{1,0:T(8,128)(2,1)}, bf16[64,2048]{1,0:T(8,128)(2,1)S(1)}, u32[]{:S(2)}, u32[]{:S(2)}) %collective-permute-start.15) | collective-permute-done | bytes 262176 | tf_op jit(solution)/shard_map/ppermute | solution.py:448
  142.2 4.9 %collective-permute-done.16.refs_3_ = bf16[64,2048]{1,0:T(8,128)(2,1)S(1)} collective-permute-done((bf16[64,2048]{1,0:T(8,128)(2,1)S(1)}, bf16[64,2048]{1,0:T(8,128)(2,1)S(1)}, u32[]{:S(2)}, u32[]{:S(2)}) %collective-permute-start.16) | collective-permute-done | bytes 262176 | tf_op jit(solution)/shard_map/ppermute | solution.py:448
  147.2 1.4 collective-permute-done.20.refs_7_
  148.6 3.2 %shard_map.98 = (f32[512,1536]{1,0:T(8,128)}, f32[512,512]{1,0:T(8,128)}) custom-call(s32[4]{0:T(128)S(1)} %pad_add_fusion.1.place_ref, bf16[64,2048]{1,0:T(8,128)(2,1)} %shard_map.95.refs_1_.refs_0_, bf16[64,2048]{1,0:T(8,128)(2,1)S(1)} %collective-permute-done.14.refs_1_, bf16[64,2048]{1,0:T(8,128)(2,1)S(1)} %collective-permute-done.15.refs_2_, ...), custom_call_target="tpu_custom_call" | custom-call | flops 12999999488 | bytes 6291472 | tf_op jit(solution)/shard_map/pallas_call | solution.py:54
  151.9 3.8 %all-to-all-done.2 = bf16[16,64,512]{2,1,0:T(8,128)(2,1)S(1)} async-done(((bf16[16,64,512]{2,1,0:T(8,128)(2,1)}), bf16[16,64,512]{2,1,0:T(8,128)(2,1)S(1)}, u32[]{:S(2)}, u32[]{:S(2)}) %all-to-all-start.2) | async-done | bytes 1048608 | tf_op jit(solution)/shard_map/all_to_all | solution.py:443
  155.7 1.5 shard_map.97
  (61 shorter events, 15.5 us)
Async XLA Ops:
  3.4 30.9 %all-to-all-start = ((bf16[16,264,128]{2,1,0:T(8,128)(2,1)}), bf16[16,264,128]{2,1,0:T(8,128)(2,1)S(1)}, u32[]{:S(2)}, u32[]{:S(2)}) async-start(bf16[16,264,128]{2,1,0:T(8,128)(2,1)} %get-tuple-element.36), calls=%async_computation | async-start | bytes 2162688 | tf_op jit(solution)/shard_map/all_to_all | solution.py:443
  10.8 1.2 slice-start
  12.1 1.3 copy-start.5
  12.1 1.3 copy-start.9
  14.2 1.0 copy-start.1
  35.6 5.8 %copy-start.6 = (bf16[256,512]{1,0:T(8,128)(2,1)}, bf16[256,512]{1,0:T(8,128)(2,1)S(1)}, u32[]{:S(2)}) copy-start(bf16[256,512]{1,0:T(8,128)(2,1)S(1)} %get-tuple-element.39.near_sent_ref) | copy-start | bytes 786436
  35.6 5.8 %copy-start.7 = (bf16[256,512]{1,0:T(8,128)(2,1)}, bf16[256,512]{1,0:T(8,128)(2,1)S(1)}, u32[]{:S(2)}) copy-start(bf16[256,512]{1,0:T(8,128)(2,1)S(1)} %get-tuple-element.40.far_sent_ref) | copy-start | bytes 786436
  35.6 10.3 %collective-permute-start = (bf16[256,512]{1,0:T(8,128)(2,1)S(1)}, bf16[256,512]{1,0:T(8,128)(2,1)S(1)}, u32[]{:S(2)}, u32[]{:S(2)}) collective-permute-start(bf16[256,512]{1,0:T(8,128)(2,1)S(1)} %get-tuple-element.39.near_sent_ref), channel_id=1, source_target_pairs={{0,2},{2,0},{4,6},{6,4},{8,10},{10,8},{12,14},{14,12},{16,18},{18,... | collective-permute-start | bytes 786440 | tf_op jit(solution)/shard_map/ppermute | solution.py:448
  36.3 9.6 %collective-permute-start.1 = (bf16[256,512]{1,0:T(8,128)(2,1)S(1)}, bf16[256,512]{1,0:T(8,128)(2,1)S(1)}, u32[]{:S(2)}, u32[]{:S(2)}) collective-permute-start(bf16[256,512]{1,0:T(8,128)(2,1)S(1)} %get-tuple-element.40.far_sent_ref), channel_id=1, source_target_pairs={{0,30},{2,4},{4,2},{6,8},{8,6},{10,12},{12,10},{14,16},{16,14},{18... | collective-permute-start | bytes 786440 | tf_op jit(solution)/shard_map/ppermute | solution.py:583
  41.4 27.3 %all-to-all-start.1 = ((bf16[16,64,512]{2,1,0:T(8,128)(2,1)}), bf16[16,64,512]{2,1,0:T(8,128)(2,1)}, u32[]{:S(2)}, u32[]{:S(2)}) async-start(bf16[16,64,512]{2,1,0:T(8,128)(2,1)} %bitcast.13), calls=%async_computation.1 | async-start | bytes 2097152 | tf_op jit(solution)/shard_map/all_to_all | solution.py:443
  82.2 3.1 %collective-permute-start.4 = (bf16[256,2048]{1,0:T(8,128)(2,1)}, bf16[256,2048]{1,0:T(8,128)(2,1)S(1)}, u32[]{:S(2)}, u32[]{:S(2)}) collective-permute-start(bf16[256,2048]{1,0:T(8,128)(2,1)} %get-tuple-element.53), channel_id=1, source_target_pairs={{0,2},{2,0},{4,6},{6,4},{8,10},{10,8},{12,14},{14,12},{16,18},{18,... | collective-permute-start | bytes 3145736 | tf_op jit(solution)/shard_map/ppermute | solution.py:448
  85.4 1.2 copy-start
  87.4 11.4 %collective-permute-start.5 = (bf16[64,2048]{1,0:T(8,128)(2,1)S(1)}, bf16[64,2048]{1,0:T(8,128)(2,1)S(1)}, u32[]{:S(2)}, u32[]{:S(2)}) collective-permute-start(bf16[64,2048]{1,0:T(8,128)(2,1)S(1)} %get-tuple-element.55), channel_id=1, source_target_pairs={{0,4},{2,6},{4,0},{6,2},{8,12},{10,14},{12,8},{14,10},{16,20},{18,... | collective-permute-start | bytes 786440 | tf_op jit(solution)/shard_map/ppermute | solution.py:448
  89.4 9.8 %collective-permute-start.6 = (bf16[64,2048]{1,0:T(8,128)(2,1)S(1)}, bf16[64,2048]{1,0:T(8,128)(2,1)S(1)}, u32[]{:S(2)}, u32[]{:S(2)}) collective-permute-start(bf16[64,2048]{1,0:T(8,128)(2,1)S(1)} %get-tuple-element.56), channel_id=1, source_target_pairs={{0,1},{1,0},{2,3},{3,2},{4,5},{5,4},{6,7},{7,6},{8,9},{9,8},{10,11... | collective-permute-start | bytes 786440 | tf_op jit(solution)/shard_map/ppermute | solution.py:448
  90.9 14.7 %collective-permute-start.7 = (bf16[64,2048]{1,0:T(8,128)(2,1)S(1)}, bf16[64,2048]{1,0:T(8,128)(2,1)S(1)}, u32[]{:S(2)}, u32[]{:S(2)}) collective-permute-start(bf16[64,2048]{1,0:T(8,128)(2,1)S(1)} %get-tuple-element.57), channel_id=1, source_target_pairs={{0,5},{1,4},{2,7},{3,6},{4,1},{5,0},{6,3},{7,2},{8,13},{9,12},{10,... | collective-permute-start | bytes 786440 | tf_op jit(solution)/shard_map/ppermute | solution.py:516
  91.0 20.8 %collective-permute-start.2 = (bf16[256,512]{1,0:T(8,128)(2,1)}, bf16[256,512]{1,0:T(8,128)(2,1)S(1)}, u32[]{:S(2)}, u32[]{:S(2)}) collective-permute-start(bf16[256,512]{1,0:T(8,128)(2,1)} %get-tuple-element.47), channel_id=1, source_target_pairs={{0,2},{2,0},{4,6},{6,4},{8,10},{10,8},{12,14},{14,12},{16,18},{18,... | collective-permute-start | bytes 786440 | tf_op jit(solution)/shard_map/ppermute | solution.py:448
  91.0 20.8 %collective-permute-start.3 = (bf16[256,512]{1,0:T(8,128)(2,1)}, bf16[256,512]{1,0:T(8,128)(2,1)}, u32[]{:S(2)}, u32[]{:S(2)}) collective-permute-start(bf16[256,512]{1,0:T(8,128)(2,1)} %get-tuple-element.48), channel_id=1, source_target_pairs={{0,30},{2,4},{4,2},{6,8},{8,6},{10,12},{12,10},{14,16},{16,14},{18... | collective-permute-start | bytes 786440 | tf_op jit(solution)/shard_map/ppermute | solution.py:583
  105.9 10.4 %collective-permute-start.8 = (bf16[16,2048]{1,0:T(8,128)(2,1)S(1)}, bf16[16,2048]{1,0:T(8,128)(2,1)S(1)}, u32[]{:S(2)}, u32[]{:S(2)}) collective-permute-start(bf16[16,2048]{1,0:T(8,128)(2,1)S(1)} %get-tuple-element.59), channel_id=1, source_target_pairs={{0,8},{2,10},{4,12},{6,14},{8,0},{10,2},{12,4},{14,6},{16,24},{18,... | collective-permute-start | bytes 196616 | tf_op jit(solution)/shard_map/ppermute | solution.py:448
  109.0 7.7 %collective-permute-start.9 = (bf16[16,2048]{1,0:T(8,128)(2,1)S(1)}, bf16[16,2048]{1,0:T(8,128)(2,1)S(1)}, u32[]{:S(2)}, u32[]{:S(2)}) collective-permute-start(bf16[16,2048]{1,0:T(8,128)(2,1)S(1)} %get-tuple-element.60), channel_id=1, source_target_pairs={{0,16},{2,18},{4,20},{6,22},{8,24},{10,26},{12,28},{14,30},{16,0},... | collective-permute-start | bytes 196616 | tf_op jit(solution)/shard_map/ppermute | solution.py:448
  110.3 6.4 %collective-permute-start.10 = (bf16[16,2048]{1,0:T(8,128)(2,1)S(1)}, bf16[16,2048]{1,0:T(8,128)(2,1)S(1)}, u32[]{:S(2)}, u32[]{:S(2)}) collective-permute-start(bf16[16,2048]{1,0:T(8,128)(2,1)S(1)} %get-tuple-element.61), channel_id=1, source_target_pairs={{0,24},{2,26},{4,28},{6,30},{8,16},{10,18},{12,20},{14,22},{16,8},... | collective-permute-start | bytes 196616 | tf_op jit(solution)/shard_map/ppermute | solution.py:448
  117.4 4.5 %collective-permute-start.11 = (bf16[16,2048]{1,0:T(8,128)(2,1)S(1)}, bf16[16,2048]{1,0:T(8,128)(2,1)S(1)}, u32[]{:S(2)}, u32[]{:S(2)}) collective-permute-start(bf16[16,2048]{1,0:T(8,128)(2,1)S(1)} %shard_map.94.refs_0_), channel_id=1, source_target_pairs={{0,8},{2,10},{4,12},{6,14},{8,0},{10,2},{12,4},{14,6},{16,24},{18,... | collective-permute-start | bytes 196616 | tf_op jit(solution)/shard_map/ppermute | solution.py:448
  118.8 6.4 %collective-permute-start.12 = (bf16[16,2048]{1,0:T(8,128)(2,1)S(1)}, bf16[16,2048]{1,0:T(8,128)(2,1)S(1)}, u32[]{:S(2)}, u32[]{:S(2)}) collective-permute-start(bf16[16,2048]{1,0:T(8,128)(2,1)S(1)} %shard_map.94.refs_0_), channel_id=1, source_target_pairs={{0,16},{2,18},{4,20},{6,22},{8,24},{10,26},{12,28},{14,30},{16,0},... | collective-permute-start | bytes 196616 | tf_op jit(solution)/shard_map/ppermute | solution.py:448
  120.4 6.1 %collective-permute-start.13 = (bf16[16,2048]{1,0:T(8,128)(2,1)S(1)}, bf16[16,2048]{1,0:T(8,128)(2,1)S(1)}, u32[]{:S(2)}, u32[]{:S(2)}) collective-permute-start(bf16[16,2048]{1,0:T(8,128)(2,1)S(1)} %shard_map.94.refs_0_), channel_id=1, source_target_pairs={{0,24},{2,26},{4,28},{6,30},{8,16},{10,18},{12,20},{14,22},{16,8},... | collective-permute-start | bytes 196616 | tf_op jit(solution)/shard_map/ppermute | solution.py:448
  127.3 6.6 %collective-permute-start.14 = (bf16[64,2048]{1,0:T(8,128)(2,1)}, bf16[64,2048]{1,0:T(8,128)(2,1)S(1)}, u32[]{:S(2)}, u32[]{:S(2)}) collective-permute-start(bf16[64,2048]{1,0:T(8,128)(2,1)} %shard_map.95.refs_1_.refs_0_), channel_id=1, source_target_pairs={{0,4},{2,6},{4,0},{6,2},{8,12},{10,14},{12,8},{14,10},{16,20},{18,... | collective-permute-start | bytes 786440 | tf_op jit(solution)/shard_map/ppermute | solution.py:448
  129.1 26.6 %all-to-all-start.2 = ((bf16[16,64,512]{2,1,0:T(8,128)(2,1)}), bf16[16,64,512]{2,1,0:T(8,128)(2,1)S(1)}, u32[]{:S(2)}, u32[]{:S(2)}) async-start(bf16[16,64,512]{2,1,0:T(8,128)(2,1)} %bitcast.15), calls=%async_computation.2 | async-start | bytes 2097152 | tf_op jit(solution)/shard_map/all_to_all | solution.py:443
  132.8 9.4 %collective-permute-start.15 = (bf16[64,2048]{1,0:T(8,128)(2,1)}, bf16[64,2048]{1,0:T(8,128)(2,1)S(1)}, u32[]{:S(2)}, u32[]{:S(2)}) collective-permute-start(bf16[64,2048]{1,0:T(8,128)(2,1)} %shard_map.95.refs_1_.refs_0_), channel_id=1, source_target_pairs={{0,1},{1,0},{2,3},{3,2},{4,5},{5,4},{6,7},{7,6},{8,9},{9,8},{10,11... | collective-permute-start | bytes 786440 | tf_op jit(solution)/shard_map/ppermute | solution.py:448
  133.8 13.3 %collective-permute-start.16 = (bf16[64,2048]{1,0:T(8,128)(2,1)S(1)}, bf16[64,2048]{1,0:T(8,128)(2,1)S(1)}, u32[]{:S(2)}, u32[]{:S(2)}) collective-permute-start(bf16[64,2048]{1,0:T(8,128)(2,1)S(1)} %collective-permute-done.14.refs_1_), channel_id=1, source_target_pairs={{0,1},{1,0},{2,3},{3,2},{4,5},{5,4},{6,7},{7,6},{8,9},{9,8},{10,11... | collective-permute-start | bytes 786440 | tf_op jit(solution)/shard_map/ppermute | solution.py:448
  134.9 12.3 %collective-permute-start.17 = (bf16[64,2048]{1,0:T(8,128)(2,1)}, bf16[64,2048]{1,0:T(8,128)(2,1)S(1)}, u32[]{:S(2)}, u32[]{:S(2)}) collective-permute-start(bf16[64,2048]{1,0:T(8,128)(2,1)} %shard_map.95.refs_1_.refs_0_), channel_id=1, source_target_pairs={{0,2},{2,0},{4,6},{6,4},{8,10},{10,8},{12,14},{14,12},{16,18},{18,... | collective-permute-start | bytes 786440 | tf_op jit(solution)/shard_map/ppermute | solution.py:448
  134.9 12.3 %collective-permute-start.18 = (bf16[64,2048]{1,0:T(8,128)(2,1)S(1)}, bf16[64,2048]{1,0:T(8,128)(2,1)S(1)}, u32[]{:S(2)}, u32[]{:S(2)}) collective-permute-start(bf16[64,2048]{1,0:T(8,128)(2,1)S(1)} %collective-permute-done.14.refs_1_), channel_id=1, source_target_pairs={{0,2},{2,0},{4,6},{6,4},{8,10},{10,8},{12,14},{14,12},{16,18},{18,... | collective-permute-start | bytes 786440 | tf_op jit(solution)/shard_map/ppermute | solution.py:448
  142.2 5.0 %collective-permute-start.19 = (bf16[64,2048]{1,0:T(8,128)(2,1)S(1)}, bf16[64,2048]{1,0:T(8,128)(2,1)S(1)}, u32[]{:S(2)}, u32[]{:S(2)}) collective-permute-start(bf16[64,2048]{1,0:T(8,128)(2,1)S(1)} %collective-permute-done.15.refs_2_), channel_id=1, source_target_pairs={{0,2},{2,0},{4,6},{6,4},{8,10},{10,8},{12,14},{14,12},{16,18},{18,... | collective-permute-start | bytes 786440 | tf_op jit(solution)/shard_map/ppermute | solution.py:448
  147.1 1.5 collective-permute-start.20
  147.2 8.5 %copy-start.2 = (bf16[512,1024]{1,0:T(8,128)(2,1)S(1)}, bf16[512,1024]{1,0:T(8,128)(2,1)}, u32[]{:S(2)}) copy-start(bf16[512,1024]{1,0:T(8,128)(2,1)} %copy-done.1) | copy-start | bytes 3145732
  (6 other events, 4.4 us)

commit v7 on v6

--- a/solution.py
+++ b/solution.py
@@ -472,7 +472,7 @@
 
 
 def second_sum_kernel(line_ref, kept_ref, *refs):
-    got, mine_ref, sends, total_ref = (refs[:3], refs[3], refs[4:-1], refs[-1])
+    got, mine_ref, sends, total_ref = (refs[:3], refs[4], refs[5:-1], refs[-1])
     rows = mine_ref.shape[0]
     total = kept_ref[...]
     for ref in got:
@@ -484,7 +484,7 @@
 
 
 def third_sum_kernel(mine_ref, *refs):
-    others, out_ref = (refs[:-2], refs[-1])
+    others, out_ref = (refs[:-1], refs[-1])
     total = mine_ref[...]
     for other in others:
         total = total + other[...].astype(jnp.float32)
@@ -516,9 +516,7 @@
     return lax.ppermute(block, ("curve", "dp"), route)
 
 
-def sum_start(keep, send, sides):
-    n_line = lax.axis_size("curve") // 4
-    line = lax.axis_index("curve") >> 2
+def sum_core(keep, send, sides):
     rows, width = keep.shape
     rows = rows // 4
     kept, send_x, send_y, send_xy = call(
@@ -528,15 +526,21 @@
         4 * rows * width,
         [SMEM, VMEM, VMEM],
     )
-    got = [swap(send_x, "curve", 2), swap(send_y, "dp", 1), swap_across(send_xy)]
+    return (kept, [swap_across(send_xy), swap(send_x, "curve", 2), swap(send_y, "dp", 1)])
+
+
+def sum_xy(kept, got, ready):
+    n_line = lax.axis_size("curve") // 4
+    line = lax.axis_index("curve") >> 2
+    rows, width = kept.shape
     rows = rows // n_line
     if rows % 16 == 0:
         mine, *sends = call(
             second_sum_kernel,
             [wide(rows, width)] + [low(rows, width)] * (n_line - 1),
-            [line.reshape(1), kept, *got],
+            [line.reshape(1), kept, *got, ready],
             kept.size,
-            [SMEM] + [VMEM] * 4,
+            [SMEM] + [VMEM] * 5,
             scratch=[space(kept)],
         )
         return (mine, sends)
@@ -548,13 +552,14 @@
     return (mine, [block.astype(jnp.bfloat16) for block in sends])
 
 
-def sum_line(mine, sends, ready):
+def sum_line(mine, sends):
     n_line = len(sends) + 1
     line = lax.axis_index("curve") >> 2
     rows, width = mine.shape
-    others = [swap(block, "curve", 4 * (k + 1)) for k, block in enumerate(sends)]
-    (mine,) = call(third_sum_kernel, [low(rows, width)], [mine, *others, ready], mine.size)
-    blocks = [mine] + [swap(mine, "curve", 4 * k) for k in range(1, n_line)]
+    others = [swap(sends[k - 1], "curve", 4 * k) for k in range(n_line - 1, 0, -1)]
+    (mine,) = call(third_sum_kernel, [low(rows, width)], [mine, *others], mine.size)
+    blocks = [swap(mine, "curve", 4 * k) for k in range(n_line - 1, 0, -1)]
+    blocks = [mine] + blocks[::-1]
     if rows % 16 == 0:
         (own,) = call(join_kernel, [low(n_line * rows, width)], blocks, mine.size)
         return (own, line, n_line)
@@ -663,7 +668,7 @@
         + [pltpu.SemaphoreType.DMA((13 + HEADS,))],
         63,
     )
-    mine, sends = sum_start(keep, send, sides)
+    kept, got = sum_core(keep, send, sides)
     near, far = halo(near, far)
     picked = low(total, width)
     picked, done = call(
@@ -676,7 +681,8 @@
         [space(x) for x in (near, far, own_input, pick_table, picked)] + [pltpu.SemaphoreType.DMA((8,))],
         63,
     )
-    gathered, line, n_line = sum_line(mine, sends, done)
+    mine, sends = sum_xy(kept, got, done)
+    gathered, line, n_line = sum_line(mine, sends)
     picked = gate(picked, gathered, flops=GATE_FLOPS)
     returned = exchange(picked.reshape(n_dev, cap, width)).reshape(total, width)
     weight_qkv, weight_out = sum_finish(gathered, line, n_line, sides, 3 * width)

time: 159 us -> 159 us (level)
  starting transfers between devices: 45.1 us -> 42.6 us
  Pallas kernels: 39.9 us -> 41.6 us
    ppermute x18, waiting for transfers between devices: 24.1 us -> 28.6 us  [swap(): return lax.ppermute(block, axis, [(i, i ^ mask) for i in range(size)])]
    ppermute x18, starting transfers between devices: 19.2 us -> 15.6 us  [swap(): return lax.ppermute(block, axis, [(i, i ^ mask) for i in range(size)])]
    ppermute x1, waiting for transfers between devices: 6.44 us -> 3.04 us  [swap_across(): return lax.ppermute(block, ('curve', 'dp'), route)]
    pallas_call x12, Pallas kernels: 39.9 us -> 41.6 us  [call(): pl.pallas_call(kernel, out_shape=outs, in_specs=ins or [VMEM] * len(args)...]
    unnamed x27 -> x25, local copies, waits for them, and re-layouts: 7.26 us -> 6.55 us
where the time goes in v7:
time: 159 us; the launch traced here: 157 us
  waiting for transfers between devices  63.8 us (40%)
  starting transfers between devices  42.6 us (27%)
  Pallas kernels  41.6 us (26%)
  local copies, waits for them, and re-layouts  7.77 us (5%)
    pallas_call x12, Pallas kernels, call(): pl.pallas_call(kernel, out_shape=outs, in_specs=ins or [VMEM] * len(args)...  41.6 us
    all_to_all x3, waiting for transfers between devices, exchange(): lax.all_to_all(blocks, 'curve', split_axis=0, concat_axis=0, tiled=True)  32.1 us
    ppermute x18, waiting for transfers between devices, swap(): return lax.ppermute(block, axis, [(i, i ^ mask) for i in range(size)])  28.6 us
    all_to_all x3, starting transfers between devices, exchange(): lax.all_to_all(blocks, 'curve', split_axis=0, concat_axis=0, tiled=True)  16.2 us
    ppermute x18, starting transfers between devices, swap(): return lax.ppermute(block, axis, [(i, i ^ mask) for i in range(size)])  15.6 us
    ppermute x2, starting transfers between devices, halo(): return (swap(near, 'curve', 1), lax.ppermute(far, 'curve', route))  10.2 us
    unnamed x25, local copies, waits for them, and re-layouts  6.55 us
  transfers between devices with their start and end apart: 24, of which 14 were waited for; matrix products, arithmetic and copies ran while one was open for 1% of the time, Pallas kernels for 13%

profile of v7, /device:TPU:0, one launch (start us, length us, event | category | flops | bytes accessed | tf_op | source)
XLA Modules:
  0.0 156.7 jit_solution(5892596287496498867)
XLA Ops:
  0.6 2.8 %shard_map.85 = (bf16[16,264,128]{2,1,0:T(8,128)(2,1)}, s32[1,512]{1,0:T(1,128)}) custom-call(s32[1,512]{1,0:T(1,128)} %dev_hbm.1, s32[1,512]{1,0:T(1,128)} %row_hbm.1, bf16[512,512]{1,0:T(8,128)(2,1)} %bitcast.18), custom_call_target="tpu_custom_call" | custom-call | flops 536870912 | bytes 1611776 | tf_op jit(solution)/shard_map/pallas_call | solution.py:54
  3.4 7.4 %all-to-all-start = ((bf16[16,264,128]{2,1,0:T(8,128)(2,1)}), bf16[16,264,128]{2,1,0:T(8,128)(2,1)S(1)}, u32[]{:S(2)}, u32[]{:S(2)}) async-start(bf16[16,264,128]{2,1,0:T(8,128)(2,1)} %get-tuple-element.36), calls=%async_computation | async-start | bytes 2162688 | tf_op jit(solution)/shard_map/all_to_all | solution.py:443
  10.8 1.2 slice-done
  12.1 1.3 copy.12
  16.2 18.2 %all-to-all-done.got_ref = bf16[16,264,128]{2,1,0:T(8,128)(2,1)S(1)} async-done(((bf16[16,264,128]{2,1,0:T(8,128)(2,1)}), bf16[16,264,128]{2,1,0:T(8,128)(2,1)S(1)}, u32[]{:S(2)}, u32[]{:S(2)}) %all-to-all-start) | async-done | bytes 1081376 | tf_op jit(solution)/shard_map/all_to_all | solution.py:443
  36.3 5.1 %collective-permute-start.1 = (bf16[256,512]{1,0:T(8,128)(2,1)S(1)}, bf16[256,512]{1,0:T(8,128)(2,1)S(1)}, u32[]{:S(2)}, u32[]{:S(2)}) collective-permute-start(bf16[256,512]{1,0:T(8,128)(2,1)S(1)} %get-tuple-element.40.far_sent_ref), channel_id=1, source_target_pairs={{0,30},{2,4},{4,2},{6,8},{8,6},{10,12},{12,10},{14,16},{16,14},{18... | collective-permute-start | bytes 786440 | tf_op jit(solution)/shard_map/ppermute | solution.py:588
  41.4 4.5 %all-to-all-start.1 = ((bf16[16,64,512]{2,1,0:T(8,128)(2,1)}), bf16[16,64,512]{2,1,0:T(8,128)(2,1)}, u32[]{:S(2)}, u32[]{:S(2)}) async-start(bf16[16,64,512]{2,1,0:T(8,128)(2,1)} %bitcast.13), calls=%async_computation.1 | async-start | bytes 2097152 | tf_op jit(solution)/shard_map/all_to_all | solution.py:443
  46.7 11.7 %shard_map.89 = (bf16[512,512]{1,0:T(8,128)(2,1)}, bf16[1024,512]{1,0:T(8,128)(2,1)}, bf16[512,1024]{1,0:T(8,128)(2,1)}, bf16[512,512]{1,0:T(8,128)(2,1)}, bf16[...) custom-call(s32[1]{0:T(128)} %bitcast.2.core_ref, f32[8,128]{1,0:T(8,128)} %copy-done.8, ...), custom_call_target="tpu_custom_call" | custom-call | flops 99999997952 | bytes 13111300 | tf_op jit(solution)/shard_map/pallas_call | solution.py:54
  58.4 10.3 %all-to-all-done.1 = bf16[16,64,512]{2,1,0:T(8,128)(2,1)} async-done(((bf16[16,64,512]{2,1,0:T(8,128)(2,1)}), bf16[16,64,512]{2,1,0:T(8,128)(2,1)}, u32[]{:S(2)}, u32[]{:S(2)}) %all-to-all-start.1) | async-done | bytes 1048608 | tf_op jit(solution)/shard_map/all_to_all | solution.py:443
  68.7 13.5 %shard_map.90 = (bf16[256,2048]{1,0:T(8,128)(2,1)}, bf16[256,2048]{1,0:T(8,128)(2,1)}, f32[512,512]{1,0:T(8,128)}, bf16[256,512]{1,0:T(8,128)(2,1)}, bf16[256,512]{1,0:T(8,128)(2,1)}) custom-call(s32[1]{0:T(128)} %bitcast.2.core_ref, f32[8,128]{1,0:T(8,128)} %copy-done.8, bf16[1024,512]{1,0:T(8,128)(2,1)} %bitcast.4.got_hbm, bf16[512,512]{1,0:T(8,128)(2,1)} %w_out_hbm.1, ...), custom_call_target="tpu_custom_call" | custom-call | flops 7247757312 | bytes 15208452 | tf_op jit(solution)/shard_map/pallas_call | solution.py:54
  82.9 5.2 %collective-permute-start.3 = (bf16[256,512]{1,0:T(8,128)(2,1)}, bf16[256,512]{1,0:T(8,128)(2,1)}, u32[]{:S(2)}, u32[]{:S(2)}) collective-permute-start(bf16[256,512]{1,0:T(8,128)(2,1)} %get-tuple-element.48), channel_id=1, source_target_pairs={{0,30},{2,4},{4,2},{6,8},{8,6},{10,12},{12,10},{14,16},{16,14},{18... | collective-permute-start | bytes 786440 | tf_op jit(solution)/shard_map/ppermute | solution.py:588
  88.2 1.2 copy-done
  89.4 1.5 shard_map.92
  91.4 2.5 %collective-permute-start.6 = (bf16[64,2048]{1,0:T(8,128)(2,1)}, bf16[64,2048]{1,0:T(8,128)(2,1)}, u32[]{:S(2)}, u32[]{:S(2)}) collective-permute-start(bf16[64,2048]{1,0:T(8,128)(2,1)} %get-tuple-element.56), channel_id=1, source_target_pairs={{0,4},{2,6},{4,0},{6,2},{8,12},{10,14},{12,8},{14,10},{16,20},{18,... | collective-permute-start | bytes 786440 | tf_op jit(solution)/shard_map/ppermute | solution.py:448
  94.4 3.9 %shard_map.91 = (bf16[1024,512]{1,0:T(8,128)(2,1)}, f32[8,128]{1,0:T(8,128)}) custom-call(s32[1]{0:T(128)} %bitcast.2.core_ref, bf16[256,512]{1,0:T(8,128)(2,1)} %collective-permute-done.2.near_hbm, bf16[256,512]{1,0:T(8,128)(2,1)} %collective-permute-done.3.far_hbm, f32[512,512]{1,0:T(8,128)} %get-tuple-element.49.own_hbm, ...), custom_call_target="tpu_custom_call" | custom-call | flops 536870912 | bytes 3674116 | tf_op jit(solution)/shard_map/pallas_call | solution.py:54
  98.3 3.0 %collective-permute-done.5.refs_0_ = bf16[64,2048]{1,0:T(8,128)(2,1)S(1)} collective-permute-done((bf16[64,2048]{1,0:T(8,128)(2,1)}, bf16[64,2048]{1,0:T(8,128)(2,1)S(1)}, u32[]{:S(2)}, u32[]{:S(2)}) %collective-permute-start.5) | collective-permute-done | bytes 262176 | tf_op jit(solution)/shard_map/ppermute | solution.py:516
  101.3 2.7 %collective-permute-done.6.refs_1_ = bf16[64,2048]{1,0:T(8,128)(2,1)} collective-permute-done((bf16[64,2048]{1,0:T(8,128)(2,1)}, bf16[64,2048]{1,0:T(8,128)(2,1)}, u32[]{:S(2)}, u32[]{:S(2)}) %collective-permute-start.6) | collective-permute-done | bytes 262176 | tf_op jit(solution)/shard_map/ppermute | solution.py:448
  105.3 1.2 shard_map.93
  106.6 3.6 %collective-permute-start.8 = (bf16[16,2048]{1,0:T(8,128)(2,1)S(1)}, bf16[16,2048]{1,0:T(8,128)(2,1)S(1)}, u32[]{:S(2)}, u32[]{:S(2)}) collective-permute-start(bf16[16,2048]{1,0:T(8,128)(2,1)S(1)} %get-tuple-element.60), channel_id=1, source_target_pairs={{0,24},{2,26},{4,28},{6,30},{8,16},{10,18},{12,20},{14,22},{16,8},... | collective-permute-start | bytes 196616 | tf_op jit(solution)/shard_map/ppermute | solution.py:448
  110.2 1.2 collective-permute-start.9
  112.8 4.1 %collective-permute-done.9.refs_1_ = bf16[16,2048]{1,0:T(8,128)(2,1)S(1)} collective-permute-done((bf16[16,2048]{1,0:T(8,128)(2,1)S(1)}, bf16[16,2048]{1,0:T(8,128)(2,1)S(1)}, u32[]{:S(2)}, u32[]{:S(2)}) %collective-permute-start.9) | collective-permute-done | bytes 65568 | tf_op jit(solution)/shard_map/ppermute | solution.py:448
  117.5 3.4 %collective-permute-start.12 = (bf16[16,2048]{1,0:T(8,128)(2,1)S(1)}, bf16[16,2048]{1,0:T(8,128)(2,1)S(1)}, u32[]{:S(2)}, u32[]{:S(2)}) collective-permute-start(bf16[16,2048]{1,0:T(8,128)(2,1)S(1)} %shard_map.94.refs_0_), channel_id=1, source_target_pairs={{0,16},{2,18},{4,20},{6,22},{8,24},{10,26},{12,28},{14,30},{16,0},... | collective-permute-start | bytes 196616 | tf_op jit(solution)/shard_map/ppermute | solution.py:448
  121.4 4.1 %collective-permute-done.12.refs_2_ = bf16[16,2048]{1,0:T(8,128)(2,1)S(1)} collective-permute-done((bf16[16,2048]{1,0:T(8,128)(2,1)S(1)}, bf16[16,2048]{1,0:T(8,128)(2,1)S(1)}, u32[]{:S(2)}, u32[]{:S(2)}) %collective-permute-start.12) | collective-permute-done | bytes 65568 | tf_op jit(solution)/shard_map/ppermute | solution.py:448
  125.5 1.5 collective-permute-done.13.refs_3_
  127.9 4.3 %all-to-all-start.2 = ((bf16[16,64,512]{2,1,0:T(8,128)(2,1)}), bf16[16,64,512]{2,1,0:T(8,128)(2,1)S(1)}, u32[]{:S(2)}, u32[]{:S(2)}) async-start(bf16[16,64,512]{2,1,0:T(8,128)(2,1)} %bitcast.15), calls=%async_computation.2 | async-start | bytes 2097152 | tf_op jit(solution)/shard_map/all_to_all | solution.py:443
  132.7 1.6 %collective-permute-done.14.refs_1_ = bf16[64,2048]{1,0:T(8,128)(2,1)S(1)} collective-permute-done((bf16[64,2048]{1,0:T(8,128)(2,1)}, bf16[64,2048]{1,0:T(8,128)(2,1)S(1)}, u32[]{:S(2)}, u32[]{:S(2)}) %collective-permute-start.14) | collective-permute-done | bytes 262176 | tf_op jit(solution)/shard_map/ppermute | solution.py:448
  135.3 6.4 %collective-permute-done.15.refs_2_ = bf16[64,2048]{1,0:T(8,128)(2,1)S(1)} collective-permute-done((bf16[64,2048]{1,0:T(8,128)(2,1)}, bf16[64,2048]{1,0:T(8,128)(2,1)S(1)}, u32[]{:S(2)}, u32[]{:S(2)}) %collective-permute-start.15) | collective-permute-done | bytes 262176 | tf_op jit(solution)/shard_map/ppermute | solution.py:448
  141.7 5.0 %collective-permute-done.16.refs_3_ = bf16[64,2048]{1,0:T(8,128)(2,1)S(1)} collective-permute-done((bf16[64,2048]{1,0:T(8,128)(2,1)S(1)}, bf16[64,2048]{1,0:T(8,128)(2,1)S(1)}, u32[]{:S(2)}, u32[]{:S(2)}) %collective-permute-start.16) | collective-permute-done | bytes 262176 | tf_op jit(solution)/shard_map/ppermute | solution.py:448
  146.8 1.4 collective-permute-done.20.refs_7_
  148.3 3.2 %shard_map.98 = (f32[512,1536]{1,0:T(8,128)}, f32[512,512]{1,0:T(8,128)}) custom-call(s32[4]{0:T(128)S(1)} %pad_add_fusion.1.place_ref, bf16[64,2048]{1,0:T(8,128)(2,1)} %shard_map.95.refs_1_.refs_0_, bf16[64,2048]{1,0:T(8,128)(2,1)S(1)} %collective-permute-done.14.refs_1_, bf16[64,2048]{1,0:T(8,128)(2,1)S(1)} %collective-permute-done.15.refs_2_, ...), custom_call_target="tpu_custom_call" | custom-call | flops 12999999488 | bytes 6291472 | tf_op jit(solution)/shard_map/pallas_call | solution.py:54
  151.5 3.7 %all-to-all-done.2 = bf16[16,64,512]{2,1,0:T(8,128)(2,1)S(1)} async-done(((bf16[16,64,512]{2,1,0:T(8,128)(2,1)}), bf16[16,64,512]{2,1,0:T(8,128)(2,1)S(1)}, u32[]{:S(2)}, u32[]{:S(2)}) %all-to-all-start.2) | async-done | bytes 1048608 | tf_op jit(solution)/shard_map/all_to_all | solution.py:443
  155.2 1.5 shard_map.97
  (59 shorter events, 13.6 us)
Async XLA Ops:
  3.4 30.9 %all-to-all-start = ((bf16[16,264,128]{2,1,0:T(8,128)(2,1)}), bf16[16,264,128]{2,1,0:T(8,128)(2,1)S(1)}, u32[]{:S(2)}, u32[]{:S(2)}) async-start(bf16[16,264,128]{2,1,0:T(8,128)(2,1)} %get-tuple-element.36), calls=%async_computation | async-start | bytes 2162688 | tf_op jit(solution)/shard_map/all_to_all | solution.py:443
  10.8 1.2 slice-start
  12.1 1.3 copy-start.5
  12.1 1.3 copy-start.9
  14.2 1.0 copy-start.1
  35.6 5.8 %copy-start.6 = (bf16[256,512]{1,0:T(8,128)(2,1)}, bf16[256,512]{1,0:T(8,128)(2,1)S(1)}, u32[]{:S(2)}) copy-start(bf16[256,512]{1,0:T(8,128)(2,1)S(1)} %get-tuple-element.39.near_sent_ref) | copy-start | bytes 786436
  35.6 5.8 %copy-start.7 = (bf16[256,512]{1,0:T(8,128)(2,1)}, bf16[256,512]{1,0:T(8,128)(2,1)S(1)}, u32[]{:S(2)}) copy-start(bf16[256,512]{1,0:T(8,128)(2,1)S(1)} %get-tuple-element.40.far_sent_ref) | copy-start | bytes 786436
  35.6 10.3 %collective-permute-start = (bf16[256,512]{1,0:T(8,128)(2,1)S(1)}, bf16[256,512]{1,0:T(8,128)(2,1)S(1)}, u32[]{:S(2)}, u32[]{:S(2)}) collective-permute-start(bf16[256,512]{1,0:T(8,128)(2,1)S(1)} %get-tuple-element.39.near_sent_ref), channel_id=1, source_target_pairs={{0,2},{2,0},{4,6},{6,4},{8,10},{10,8},{12,14},{14,12},{16,18},{18,... | collective-permute-start | bytes 786440 | tf_op jit(solution)/shard_map/ppermute | solution.py:448
  36.3 9.6 %collective-permute-start.1 = (bf16[256,512]{1,0:T(8,128)(2,1)S(1)}, bf16[256,512]{1,0:T(8,128)(2,1)S(1)}, u32[]{:S(2)}, u32[]{:S(2)}) collective-permute-start(bf16[256,512]{1,0:T(8,128)(2,1)S(1)} %get-tuple-element.40.far_sent_ref), channel_id=1, source_target_pairs={{0,30},{2,4},{4,2},{6,8},{8,6},{10,12},{12,10},{14,16},{16,14},{18... | collective-permute-start | bytes 786440 | tf_op jit(solution)/shard_map/ppermute | solution.py:588
  41.4 27.3 %all-to-all-start.1 = ((bf16[16,64,512]{2,1,0:T(8,128)(2,1)}), bf16[16,64,512]{2,1,0:T(8,128)(2,1)}, u32[]{:S(2)}, u32[]{:S(2)}) async-start(bf16[16,64,512]{2,1,0:T(8,128)(2,1)} %bitcast.13), calls=%async_computation.1 | async-start | bytes 2097152 | tf_op jit(solution)/shard_map/all_to_all | solution.py:443
  82.2 6.0 %collective-permute-start.4 = (bf16[256,2048]{1,0:T(8,128)(2,1)}, bf16[256,2048]{1,0:T(8,128)(2,1)S(1)}, u32[]{:S(2)}, u32[]{:S(2)}) collective-permute-start(bf16[256,2048]{1,0:T(8,128)(2,1)} %get-tuple-element.53), channel_id=1, source_target_pairs={{0,2},{2,0},{4,6},{6,4},{8,10},{10,8},{12,14},{14,12},{16,18},{18,... | collective-permute-start | bytes 3145736 | tf_op jit(solution)/shard_map/ppermute | solution.py:448
  82.8 11.6 %collective-permute-start.2 = (bf16[256,512]{1,0:T(8,128)(2,1)}, bf16[256,512]{1,0:T(8,128)(2,1)}, u32[]{:S(2)}, u32[]{:S(2)}) collective-permute-start(bf16[256,512]{1,0:T(8,128)(2,1)} %get-tuple-element.47), channel_id=1, source_target_pairs={{0,2},{2,0},{4,6},{6,4},{8,10},{10,8},{12,14},{14,12},{16,18},{18,... | collective-permute-start | bytes 786440 | tf_op jit(solution)/shard_map/ppermute | solution.py:448
  82.9 11.5 %collective-permute-start.3 = (bf16[256,512]{1,0:T(8,128)(2,1)}, bf16[256,512]{1,0:T(8,128)(2,1)}, u32[]{:S(2)}, u32[]{:S(2)}) collective-permute-start(bf16[256,512]{1,0:T(8,128)(2,1)} %get-tuple-element.48), channel_id=1, source_target_pairs={{0,30},{2,4},{4,2},{6,8},{8,6},{10,12},{12,10},{14,16},{16,14},{18... | collective-permute-start | bytes 786440 | tf_op jit(solution)/shard_map/ppermute | solution.py:588
  88.2 1.2 copy-start
  90.9 10.4 %collective-permute-start.5 = (bf16[64,2048]{1,0:T(8,128)(2,1)}, bf16[64,2048]{1,0:T(8,128)(2,1)S(1)}, u32[]{:S(2)}, u32[]{:S(2)}) collective-permute-start(bf16[64,2048]{1,0:T(8,128)(2,1)} %get-tuple-element.55), channel_id=1, source_target_pairs={{0,5},{1,4},{2,7},{3,6},{4,1},{5,0},{6,3},{7,2},{8,13},{9,12},{10,... | collective-permute-start | bytes 786440 | tf_op jit(solution)/shard_map/ppermute | solution.py:516
  91.4 12.6 %collective-permute-start.6 = (bf16[64,2048]{1,0:T(8,128)(2,1)}, bf16[64,2048]{1,0:T(8,128)(2,1)}, u32[]{:S(2)}, u32[]{:S(2)}) collective-permute-start(bf16[64,2048]{1,0:T(8,128)(2,1)} %get-tuple-element.56), channel_id=1, source_target_pairs={{0,4},{2,6},{4,0},{6,2},{8,12},{10,14},{12,8},{14,10},{16,20},{18,... | collective-permute-start | bytes 786440 | tf_op jit(solution)/shard_map/ppermute | solution.py:448
  93.9 10.7 %collective-permute-start.7 = (bf16[64,2048]{1,0:T(8,128)(2,1)}, bf16[64,2048]{1,0:T(8,128)(2,1)}, u32[]{:S(2)}, u32[]{:S(2)}) collective-permute-start(bf16[64,2048]{1,0:T(8,128)(2,1)} %get-tuple-element.57), channel_id=1, source_target_pairs={{0,1},{1,0},{2,3},{3,2},{4,5},{5,4},{6,7},{7,6},{8,9},{9,8},{10,11... | collective-permute-start | bytes 786440 | tf_op jit(solution)/shard_map/ppermute | solution.py:448
  106.6 6.2 %collective-permute-start.8 = (bf16[16,2048]{1,0:T(8,128)(2,1)S(1)}, bf16[16,2048]{1,0:T(8,128)(2,1)S(1)}, u32[]{:S(2)}, u32[]{:S(2)}) collective-permute-start(bf16[16,2048]{1,0:T(8,128)(2,1)S(1)} %get-tuple-element.60), channel_id=1, source_target_pairs={{0,24},{2,26},{4,28},{6,30},{8,16},{10,18},{12,20},{14,22},{16,8},... | collective-permute-start | bytes 196616 | tf_op jit(solution)/shard_map/ppermute | solution.py:448
  110.2 6.7 %collective-permute-start.9 = (bf16[16,2048]{1,0:T(8,128)(2,1)S(1)}, bf16[16,2048]{1,0:T(8,128)(2,1)S(1)}, u32[]{:S(2)}, u32[]{:S(2)}) collective-permute-start(bf16[16,2048]{1,0:T(8,128)(2,1)S(1)} %get-tuple-element.61), channel_id=1, source_target_pairs={{0,16},{2,18},{4,20},{6,22},{8,24},{10,26},{12,28},{14,30},{16,0},... | collective-permute-start | bytes 196616 | tf_op jit(solution)/shard_map/ppermute | solution.py:448
  111.4 5.5 %collective-permute-start.10 = (bf16[16,2048]{1,0:T(8,128)(2,1)S(1)}, bf16[16,2048]{1,0:T(8,128)(2,1)S(1)}, u32[]{:S(2)}, u32[]{:S(2)}) collective-permute-start(bf16[16,2048]{1,0:T(8,128)(2,1)S(1)} %get-tuple-element.62), channel_id=1, source_target_pairs={{0,8},{2,10},{4,12},{6,14},{8,0},{10,2},{12,4},{14,6},{16,24},{18,... | collective-permute-start | bytes 196616 | tf_op jit(solution)/shard_map/ppermute | solution.py:448
  117.0 4.5 %collective-permute-start.11 = (bf16[16,2048]{1,0:T(8,128)(2,1)S(1)}, bf16[16,2048]{1,0:T(8,128)(2,1)S(1)}, u32[]{:S(2)}, u32[]{:S(2)}) collective-permute-start(bf16[16,2048]{1,0:T(8,128)(2,1)S(1)} %shard_map.94.refs_0_), channel_id=1, source_target_pairs={{0,8},{2,10},{4,12},{6,14},{8,0},{10,2},{12,4},{14,6},{16,24},{18,... | collective-permute-start | bytes 196616 | tf_op jit(solution)/shard_map/ppermute | solution.py:448
  117.5 8.0 %collective-permute-start.12 = (bf16[16,2048]{1,0:T(8,128)(2,1)S(1)}, bf16[16,2048]{1,0:T(8,128)(2,1)S(1)}, u32[]{:S(2)}, u32[]{:S(2)}) collective-permute-start(bf16[16,2048]{1,0:T(8,128)(2,1)S(1)} %shard_map.94.refs_0_), channel_id=1, source_target_pairs={{0,16},{2,18},{4,20},{6,22},{8,24},{10,26},{12,28},{14,30},{16,0},... | collective-permute-start | bytes 196616 | tf_op jit(solution)/shard_map/ppermute | solution.py:448
  120.9 6.1 %collective-permute-start.13 = (bf16[16,2048]{1,0:T(8,128)(2,1)S(1)}, bf16[16,2048]{1,0:T(8,128)(2,1)S(1)}, u32[]{:S(2)}, u32[]{:S(2)}) collective-permute-start(bf16[16,2048]{1,0:T(8,128)(2,1)S(1)} %shard_map.94.refs_0_), channel_id=1, source_target_pairs={{0,24},{2,26},{4,28},{6,30},{8,16},{10,18},{12,20},{14,22},{16,8},... | collective-permute-start | bytes 196616 | tf_op jit(solution)/shard_map/ppermute | solution.py:448
  127.7 6.7 %collective-permute-start.14 = (bf16[64,2048]{1,0:T(8,128)(2,1)}, bf16[64,2048]{1,0:T(8,128)(2,1)S(1)}, u32[]{:S(2)}, u32[]{:S(2)}) collective-permute-start(bf16[64,2048]{1,0:T(8,128)(2,1)} %shard_map.95.refs_1_.refs_0_), channel_id=1, source_target_pairs={{0,4},{2,6},{4,0},{6,2},{8,12},{10,14},{12,8},{14,10},{16,20},{18,... | collective-permute-start | bytes 786440 | tf_op jit(solution)/shard_map/ppermute | solution.py:448
  127.9 27.3 %all-to-all-start.2 = ((bf16[16,64,512]{2,1,0:T(8,128)(2,1)}), bf16[16,64,512]{2,1,0:T(8,128)(2,1)S(1)}, u32[]{:S(2)}, u32[]{:S(2)}) async-start(bf16[16,64,512]{2,1,0:T(8,128)(2,1)} %bitcast.15), calls=%async_computation.2 | async-start | bytes 2097152 | tf_op jit(solution)/shard_map/all_to_all | solution.py:443
  132.3 9.4 %collective-permute-start.15 = (bf16[64,2048]{1,0:T(8,128)(2,1)}, bf16[64,2048]{1,0:T(8,128)(2,1)S(1)}, u32[]{:S(2)}, u32[]{:S(2)}) collective-permute-start(bf16[64,2048]{1,0:T(8,128)(2,1)} %shard_map.95.refs_1_.refs_0_), channel_id=1, source_target_pairs={{0,1},{1,0},{2,3},{3,2},{4,5},{5,4},{6,7},{7,6},{8,9},{9,8},{10,11... | collective-permute-start | bytes 786440 | tf_op jit(solution)/shard_map/ppermute | solution.py:448
  134.4 12.4 %collective-permute-start.16 = (bf16[64,2048]{1,0:T(8,128)(2,1)S(1)}, bf16[64,2048]{1,0:T(8,128)(2,1)S(1)}, u32[]{:S(2)}, u32[]{:S(2)}) collective-permute-start(bf16[64,2048]{1,0:T(8,128)(2,1)S(1)} %collective-permute-done.14.refs_1_), channel_id=1, source_target_pairs={{0,1},{1,0},{2,3},{3,2},{4,5},{5,4},{6,7},{7,6},{8,9},{9,8},{10,11... | collective-permute-start | bytes 786440 | tf_op jit(solution)/shard_map/ppermute | solution.py:448
  134.8 12.0 %collective-permute-start.17 = (bf16[64,2048]{1,0:T(8,128)(2,1)}, bf16[64,2048]{1,0:T(8,128)(2,1)S(1)}, u32[]{:S(2)}, u32[]{:S(2)}) collective-permute-start(bf16[64,2048]{1,0:T(8,128)(2,1)} %shard_map.95.refs_1_.refs_0_), channel_id=1, source_target_pairs={{0,2},{2,0},{4,6},{6,4},{8,10},{10,8},{12,14},{14,12},{16,18},{18,... | collective-permute-start | bytes 786440 | tf_op jit(solution)/shard_map/ppermute | solution.py:448
  134.8 12.0 %collective-permute-start.18 = (bf16[64,2048]{1,0:T(8,128)(2,1)S(1)}, bf16[64,2048]{1,0:T(8,128)(2,1)S(1)}, u32[]{:S(2)}, u32[]{:S(2)}) collective-permute-start(bf16[64,2048]{1,0:T(8,128)(2,1)S(1)} %collective-permute-done.14.refs_1_), channel_id=1, source_target_pairs={{0,2},{2,0},{4,6},{6,4},{8,10},{10,8},{12,14},{14,12},{16,18},{18,... | collective-permute-start | bytes 786440 | tf_op jit(solution)/shard_map/ppermute | solution.py:448
  141.7 5.1 %collective-permute-start.19 = (bf16[64,2048]{1,0:T(8,128)(2,1)S(1)}, bf16[64,2048]{1,0:T(8,128)(2,1)S(1)}, u32[]{:S(2)}, u32[]{:S(2)}) collective-permute-start(bf16[64,2048]{1,0:T(8,128)(2,1)S(1)} %collective-permute-done.15.refs_2_), channel_id=1, source_target_pairs={{0,2},{2,0},{4,6},{6,4},{8,10},{10,8},{12,14},{14,12},{16,18},{18,... | collective-permute-start | bytes 786440 | tf_op jit(solution)/shard_map/ppermute | solution.py:448
  146.7 1.5 collective-permute-start.20
  146.8 8.4 %copy-start.2 = (bf16[512,1024]{1,0:T(8,128)(2,1)S(1)}, bf16[512,1024]{1,0:T(8,128)(2,1)}, u32[]{:S(2)}) copy-start(bf16[512,1024]{1,0:T(8,128)(2,1)} %copy-done.1) | copy-start | bytes 3145732
  (5 other events, 3.7 us)

commit v8 on v7

--- a/solution.py
+++ b/solution.py
@@ -165,30 +165,40 @@
     core_ref,
     near_hbm,
     far_hbm,
-    own_hbm,
+    grad_query_hbm,
+    grad_kv_hbm,
+    w_hbm,
     table_hbm,
     out_hbm,
     done_ref,
     near_ref,
     far_ref,
-    own_ref,
+    grad_query_ref,
+    grad_kv_ref,
+    w_ref,
     table_ref,
     out_ref,
     sems,
 ):
     done_ref[...] = jnp.zeros_like(done_ref)
     copies = fetch(
-        [near_hbm, far_hbm, own_hbm, table_hbm], [near_ref, far_ref, own_ref, table_ref], sems
+        [grad_query_hbm, w_hbm, grad_kv_hbm, near_hbm, far_hbm, table_hbm],
+        [grad_query_ref, w_ref, grad_kv_ref, near_ref, far_ref, table_ref],
+        sems,
+        4,
     )
     for copy in copies:
         copy.wait()
-    half = near_ref.shape[0]
+    half, width = near_ref.shape
+    own = contract(grad_query_ref[...], w_ref[:, :width], 1, 1) + contract(
+        grad_kv_ref[...], w_ref[:, width:], 1, 1
+    )
     near = near_ref[...].astype(jnp.float32)
     far = far_ref[...].astype(jnp.float32)
     own = jnp.concatenate(
         [
-            own_ref[:half, :] + jnp.where(core_ref[0] == 0, far, near),
-            own_ref[half:, :] + jnp.where(core_ref[0] == 0, near, far),
+            own[:half] + jnp.where(core_ref[0] == 0, far, near),
+            own[half:] + jnp.where(core_ref[0] == 0, near, far),
         ],
         axis=0,
     ).astype(jnp.bfloat16)
@@ -198,7 +208,7 @@
     for i in range(parts):
         rows = pl.ds(i * part, part)
         out_ref[rows, :] = contract(table_ref[rows, :], own, 1, 0).astype(jnp.bfloat16)
-        stores += fetch([out_ref.at[rows, :]], [out_hbm.at[rows, :]], sems, 4 + i)
+        stores += fetch([out_ref.at[rows, :]], [out_hbm.at[rows, :]], sems, i)
     for store in stores:
         store.wait()
 
@@ -317,7 +327,8 @@
     probs_hbm,
     send_hbm,
     keep_hbm,
-    own_hbm,
+    grad_query_hbm,
+    grad_kv_hbm,
     near_hbm,
     far_hbm,
     got_ref,
@@ -334,7 +345,6 @@
     query_t_ref,
     send_ref,
     keep_ref,
-    own_ref,
     near_ref,
     far_ref,
     sems,
@@ -407,13 +417,15 @@
             grad_kv_ref[patch, cols] = (grad_key * scale).astype(jnp.bfloat16)
             grad_kv_ref[patch, value_cols] = grad_value.astype(jnp.bfloat16)
     grad_query_ref[...] = query_t_ref[...].T.astype(jnp.bfloat16)
+    stores = fetch(
+        [grad_query_ref, grad_kv_ref.at[pl.ds(half, 2 * half), :]],
+        [grad_query_hbm, grad_kv_hbm],
+        sems,
+        13 + HEADS,
+    )
     for copy in late:
         copy.wait()
     w_kv = w_ref[:, width:]
-    own_ref[...] = contract(grad_query_ref[...], w_ref[:, :width], 1, 1) + contract(
-        grad_kv_ref[half : 3 * half, :], w_kv, 1, 1
-    )
-    stores = fetch([own_ref], [own_hbm], sems, 8 + HEADS)
     before = contract(grad_kv_ref[:half, :], w_kv, 1, 1).astype(jnp.bfloat16)
     after = contract(grad_kv_ref[3 * half :, :], w_kv, 1, 1).astype(jnp.bfloat16)
     near_ref[...] = jnp.where(core_ref[0] == 0, after, before)
@@ -651,11 +663,12 @@
     made = [
         low(width // 2, 4 * width),
         low(width // 2, 4 * width),
-        wide(rows, width),
+        low(rows, width),
+        low(rows, 2 * width),
         low(half, width),
         low(half, width),
     ]
-    send, keep, own_input, near, far = call(
+    send, keep, grad_query, grad_kv, near, far = call(
         backward_kernel,
         made,
         [core, at, *held],
@@ -664,8 +677,8 @@
         [HBM] * len(made),
         [space(x) for x in held]
         + [space(low(rows, width)), space(low(2 * rows, 2 * width)), space(wide(width, rows))]
-        + [space(x) for x in made]
-        + [pltpu.SemaphoreType.DMA((13 + HEADS,))],
+        + [space(x) for x in (*made[:2], *made[4:])]
+        + [pltpu.SemaphoreType.DMA((15 + HEADS,))],
         63,
     )
     kept, got = sum_core(keep, send, sides)
@@ -674,11 +687,11 @@
     picked, done = call(
         pick_kernel,
         [picked, wide(8, LANES)],
-        [core, near, far, own_input, pick_table],
+        [core, near, far, grad_query, grad_kv, w_qkv, pick_table],
         place_flops,
-        [SMEM] + [HBM] * 4,
+        [SMEM] + [HBM] * 6,
         [HBM, VMEM],
-        [space(x) for x in (near, far, own_input, pick_table, picked)] + [pltpu.SemaphoreType.DMA((8,))],
+        [space(x) for x in (near, far, grad_query, grad_kv, w_qkv, pick_table, picked)] + [pltpu.SemaphoreType.DMA((10,))],
         63,
     )
     mine, sends = sum_xy(kept, got, done)

time: 159 us -> 158 us (level)
  transfers between devices with their start and end apart: 24 -> 24, of which waited for: 14 -> 14; matrix products, arithmetic and copies ran while one was open for 1% -> 1% of each run, Pallas kernels for 13% -> 15%
where the time goes in v8:
time: 158 us; the launch traced here: 156 us
  waiting for transfers between devices  62.3 us (39%)
  starting transfers between devices  42.6 us (27%)
  Pallas kernels  42.4 us (27%)
  local copies, waits for them, and re-layouts  7.78 us (5%)
    pallas_call x12, Pallas kernels, call(): pl.pallas_call(kernel, out_shape=outs, in_specs=ins or [VMEM] * len(args)...  42.4 us
    all_to_all x3, waiting for transfers between devices, exchange(): lax.all_to_all(blocks, 'curve', split_axis=0, concat_axis=0, tiled=True)  32.1 us
    ppermute x18, waiting for transfers between devices, swap(): return lax.ppermute(block, axis, [(i, i ^ mask) for i in range(size)])  28.6 us
    all_to_all x3, starting transfers between devices, exchange(): lax.all_to_all(blocks, 'curve', split_axis=0, concat_axis=0, tiled=True)  16.2 us
    ppermute x18, starting transfers between devices, swap(): return lax.ppermute(block, axis, [(i, i ^ mask) for i in range(size)])  15.7 us
    ppermute x2, starting transfers between devices, halo(): return (swap(near, 'curve', 1), lax.ppermute(far, 'curve', route))  10.2 us
    unnamed x25, local copies, waits for them, and re-layouts  6.56 us
  transfers between devices with their start and end apart: 24, of which 14 were waited for; matrix products, arithmetic and copies ran while one was open for 1% of the time, Pallas kernels for 15%

profile of v8, /device:TPU:0, one launch (start us, length us, event | category | flops | bytes accessed | tf_op | source)
XLA Modules:
  0.0 156.0 jit_solution(13339487828565502568)
XLA Ops:
  0.6 2.8 %shard_map.85 = (bf16[16,264,128]{2,1,0:T(8,128)(2,1)}, s32[1,512]{1,0:T(1,128)}) custom-call(s32[1,512]{1,0:T(1,128)} %dev_hbm.1, s32[1,512]{1,0:T(1,128)} %row_hbm.1, bf16[512,512]{1,0:T(8,128)(2,1)} %bitcast.18), custom_call_target="tpu_custom_call" | custom-call | flops 536870912 | bytes 1611776 | tf_op jit(solution)/shard_map/pallas_call | solution.py:54
  3.4 7.4 %all-to-all-start = ((bf16[16,264,128]{2,1,0:T(8,128)(2,1)}), bf16[16,264,128]{2,1,0:T(8,128)(2,1)S(1)}, u32[]{:S(2)}, u32[]{:S(2)}) async-start(bf16[16,264,128]{2,1,0:T(8,128)(2,1)} %get-tuple-element.37), calls=%async_computation | async-start | bytes 2162688 | tf_op jit(solution)/shard_map/all_to_all | solution.py:455
  10.8 1.2 slice-done
  12.1 1.3 copy.12
  16.2 18.2 %all-to-all-done.got_ref = bf16[16,264,128]{2,1,0:T(8,128)(2,1)S(1)} async-done(((bf16[16,264,128]{2,1,0:T(8,128)(2,1)}), bf16[16,264,128]{2,1,0:T(8,128)(2,1)S(1)}, u32[]{:S(2)}, u32[]{:S(2)}) %all-to-all-start) | async-done | bytes 1081376 | tf_op jit(solution)/shard_map/all_to_all | solution.py:455
  36.3 5.1 %collective-permute-start.1 = (bf16[256,512]{1,0:T(8,128)(2,1)S(1)}, bf16[256,512]{1,0:T(8,128)(2,1)S(1)}, u32[]{:S(2)}, u32[]{:S(2)}) collective-permute-start(bf16[256,512]{1,0:T(8,128)(2,1)S(1)} %get-tuple-element.41.far_sent_ref), channel_id=1, source_target_pairs={{0,30},{2,4},{4,2},{6,8},{8,6},{10,12},{12,10},{14,16},{16,14},{18... | collective-permute-start | bytes 786440 | tf_op jit(solution)/shard_map/ppermute | solution.py:600
  41.4 4.5 %all-to-all-start.1 = ((bf16[16,64,512]{2,1,0:T(8,128)(2,1)}), bf16[16,64,512]{2,1,0:T(8,128)(2,1)}, u32[]{:S(2)}, u32[]{:S(2)}) async-start(bf16[16,64,512]{2,1,0:T(8,128)(2,1)} %bitcast.13), calls=%async_computation.1 | async-start | bytes 2097152 | tf_op jit(solution)/shard_map/all_to_all | solution.py:455
  46.7 11.7 %shard_map.89 = (bf16[512,512]{1,0:T(8,128)(2,1)}, bf16[1024,512]{1,0:T(8,128)(2,1)}, bf16[512,1024]{1,0:T(8,128)(2,1)}, bf16[512,512]{1,0:T(8,128)(2,1)}, bf16[...) custom-call(s32[1]{0:T(128)} %bitcast.2.core_ref, f32[8,128]{1,0:T(8,128)} %copy-done.8, ...), custom_call_target="tpu_custom_call" | custom-call | flops 99999997952 | bytes 13111300 | tf_op jit(solution)/shard_map/pallas_call | solution.py:54
  58.5 10.2 %all-to-all-done.1 = bf16[16,64,512]{2,1,0:T(8,128)(2,1)} async-done(((bf16[16,64,512]{2,1,0:T(8,128)(2,1)}), bf16[16,64,512]{2,1,0:T(8,128)(2,1)}, u32[]{:S(2)}, u32[]{:S(2)}) %all-to-all-start.1) | async-done | bytes 1048608 | tf_op jit(solution)/shard_map/all_to_all | solution.py:455
  68.7 12.7 %shard_map.90 = (bf16[256,2048]{1,0:T(8,128)(2,1)}, bf16[256,2048]{1,0:T(8,128)(2,1)}, bf16[512,512]{1,0:T(8,128)(2,1)}, bf16[512,1024]{1,0:T(8,128)(2,1)}, bf16...) custom-call(s32[1]{0:T(128)} %bitcast.2.core_ref, f32[8,128]{1,0:T(8,128)} %copy-done.8, ...), custom_call_target="tpu_custom_call" | custom-call | flops 7247757312 | bytes 15732740 | tf_op jit(solution)/shard_map/pallas_call | solution.py:54
  82.1 5.2 %collective-permute-start.3 = (bf16[256,512]{1,0:T(8,128)(2,1)}, bf16[256,512]{1,0:T(8,128)(2,1)}, u32[]{:S(2)}, u32[]{:S(2)}) collective-permute-start(bf16[256,512]{1,0:T(8,128)(2,1)} %get-tuple-element.49), channel_id=1, source_target_pairs={{0,30},{2,4},{4,2},{6,8},{8,6},{10,12},{12,10},{14,16},{16,14},{18... | collective-permute-start | bytes 786440 | tf_op jit(solution)/shard_map/ppermute | solution.py:600
  87.4 1.2 copy-done
  88.6 1.5 shard_map.92
  90.6 2.5 %collective-permute-start.6 = (bf16[64,2048]{1,0:T(8,128)(2,1)}, bf16[64,2048]{1,0:T(8,128)(2,1)}, u32[]{:S(2)}, u32[]{:S(2)}) collective-permute-start(bf16[64,2048]{1,0:T(8,128)(2,1)} %get-tuple-element.58), channel_id=1, source_target_pairs={{0,4},{2,6},{4,0},{6,2},{8,12},{10,14},{12,8},{14,10},{16,20},{18,... | collective-permute-start | bytes 786440 | tf_op jit(solution)/shard_map/ppermute | solution.py:460
  93.7 5.3 %shard_map.91 = (bf16[1024,512]{1,0:T(8,128)(2,1)}, f32[8,128]{1,0:T(8,128)}) custom-call(s32[1]{0:T(128)} %bitcast.2.core_ref, bf16[256,512]{1,0:T(8,128)(2,1)} %collective-permute-done.2.near_hbm, bf16[256,512]{1,0:T(8,128)(2,1)} %collective-permute-done.3.far_hbm, bf16[512,512]{1,0:T(8,128)(2,1)} %get-tuple-element.50.grad_query_hbm, ...), custom_call_target="tpu_custom_call" | custom-call | flops 536870912 | bytes 5771268 | tf_op jit(solution)/shard_map/pallas_call | solution.py:54
  99.0 1.5 collective-permute-done.5.refs_0_
  100.6 2.7 %collective-permute-done.6.refs_1_ = bf16[64,2048]{1,0:T(8,128)(2,1)} collective-permute-done((bf16[64,2048]{1,0:T(8,128)(2,1)}, bf16[64,2048]{1,0:T(8,128)(2,1)}, u32[]{:S(2)}, u32[]{:S(2)}) %collective-permute-start.6) | collective-permute-done | bytes 262176 | tf_op jit(solution)/shard_map/ppermute | solution.py:460
  104.6 1.2 shard_map.93
  105.8 3.6 %collective-permute-start.8 = (bf16[16,2048]{1,0:T(8,128)(2,1)S(1)}, bf16[16,2048]{1,0:T(8,128)(2,1)S(1)}, u32[]{:S(2)}, u32[]{:S(2)}) collective-permute-start(bf16[16,2048]{1,0:T(8,128)(2,1)S(1)} %get-tuple-element.62), channel_id=1, source_target_pairs={{0,24},{2,26},{4,28},{6,30},{8,16},{10,18},{12,20},{14,22},{16,8},... | collective-permute-start | bytes 196616 | tf_op jit(solution)/shard_map/ppermute | solution.py:460
  109.4 1.2 collective-permute-start.9
  112.0 4.1 %collective-permute-done.9.refs_1_ = bf16[16,2048]{1,0:T(8,128)(2,1)S(1)} collective-permute-done((bf16[16,2048]{1,0:T(8,128)(2,1)S(1)}, bf16[16,2048]{1,0:T(8,128)(2,1)S(1)}, u32[]{:S(2)}, u32[]{:S(2)}) %collective-permute-start.9) | collective-permute-done | bytes 65568 | tf_op jit(solution)/shard_map/ppermute | solution.py:460
  116.8 3.4 %collective-permute-start.12 = (bf16[16,2048]{1,0:T(8,128)(2,1)S(1)}, bf16[16,2048]{1,0:T(8,128)(2,1)S(1)}, u32[]{:S(2)}, u32[]{:S(2)}) collective-permute-start(bf16[16,2048]{1,0:T(8,128)(2,1)S(1)} %shard_map.94.refs_0_), channel_id=1, source_target_pairs={{0,16},{2,18},{4,20},{6,22},{8,24},{10,26},{12,28},{14,30},{16,0},... | collective-permute-start | bytes 196616 | tf_op jit(solution)/shard_map/ppermute | solution.py:460
  120.6 4.1 %collective-permute-done.12.refs_2_ = bf16[16,2048]{1,0:T(8,128)(2,1)S(1)} collective-permute-done((bf16[16,2048]{1,0:T(8,128)(2,1)S(1)}, bf16[16,2048]{1,0:T(8,128)(2,1)S(1)}, u32[]{:S(2)}, u32[]{:S(2)}) %collective-permute-start.12) | collective-permute-done | bytes 65568 | tf_op jit(solution)/shard_map/ppermute | solution.py:460
  124.7 1.5 collective-permute-done.13.refs_3_
  127.2 4.3 %all-to-all-start.2 = ((bf16[16,64,512]{2,1,0:T(8,128)(2,1)}), bf16[16,64,512]{2,1,0:T(8,128)(2,1)S(1)}, u32[]{:S(2)}, u32[]{:S(2)}) async-start(bf16[16,64,512]{2,1,0:T(8,128)(2,1)} %bitcast.15), calls=%async_computation.2 | async-start | bytes 2097152 | tf_op jit(solution)/shard_map/all_to_all | solution.py:455
  132.0 1.6 %collective-permute-done.14.refs_1_ = bf16[64,2048]{1,0:T(8,128)(2,1)S(1)} collective-permute-done((bf16[64,2048]{1,0:T(8,128)(2,1)}, bf16[64,2048]{1,0:T(8,128)(2,1)S(1)}, u32[]{:S(2)}, u32[]{:S(2)}) %collective-permute-start.14) | collective-permute-done | bytes 262176 | tf_op jit(solution)/shard_map/ppermute | solution.py:460
  134.5 6.4 %collective-permute-done.15.refs_2_ = bf16[64,2048]{1,0:T(8,128)(2,1)S(1)} collective-permute-done((bf16[64,2048]{1,0:T(8,128)(2,1)}, bf16[64,2048]{1,0:T(8,128)(2,1)S(1)}, u32[]{:S(2)}, u32[]{:S(2)}) %collective-permute-start.15) | collective-permute-done | bytes 262176 | tf_op jit(solution)/shard_map/ppermute | solution.py:460
  140.9 5.0 %collective-permute-done.16.refs_3_ = bf16[64,2048]{1,0:T(8,128)(2,1)S(1)} collective-permute-done((bf16[64,2048]{1,0:T(8,128)(2,1)S(1)}, bf16[64,2048]{1,0:T(8,128)(2,1)S(1)}, u32[]{:S(2)}, u32[]{:S(2)}) %collective-permute-start.16) | collective-permute-done | bytes 262176 | tf_op jit(solution)/shard_map/ppermute | solution.py:460
  146.1 1.4 collective-permute-done.20.refs_7_
  147.5 3.2 %shard_map.98 = (f32[512,1536]{1,0:T(8,128)}, f32[512,512]{1,0:T(8,128)}) custom-call(s32[4]{0:T(128)S(1)} %pad_add_fusion.1.place_ref, bf16[64,2048]{1,0:T(8,128)(2,1)} %shard_map.95.refs_1_.refs_0_, bf16[64,2048]{1,0:T(8,128)(2,1)S(1)} %collective-permute-done.14.refs_1_, bf16[64,2048]{1,0:T(8,128)(2,1)S(1)} %collective-permute-done.15.refs_2_, ...), custom_call_target="tpu_custom_call" | custom-call | flops 12999999488 | bytes 6291472 | tf_op jit(solution)/shard_map/pallas_call | solution.py:54
  150.8 3.7 %all-to-all-done.2 = bf16[16,64,512]{2,1,0:T(8,128)(2,1)S(1)} async-done(((bf16[16,64,512]{2,1,0:T(8,128)(2,1)}), bf16[16,64,512]{2,1,0:T(8,128)(2,1)S(1)}, u32[]{:S(2)}, u32[]{:S(2)}) %all-to-all-start.2) | async-done | bytes 1048608 | tf_op jit(solution)/shard_map/all_to_all | solution.py:455
  154.5 1.5 shard_map.97
  (59 shorter events, 13.6 us)
Async XLA Ops:
  3.4 30.9 %all-to-all-start = ((bf16[16,264,128]{2,1,0:T(8,128)(2,1)}), bf16[16,264,128]{2,1,0:T(8,128)(2,1)S(1)}, u32[]{:S(2)}, u32[]{:S(2)}) async-start(bf16[16,264,128]{2,1,0:T(8,128)(2,1)} %get-tuple-element.37), calls=%async_computation | async-start | bytes 2162688 | tf_op jit(solution)/shard_map/all_to_all | solution.py:455
  10.8 1.2 slice-start
  12.1 1.3 copy-start.5
  12.1 1.3 copy-start.9
  14.2 1.0 copy-start.1
  35.6 5.8 %copy-start.6 = (bf16[256,512]{1,0:T(8,128)(2,1)}, bf16[256,512]{1,0:T(8,128)(2,1)S(1)}, u32[]{:S(2)}) copy-start(bf16[256,512]{1,0:T(8,128)(2,1)S(1)} %get-tuple-element.40.near_sent_ref) | copy-start | bytes 786436
  35.6 5.8 %copy-start.7 = (bf16[256,512]{1,0:T(8,128)(2,1)}, bf16[256,512]{1,0:T(8,128)(2,1)S(1)}, u32[]{:S(2)}) copy-start(bf16[256,512]{1,0:T(8,128)(2,1)S(1)} %get-tuple-element.41.far_sent_ref) | copy-start | bytes 786436
  35.6 10.3 %collective-permute-start = (bf16[256,512]{1,0:T(8,128)(2,1)S(1)}, bf16[256,512]{1,0:T(8,128)(2,1)S(1)}, u32[]{:S(2)}, u32[]{:S(2)}) collective-permute-start(bf16[256,512]{1,0:T(8,128)(2,1)S(1)} %get-tuple-element.40.near_sent_ref), channel_id=1, source_target_pairs={{0,2},{2,0},{4,6},{6,4},{8,10},{10,8},{12,14},{14,12},{16,18},{18,... | collective-permute-start | bytes 786440 | tf_op jit(solution)/shard_map/ppermute | solution.py:460
  36.3 9.6 %collective-permute-start.1 = (bf16[256,512]{1,0:T(8,128)(2,1)S(1)}, bf16[256,512]{1,0:T(8,128)(2,1)S(1)}, u32[]{:S(2)}, u32[]{:S(2)}) collective-permute-start(bf16[256,512]{1,0:T(8,128)(2,1)S(1)} %get-tuple-element.41.far_sent_ref), channel_id=1, source_target_pairs={{0,30},{2,4},{4,2},{6,8},{8,6},{10,12},{12,10},{14,16},{16,14},{18... | collective-permute-start | bytes 786440 | tf_op jit(solution)/shard_map/ppermute | solution.py:600
  41.4 27.3 %all-to-all-start.1 = ((bf16[16,64,512]{2,1,0:T(8,128)(2,1)}), bf16[16,64,512]{2,1,0:T(8,128)(2,1)}, u32[]{:S(2)}, u32[]{:S(2)}) async-start(bf16[16,64,512]{2,1,0:T(8,128)(2,1)} %bitcast.13), calls=%async_computation.1 | async-start | bytes 2097152 | tf_op jit(solution)/shard_map/all_to_all | solution.py:455
  81.4 6.0 %collective-permute-start.4 = (bf16[256,2048]{1,0:T(8,128)(2,1)}, bf16[256,2048]{1,0:T(8,128)(2,1)S(1)}, u32[]{:S(2)}, u32[]{:S(2)}) collective-permute-start(bf16[256,2048]{1,0:T(8,128)(2,1)} %get-tuple-element.55), channel_id=1, source_target_pairs={{0,2},{2,0},{4,6},{6,4},{8,10},{10,8},{12,14},{14,12},{16,18},{18,... | collective-permute-start | bytes 3145736 | tf_op jit(solution)/shard_map/ppermute | solution.py:460
  82.1 11.6 %collective-permute-start.2 = (bf16[256,512]{1,0:T(8,128)(2,1)}, bf16[256,512]{1,0:T(8,128)(2,1)}, u32[]{:S(2)}, u32[]{:S(2)}) collective-permute-start(bf16[256,512]{1,0:T(8,128)(2,1)} %get-tuple-element.48), channel_id=1, source_target_pairs={{0,2},{2,0},{4,6},{6,4},{8,10},{10,8},{12,14},{14,12},{16,18},{18,... | collective-permute-start | bytes 786440 | tf_op jit(solution)/shard_map/ppermute | solution.py:460
  82.1 11.5 %collective-permute-start.3 = (bf16[256,512]{1,0:T(8,128)(2,1)}, bf16[256,512]{1,0:T(8,128)(2,1)}, u32[]{:S(2)}, u32[]{:S(2)}) collective-permute-start(bf16[256,512]{1,0:T(8,128)(2,1)} %get-tuple-element.49), channel_id=1, source_target_pairs={{0,30},{2,4},{4,2},{6,8},{8,6},{10,12},{12,10},{14,16},{16,14},{18... | collective-permute-start | bytes 786440 | tf_op jit(solution)/shard_map/ppermute | solution.py:600
  87.4 1.2 copy-start
  90.2 10.4 %collective-permute-start.5 = (bf16[64,2048]{1,0:T(8,128)(2,1)}, bf16[64,2048]{1,0:T(8,128)(2,1)S(1)}, u32[]{:S(2)}, u32[]{:S(2)}) collective-permute-start(bf16[64,2048]{1,0:T(8,128)(2,1)} %get-tuple-element.57), channel_id=1, source_target_pairs={{0,5},{1,4},{2,7},{3,6},{4,1},{5,0},{6,3},{7,2},{8,13},{9,12},{10,... | collective-permute-start | bytes 786440 | tf_op jit(solution)/shard_map/ppermute | solution.py:528
  90.6 12.6 %collective-permute-start.6 = (bf16[64,2048]{1,0:T(8,128)(2,1)}, bf16[64,2048]{1,0:T(8,128)(2,1)}, u32[]{:S(2)}, u32[]{:S(2)}) collective-permute-start(bf16[64,2048]{1,0:T(8,128)(2,1)} %get-tuple-element.58), channel_id=1, source_target_pairs={{0,4},{2,6},{4,0},{6,2},{8,12},{10,14},{12,8},{14,10},{16,20},{18,... | collective-permute-start | bytes 786440 | tf_op jit(solution)/shard_map/ppermute | solution.py:460
  93.2 10.7 %collective-permute-start.7 = (bf16[64,2048]{1,0:T(8,128)(2,1)}, bf16[64,2048]{1,0:T(8,128)(2,1)}, u32[]{:S(2)}, u32[]{:S(2)}) collective-permute-start(bf16[64,2048]{1,0:T(8,128)(2,1)} %get-tuple-element.59), channel_id=1, source_target_pairs={{0,1},{1,0},{2,3},{3,2},{4,5},{5,4},{6,7},{7,6},{8,9},{9,8},{10,11... | collective-permute-start | bytes 786440 | tf_op jit(solution)/shard_map/ppermute | solution.py:460
  105.8 6.2 %collective-permute-start.8 = (bf16[16,2048]{1,0:T(8,128)(2,1)S(1)}, bf16[16,2048]{1,0:T(8,128)(2,1)S(1)}, u32[]{:S(2)}, u32[]{:S(2)}) collective-permute-start(bf16[16,2048]{1,0:T(8,128)(2,1)S(1)} %get-tuple-element.62), channel_id=1, source_target_pairs={{0,24},{2,26},{4,28},{6,30},{8,16},{10,18},{12,20},{14,22},{16,8},... | collective-permute-start | bytes 196616 | tf_op jit(solution)/shard_map/ppermute | solution.py:460
  109.4 6.7 %collective-permute-start.9 = (bf16[16,2048]{1,0:T(8,128)(2,1)S(1)}, bf16[16,2048]{1,0:T(8,128)(2,1)S(1)}, u32[]{:S(2)}, u32[]{:S(2)}) collective-permute-start(bf16[16,2048]{1,0:T(8,128)(2,1)S(1)} %get-tuple-element.63), channel_id=1, source_target_pairs={{0,16},{2,18},{4,20},{6,22},{8,24},{10,26},{12,28},{14,30},{16,0},... | collective-permute-start | bytes 196616 | tf_op jit(solution)/shard_map/ppermute | solution.py:460
  110.7 5.5 %collective-permute-start.10 = (bf16[16,2048]{1,0:T(8,128)(2,1)S(1)}, bf16[16,2048]{1,0:T(8,128)(2,1)S(1)}, u32[]{:S(2)}, u32[]{:S(2)}) collective-permute-start(bf16[16,2048]{1,0:T(8,128)(2,1)S(1)} %get-tuple-element.64), channel_id=1, source_target_pairs={{0,8},{2,10},{4,12},{6,14},{8,0},{10,2},{12,4},{14,6},{16,24},{18,... | collective-permute-start | bytes 196616 | tf_op jit(solution)/shard_map/ppermute | solution.py:460
  116.2 4.5 %collective-permute-start.11 = (bf16[16,2048]{1,0:T(8,128)(2,1)S(1)}, bf16[16,2048]{1,0:T(8,128)(2,1)S(1)}, u32[]{:S(2)}, u32[]{:S(2)}) collective-permute-start(bf16[16,2048]{1,0:T(8,128)(2,1)S(1)} %shard_map.94.refs_0_), channel_id=1, source_target_pairs={{0,8},{2,10},{4,12},{6,14},{8,0},{10,2},{12,4},{14,6},{16,24},{18,... | collective-permute-start | bytes 196616 | tf_op jit(solution)/shard_map/ppermute | solution.py:460
  116.8 8.0 %collective-permute-start.12 = (bf16[16,2048]{1,0:T(8,128)(2,1)S(1)}, bf16[16,2048]{1,0:T(8,128)(2,1)S(1)}, u32[]{:S(2)}, u32[]{:S(2)}) collective-permute-start(bf16[16,2048]{1,0:T(8,128)(2,1)S(1)} %shard_map.94.refs_0_), channel_id=1, source_target_pairs={{0,16},{2,18},{4,20},{6,22},{8,24},{10,26},{12,28},{14,30},{16,0},... | collective-permute-start | bytes 196616 | tf_op jit(solution)/shard_map/ppermute | solution.py:460
  120.1 6.1 %collective-permute-start.13 = (bf16[16,2048]{1,0:T(8,128)(2,1)S(1)}, bf16[16,2048]{1,0:T(8,128)(2,1)S(1)}, u32[]{:S(2)}, u32[]{:S(2)}) collective-permute-start(bf16[16,2048]{1,0:T(8,128)(2,1)S(1)} %shard_map.94.refs_0_), channel_id=1, source_target_pairs={{0,24},{2,26},{4,28},{6,30},{8,16},{10,18},{12,20},{14,22},{16,8},... | collective-permute-start | bytes 196616 | tf_op jit(solution)/shard_map/ppermute | solution.py:460
  126.9 6.7 %collective-permute-start.14 = (bf16[64,2048]{1,0:T(8,128)(2,1)}, bf16[64,2048]{1,0:T(8,128)(2,1)S(1)}, u32[]{:S(2)}, u32[]{:S(2)}) collective-permute-start(bf16[64,2048]{1,0:T(8,128)(2,1)} %shard_map.95.refs_1_.refs_0_), channel_id=1, source_target_pairs={{0,4},{2,6},{4,0},{6,2},{8,12},{10,14},{12,8},{14,10},{16,20},{18,... | collective-permute-start | bytes 786440 | tf_op jit(solution)/shard_map/ppermute | solution.py:460
  127.2 27.3 %all-to-all-start.2 = ((bf16[16,64,512]{2,1,0:T(8,128)(2,1)}), bf16[16,64,512]{2,1,0:T(8,128)(2,1)S(1)}, u32[]{:S(2)}, u32[]{:S(2)}) async-start(bf16[16,64,512]{2,1,0:T(8,128)(2,1)} %bitcast.15), calls=%async_computation.2 | async-start | bytes 2097152 | tf_op jit(solution)/shard_map/all_to_all | solution.py:455
  131.5 9.4 %collective-permute-start.15 = (bf16[64,2048]{1,0:T(8,128)(2,1)}, bf16[64,2048]{1,0:T(8,128)(2,1)S(1)}, u32[]{:S(2)}, u32[]{:S(2)}) collective-permute-start(bf16[64,2048]{1,0:T(8,128)(2,1)} %shard_map.95.refs_1_.refs_0_), channel_id=1, source_target_pairs={{0,1},{1,0},{2,3},{3,2},{4,5},{5,4},{6,7},{7,6},{8,9},{9,8},{10,11... | collective-permute-start | bytes 786440 | tf_op jit(solution)/shard_map/ppermute | solution.py:460
  133.6 12.4 %collective-permute-start.16 = (bf16[64,2048]{1,0:T(8,128)(2,1)S(1)}, bf16[64,2048]{1,0:T(8,128)(2,1)S(1)}, u32[]{:S(2)}, u32[]{:S(2)}) collective-permute-start(bf16[64,2048]{1,0:T(8,128)(2,1)S(1)} %collective-permute-done.14.refs_1_), channel_id=1, source_target_pairs={{0,1},{1,0},{2,3},{3,2},{4,5},{5,4},{6,7},{7,6},{8,9},{9,8},{10,11... | collective-permute-start | bytes 786440 | tf_op jit(solution)/shard_map/ppermute | solution.py:460
  134.0 12.0 %collective-permute-start.17 = (bf16[64,2048]{1,0:T(8,128)(2,1)}, bf16[64,2048]{1,0:T(8,128)(2,1)S(1)}, u32[]{:S(2)}, u32[]{:S(2)}) collective-permute-start(bf16[64,2048]{1,0:T(8,128)(2,1)} %shard_map.95.refs_1_.refs_0_), channel_id=1, source_target_pairs={{0,2},{2,0},{4,6},{6,4},{8,10},{10,8},{12,14},{14,12},{16,18},{18,... | collective-permute-start | bytes 786440 | tf_op jit(solution)/shard_map/ppermute | solution.py:460
  134.0 12.0 %collective-permute-start.18 = (bf16[64,2048]{1,0:T(8,128)(2,1)S(1)}, bf16[64,2048]{1,0:T(8,128)(2,1)S(1)}, u32[]{:S(2)}, u32[]{:S(2)}) collective-permute-start(bf16[64,2048]{1,0:T(8,128)(2,1)S(1)} %collective-permute-done.14.refs_1_), channel_id=1, source_target_pairs={{0,2},{2,0},{4,6},{6,4},{8,10},{10,8},{12,14},{14,12},{16,18},{18,... | collective-permute-start | bytes 786440 | tf_op jit(solution)/shard_map/ppermute | solution.py:460
  140.9 5.1 %collective-permute-start.19 = (bf16[64,2048]{1,0:T(8,128)(2,1)S(1)}, bf16[64,2048]{1,0:T(8,128)(2,1)S(1)}, u32[]{:S(2)}, u32[]{:S(2)}) collective-permute-start(bf16[64,2048]{1,0:T(8,128)(2,1)S(1)} %collective-permute-done.15.refs_2_), channel_id=1, source_target_pairs={{0,2},{2,0},{4,6},{6,4},{8,10},{10,8},{12,14},{14,12},{16,18},{18,... | collective-permute-start | bytes 786440 | tf_op jit(solution)/shard_map/ppermute | solution.py:460
  146.0 1.5 collective-permute-start.20
  146.0 8.4 %copy-start.2 = (bf16[512,1024]{1,0:T(8,128)(2,1)S(1)}, bf16[512,1024]{1,0:T(8,128)(2,1)}, u32[]{:S(2)}) copy-start(bf16[512,1024]{1,0:T(8,128)(2,1)} %copy-done.1) | copy-start | bytes 3145732
  (5 other events, 3.7 us)
